TPU v7x, 32 devices: a whole 2x2x4 slice. The times are simulated.
32 devices in a mesh: groups: 2 (over x), bulk: 16 (over z, y, core).
Axes of the slice: x: 2, y: 2, z: 4, core: 2. Of those that a mesh axis runs over, the one named last changes fastest.
Arguments:
- grid_in: bfloat16 [65536, 474], P(('groups', 'bulk')), parts along dimension 0, may hold values from -6 to 6
- grid_first: bfloat16 [474, 512], replicated, may hold values from -0.25 to 0.25
- grid_bias: float32 [512], replicated, may hold values from -4 to 4
- grid_second: bfloat16 [512, 512], replicated, may hold values from -0.25 to 0.25
- send_weight: bfloat16 [512, 512], replicated, may hold values from -0.25 to 0.25
- edge_bias: float32 [512], replicated, may hold values from -4 to 4
- feat_weight: bfloat16 [4, 512], replicated, may hold values from -3 to 3
- edge_out: bfloat16 [512, 512], replicated, may hold values from -0.0625 to 0.0625
- node_input: bfloat16 [1024, 512], replicated, may hold values from -0.1875 to 0.1875
- node_bias: float32 [512], replicated, may hold values from -4 to 4
- node_out: bfloat16 [512, 512], replicated, may hold values from -0.25 to 0.25
- node_gain: float32 [512], replicated, may hold values from 0.1 to 1.9
- mesh_sender: bfloat16 [512, 512], replicated, may hold values from -0.25 to 0.25
- mesh_receiver: bfloat16 [512, 512], replicated, may hold values from -0.25 to 0.25
- message_bias: float32 [512], replicated, may hold values from -4 to 4
- message_out: bfloat16 [512, 512], replicated, may hold values from -0.09375 to 0.09375
- update_input: bfloat16 [1024, 512], replicated, may hold values from -0.1875 to 0.1875
- update_bias: float32 [512], replicated, may hold values from -4 to 4
- update_out: bfloat16 [512, 512], replicated, may hold values from -0.25 to 0.25
- update_gain: float32 [512], replicated, may hold values from 0.1 to 1.9
- mesh_latent: bfloat16 [1024, 512], P('bulk'), may hold values from -6 to 6
- g2m_send: int32 [384, 128], P('bulk'), may hold values from 0 to 2047
- g2m_recv: int32 [384, 128], P('bulk'), may hold values from 0 to 1023, as said below
- g2m_feat: float32 [384, 4, 128], P('bulk'), may hold values from -6 to 6
- g2m_count: int32 [16], P('bulk'), may hold values from 1 to 24, as said below
- mesh_slot: int32 [1024], replicated, may hold values from 0 to 1023, as said below
- mesh_send: int32 [64, 128], P('bulk'), may hold values from 0 to 1023, as said below
- mesh_recv: int32 [64, 128], P('bulk'), may hold values from 0 to 1023, as said below
Outputs:
- mesh_out: bfloat16 [2048, 512], P(('groups', 'bulk')), parts along dimension 0
There are 2 independent parts, one for each index of `groups`. A program takes and returns all parts, laid end to end along the dimension named above; an argument that names none is the same for every part. Nothing has to cross between parts.
Inputs may be any that keep to these rules, and one draw needn't show every extreme that they name: `mesh_slot`: A permutation: mesh node id to storage row; row r belongs to bulk device r // 64. `g2m_recv`: in every block, used or not, mesh_slot[id] // 64 differs by at most 1 from the bulk index of the device holding the block. `g2m_count`: blocks past the count are padding; some device is full and some device uses one block. `mesh_send`: among the edges of one device's blocks, the senders owned by any one bulk device (mesh_slot[id] // 64) are at most 16 distinct nodes; every device reaches 16 for some owner. `mesh_recv`: mesh_slot[id] // 64 equals the bulk index of the device holding the block.
All inputs are finite; a program needn't handle non-finite values.
Results may differ from a plain program's by a relative error of at most 0.015.
Values may be sent and summed in bfloat16 or wider, within the bound.
No kernel may reach another device: no remote copies, remote signals or barrier semaphores. Data moves between devices by JAX's collectives and lax.ppermute only.
A program may use at most 64 MiB of HBM per device.

v0:
```python
import math

import jax
import jax.numpy as jnp
from jax import lax
from jax.sharding import PartitionSpec as P


def from_behind(value, axis, steps):
    count = lax.axis_size(axis)
    leading, last = (max(0, -steps), min(count, count - steps))
    return lax.ppermute(value, axis, [(source, source + steps) for source in range(leading, last)])


def layer_norm(value):
    center = value - jnp.mean(value, axis=-1, keepdims=True)
    spread = jnp.mean(center * center, axis=-1, keepdims=True)
    return center * lax.rsqrt(spread + 1e-05)


def per_device(
    grid_in,
    grid_first,
    grid_bias,
    grid_second,
    send_weight,
    edge_bias,
    feat_weight,
    edge_out,
    node_input,
    node_bias,
    node_out,
    node_gain,
    mesh_sender,
    mesh_receiver,
    message_bias,
    message_out,
    update_input,
    update_bias,
    update_out,
    update_gain,
    mesh_latent,
    g2m_send,
    g2m_recv,
    g2m_feat,
    g2m_count,
    mesh_slot,
    mesh_send,
    mesh_recv,
):
    f32 = jnp.float32
    bf16 = jnp.bfloat16
    position = lax.axis_index("bulk")
    owned = mesh_latent.shape[0]
    width = grid_second.shape[1]
    blocks = g2m_send.shape[0]
    block_edges = g2m_send.shape[1]
    grid_rows = grid_in.shape[0]
    grid_hidden = jax.nn.silu(
        jnp.dot(grid_in, grid_first, preferred_element_type=f32) + grid_bias
    ).astype(bf16)
    grid_code = layer_norm(jnp.dot(grid_hidden, grid_second, preferred_element_type=f32)).astype(
        bf16
    )
    sender_part = (jnp.dot(grid_code, send_weight, preferred_element_type=f32) + edge_bias).astype(
        bf16
    )
    group = math.gcd(blocks, max(1, 512 // block_edges))
    feat_width = g2m_feat.shape[1]
    send_groups = g2m_send.reshape(blocks // group, group * block_edges)
    feat_groups = g2m_feat.reshape(blocks // group, group, feat_width, block_edges)
    feat_table = feat_weight.astype(f32)
    grid_iota = jnp.arange(grid_rows, dtype=jnp.int32)

    def edge_group(operands):
        senders, feats = operands
        picker = (senders[:, None] == grid_iota[None, :]).astype(bf16)
        chosen = jnp.dot(picker, sender_part, preferred_element_type=f32)
        extra = jnp.einsum("bfe,fl->bel", feats, feat_table).reshape(-1, width)
        return jax.nn.silu(chosen + extra).astype(bf16)

    hidden = lax.map(edge_group, (send_groups, feat_groups)).reshape(-1, width)
    keep = jnp.arange(blocks, dtype=jnp.int32) < g2m_count[0]
    keep_edges = jnp.repeat(keep, block_edges)
    target = mesh_slot[g2m_recv.reshape(-1)]
    local_rows = target - (position - 1) * owned
    spread_rows = (
        (jnp.arange(3 * owned, dtype=jnp.int32)[:, None] == local_rows[None, :])
        & keep_edges[None, :]
    ).astype(bf16)
    buffer = jnp.dot(spread_rows, hidden, preferred_element_type=f32)
    from_below = from_behind(buffer[2 * owned :].astype(jnp.bfloat16), "bulk", 1).astype(
        jnp.float32
    )
    from_above = from_behind(buffer[:owned].astype(jnp.bfloat16), "bulk", -1).astype(jnp.float32)
    node_total = buffer[owned : 2 * owned] + from_below + from_above
    node_sum = node_total.astype(bf16)
    aggregate = jnp.dot(node_sum, edge_out, preferred_element_type=f32).astype(bf16)
    joined = jnp.concatenate([mesh_latent, aggregate], axis=1)
    node_hidden = jax.nn.silu(
        jnp.dot(joined, node_input, preferred_element_type=f32) + node_bias
    ).astype(bf16)
    encoded = (
        mesh_latent.astype(f32)
        + layer_norm(jnp.dot(node_hidden, node_out, preferred_element_type=f32)) * node_gain
    ).astype(bf16)
    sender_code = jnp.dot(encoded, mesh_sender, preferred_element_type=f32).astype(bf16)
    receiver_code = jnp.dot(encoded, mesh_receiver, preferred_element_type=f32) + message_bias
    send_rows = mesh_slot[mesh_send.reshape(-1)]
    recv_rows = mesh_slot[mesh_recv.reshape(-1)] - position * owned
    owned_iota = jnp.arange(owned, dtype=jnp.int32)
    piece = lax.all_gather(sender_code, "bulk", axis=0, tiled=True)
    wanted = send_rows[:, None] == jnp.arange(piece.shape[0], dtype=jnp.int32)[None, :]
    gathered = jnp.dot(wanted.astype(bf16), piece, preferred_element_type=f32)
    recv_pick = (recv_rows[:, None] == owned_iota[None, :]).astype(f32)
    receiver_rows = jnp.dot(
        recv_pick, receiver_code, preferred_element_type=f32, precision=lax.Precision.HIGHEST
    )
    message = jax.nn.silu(gathered + receiver_rows).astype(bf16)
    incoming = (owned_iota[:, None] == recv_rows[None, :]).astype(bf16)
    message_sum = jnp.dot(incoming, message, preferred_element_type=f32).astype(bf16)
    update = jnp.dot(message_sum, message_out, preferred_element_type=f32).astype(bf16)
    joined_two = jnp.concatenate([encoded, update], axis=1)
    update_hidden = jax.nn.silu(
        jnp.dot(joined_two, update_input, preferred_element_type=f32) + update_bias
    ).astype(bf16)
    mesh_out = (
        encoded.astype(f32)
        + layer_norm(jnp.dot(update_hidden, update_out, preferred_element_type=f32)) * update_gain
    )
    return mesh_out.astype(bf16)


def solution(mesh):
    placed = (
        P(("groups", "bulk"), None),
        P(),
        P(),
        P(),
        P(),
        P(),
        P(),
        P(),
        P(),
        P(),
        P(),
        P(),
        P(),
        P(),
        P(),
        P(),
        P(),
        P(),
        P(),
        P(),
        P("bulk", None),
        P("bulk", None),
        P("bulk", None),
        P("bulk", None, None),
        P("bulk"),
        P(),
        P("bulk", None),
        P("bulk", None),
    )
    return jax.shard_map(
        per_device,
        mesh=mesh,
        in_specs=placed,
        out_specs=P(("groups", "bulk"), None),
        check_vma=False,
    )
```

profile of v0, /device:TPU:0, one launch (start us, length us, event | category | flops | bytes accessed | tf_op | source)
XLA Modules:
  0.0 130.4 jit_solution(14765138865223718868)
XLA Ops:
  6.5 0.0 copy-start
  6.5 0.0 all-gather.2.cloned.1.call-start
  6.5 1.5 %copy-done = bf16[2048,474]{0,1:T(8,128)(2,1)S(1)} copy-done((bf16[2048,474]{0,1:T(8,128)(2,1)S(1)}, bf16[2048,474]{0,1:T(8,128)(2,1)}, u32[]{:S(2)}) %copy-start) | copy-done | bytes 1941528
  8.1 6.0 %fusion.55 = (f32[2048]{0:T(1024)S(1)}, f32[2048,512]{0,1:T(8,128)}) fusion(bf16[512,512]{1,0:T(8,128)(2,1)} %param.33, bf16[2048,474]{0,1:T(8,128)(2,1)S(1)} %copy-done, bf16[474,512]{1,0:T(8,128)(2,1)} %param.31, f32[512]{0:T(512)} %param.32), kind=kOutput, calls=%fused_computation.87 | convolution fusion | flops 2075129856 | bytes 7155712 | tf_op jit(solution)/shard_map/dot_general | solution.py:62
  14.1 2.7 %multiply_reduce_fusion = f32[2048]{0:T(1024)S(1)} fusion(f32[2048,512]{0,1:T(8,128)} %get-tuple-element.72, f32[2048]{0:T(1024)S(1)} %broadcast_multiply_fusion), kind=kLoop, calls=%fused_computation.17 | loop fusion | flops 3143680 | bytes 4210688 | tf_op jit(solution)/shard_map/reduce_sum | solution.py:17
  16.8 0.0 copy-done.6
  16.8 0.0 copy-done.7
  16.9 0.0 copy-done.14
  16.9 0.0 copy-done.16
  16.9 0.0 copy-start.15
  16.9 4.9 %add_convert_fusion = bf16[2048,512]{1,0:T(8,128)(2,1)} fusion(bf16[512,512]{1,0:T(8,128)(2,1)S(1)} %copy-done.14, f32[2048,512]{0,1:T(8,128)} %get-tuple-element.72, f32[512]{0:T(512)S(1)} %copy-done.16, f32[2048]{0:T(1024)S(1)} %add_rsqrt_fusion, f32[2048]{0:T(1024)S(1)} %broadcast_multiply_fusion), kind=kOutput, calls=%fused_computation.15 | convolution fusion | flops 1078984704 | bytes 6834176 | tf_op jit(solution)/shard_map/dot_general | solution.py:65
  21.8 0.0 copy-done.15
  21.8 25.2 %while.11 = (s32[]{:T(128)}, bf16[6,512,512]{2,1,0:T(8,128)(2,1)}, s32[6,512]{1,0:T(8,128)S(1)}, bf16[2048,512]{1,0:T(8,128)(2,1)}, bf16[6,4,4,128]{3,2,1,0:T(4,...) while((s32[]{:T(128)}, bf16[6,512,512]{2,1,0:T(8,128)(2,1)}, s32[6,512]{1,0:T(8,128)S(1)}, ...), condition=%wide.region_3.4_spmd.clone, body=%wide.region_2.3_spmd.clone.sunk | while | flops 1078460416 | bytes 4734033 | solution.py:82
  21.8 2.9 %fusion.91 = f32[512,512]{1,0:T(8,128)S(1)} fusion(bf16[2048,512]{1,0:T(8,128)(2,1)} %get-tuple-element.133, s32[512]{0:T(512)S(1)} %bitcast.54), kind=kOutput, calls=%fused_computation.5.clone.1 | convolution fusion | flops 1074790400 | bytes 3147776 | tf_op jit(solution)/shard_map/while/body/eval_jaxpr/dot_general | solution.py:78
  24.7 1.3 fusion.92
  26.0 2.9 %fusion.91 = f32[512,512]{1,0:T(8,128)S(1)} fusion(bf16[2048,512]{1,0:T(8,128)(2,1)} %get-tuple-element.133, s32[512]{0:T(512)S(1)} %bitcast.54), kind=kOutput, calls=%fused_computation.5.clone.1 | convolution fusion | flops 1074790400 | bytes 3147776 | tf_op jit(solution)/shard_map/while/body/eval_jaxpr/dot_general | solution.py:78
  28.9 1.3 fusion.92
  30.2 2.9 %fusion.91 = f32[512,512]{1,0:T(8,128)S(1)} fusion(bf16[2048,512]{1,0:T(8,128)(2,1)} %get-tuple-element.133, s32[512]{0:T(512)S(1)} %bitcast.54), kind=kOutput, calls=%fused_computation.5.clone.1 | convolution fusion | flops 1074790400 | bytes 3147776 | tf_op jit(solution)/shard_map/while/body/eval_jaxpr/dot_general | solution.py:78
  33.1 1.4 %fusion.92 = bf16[6,512,512]{2,1,0:T(8,128)(2,1)} fusion(bf16[6,512,512]{2,1,0:T(8,128)(2,1)} %get-tuple-element.124, s32[]{:T(128)} %get-tuple-element.123, f32[512,512]{1,0:T(8,128)S(1)} %fusion.91, bf16[4,512]{1,0:T(4,128)(2,1)S(1)} %get-tuple-element.135, bf16[6,4,4,128]{3,2,1,0:T(4,128)(2,1)S(1)} %get-tuple-element.134), kind=kOutput, calls=%fused_computation.10.clone.1 | convolution fusion | flops 3670016 | bytes 1582080 | tf_op jit(solution)/shard_map/while/body/eval_jaxpr/bfe,fl->bel/dot_general | solution.py:79
  34.4 2.9 %fusion.91 = f32[512,512]{1,0:T(8,128)S(1)} fusion(bf16[2048,512]{1,0:T(8,128)(2,1)} %get-tuple-element.133, s32[512]{0:T(512)S(1)} %bitcast.54), kind=kOutput, calls=%fused_computation.5.clone.1 | convolution fusion | flops 1074790400 | bytes 3147776 | tf_op jit(solution)/shard_map/while/body/eval_jaxpr/dot_general | solution.py:78
  37.3 1.3 fusion.92
  38.6 2.9 %fusion.91 = f32[512,512]{1,0:T(8,128)S(1)} fusion(bf16[2048,512]{1,0:T(8,128)(2,1)} %get-tuple-element.133, s32[512]{0:T(512)S(1)} %bitcast.54), kind=kOutput, calls=%fused_computation.5.clone.1 | convolution fusion | flops 1074790400 | bytes 3147776 | tf_op jit(solution)/shard_map/while/body/eval_jaxpr/dot_general | solution.py:78
  41.5 1.3 %fusion.92 = bf16[6,512,512]{2,1,0:T(8,128)(2,1)} fusion(bf16[6,512,512]{2,1,0:T(8,128)(2,1)} %get-tuple-element.124, s32[]{:T(128)} %get-tuple-element.123, f32[512,512]{1,0:T(8,128)S(1)} %fusion.91, bf16[4,512]{1,0:T(4,128)(2,1)S(1)} %get-tuple-element.135, bf16[6,4,4,128]{3,2,1,0:T(4,128)(2,1)S(1)} %get-tuple-element.134), kind=kOutput, calls=%fused_computation.10.clone.1 | convolution fusion | flops 3670016 | bytes 1582080 | tf_op jit(solution)/shard_map/while/body/eval_jaxpr/bfe,fl->bel/dot_general | solution.py:79
  42.8 2.9 %fusion.91 = f32[512,512]{1,0:T(8,128)S(1)} fusion(bf16[2048,512]{1,0:T(8,128)(2,1)} %get-tuple-element.133, s32[512]{0:T(512)S(1)} %bitcast.54), kind=kOutput, calls=%fused_computation.5.clone.1 | convolution fusion | flops 1074790400 | bytes 3147776 | tf_op jit(solution)/shard_map/while/body/eval_jaxpr/dot_general | solution.py:78
  45.7 1.3 fusion.92
  47.0 0.0 copy-done.8
  47.7 0.1 broadcast_bitcast_fusion
  47.8 0.0 copy-done.1
  47.8 12.6 %gather_fusion = s32[3072]{0:T(1024)S(1)} fusion(s32[1024]{0:T(1024)S(1)} %copy-done.1, s32[3072]{0:T(1024)S(1)} %broadcast_clamp_fusion), kind=kCustom, calls=%fused_computation | custom fusion | bytes 36864 | tf_op jit(solution)/shard_map/gather | solution.py:85
  60.4 0.0 copy-start.4
  60.4 0.0 copy-start.5
  60.4 0.0 copy-start.17
  60.4 0.0 copy-start.9
  60.5 0.0 copy-start.2
  60.5 2.7 %fusion.56 = (bf16[192,512]{1,0:T(8,128)(2,1)S(1)}, f32[192,512]{1,0:T(8,128)S(1)}) fusion(bf16[3072,512]{1,0:T(8,128)(2,1)} %bitcast.5, s32[3072]{0:T(1024)S(1)} %broadcast_subtract_fusion, pred[3072]{0:T(1024)(128)(4,1)S(1)} %broadcast_bitcast_fusion), kind=kOutput, calls=%fused_computation.88 | convolution fusion | flops 605257728 | bytes 3750912 | tf_op jit(solution)/shard_map/dot_general | solution.py:91
  63.2 0.0 copy-start.12
  63.2 0.0 copy-start.13
  63.3 2.4 %collective-permute-start = (bf16[64,512]{1,0:T(8,128)(2,1)S(1)}, bf16[64,512]{1,0:T(8,128)(2,1)S(1)}, u32[]{:S(2)}, u32[]{:S(2)}) collective-permute-start(bf16[64,512]{1,0:T(8,128)(2,1)S(1)} %get-tuple-element.69), channel_id=1, source_target_pairs={{0,1},{1,2},{2,3},{3,4},{4,5},{5,6},{6,7},{7,8},{8,9},{9,10},{10,1... | collective-permute-start | bytes 196616 | tf_op jit(solution)/shard_map/ppermute | solution.py:12
  65.6 1.3 collective-permute-start.1
  66.9 0.0 collective-permute-done
  66.9 4.0 %collective-permute-done.1 = bf16[64,512]{1,0:T(8,128)(2,1)S(1)} collective-permute-done((bf16[64,512]{1,0:T(8,128)(2,1)S(1)}, bf16[64,512]{1,0:T(8,128)(2,1)S(1)}, u32[]{:S(2)}, u32[]{:S(2)}) %collective-permute-start.1) | collective-permute-done | bytes 65568 | tf_op jit(solution)/shard_map/ppermute | solution.py:12
  70.9 0.0 copy-done.4
  70.9 0.2 convolution_convert_fusion.3
  71.1 0.0 copy-done.5
  71.1 1.9 %fusion.57 = (f32[64]{0:T(128)S(1)}, f32[64,512]{1,0:T(8,128)S(1)}) fusion(bf16[512,512]{1,0:T(8,128)(2,1)} %param.40, bf16[1024,512]{1,0:T(8,128)(2,1)} %param.38, bf16[64,512]{1,0:T(8,128)(2,1)S(1)} %convolution_convert_fusion.3, bf16[64,512]{1,0:T(8,128)(2,1)S(1)} %copy-done.5, f32[512]{0:T(512)S(1)} %copy-done.17), kind=kOutput, calls=%fused_computation.89 | convolution fusion | flops 101154752 | bytes 1837312 | tf_op jit(solution)/shard_map/dot_general | solution.py:105
  73.1 0.0 copy-start.3
  73.1 0.0 copy-start.10
  73.1 0.2 multiply_reduce_fusion.2
  73.3 0.1 add_convert_fusion.2
  73.4 0.8 convolution_convert_fusion.2
  74.3 0.0 all-gather.2.cloned.1.call-update
  74.3 0.0 copy-done.12
  74.3 2.3 %gather_fusion.1 = s32[512]{0:T(512)S(1)} fusion(s32[1024]{0:T(1024)S(1)} %copy-done.1, s32[1024]{0:T(1024)S(1)} %pad_clamp_fusion.1), kind=kCustom, calls=%fused_computation.1 | custom fusion | bytes 6144 | tf_op jit(solution)/shard_map/gather | solution.py:110
  76.7 2.3 %gather_fusion.2 = s32[512]{0:T(512)S(1)} fusion(s32[1024]{0:T(1024)S(1)} %copy-done.1, s32[1024]{0:T(1024)S(1)} %pad_clamp_fusion), kind=kCustom, calls=%fused_computation.2 | custom fusion | bytes 6144 | tf_op jit(solution)/shard_map/gather | solution.py:109
  79.0 0.2 convolution_add_fusion.1
  79.2 0.6 fusion.20
  79.8 0.0 copy-start.18
  79.9 36.3 %all-gather.2.cloned.1.call-done = bf16[1024,512]{1,0:T(8,128)(2,1)} async-done(((bf16[64,512]{1,0:T(8,128)(2,1)}), bf16[1024,512]{1,0:T(8,128)(2,1)}) %all-gather.2.cloned.1.call-update) | async-done | bytes 1048592 | tf_op jit(solution)/shard_map/all_gather | solution.py:112
  116.1 2.9 %multiply_convert_fusion.4 = bf16[512,512]{1,0:T(8,128)(2,1)} fusion(f32[512,512]{1,0:T(8,128)S(1)} %fusion.20, bf16[1024,512]{1,0:T(8,128)(2,1)} %all-gather.2.cloned.1.call-done, s32[512]{0:T(512)S(1)} %gather_fusion.2), kind=kOutput, calls=%fused_computation.37 | convolution fusion | flops 538968064 | bytes 2623488 | tf_op jit(solution)/shard_map/dot_general | solution.py:114
  119.1 1.6 %convolution_convert_fusion = bf16[64,512]{1,0:T(8,128)(2,1)S(1)} fusion(bf16[512,512]{1,0:T(8,128)(2,1)} %param.45, bf16[512,512]{1,0:T(8,128)(2,1)} %multiply_convert_fusion.4, s32[512]{0:T(512)S(1)} %broadcast_subtract_fusion.1), kind=kOutput, calls=%fused_computation.33 | convolution fusion | flops 67207168 | bytes 1116160 | tf_op jit(solution)/shard_map/dot_general | solution.py:122
  120.7 1.9 %fusion.60 = (f32[64]{0:T(128)S(1)}, f32[64,512]{1,0:T(8,128)S(1)}) fusion(bf16[512,512]{1,0:T(8,128)(2,1)} %param.48, bf16[1024,512]{1,0:T(8,128)(2,1)} %param.46, bf16[64,512]{1,0:T(8,128)(2,1)S(1)} %convolution_convert_fusion, bf16[64,512]{1,0:T(8,128)(2,1)S(1)} %add_convert_fusion.2, f32[512]{0:T(512)S(1)} %copy-done.18), kind=kOutput, calls=%fused_computation.90 | convolution fusion | flops 101154752 | bytes 1837312 | tf_op jit(solution)/shard_map/dot_general | solution.py:129
  122.6 0.2 multiply_reduce_fusion.1
  122.8 0.0 copy-done.11
  122.8 0.7 add_convert_fusion.1
  (39 shorter events, 0.2 us)
Async XLA Ops:
  6.5 1.5 %copy-start = (bf16[2048,474]{0,1:T(8,128)(2,1)S(1)}, bf16[2048,474]{0,1:T(8,128)(2,1)}, u32[]{:S(2)}) copy-start(bf16[2048,474]{0,1:T(8,128)(2,1)} %param.30) | copy-start | bytes 5824516
  6.5 109.6 %all-gather.2.cloned.1.call-start = ((), (), s32[]{:S(2)}) async-start(), calls=%async_computation | async-start | bytes 1114112 | tf_op jit(solution)/shard_map/all_gather | solution.py:112
  14.1 2.7 %copy-start.6 = (f32[24,4,128]{2,1,0:T(4,128)S(1)}, f32[24,4,128]{2,1,0:T(4,128)}, u32[]{:S(2)}) copy-start(f32[24,4,128]{2,1,0:T(4,128)} %param.53) | copy-start | bytes 147460
  14.1 2.8 %copy-start.7 = (s32[24,128]{1,0:T(8,128)S(1)}, s32[24,128]{1,0:T(8,128)}, u32[]{:S(2)}) copy-start(s32[24,128]{1,0:T(8,128)} %param.51) | copy-start | bytes 36868
  14.1 2.8 %copy-start.14 = (bf16[512,512]{1,0:T(8,128)(2,1)S(1)}, bf16[512,512]{1,0:T(8,128)(2,1)}, u32[]{:S(2)}) copy-start(bf16[512,512]{1,0:T(8,128)(2,1)} %param.34) | copy-start | bytes 1572868
  14.1 2.8 %copy-start.16 = (f32[512]{0:T(512)S(1)}, f32[512]{0:T(512)}, u32[]{:S(2)}) copy-start(f32[512]{0:T(512)} %param.35) | copy-start | bytes 6148
  16.9 4.9 %copy-start.15 = (bf16[4,512]{1,0:T(4,128)(2,1)S(1)}, bf16[4,512]{1,0:T(4,128)(2,1)}, u32[]{:S(2)}) copy-start(bf16[4,512]{1,0:T(4,128)(2,1)} %param.36) | copy-start | bytes 12292
  21.8 25.2 %copy-start.8 = (s32[24,128]{1,0:T(8,128)S(1)}, s32[24,128]{1,0:T(8,128)}, u32[]{:S(2)}) copy-start(s32[24,128]{1,0:T(8,128)} %param.52) | copy-start | bytes 36868
  47.0 0.8 copy-start.1
  60.4 10.5 %copy-start.4 = (bf16[512,512]{1,0:T(8,128)(2,1)S(1)}, bf16[512,512]{1,0:T(8,128)(2,1)}, u32[]{:S(2)}) copy-start(bf16[512,512]{1,0:T(8,128)(2,1)} %param.37) | copy-start | bytes 1572868
  60.4 10.7 %copy-start.5 = (bf16[64,512]{1,0:T(8,128)(2,1)S(1)}, bf16[64,512]{1,0:T(8,128)(2,1)}, u32[]{:S(2)}) copy-start(bf16[64,512]{1,0:T(8,128)(2,1)} %param.50) | copy-start | bytes 196612
  60.4 10.7 %copy-start.17 = (f32[512]{0:T(512)S(1)}, f32[512]{0:T(512)}, u32[]{:S(2)}) copy-start(f32[512]{0:T(512)} %param.39) | copy-start | bytes 6148
  60.4 12.9 %copy-start.9 = (f32[512]{0:T(512)S(1)}, f32[512]{0:T(512)}, u32[]{:S(2)}) copy-start(f32[512]{0:T(512)} %param.41) | copy-start | bytes 6148
  60.5 13.0 %copy-start.2 = (bf16[512,512]{1,0:T(8,128)(2,1)S(1)}, bf16[512,512]{1,0:T(8,128)(2,1)}, u32[]{:S(2)}) copy-start(bf16[512,512]{1,0:T(8,128)(2,1)} %param.42) | copy-start | bytes 1572868
  63.2 11.1 %copy-start.12 = (s32[4,128]{1,0:T(4,128)S(1)}, s32[4,128]{1,0:T(4,128)}, u32[]{:S(2)}) copy-start(s32[4,128]{1,0:T(4,128)} %param.57) | copy-start | bytes 6148
  63.2 13.4 %copy-start.13 = (s32[4,128]{1,0:T(4,128)S(1)}, s32[4,128]{1,0:T(4,128)}, u32[]{:S(2)}) copy-start(s32[4,128]{1,0:T(4,128)} %param.56) | copy-start | bytes 6148
  63.3 3.7 %collective-permute-start = (bf16[64,512]{1,0:T(8,128)(2,1)S(1)}, bf16[64,512]{1,0:T(8,128)(2,1)S(1)}, u32[]{:S(2)}, u32[]{:S(2)}) collective-permute-start(bf16[64,512]{1,0:T(8,128)(2,1)S(1)} %get-tuple-element.69), channel_id=1, source_target_pairs={{0,1},{1,2},{2,3},{3,4},{4,5},{5,6},{6,7},{7,8},{8,9},{9,10},{10,1... | collective-permute-start | bytes 196616 | tf_op jit(solution)/shard_map/ppermute | solution.py:12
  65.6 5.3 %collective-permute-start.1 = (bf16[64,512]{1,0:T(8,128)(2,1)S(1)}, bf16[64,512]{1,0:T(8,128)(2,1)S(1)}, u32[]{:S(2)}, u32[]{:S(2)}) collective-permute-start(bf16[64,512]{1,0:T(8,128)(2,1)S(1)} %get-tuple-element.70), channel_id=1, source_target_pairs={{1,0},{2,1},{3,2},{4,3},{5,4},{6,5},{7,6},{8,7},{9,8},{10,9},{11,1... | collective-permute-start | bytes 196616 | tf_op jit(solution)/shard_map/ppermute | solution.py:12
  73.1 5.9 %copy-start.3 = (bf16[512,512]{1,0:T(8,128)(2,1)S(1)}, bf16[512,512]{1,0:T(8,128)(2,1)}, u32[]{:S(2)}) copy-start(bf16[512,512]{1,0:T(8,128)(2,1)} %param.43) | copy-start | bytes 1572868
  73.1 5.9 %copy-start.10 = (f32[512]{0:T(512)S(1)}, f32[512]{0:T(512)}, u32[]{:S(2)}) copy-start(f32[512]{0:T(512)} %param.44) | copy-start | bytes 6148
  79.8 40.8 %copy-start.18 = (f32[512]{0:T(512)S(1)}, f32[512]{0:T(512)}, u32[]{:S(2)}) copy-start(f32[512]{0:T(512)} %param.47) | copy-start | bytes 6148
  119.1 3.7 %copy-start.11 = (f32[512]{0:T(512)S(1)}, f32[512]{0:T(512)}, u32[]{:S(2)}) copy-start(f32[512]{0:T(512)} %param.49) | copy-start | bytes 6148
Sparse Core Ops, SparseCore 0:
  74.4 41.6 all-gather.1
where the time goes:
time: 131 us; the launch traced here: 130 us
  matrix products  49 us (37%)
  waiting for transfers between devices  40.3 us (31%)
  local copies, waits for them, and re-layouts  19 us (15%)
  between operations  14.5 us (11%)
  other arithmetic  3.99 us (3%)
  starting transfers between devices  3.65 us (3%)
    all_gather x1, waiting for transfers between devices, per_device(): piece = lax.all_gather(sender_code, 'bulk', axis=0, tiled=True)  36.3 us
    dot_general x6, matrix products, edge_group(): chosen = jnp.dot(picker, sender_part, preferred_element_type=f32)  17.2 us
    gather x1, local copies, waits for them, and re-layouts, per_device(): target = mesh_slot[g2m_recv.reshape(-1)]  12.6 us
    dot_general x6, matrix products, edge_group(): extra = jnp.einsum('bfe,fl->bel', feats, feat_table).reshape(-1, width)  7.86 us
    dot_general x1, matrix products, per_device(): jnp.dot(grid_hidden, grid_second, preferred_element_type=f32)  5.99 us
    dot_general x1, matrix products, per_device(): jnp.dot(grid_code, send_weight, preferred_element_type=f32) + edge_bias  4.91 us
    ppermute x2, waiting for transfers between devices, from_behind(): lax.ppermute(value, axis, [(source, source + steps) for source in range(l...  3.97 us
    ppermute x2, starting transfers between devices, from_behind(): lax.ppermute(value, axis, [(source, source + steps) for source in range(l...  3.65 us
  transfers between devices with their start and end apart: 3, of which 2 were waited for; matrix products, arithmetic and copies ran while one was open for 4% of the time, Pallas kernels for 0%

commit v1 on v0

v1 whole, which is shorter than its diff:
```python
import functools
import math

import jax
import jax.numpy as jnp
from jax import lax
from jax.experimental import pallas as pl
from jax.experimental.pallas import tpu as pltpu
from jax.sharding import PartitionSpec as P

F32 = jnp.float32
BF16 = jnp.bfloat16
I32 = jnp.int32
SEND_CAP = 16
LANES = 128
VMEM = pltpu.VMEM
SMEM = pltpu.SMEM
PARAMS = pltpu.CompilerParams(vmem_limit_bytes=40 * 1024 * 1024)


def mm(left, right):
    return jnp.dot(left, right, preferred_element_type=F32)


def mm_nt(left, right):
    return lax.dot_general(left, right, (((1,), (1,)), ((), ())), preferred_element_type=F32)


def silu_half(half):
    return half + half * jnp.tanh(half)


def silu(value):
    return silu_half(0.5 * value)


def layer_norm(value):
    center = value - jnp.mean(value, axis=-1, keepdims=True)
    spread = jnp.mean(center * center, axis=-1, keepdims=True)
    return center * lax.rsqrt(spread + 1e-05)


def iota(shape, dim):
    return lax.broadcasted_iota(I32, shape, dim)


def ids_of_rows(slot, first, count):
    nodes = slot.shape[1]
    rows = iota((count, nodes), 0) + first
    return jnp.max(jnp.where(slot == rows, iota((count, nodes), 1), -1), axis=1, keepdims=True)


def edge_kernel(
    place_ref,
    count_ref,
    grid_ref,
    first_ref,
    grid_bias_ref,
    second_ref,
    send_weight_ref,
    edge_bias_ref,
    feat_weight_ref,
    slot_ref,
    send_ref,
    recv_ref,
    feat_ref,
    below_ref,
    own_ref,
    above_ref,
    table,
    weight_t,
    bias_t,
    feat_weight_t,
    total,
):
    grid_rows = grid_ref.shape[0]
    width = second_ref.shape[1]
    blocks, block_edges = send_ref.shape
    owned = own_ref.shape[0]
    step_rows = 256
    weight_t[...] = (0.5 * send_weight_ref[...].astype(F32)).T.astype(BF16)
    bias_t[...] = jnp.broadcast_to(0.5 * edge_bias_ref[...], (LANES, width)).T
    feat_weight_t[...] = jnp.concatenate(
        [0.5 * feat_weight_ref[...].astype(F32), jnp.zeros((LANES - feat_weight_ref.shape[0], width), F32)],
        axis=0,
    ).T.astype(BF16)
    total[...] = jnp.zeros_like(total)

    def grid_step(step, carry):
        start = pl.multiple_of(step * step_rows, step_rows)
        value = grid_ref[pl.ds(start, step_rows), :]
        hidden = silu(mm(value, first_ref[...]) + grid_bias_ref[...]).astype(BF16)
        code = layer_norm(mm(hidden, second_ref[...])).astype(BF16)
        bias = jnp.concatenate([bias_t[...]] * (step_rows // LANES), axis=1)
        table[:, pl.ds(start, step_rows)] = (mm_nt(weight_t[...], code) + bias).astype(BF16)
        return carry

    lax.fori_loop(0, grid_rows // step_rows, grid_step, 0)

    ids = ids_of_rows(slot_ref[...], (place_ref[0] - 1) * owned, 3 * owned)
    used = count_ref[0]
    group = math.gcd(blocks, 2)
    feats = feat_ref.shape[1]

    def edge_step(step, carry):
        first = step * group
        senders = jnp.concatenate([send_ref[pl.ds(first + b, 1), :] for b in range(group)], axis=1)
        picker = (senders == iota((grid_rows, group * block_edges), 0)).astype(F32).astype(BF16)
        feat = jnp.concatenate([feat_ref[first + b] for b in range(group)], axis=1)
        half = mm(table[...], picker) + mm(feat_weight_t[:, :feats], feat.astype(BF16))
        hidden = silu_half(half).astype(BF16)
        spread = jnp.concatenate(
            [
                (ids == jnp.where(first + b < used, recv_ref[pl.ds(first + b, 1), :], -2))
                for b in range(group)
            ],
            axis=1,
        )
        total[...] += mm_nt(spread.astype(F32).astype(BF16), hidden)
        return carry

    lax.fori_loop(0, blocks // group, edge_step, 0)
    below_ref[...] = total[:owned].astype(BF16)
    own_ref[...] = total[owned : 2 * owned]
    above_ref[...] = total[2 * owned :].astype(BF16)


def wanted_kernel(owned, slot_ref, send_ref, wanted_ref):
    nodes = slot_ref.shape[1]
    blocks, block_edges = send_ref.shape
    places = wanted_ref.shape[1]
    chunk = LANES
    per_chunk = chunk // owned * SEND_CAP
    row, column = iota((chunk, chunk), 0), iota((chunk, chunk), 1)
    before = ((row > column) & (row // owned == column // owned)).astype(F32).astype(BF16)
    local_owner = (iota((chunk, LANES), 0) // owned * SEND_CAP).astype(F32)

    def find(index, best):
        ids = ids_of_rows(slot_ref[...], index * chunk, chunk)
        hit = jnp.zeros((chunk, block_edges), F32)
        for b in range(blocks):
            hit = jnp.maximum(hit, (ids == send_ref[b : b + 1, :]).astype(F32))
        hit = jnp.broadcast_to(jnp.max(hit, axis=1, keepdims=True), (chunk, LANES))
        rank = mm(before, hit.astype(BF16)) + local_owner
        spot = jnp.where(hit > 0, rank.astype(I32) + index * per_chunk, -1)
        spot = jnp.concatenate([spot] * (places // LANES), axis=1)
        found = jnp.where(spot == iota((chunk, places), 1), ids, -1)
        return jnp.maximum(best, jnp.max(found, axis=0, keepdims=True))

    best = lax.fori_loop(0, nodes // chunk, find, jnp.full((1, places), -1, I32))
    best = best.astype(F32)
    for b in range(blocks):
        senders = jnp.broadcast_to(send_ref[b : b + 1, :].astype(F32), (block_edges, block_edges)).T
        senders = jnp.concatenate([senders] * (places // LANES), axis=1)
        wanted_ref[b * block_edges : (b + 1) * block_edges, :] = (
            (senders == best).astype(F32).astype(BF16)
        )


def supply_kernel(place_ref, slot_ref, request_ref, supply_ref):
    owned = supply_ref.shape[1]
    devices = supply_ref.shape[0] // SEND_CAP
    per_device = request_ref.shape[0] // devices
    ids = ids_of_rows(slot_ref[...], place_ref[0] * owned, owned)
    lane = iota((owned, LANES), 1)
    used = jnp.zeros((owned, LANES), F32)
    for d in range(devices):
        hit = jnp.zeros((owned, request_ref.shape[1]), F32)
        for b in range(per_device):
            at = d * per_device + b
            hit = jnp.maximum(hit, (ids == request_ref[at : at + 1, :]).astype(F32))
        used = jnp.where(lane == d, jnp.max(hit, axis=1, keepdims=True), used)
    before = (iota((owned, owned), 0) > iota((owned, owned), 1)).astype(F32).astype(BF16)
    rank = jnp.where(used > 0, mm(before, used.astype(BF16)), -1.0)
    rank = jnp.concatenate([rank, jnp.full((LANES - owned, LANES), -1.0, F32)], axis=0).T
    slots = iota((SEND_CAP, owned), 0).astype(F32)
    for d in range(devices):
        supply_ref[d * SEND_CAP : (d + 1) * SEND_CAP, :] = (
            (rank[d : d + 1, :owned] == slots).astype(F32).astype(BF16)
        )


def node_kernel(
    own_ref,
    from_below_ref,
    from_above_ref,
    latent_ref,
    edge_out_ref,
    node_input_ref,
    node_bias_ref,
    node_out_ref,
    node_gain_ref,
    mesh_sender_ref,
    mesh_receiver_ref,
    message_bias_ref,
    supply_ref,
    rows_ref,
    encoded_ref,
    receiver_ref,
):
    width = latent_ref.shape[1]
    latent = latent_ref[...]
    node_sum = own_ref[...] + from_below_ref[...].astype(F32) + from_above_ref[...].astype(F32)
    aggregate = mm(node_sum.astype(BF16), edge_out_ref[...]).astype(BF16)
    hidden = mm(latent, node_input_ref[:width]) + mm(aggregate, node_input_ref[width:])
    hidden = silu(hidden + node_bias_ref[...]).astype(BF16)
    encoded = latent.astype(F32) + layer_norm(mm(hidden, node_out_ref[...])) * node_gain_ref[...]
    encoded = encoded.astype(BF16)
    encoded_ref[...] = encoded
    sender_code = mm(encoded, mesh_sender_ref[...]).astype(BF16)
    rows_ref[...] = mm(supply_ref[...], sender_code).astype(BF16)
    receiver_ref[...] = mm(encoded, mesh_receiver_ref[...]) + message_bias_ref[...]


def message_kernel(
    place_ref,
    slot_ref,
    recv_ref,
    wanted_ref,
    piece_ref,
    encoded_ref,
    receiver_ref,
    message_out_ref,
    update_input_ref,
    update_bias_ref,
    update_out_ref,
    update_gain_ref,
    out_ref,
):
    owned, width = encoded_ref.shape
    blocks = recv_ref.shape[0]
    ids = ids_of_rows(slot_ref[...], place_ref[0] * owned, owned)
    incoming = jnp.concatenate(
        [(ids == recv_ref[b : b + 1, :]).astype(F32) for b in range(blocks)], axis=1
    )
    pick = incoming.T.astype(BF16)
    incoming = incoming.astype(BF16)
    receiver = receiver_ref[...]
    high = receiver.astype(BF16)
    low = (receiver - high.astype(F32)).astype(BF16)
    encoded = encoded_ref[...]
    value = mm(wanted_ref[...], piece_ref[...]) + (mm(pick, high) + mm(pick, low))
    message = silu(value).astype(BF16)
    message_sum = mm(incoming, message).astype(BF16)
    update = mm(message_sum, message_out_ref[...]).astype(BF16)
    hidden = mm(encoded, update_input_ref[:width]) + mm(update, update_input_ref[width:])
    hidden = silu(hidden + update_bias_ref[...]).astype(BF16)
    out = encoded.astype(F32) + layer_norm(mm(hidden, update_out_ref[...])) * update_gain_ref[...]
    out_ref[...] = out.astype(BF16)


def call(kernel, out_shape, spaces, scratch=(), flops=0, moved=0):
    return pl.pallas_call(
        kernel,
        out_shape=out_shape,
        in_specs=[pl.BlockSpec(memory_space=space) for space in spaces],
        out_specs=jax.tree.map(lambda _: pl.BlockSpec(memory_space=VMEM), out_shape),
        scratch_shapes=scratch,
        compiler_params=PARAMS,
        cost_estimate=pl.CostEstimate(flops=flops, bytes_accessed=moved, transcendentals=0),
    )


def shape(*sizes, kind=BF16):
    return jax.ShapeDtypeStruct(sizes, kind)


def per_device(
    grid_in,
    grid_first,
    grid_bias,
    grid_second,
    send_weight,
    edge_bias,
    feat_weight,
    edge_out,
    node_input,
    node_bias,
    node_out,
    node_gain,
    mesh_sender,
    mesh_receiver,
    message_bias,
    message_out,
    update_input,
    update_bias,
    update_out,
    update_gain,
    mesh_latent,
    g2m_send,
    g2m_recv,
    g2m_feat,
    g2m_count,
    mesh_slot,
    mesh_send,
    mesh_recv,
):
    devices = lax.axis_size("bulk")
    position = lax.axis_index("bulk")
    place = position.astype(I32).reshape(1)
    owned, width = mesh_latent.shape
    grid_rows = grid_in.shape[0]
    places = devices * SEND_CAP
    edges = mesh_send.size
    slot = mesh_slot.reshape(1, -1)
    row = lambda vector: vector.reshape(1, -1)

    requests = lax.all_gather(mesh_send, "bulk", axis=0, tiled=True)

    below, own, above = call(
        edge_kernel,
        (shape(owned, width), shape(owned, width, kind=F32), shape(owned, width)),
        [SMEM, SMEM] + [VMEM] * 11,
        scratch=[
            pltpu.VMEM((width, grid_rows), BF16),
            pltpu.VMEM((width, width), BF16),
            pltpu.VMEM((width, LANES), F32),
            pltpu.VMEM((width, LANES), BF16),
            pltpu.VMEM((3 * owned, width), F32),
        ],
        flops=10_000_000_000,
        moved=4_000_000,
    )(
        place,
        g2m_count,
        grid_in,
        grid_first,
        row(grid_bias),
        grid_second,
        send_weight,
        row(edge_bias),
        feat_weight,
        slot,
        g2m_send,
        g2m_recv,
        g2m_feat,
    )
    from_below = lax.ppermute(above, "bulk", [(d, d + 1) for d in range(devices - 1)])
    from_above = lax.ppermute(below, "bulk", [(d + 1, d) for d in range(devices - 1)])
    wanted = call(
        functools.partial(wanted_kernel, owned),
        shape(edges, places),
        [VMEM] * 2,
        flops=1_000_000_000,
        moved=500_000,
    )(slot, mesh_send)
    supply = call(
        supply_kernel,
        shape(places, owned),
        [SMEM] + [VMEM] * 2,
        flops=500_000_000,
        moved=500_000,
    )(place, slot, requests)
    rows, encoded, receiver = call(
        node_kernel,
        (shape(places, width), shape(owned, width), shape(owned, width, kind=F32)),
        [VMEM] * 13,
        flops=500_000_000,
        moved=4_000_000,
    )(
        own,
        from_below,
        from_above,
        mesh_latent,
        edge_out,
        node_input,
        row(node_bias),
        node_out,
        row(node_gain),
        mesh_sender,
        mesh_receiver,
        row(message_bias),
        supply,
    )
    piece = lax.all_to_all(rows, "bulk", 0, 0, tiled=True)
    return call(
        message_kernel,
        shape(owned, width),
        [SMEM] + [VMEM] * 11,
        flops=1_000_000_000,
        moved=4_000_000,
    )(
        place,
        slot,
        mesh_recv,
        wanted,
        piece,
        encoded,
        receiver,
        message_out,
        update_input,
        row(update_bias),
        update_out,
        row(update_gain),
    )


def solution(mesh):
    split = {0: ("groups", "bulk"), 20: "bulk", 21: "bulk", 22: "bulk", 23: "bulk", 24: "bulk"}
    split.update({26: "bulk", 27: "bulk"})
    placed = tuple(P(split[at]) if at in split else P() for at in range(28))
    return jax.shard_map(
        per_device,
        mesh=mesh,
        in_specs=placed,
        out_specs=P(("groups", "bulk"), None),
        check_vma=False,
    )
```

time: 131 us -> 75.6 us (0.58)
  matrix products: 49 us -> 0 us
  waiting for transfers between devices: 40.3 us -> 6.01 us
  Pallas kernels: 0 us -> 31.6 us
  blocking collectives: 0 us -> 25.1 us
  local copies, waits for them, and re-layouts: 19 us -> 4.06 us
  between operations: 14.5 us -> 1.02 us
  other arithmetic: 3.99 us -> 0 us
  starting transfers between devices: 3.65 us -> 7.47 us
    dot_general x23 -> x0, matrix products: 49 us -> none  [the longest x6 17.2 us: edge_group(): chosen = jnp.dot(picker, sender_part, preferred_element_type=f32)]
    all_gather x1 -> x0, waiting for transfers between devices: 36.3 us -> none  [per_device(): piece = lax.all_gather(sender_code, 'bulk', axis=0, tiled=True)]
    pallas_call x0 -> x5, Pallas kernels: none -> 31.6 us  [the longest x1 22.6 us: per_device(): call(edge_kernel, (shape(owned, width), shape(owned, width, kind=F32), sh...]
    all_gather x0 -> x1, blocking collectives: none -> 25.1 us  [per_device(): requests = lax.all_gather(mesh_send, 'bulk', axis=0, tiled=True)]
    gather x3 -> x0, local copies, waits for them, and re-layouts: 17.2 us -> none  [the longest x1 12.6 us: per_device(): target = mesh_slot[g2m_recv.reshape(-1)]]
    all_to_all x0 -> x1, waiting for transfers between devices: none -> 6 us  [per_device(): piece = lax.all_to_all(rows, 'bulk', 0, 0, tiled=True)]
    ppermute x2, waiting for transfers between devices: 3.97 us -> 0.01 us  [the longest x1 0.01 us: per_device(): lax.ppermute(below, 'bulk', [(d + 1, d) for d in range(devices - 1)])]
    all_to_all x0 -> x1, starting transfers between devices: none -> 3.67 us  [per_device(): piece = lax.all_to_all(rows, 'bulk', 0, 0, tiled=True)]
  transfers between devices with their start and end apart: 3 -> 3, of which waited for: 2 -> 1; matrix products, arithmetic and copies ran while one was open for 4% -> 0% of each run, Pallas kernels for 0% -> 6%
where the time goes in v1:
time: 75.6 us; the launch traced here: 75.2 us
  Pallas kernels  31.6 us (42%)
  blocking collectives  25.1 us (33%)
  starting transfers between devices  7.47 us (10%)
  waiting for transfers between devices  6.01 us (8%)
  local copies, waits for them, and re-layouts  4.06 us (5%)
  between operations  1.02 us (1%)
    all_gather x1, blocking collectives, per_device(): requests = lax.all_gather(mesh_send, 'bulk', axis=0, tiled=True)  25.1 us
    pallas_call x1, Pallas kernels, per_device(): call(edge_kernel, (shape(owned, width), shape(owned, width, kind=F32), sh...  22.6 us
    all_to_all x1, waiting for transfers between devices, per_device(): piece = lax.all_to_all(rows, 'bulk', 0, 0, tiled=True)  6 us
    unnamed x53, local copies, waits for them, and re-layouts  4.06 us
    pallas_call x1, Pallas kernels, per_device(): call(functools.partial(wanted_kernel, owned), shape(edges, places), [VMEM...  3.99 us
    all_to_all x1, starting transfers between devices, per_device(): piece = lax.all_to_all(rows, 'bulk', 0, 0, tiled=True)  3.67 us
    ppermute x1, starting transfers between devices, per_device(): lax.ppermute(above, 'bulk', [(d, d + 1) for d in range(devices - 1)])  2.51 us
    pallas_call x1, Pallas kernels, per_device(): call(message_kernel, shape(owned, width), [SMEM] + [VMEM] * 11, flops=100...  2.41 us
  transfers between devices with their start and end apart: 3, of which 1 were waited for; matrix products, arithmetic and copies ran while one was open for 0% of the time, Pallas kernels for 6%

profile of v1, /device:TPU:0, one launch (start us, length us, event | category | flops | bytes accessed | tf_op | source)
XLA Modules:
  0.0 75.2 jit_solution(11670919530237222730)
XLA Ops:
  0.0 0.0 copy-start.20
  0.0 0.0 copy-start.21
  0.0 0.0 copy-start.11
  0.0 0.0 copy-start.12
  0.0 0.0 copy-start.19
  0.0 0.0 copy-start.17
  0.0 0.0 copy-start.18
  0.0 0.0 copy-start.16
  0.1 2.9 %copy.30.grid_ref = bf16[2048,474]{1,0:T(8,128)(2,1)S(1)} copy(bf16[2048,474]{0,1:T(8,128)(2,1)} %param.28) | data formatting | bytes 3883008 | tf_op args[0]
  3.6 0.0 copy-done.20
  3.6 0.0 copy-done.21
  3.7 0.0 copy-done.22
  3.7 0.0 copy-done.11
  3.7 0.0 copy-done.12
  3.7 0.0 copy-done.19
  3.7 0.0 copy-done.17
  3.7 0.0 copy-done.18
  3.7 0.0 copy-done.16
  3.7 0.0 copy-start.15
  3.7 1.0 %copy-done.15 = bf16[474,512]{1,0:T(8,128)(2,1)S(1)} copy-done((bf16[474,512]{1,0:T(8,128)(2,1)S(1)}, bf16[474,512]{1,0:T(8,128)(2,1)}, u32[]{:S(2)}) %copy-start.15) | copy-done | bytes 485400
  4.8 0.0 copy-start.9
  4.8 0.0 copy-start.2
  4.8 0.0 copy-start.3
  4.8 0.0 copy-start.4
  4.8 0.0 copy-start.5
  4.8 0.0 copy-start.6
  4.8 0.0 copy-start.7
  4.8 0.0 copy-start.8
  4.8 22.6 %shard_map.263 = (bf16[64,512]{1,0:T(8,128)(2,1)S(1)}, f32[64,512]{1,0:T(8,128)S(1)}, bf16[64,512]{1,0:T(8,128)(2,1)S(1)}) custom-call(s32[1]{0:T(128)} %bitcast.place_ref, s32[1]{0:T(128)S(6)} %copy.31.count_ref, bf16[2048,474]{1,0:T(8,128)(2,1)S(1)} %copy.30.grid_ref, bf16[474,512]{1,0:T(8,128)(2,1)S(1)} %copy-done.15, f32[1,512]{1,0:T(1,128)S(1)} %bitcast.23, ...), custom_call_target="tpu_custom_call" | custom-call | flops 10000000000 | bytes 4000000 | tf_op jit(solution)/shard_map/pallas_call | solution.py:310
  27.4 0.0 copy-start
  27.5 0.0 copy-start.1
  27.5 2.5 %collective-permute-start = (bf16[64,512]{1,0:T(8,128)(2,1)S(1)}, bf16[64,512]{1,0:T(8,128)(2,1)S(1)}, u32[]{:S(2)}, u32[]{:S(2)}) collective-permute-start(bf16[64,512]{1,0:T(8,128)(2,1)S(1)} %get-tuple-element.12), channel_id=1, source_target_pairs={{0,1},{1,2},{2,3},{3,4},{4,5},{5,6},{6,7},{7,8},{8,9},{9,10},{10,1... | collective-permute-start | bytes 196616 | tf_op jit(solution)/shard_map/ppermute | solution.py:338
  30.0 1.3 %collective-permute-start.1 = (bf16[64,512]{1,0:T(8,128)(2,1)S(1)}, bf16[64,512]{1,0:T(8,128)(2,1)S(1)}, u32[]{:S(2)}, u32[]{:S(2)}) collective-permute-start(bf16[64,512]{1,0:T(8,128)(2,1)S(1)} %get-tuple-element.13), channel_id=1, source_target_pairs={{1,0},{2,1},{3,2},{4,3},{5,4},{6,5},{7,6},{8,7},{9,8},{10,9},{11,1... | collective-permute-start | bytes 196616 | tf_op jit(solution)/shard_map/ppermute | solution.py:339
  31.3 0.0 copy-done.9
  31.3 25.1 %all-gather = s32[16,4,128]{2,1,0:T(4,128)S(1)} all-gather(s32[1,4,128]{2,1,0:T(4,128)S(1)} %bitcast.18), channel_id=1, replica_groups=mesh['groups'=2,'bulk'=16] {'bulk'}, dimensions={0}, use_global_device_ids=true | all-gather | bytes 34816 | tf_op jit(solution)/shard_map/all_gather | solution.py:308
  56.4 0.7 shard_map.264.supply_ref
  57.0 0.0 collective-permute-done.from_below_ref
  57.0 0.0 collective-permute-done.1.from_above_ref
  57.1 0.0 copy-done.2
  57.1 0.0 copy-done.3
  57.1 0.0 copy-done.4
  57.1 0.0 copy-done.5
  57.1 0.0 copy-done.6
  57.1 0.0 copy-done.7
  57.1 0.0 copy-done.8
  57.1 0.0 copy-done
  57.1 0.0 copy-done.1
  57.1 1.9 %shard_map.265 = (bf16[256,512]{1,0:T(8,128)(2,1)}, bf16[64,512]{1,0:T(8,128)(2,1)S(1)}, f32[64,512]{1,0:T(8,128)S(1)}) custom-call(f32[64,512]{1,0:T(8,128)S(1)} %get-tuple-element.11.own_ref, bf16[64,512]{1,0:T(8,128)(2,1)S(1)} %collective-permute-done.from_below_ref, bf16[64,512]{1,0:T(8,128)(2,1)S(1)} %collective-permute-done.1.from_above_ref, ...), custom_call_target="tpu_custom_call" | custom-call | flops 500000000 | bytes 4000000 | tf_op jit(solution)/shard_map/pallas_call | solution.py:354
  59.0 0.0 copy-start.10
  59.0 0.0 copy-start.13
  59.0 0.0 copy-start.14
  59.0 0.0 copy-start.23
  59.0 0.0 copy-start.24
  59.1 0.0 copy-start.25
  59.1 3.7 %all-to-all-start = ((bf16[16,16,512]{2,1,0:T(8,128)(2,1)}), bf16[16,16,512]{2,1,0:T(8,128)(2,1)S(1)}, u32[]{:S(2)}, u32[]{:S(2)}) async-start(bf16[16,16,512]{2,1,0:T(8,128)(2,1)} %bitcast.9), calls=%async_computation | async-start | bytes 524288 | tf_op jit(solution)/shard_map/all_to_all | solution.py:375
  62.8 4.0 %shard_map.262.wanted_ref = bf16[512,256]{1,0:T(8,128)(2,1)S(1)} custom-call(s32[1,1024]{1,0:T(1,128)S(1)} %bitcast.21, s32[4,128]{1,0:T(4,128)S(1)} %copy-done.9), custom_call_target="tpu_custom_call" | custom-call | flops 1000000000 | bytes 500000 | tf_op jit(solution)/shard_map/pallas_call | solution.py:340
  66.8 6.0 %all-to-all-done = bf16[16,16,512]{2,1,0:T(8,128)(2,1)S(1)} async-done(((bf16[16,16,512]{2,1,0:T(8,128)(2,1)}), bf16[16,16,512]{2,1,0:T(8,128)(2,1)S(1)}, u32[]{:S(2)}, u32[]{:S(2)}) %all-to-all-start) | async-done | bytes 262176 | tf_op jit(solution)/shard_map/all_to_all | solution.py:375
  72.8 0.0 copy-done.10
  72.8 0.0 copy-done.13
  72.8 0.0 copy-done.14
  72.8 0.0 copy-done.23
  72.8 0.0 copy-done.24
  72.8 0.0 copy-done.25
  72.8 2.4 %shard_map.266 = bf16[64,512]{1,0:T(8,128)(2,1)} custom-call(s32[1]{0:T(128)} %bitcast.place_ref, s32[1,1024]{1,0:T(1,128)S(1)} %bitcast.22, s32[4,128]{1,0:T(4,128)S(1)} %copy-done.23, bf16[512,256]{1,0:T(8,128)(2,1)S(1)} %shard_map.262.wanted_ref, bf16[256,512]{1,0:T(8,128)(2,1)S(1)} %bitcast.13, bf16[64,512]{1,0:T(8,128)(2,1)S(1)} %get-tuple-element.15.encoded_ref, ...), custom_call_target="tpu_custom_call" | custom-call | flops 1000000000 | bytes 4000000 | tf_op jit(solution)/shard_map/pallas_call | solution.py:376
  (1 shorter events, 0.0 us)
Async XLA Ops:
  0.0 3.6 %copy-start.20 = (s32[1024]{0:T(1024)S(1)}, s32[1024]{0:T(1024)}, u32[]{:S(2)}) copy-start(s32[1024]{0:T(1024)} %param.53) | copy-start | bytes 12292
  0.0 3.6 %copy-start.21 = (f32[512]{0:T(512)S(1)}, f32[512]{0:T(512)}, u32[]{:S(2)}) copy-start(f32[512]{0:T(512)} %param.30) | copy-start | bytes 6148
  0.0 3.7 %copy-start.22 = (f32[512]{0:T(512)S(1)}, f32[512]{0:T(512)}, u32[]{:S(2)}) copy-start(f32[512]{0:T(512)} %param.33) | copy-start | bytes 6148
  0.0 3.7 %copy-start.11 = (bf16[512,512]{1,0:T(8,128)(2,1)S(1)}, bf16[512,512]{1,0:T(8,128)(2,1)}, u32[]{:S(2)}) copy-start(bf16[512,512]{1,0:T(8,128)(2,1)} %second_ref.1) | copy-start | bytes 1572868
  0.0 3.7 %copy-start.12 = (bf16[512,512]{1,0:T(8,128)(2,1)S(1)}, bf16[512,512]{1,0:T(8,128)(2,1)}, u32[]{:S(2)}) copy-start(bf16[512,512]{1,0:T(8,128)(2,1)} %send_weight_ref.1) | copy-start | bytes 1572868
  0.0 3.7 %copy-start.19 = (bf16[4,512]{1,0:T(4,128)(2,1)S(1)}, bf16[4,512]{1,0:T(4,128)(2,1)}, u32[]{:S(2)}) copy-start(bf16[4,512]{1,0:T(4,128)(2,1)} %feat_weight_ref.1) | copy-start | bytes 12292
  0.0 3.7 %copy-start.17 = (s32[24,128]{1,0:T(8,128)S(1)}, s32[24,128]{1,0:T(8,128)}, u32[]{:S(2)}) copy-start(s32[24,128]{1,0:T(8,128)} %send_ref.3) | copy-start | bytes 36868
  0.0 3.7 %copy-start.18 = (s32[24,128]{1,0:T(8,128)S(1)}, s32[24,128]{1,0:T(8,128)}, u32[]{:S(2)}) copy-start(s32[24,128]{1,0:T(8,128)} %recv_ref.2) | copy-start | bytes 36868
  0.0 3.7 %copy-start.16 = (f32[24,4,128]{2,1,0:T(4,128)S(1)}, f32[24,4,128]{2,1,0:T(4,128)}, u32[]{:S(2)}) copy-start(f32[24,4,128]{2,1,0:T(4,128)} %feat_ref.1) | copy-start | bytes 147460
  3.7 1.0 %copy-start.15 = (bf16[474,512]{1,0:T(8,128)(2,1)S(1)}, bf16[474,512]{1,0:T(8,128)(2,1)}, u32[]{:S(2)}) copy-start(bf16[474,512]{1,0:T(8,128)(2,1)} %first_ref.1) | copy-start | bytes 1456132
  4.8 26.5 %copy-start.9 = (s32[4,128]{1,0:T(4,128)S(1)}, s32[4,128]{1,0:T(4,128)}, u32[]{:S(2)}) copy-start(s32[4,128]{1,0:T(4,128)} %send_ref.2) | copy-start | bytes 6148
  4.8 52.3 %copy-start.2 = (bf16[512,512]{1,0:T(8,128)(2,1)S(1)}, bf16[512,512]{1,0:T(8,128)(2,1)}, u32[]{:S(2)}) copy-start(bf16[512,512]{1,0:T(8,128)(2,1)} %node_out_ref.1) | copy-start | bytes 1572868
  4.8 52.3 %copy-start.3 = (bf16[512,512]{1,0:T(8,128)(2,1)S(1)}, bf16[512,512]{1,0:T(8,128)(2,1)}, u32[]{:S(2)}) copy-start(bf16[512,512]{1,0:T(8,128)(2,1)} %mesh_sender_ref.1) | copy-start | bytes 1572868
  4.8 52.3 %copy-start.4 = (bf16[512,512]{1,0:T(8,128)(2,1)S(1)}, bf16[512,512]{1,0:T(8,128)(2,1)}, u32[]{:S(2)}) copy-start(bf16[512,512]{1,0:T(8,128)(2,1)} %mesh_receiver_ref.1) | copy-start | bytes 1572868
  4.8 52.3 %copy-start.5 = (bf16[64,512]{1,0:T(8,128)(2,1)S(1)}, bf16[64,512]{1,0:T(8,128)(2,1)}, u32[]{:S(2)}) copy-start(bf16[64,512]{1,0:T(8,128)(2,1)} %latent_ref.1) | copy-start | bytes 196612
  4.8 52.3 %copy-start.6 = (f32[512]{0:T(512)S(1)}, f32[512]{0:T(512)}, u32[]{:S(2)}) copy-start(f32[512]{0:T(512)} %param.37) | copy-start | bytes 6148
  4.8 52.3 %copy-start.7 = (f32[512]{0:T(512)S(1)}, f32[512]{0:T(512)}, u32[]{:S(2)}) copy-start(f32[512]{0:T(512)} %param.39) | copy-start | bytes 6148
  4.8 52.3 %copy-start.8 = (f32[512]{0:T(512)S(1)}, f32[512]{0:T(512)}, u32[]{:S(2)}) copy-start(f32[512]{0:T(512)} %param.42) | copy-start | bytes 6148
  27.4 29.7 %copy-start = (bf16[1024,512]{1,0:T(8,128)(2,1)S(1)}, bf16[1024,512]{1,0:T(8,128)(2,1)}, u32[]{:S(2)}) copy-start(bf16[1024,512]{1,0:T(8,128)(2,1)} %node_input_ref.1) | copy-start | bytes 3145732
  27.5 29.7 %copy-start.1 = (bf16[512,512]{1,0:T(8,128)(2,1)S(1)}, bf16[512,512]{1,0:T(8,128)(2,1)}, u32[]{:S(2)}) copy-start(bf16[512,512]{1,0:T(8,128)(2,1)} %edge_out_ref.1) | copy-start | bytes 1572868
  27.5 29.6 %collective-permute-start = (bf16[64,512]{1,0:T(8,128)(2,1)S(1)}, bf16[64,512]{1,0:T(8,128)(2,1)S(1)}, u32[]{:S(2)}, u32[]{:S(2)}) collective-permute-start(bf16[64,512]{1,0:T(8,128)(2,1)S(1)} %get-tuple-element.12), channel_id=1, source_target_pairs={{0,1},{1,2},{2,3},{3,4},{4,5},{5,6},{6,7},{7,8},{8,9},{9,10},{10,1... | collective-permute-start | bytes 196616 | tf_op jit(solution)/shard_map/ppermute | solution.py:338
  30.0 27.1 %collective-permute-start.1 = (bf16[64,512]{1,0:T(8,128)(2,1)S(1)}, bf16[64,512]{1,0:T(8,128)(2,1)S(1)}, u32[]{:S(2)}, u32[]{:S(2)}) collective-permute-start(bf16[64,512]{1,0:T(8,128)(2,1)S(1)} %get-tuple-element.13), channel_id=1, source_target_pairs={{1,0},{2,1},{3,2},{4,3},{5,4},{6,5},{7,6},{8,7},{9,8},{10,9},{11,1... | collective-permute-start | bytes 196616 | tf_op jit(solution)/shard_map/ppermute | solution.py:339
  59.0 13.7 %copy-start.10 = (bf16[1024,512]{1,0:T(8,128)(2,1)S(1)}, bf16[1024,512]{1,0:T(8,128)(2,1)}, u32[]{:S(2)}) copy-start(bf16[1024,512]{1,0:T(8,128)(2,1)} %update_input_ref.1) | copy-start | bytes 3145732
  59.0 13.7 %copy-start.13 = (bf16[512,512]{1,0:T(8,128)(2,1)S(1)}, bf16[512,512]{1,0:T(8,128)(2,1)}, u32[]{:S(2)}) copy-start(bf16[512,512]{1,0:T(8,128)(2,1)} %message_out_ref.1) | copy-start | bytes 1572868
  59.0 13.7 %copy-start.14 = (bf16[512,512]{1,0:T(8,128)(2,1)S(1)}, bf16[512,512]{1,0:T(8,128)(2,1)}, u32[]{:S(2)}) copy-start(bf16[512,512]{1,0:T(8,128)(2,1)} %update_out_ref.1) | copy-start | bytes 1572868
  59.0 13.7 %copy-start.23 = (s32[4,128]{1,0:T(4,128)S(1)}, s32[4,128]{1,0:T(4,128)}, u32[]{:S(2)}) copy-start(s32[4,128]{1,0:T(4,128)} %recv_ref.3) | copy-start | bytes 6148
  59.0 13.7 %copy-start.24 = (f32[512]{0:T(512)S(1)}, f32[512]{0:T(512)}, u32[]{:S(2)}) copy-start(f32[512]{0:T(512)} %param.45) | copy-start | bytes 6148
  59.1 13.7 %copy-start.25 = (f32[512]{0:T(512)S(1)}, f32[512]{0:T(512)}, u32[]{:S(2)}) copy-start(f32[512]{0:T(512)} %param.47) | copy-start | bytes 6148
  59.1 13.7 %all-to-all-start = ((bf16[16,16,512]{2,1,0:T(8,128)(2,1)}), bf16[16,16,512]{2,1,0:T(8,128)(2,1)S(1)}, u32[]{:S(2)}, u32[]{:S(2)}) async-start(bf16[16,16,512]{2,1,0:T(8,128)(2,1)} %bitcast.9), calls=%async_computation | async-start | bytes 524288 | tf_op jit(solution)/shard_map/all_to_all | solution.py:375

commit v2 on v1

v2 whole, which is shorter than its diff:
```python
import functools
import math

import jax
import jax.numpy as jnp
from jax import lax
from jax.experimental import pallas as pl
from jax.experimental.pallas import tpu as pltpu
from jax.sharding import PartitionSpec as P

F32 = jnp.float32
BF16 = jnp.bfloat16
I32 = jnp.int32
SEND_CAP = 16
LANES = 128
VMEM = pltpu.VMEM
SMEM = pltpu.SMEM
PARAMS = pltpu.CompilerParams(vmem_limit_bytes=40 * 1024 * 1024)


def mm(left, right):
    return jnp.dot(left, right, preferred_element_type=F32)


def mm_nt(left, right):
    return lax.dot_general(left, right, (((1,), (1,)), ((), ())), preferred_element_type=F32)


def silu_half(half):
    return half + half * jnp.tanh(half)


def silu(value):
    return silu_half(0.5 * value)


def layer_norm(value):
    center = value - jnp.mean(value, axis=-1, keepdims=True)
    spread = jnp.mean(center * center, axis=-1, keepdims=True)
    return center * lax.rsqrt(spread + 1e-05)


def iota(shape, dim):
    return lax.broadcasted_iota(I32, shape, dim)


def one_hot(columns, rows):
    hit = columns.astype(jnp.int16) == lax.broadcasted_iota(jnp.int16, (rows, columns.shape[1]), 0)
    return jnp.where(hit, jnp.ones((), BF16), jnp.zeros((), BF16))


def ids_of_rows(slot, first, count):
    nodes = slot.shape[1]
    rows = iota((count, nodes), 0) + first
    return jnp.max(jnp.where(slot == rows, iota((count, nodes), 1), -1), axis=1, keepdims=True)


def grid_kernel(
    grid_ref,
    first_ref,
    grid_bias_ref,
    second_ref,
    send_weight_ref,
    edge_bias_ref,
    table_ref,
):
    channels, grid_rows = grid_ref.shape
    width = second_ref.shape[1]
    step_rows = 512
    first_t = (0.5 * first_ref[...].astype(F32)).T.astype(BF16)
    second_t = second_ref[...].T
    weight_t = (0.5 * send_weight_ref[...].astype(F32)).T.astype(BF16)
    grid_bias = jnp.broadcast_to(0.5 * grid_bias_ref[...], (LANES, width)).T
    edge_bias = jnp.broadcast_to(0.5 * edge_bias_ref[...], (LANES, width)).T
    wide = lambda column: jnp.concatenate([column] * (step_rows // LANES), axis=1)
    for start in range(0, grid_rows, step_rows):
        half = mm(first_t, grid_ref[:, start : start + step_rows]) + wide(grid_bias)
        value = mm(second_t, silu_half(half).astype(BF16))
        center = value - jnp.mean(value, axis=0, keepdims=True)
        spread = jnp.mean(center * center, axis=0, keepdims=True)
        code = (center * lax.rsqrt(spread + 1e-05)).astype(BF16)
        part = mm(weight_t, code) + wide(edge_bias)
        table_ref[:, start : start + step_rows] = part.astype(BF16)


def edge_kernel(
    place_ref,
    count_ref,
    table_ref,
    feat_weight_ref,
    slot_ref,
    send_ref,
    recv_ref,
    feat_ref,
    own_ref,
    cross_ref,
    chip_ref,
    total,
):
    grid_rows = table_ref.shape[1]
    width = table_ref.shape[0]
    blocks, block_edges = send_ref.shape
    owned = own_ref.shape[0]
    feats = feat_ref.shape[1]
    place = place_ref[0]
    used = count_ref[0]
    feat_weight = jnp.concatenate(
        [0.5 * feat_weight_ref[...].astype(F32), jnp.zeros((LANES - feats, width), F32)], axis=0
    )
    feat_weight = feat_weight.T.astype(BF16)[:, :feats]
    ids = ids_of_rows(slot_ref[...], (place - 1) * owned, 3 * owned)
    group = math.gcd(blocks, 4)
    total[...] = jnp.zeros_like(total)

    def edge_step(step, carry):
        first = step * group
        senders = jnp.concatenate([send_ref[pl.ds(first + b, 1), :] for b in range(group)], axis=1)
        picker = one_hot(senders, grid_rows)
        feat = jnp.concatenate([feat_ref[first + b] for b in range(group)], axis=1)
        half = mm(table_ref[...], picker) + mm(feat_weight, feat.astype(BF16))
        hidden = silu_half(half).astype(BF16)
        receivers = jnp.concatenate(
            [
                jnp.where(first + b < used, recv_ref[pl.ds(first + b, 1), :], -2)
                for b in range(group)
            ],
            axis=1,
        )
        spread = (ids == receivers).astype(F32).astype(BF16)
        total[...] += mm_nt(hidden, spread)
        return carry

    lax.fori_loop(0, blocks // group, edge_step, 0)
    pad = -3 * owned % LANES
    sums = jnp.concatenate([total[...], jnp.zeros((width, pad), F32)], axis=1).T
    below, above = sums[:owned].astype(BF16), sums[2 * owned : 3 * owned].astype(BF16)
    own_ref[...] = sums[owned : 2 * owned]
    odd = place % 2 == 1
    cross_ref[...] = jnp.where(odd, above, below)
    chip_ref[...] = jnp.where(odd, below, above)


def wanted_kernel(owned, slot_ref, send_ref, wanted_ref):
    nodes = slot_ref.shape[1]
    blocks, block_edges = send_ref.shape
    places = wanted_ref.shape[1]
    chunk = LANES
    per_chunk = chunk // owned * SEND_CAP
    row, column = iota((chunk, chunk), 0), iota((chunk, chunk), 1)
    before = ((row > column) & (row // owned == column // owned)).astype(F32).astype(BF16)
    local_owner = (iota((chunk, LANES), 0) // owned * SEND_CAP).astype(F32)

    def find(index, best):
        ids = ids_of_rows(slot_ref[...], index * chunk, chunk)
        hit = jnp.zeros((chunk, block_edges), F32)
        for b in range(blocks):
            hit = jnp.maximum(hit, (ids == send_ref[b : b + 1, :]).astype(F32))
        hit = jnp.broadcast_to(jnp.max(hit, axis=1, keepdims=True), (chunk, LANES))
        rank = mm(before, hit.astype(BF16)) + local_owner
        spot = jnp.where(hit > 0, rank.astype(I32) + index * per_chunk, -1)
        spot = jnp.concatenate([spot] * (places // LANES), axis=1)
        found = jnp.where(spot == iota((chunk, places), 1), ids, -1)
        return jnp.maximum(best, jnp.max(found, axis=0, keepdims=True))

    best = lax.fori_loop(0, nodes // chunk, find, jnp.full((1, places), -1, I32))
    best = best.astype(F32)
    for b in range(blocks):
        senders = jnp.broadcast_to(send_ref[b : b + 1, :].astype(F32), (block_edges, block_edges)).T
        senders = jnp.concatenate([senders] * (places // LANES), axis=1)
        wanted_ref[b * block_edges : (b + 1) * block_edges, :] = (
            (senders == best).astype(F32).astype(BF16)
        )


def supply_kernel(place_ref, slot_ref, request_ref, code_ref, rows_ref):
    owned = code_ref.shape[0]
    devices = rows_ref.shape[0] // SEND_CAP
    per_device = request_ref.shape[0] // devices
    ids = ids_of_rows(slot_ref[...], place_ref[0] * owned, owned)
    lane = iota((owned, LANES), 1)
    used = jnp.zeros((owned, LANES), F32)
    for d in range(devices):
        hit = jnp.zeros((owned, request_ref.shape[1]), F32)
        for b in range(per_device):
            at = d * per_device + b
            hit = jnp.maximum(hit, (ids == request_ref[at : at + 1, :]).astype(F32))
        used = jnp.where(lane == d, jnp.max(hit, axis=1, keepdims=True), used)
    before = (iota((owned, owned), 0) > iota((owned, owned), 1)).astype(F32).astype(BF16)
    rank = jnp.where(used > 0, mm(before, used.astype(BF16)), -1.0)
    rank = jnp.concatenate([rank, jnp.full((LANES - owned, LANES), -1.0, F32)], axis=0).T
    slots = iota((SEND_CAP, owned), 0).astype(F32)
    supply = jnp.concatenate(
        [(rank[d : d + 1, :owned] == slots).astype(F32) for d in range(devices)], axis=0
    )
    rows_ref[...] = mm(supply.astype(BF16), code_ref[...]).astype(BF16)


def node_kernel(
    own_ref,
    from_cross_ref,
    from_chip_ref,
    latent_ref,
    edge_out_ref,
    node_input_ref,
    node_bias_ref,
    node_out_ref,
    node_gain_ref,
    mesh_sender_ref,
    encoded_ref,
    code_ref,
):
    width = latent_ref.shape[1]
    latent = latent_ref[...]
    node_sum = own_ref[...] + from_cross_ref[...].astype(F32) + from_chip_ref[...].astype(F32)
    aggregate = mm(node_sum.astype(BF16), edge_out_ref[...]).astype(BF16)
    hidden = mm(latent, node_input_ref[:width]) + mm(aggregate, node_input_ref[width:])
    hidden = silu(hidden + node_bias_ref[...]).astype(BF16)
    encoded = latent.astype(F32) + layer_norm(mm(hidden, node_out_ref[...])) * node_gain_ref[...]
    encoded = encoded.astype(BF16)
    encoded_ref[...] = encoded
    code_ref[...] = mm(encoded, mesh_sender_ref[...]).astype(BF16)


def receiver_kernel(
    place_ref,
    slot_ref,
    recv_ref,
    encoded_ref,
    mesh_receiver_ref,
    message_bias_ref,
    update_input_ref,
    update_bias_ref,
    incoming_ref,
    receiver_ref,
    upper_ref,
):
    owned, width = encoded_ref.shape
    blocks = recv_ref.shape[0]
    ids = ids_of_rows(slot_ref[...], place_ref[0] * owned, owned)
    incoming = jnp.concatenate(
        [(ids == recv_ref[b : b + 1, :]).astype(F32) for b in range(blocks)], axis=1
    )
    pick = incoming.T.astype(BF16)
    incoming_ref[...] = incoming.astype(BF16)
    encoded = encoded_ref[...]
    receiver = mm(encoded, mesh_receiver_ref[...]) + message_bias_ref[...]
    high = receiver.astype(BF16)
    low = (receiver - high.astype(F32)).astype(BF16)
    receiver_ref[...] = mm(pick, high) + mm(pick, low)
    upper_ref[...] = mm(encoded, update_input_ref[:width]) + update_bias_ref[...]


def message_kernel(
    wanted_ref,
    piece_ref,
    incoming_ref,
    receiver_ref,
    upper_ref,
    encoded_ref,
    message_out_ref,
    update_input_ref,
    update_out_ref,
    update_gain_ref,
    out_ref,
):
    width = encoded_ref.shape[1]
    message = silu(mm(wanted_ref[...], piece_ref[...]) + receiver_ref[...]).astype(BF16)
    message_sum = mm(incoming_ref[...], message).astype(BF16)
    update = mm(message_sum, message_out_ref[...]).astype(BF16)
    hidden = silu(upper_ref[...] + mm(update, update_input_ref[width:])).astype(BF16)
    out = layer_norm(mm(hidden, update_out_ref[...])) * update_gain_ref[...]
    out_ref[...] = (encoded_ref[...].astype(F32) + out).astype(BF16)


def call(kernel, out_shape, spaces, scratch=(), flops=0, moved=0):
    return pl.pallas_call(
        kernel,
        out_shape=out_shape,
        in_specs=[pl.BlockSpec(memory_space=space) for space in spaces],
        out_specs=jax.tree.map(lambda _: pl.BlockSpec(memory_space=VMEM), out_shape),
        scratch_shapes=scratch,
        compiler_params=PARAMS,
        cost_estimate=pl.CostEstimate(flops=flops, bytes_accessed=moved, transcendentals=0),
    )


def shape(*sizes, kind=BF16):
    return jax.ShapeDtypeStruct(sizes, kind)


def per_device(
    grid_in,
    grid_first,
    grid_bias,
    grid_second,
    send_weight,
    edge_bias,
    feat_weight,
    edge_out,
    node_input,
    node_bias,
    node_out,
    node_gain,
    mesh_sender,
    mesh_receiver,
    message_bias,
    message_out,
    update_input,
    update_bias,
    update_out,
    update_gain,
    mesh_latent,
    g2m_send,
    g2m_recv,
    g2m_feat,
    g2m_count,
    mesh_slot,
    mesh_send,
    mesh_recv,
):
    devices = lax.axis_size("bulk")
    position = lax.axis_index("bulk")
    place = position.astype(I32).reshape(1)
    owned, width = mesh_latent.shape
    grid_rows = grid_in.shape[0]
    places = devices * SEND_CAP
    edges = mesh_send.size
    slot = mesh_slot.reshape(1, -1)
    row = lambda vector: vector.reshape(1, -1)

    table = call(
        grid_kernel,
        shape(width, grid_rows),
        [VMEM] * 6,
        flops=3_000_000_000,
        moved=4_000_000,
    )(grid_in.T, grid_first, row(grid_bias), grid_second, send_weight, row(edge_bias))
    own, cross, chip = call(
        edge_kernel,
        (shape(owned, width, kind=F32), shape(owned, width), shape(owned, width)),
        [SMEM, SMEM] + [VMEM] * 6,
        scratch=[pltpu.VMEM((width, 3 * owned), F32)],
        flops=7_000_000_000,
        moved=4_000_000,
    )(place, g2m_count, table, feat_weight, slot, g2m_send, g2m_recv, g2m_feat)
    crossing = [(d, d + 1) for d in range(1, devices - 1, 2)]
    within = [(d, d + 1) for d in range(0, devices, 2)]
    both = lambda pairs: pairs + [(b, a) for a, b in pairs]
    from_cross = lax.ppermute(cross, "bulk", both(crossing))
    from_chip = lax.ppermute(chip, "bulk", both(within))
    asked = jnp.tile(mesh_send, (devices, 1))
    asked, _ = lax.optimization_barrier((asked, chip))
    requests = lax.all_to_all(asked, "bulk", 0, 0, tiled=True)
    encoded, code = call(
        node_kernel,
        (shape(owned, width), shape(owned, width)),
        [VMEM] * 10,
        flops=500_000_000,
        moved=4_000_000,
    )(
        own,
        from_cross,
        from_chip,
        mesh_latent,
        edge_out,
        node_input,
        row(node_bias),
        node_out,
        row(node_gain),
        mesh_sender,
    )
    rows = call(
        supply_kernel,
        shape(places, width),
        [SMEM] + [VMEM] * 3,
        flops=500_000_000,
        moved=500_000,
    )(place, slot, requests, code)
    piece = lax.all_to_all(rows, "bulk", 0, 0, tiled=True)
    wanted = call(
        functools.partial(wanted_kernel, owned),
        shape(edges, places),
        [VMEM] * 2,
        flops=1_000_000_000,
        moved=500_000,
    )(slot, mesh_send)
    incoming, receiver, upper = call(
        receiver_kernel,
        (shape(owned, edges), shape(edges, width, kind=F32), shape(owned, width, kind=F32)),
        [SMEM] + [VMEM] * 7,
        flops=1_000_000_000,
        moved=4_000_000,
    )(
        place,
        slot,
        mesh_recv,
        encoded,
        mesh_receiver,
        row(message_bias),
        update_input,
        row(update_bias),
    )
    return call(
        message_kernel,
        shape(owned, width),
        [VMEM] * 10,
        flops=1_000_000_000,
        moved=4_000_000,
    )(
        wanted,
        piece,
        incoming,
        receiver,
        upper,
        encoded,
        message_out,
        update_input,
        update_out,
        row(update_gain),
    )


def solution(mesh):
    split = {0: ("groups", "bulk"), 20: "bulk", 21: "bulk", 22: "bulk", 23: "bulk", 24: "bulk"}
    split.update({26: "bulk", 27: "bulk"})
    placed = tuple(P(split[at]) if at in split else P() for at in range(28))
    return jax.shard_map(
        per_device,
        mesh=mesh,
        in_specs=placed,
        out_specs=P(("groups", "bulk"), None),
        check_vma=False,
    )
```

time: 75.6 us -> 60.1 us (0.79)
  blocking collectives: 25.1 us -> 0 us
  local copies, waits for them, and re-layouts: 4.06 us -> 11.3 us
  Pallas kernels: 31.6 us -> 24.7 us
  starting transfers between devices: 7.47 us -> 13.6 us
  waiting for transfers between devices: 6.01 us -> 8.77 us
    all_gather x1 -> x0, blocking collectives: 25.1 us -> none  [per_device(): requests = lax.all_gather(mesh_send, 'bulk', axis=0, tiled=True)]
    all_to_all x0 -> x1, starting transfers between devices: none -> 8.8 us  [per_device(): requests = lax.all_to_all(asked, 'bulk', 0, 0, tiled=True)]
    pallas_call x4 -> x6, Pallas kernels: 27.6 us -> 20.7 us  [the longest x1 10.3 us: per_device(): call(edge_kernel, (shape(owned, width, kind=F32), shape(owned, width), sh...]
    unnamed x53 -> x68, local copies, waits for them, and re-layouts: 4.06 us -> 10.7 us
    all_to_all x0 -> x1, waiting for transfers between devices: none -> 4.93 us  [per_device(): requests = lax.all_to_all(asked, 'bulk', 0, 0, tiled=True)]
    ppermute x2, starting transfers between devices: 3.8 us -> 1.17 us  [the longest x1 0.65 us: per_device(): from_cross = lax.ppermute(cross, 'bulk', both(crossing))]
    all_to_all x1, waiting for transfers between devices: 6 us -> 3.84 us  [per_device(): piece = lax.all_to_all(rows, 'bulk', 0, 0, tiled=True)]
  transfers between devices with their start and end apart: 3 -> 4, of which waited for: 1 -> 2; matrix products, arithmetic and copies ran while one was open for 0% -> 1% of each run, Pallas kernels for 6% -> 10%
where the time goes in v2:
time: 60.1 us; the launch traced here: 59.4 us
  Pallas kernels  24.7 us (41%)
  starting transfers between devices  13.6 us (23%)
  local copies, waits for them, and re-layouts  11.3 us (19%)
  waiting for transfers between devices  8.77 us (15%)
  between operations  1.03 us (2%)
    unnamed x68, local copies, waits for them, and re-layouts  10.7 us
    pallas_call x1, Pallas kernels, per_device(): call(edge_kernel, (shape(owned, width, kind=F32), shape(owned, width), sh...  10.3 us
    all_to_all x1, starting transfers between devices, per_device(): requests = lax.all_to_all(asked, 'bulk', 0, 0, tiled=True)  8.8 us
    pallas_call x1, Pallas kernels, per_device(): call(grid_kernel, shape(width, grid_rows), [VMEM] * 6, flops=3000000000,...  5.4 us
    all_to_all x1, waiting for transfers between devices, per_device(): requests = lax.all_to_all(asked, 'bulk', 0, 0, tiled=True)  4.93 us
    pallas_call x1, Pallas kernels, per_device(): call(functools.partial(wanted_kernel, owned), shape(edges, places), [VMEM...  3.99 us
    all_to_all x1, waiting for transfers between devices, per_device(): piece = lax.all_to_all(rows, 'bulk', 0, 0, tiled=True)  3.84 us
    all_to_all x1, starting transfers between devices, per_device(): piece = lax.all_to_all(rows, 'bulk', 0, 0, tiled=True)  3.66 us
  transfers between devices with their start and end apart: 4, of which 2 were waited for; matrix products, arithmetic and copies ran while one was open for 1% of the time, Pallas kernels for 10%

profile of v2, /device:TPU:0, one launch (start us, length us, event | category | flops | bytes accessed | tf_op | source)
XLA Modules:
  0.0 59.4 jit_solution(13303224380685224960)
XLA Ops:
  0.7 0.0 copy-start.19
  0.7 1.5 %copy-done.19 = bf16[2048,474]{0,1:T(8,128)(2,1)S(1)} copy-done((bf16[2048,474]{0,1:T(8,128)(2,1)S(1)}, bf16[2048,474]{0,1:T(8,128)(2,1)}, u32[]{:S(2)}) %copy-start.19) | copy-done | bytes 1941528
  2.2 1.0 %copy-done.20 = bf16[512,512]{1,0:T(8,128)(2,1)S(1)} copy-done((bf16[512,512]{1,0:T(8,128)(2,1)S(1)}, bf16[512,512]{1,0:T(8,128)(2,1)}, u32[]{:S(2)}) %copy-start.20) | copy-done | bytes 524312
  3.2 1.0 %copy-done.21 = bf16[512,512]{1,0:T(8,128)(2,1)S(1)} copy-done((bf16[512,512]{1,0:T(8,128)(2,1)S(1)}, bf16[512,512]{1,0:T(8,128)(2,1)}, u32[]{:S(2)}) %copy-start.21) | copy-done | bytes 524312
  4.3 1.0 %copy-done.23 = bf16[474,512]{1,0:T(8,128)(2,1)S(1)} copy-done((bf16[474,512]{1,0:T(8,128)(2,1)S(1)}, bf16[474,512]{1,0:T(8,128)(2,1)}, u32[]{:S(2)}) %copy-start.23) | copy-done | bytes 485400
  5.3 0.7 %copy-done.29 = f32[512]{0:T(512)S(1)} copy-done((f32[512]{0:T(512)S(1)}, f32[512]{0:T(512)}, u32[]{:S(2)}) %copy-start.29) | copy-done | bytes 2072
  6.0 0.7 %copy-done.30 = f32[512]{0:T(512)S(1)} copy-done((f32[512]{0:T(512)S(1)}, f32[512]{0:T(512)}, u32[]{:S(2)}) %copy-start.30) | copy-done | bytes 2072
  6.7 0.0 copy-start.28
  6.7 5.4 %shard_map.263.table_ref = bf16[512,2048]{1,0:T(8,128)(2,1)S(1)} custom-call(bf16[474,2048]{1,0:T(8,128)(2,1)S(1)} %bitcast.20, bf16[474,512]{1,0:T(8,128)(2,1)S(1)} %copy-done.23, f32[1,512]{1,0:T(1,128)S(1)} %bitcast.25, bf16[512,512]{1,0:T(8,128)(2,1)S(1)} %copy-done.20, bf16[512,512]{1,0:T(8,128)(2,1)S(1)} %copy-done.21, f32[1,512]{1,0:T(1,128)S(1)} %bitcast.26), custom_call_target="tpu_custom_call" | custom-call | flops 3000000000 | bytes 4000000 | tf_op jit(solution)/shard_map/pallas_call | solution.py:331
  12.1 0.0 copy-done.24
  12.1 0.0 copy-done.25
  12.1 0.0 copy-done.26
  12.1 0.0 copy-done.27
  12.1 0.0 copy-done.28
  12.2 0.0 copy-start.16
  12.2 0.0 copy-start.1
  12.2 0.0 copy-start.4
  12.2 0.0 copy-start.5
  12.2 0.0 copy-start.6
  12.2 0.0 copy-start.14
  12.2 0.0 copy-start.17
  12.2 0.0 copy-start.18
  12.3 10.3 %shard_map.264 = (f32[64,512]{1,0:T(8,128)S(1)}, bf16[64,512]{1,0:T(8,128)(2,1)S(1)}, bf16[64,512]{1,0:T(8,128)(2,1)S(1)}) custom-call(s32[1]{0:T(128)} %bitcast.1.place_ref, s32[1]{0:T(128)S(6)} %copy.29.count_ref, bf16[512,2048]{1,0:T(8,128)(2,1)S(1)} %shard_map.263.table_ref, bf16[4,512]{1,0:T(4,128)(2,1)S(1)} %copy-done.27, s32[1,1024]{1,0:T(1,128)S(1)} %bitcast.21, ...), custom_call_target="tpu_custom_call" | custom-call | flops 7000000000 | bytes 4000000 | tf_op jit(solution)/shard_map/pallas_call | solution.py:338
  22.5 0.5 collective-permute-start.1
  23.0 0.7 %collective-permute-start = (bf16[64,512]{1,0:T(8,128)(2,1)S(1)}, bf16[64,512]{1,0:T(8,128)(2,1)S(1)}, u32[]{:S(2)}, u32[]{:S(2)}) collective-permute-start(bf16[64,512]{1,0:T(8,128)(2,1)S(1)} %get-tuple-element.17), channel_id=1, source_target_pairs={{1,2},{3,4},{5,6},{7,8},{9,10},{11,12},{13,14},{2,1},{4,3},{6,5},{... | collective-permute-start | bytes 196616 | tf_op jit(solution)/shard_map/ppermute | solution.py:349
  23.7 0.0 copy-done.16
  23.7 0.6 %tile.4 = s32[16,4,128]{2,1,0:T(4,128)} broadcast(s32[4,128]{1,0:T(4,128)S(1)} %copy-done.16), dimensions={1,2} | broadcast | bytes 34816 | tf_op jit(solution)/shard_map/tile | solution.py:351
  24.3 8.8 %all-to-all-start = ((s32[16,4,128]{2,1,0:T(4,128)}), s32[16,4,128]{2,1,0:T(4,128)S(1)}, u32[]{:S(2)}, u32[]{:S(2)}) async-start(s32[16,4,128]{2,1,0:T(4,128)} %bitcast.6), calls=%async_computation | async-start | bytes 65536 | tf_op jit(solution)/shard_map/all_to_all | solution.py:353
  33.1 0.0 collective-permute-done.1.from_chip_ref
  33.1 0.0 collective-permute-done.from_cross_ref
  33.1 0.0 copy-done.1
  33.2 0.0 copy-done.4
  33.2 0.0 copy-done.5
  33.2 0.0 copy-done.6
  33.2 0.0 copy-done.14
  33.2 0.0 copy-done.17
  33.2 0.0 copy-done.18
  33.2 1.0 %shard_map.265 = (bf16[64,512]{1,0:T(8,128)(2,1)S(1)}, bf16[64,512]{1,0:T(8,128)(2,1)S(1)}) custom-call(f32[64,512]{1,0:T(8,128)S(1)} %get-tuple-element.16.own_ref, bf16[64,512]{1,0:T(8,128)(2,1)S(1)} %collective-permute-done.from_cross_ref, bf16[64,512]{1,0:T(8,128)(2,1)S(1)} %collective-permute-done.1.from_chip_ref, bf16[64,512]{1,0:T(8,128)(2,1)S(1)} %copy-done.14, ...), custom_call_target="tpu_custom_call" | custom-call | flops 500000000 | bytes 4000000 | tf_op jit(solution)/shard_map/pallas_call | solution.py:354
  34.2 0.0 copy-start.9
  34.2 0.6 %copy-done.9 = bf16[64,512]{1,0:T(8,128)(2,1)} copy-done((bf16[64,512]{1,0:T(8,128)(2,1)}, bf16[64,512]{1,0:T(8,128)(2,1)S(1)}, u32[]{:S(2)}) %copy-start.9) | copy-done | bytes 65560
  34.8 4.9 %all-to-all-done = s32[16,4,128]{2,1,0:T(4,128)S(1)} async-done(((s32[16,4,128]{2,1,0:T(4,128)}), s32[16,4,128]{2,1,0:T(4,128)S(1)}, u32[]{:S(2)}, u32[]{:S(2)}) %all-to-all-start) | async-done | bytes 32800 | tf_op jit(solution)/shard_map/all_to_all | solution.py:353
  39.8 1.5 %shard_map.266 = bf16[256,512]{1,0:T(8,128)(2,1)} custom-call(s32[1]{0:T(128)} %bitcast.1.place_ref, s32[1,1024]{1,0:T(1,128)S(1)} %bitcast.22, s32[64,128]{1,0:T(8,128)S(1)} %bitcast.16, bf16[64,512]{1,0:T(8,128)(2,1)S(1)} %get-tuple-element.18.code_ref), custom_call_target="tpu_custom_call" | custom-call | flops 500000000 | bytes 500000 | tf_op jit(solution)/shard_map/pallas_call | solution.py:372
  41.3 3.7 %all-to-all-start.1 = ((bf16[16,16,512]{2,1,0:T(8,128)(2,1)}), bf16[16,16,512]{2,1,0:T(8,128)(2,1)S(1)}, u32[]{:S(2)}, u32[]{:S(2)}) async-start(bf16[16,16,512]{2,1,0:T(8,128)(2,1)} %bitcast.10), calls=%async_computation.1 | async-start | bytes 524288 | tf_op jit(solution)/shard_map/all_to_all | solution.py:379
  45.0 0.0 copy-start.10
  45.0 0.0 copy-start.22
  45.0 0.0 copy-start.33
  45.0 4.0 %shard_map.262.wanted_ref = bf16[512,256]{1,0:T(8,128)(2,1)S(1)} custom-call(s32[1,1024]{1,0:T(1,128)S(1)} %bitcast.23, s32[4,128]{1,0:T(4,128)S(1)} %copy-done.16), custom_call_target="tpu_custom_call" | custom-call | flops 1000000000 | bytes 500000 | tf_op jit(solution)/shard_map/pallas_call | solution.py:380
  49.0 0.0 copy-start.7
  49.0 0.7 %copy-done.7 = bf16[512,256]{1,0:T(8,128)(2,1)} copy-done((bf16[512,256]{1,0:T(8,128)(2,1)}, bf16[512,256]{1,0:T(8,128)(2,1)S(1)}, u32[]{:S(2)}) %copy-start.7) | copy-done | bytes 262168
  49.7 0.0 copy-done
  49.7 0.0 copy-done.31
  49.7 0.0 copy-done.32
  49.7 0.0 copy-done.10
  49.7 0.0 copy-done.22
  49.8 0.0 copy-done.33
  49.8 0.7 %shard_map.267 = (bf16[64,512]{1,0:T(8,128)(2,1)S(1)}, f32[512,512]{1,0:T(8,128)S(1)}, f32[64,512]{1,0:T(8,128)S(1)}) custom-call(s32[1]{0:T(128)} %bitcast.1.place_ref, s32[1,1024]{1,0:T(1,128)S(1)} %bitcast.24, s32[4,128]{1,0:T(4,128)S(1)} %copy-done.31, bf16[64,512]{1,0:T(8,128)(2,1)S(1)} %copy-done.10, bf16[512,512]{1,0:T(8,128)(2,1)S(1)} %copy-done.22, ...), custom_call_target="tpu_custom_call" | custom-call | flops 1000000000 | bytes 4000000 | tf_op jit(solution)/shard_map/pallas_call | solution.py:387
  50.5 0.0 copy-start.12
  50.5 0.6 %copy-done.12 = bf16[64,512]{1,0:T(8,128)(2,1)} copy-done((bf16[64,512]{1,0:T(8,128)(2,1)}, bf16[64,512]{1,0:T(8,128)(2,1)S(1)}, u32[]{:S(2)}) %copy-start.12) | copy-done | bytes 65560
  51.1 3.8 %all-to-all-done.1 = bf16[16,16,512]{2,1,0:T(8,128)(2,1)S(1)} async-done(((bf16[16,16,512]{2,1,0:T(8,128)(2,1)}), bf16[16,16,512]{2,1,0:T(8,128)(2,1)S(1)}, u32[]{:S(2)}, u32[]{:S(2)}) %all-to-all-start.1) | async-done | bytes 262176 | tf_op jit(solution)/shard_map/all_to_all | solution.py:379
  55.0 0.0 copy-done.2
  55.0 0.9 %copy-done.8 = bf16[512,256]{1,0:T(8,128)(2,1)S(1)} copy-done((bf16[512,256]{1,0:T(8,128)(2,1)S(1)}, bf16[512,256]{1,0:T(8,128)(2,1)}, u32[]{:S(2)}) %copy-start.8) | copy-done | bytes 262168
  55.9 0.8 %copy-done.11 = bf16[64,512]{1,0:T(8,128)(2,1)S(1)} copy-done((bf16[64,512]{1,0:T(8,128)(2,1)S(1)}, bf16[64,512]{1,0:T(8,128)(2,1)}, u32[]{:S(2)}) %copy-start.11) | copy-done | bytes 65560
  56.8 0.8 %copy-done.13 = bf16[64,512]{1,0:T(8,128)(2,1)S(1)} copy-done((bf16[64,512]{1,0:T(8,128)(2,1)S(1)}, bf16[64,512]{1,0:T(8,128)(2,1)}, u32[]{:S(2)}) %copy-start.13) | copy-done | bytes 65560
  57.6 1.8 %shard_map.268 = bf16[64,512]{1,0:T(8,128)(2,1)} custom-call(bf16[512,256]{1,0:T(8,128)(2,1)S(1)} %copy-done.8, bf16[256,512]{1,0:T(8,128)(2,1)S(1)} %bitcast.15, bf16[64,512]{1,0:T(8,128)(2,1)S(1)} %copy-done.13, f32[512,512]{1,0:T(8,128)S(1)} %get-tuple-element.21.receiver_ref, f32[64,512]{1,0:T(8,128)S(1)} %get-tuple-element.22.upper_ref, ...), custom_call_target="tpu_custom_call" | custom-call | flops 1000000000 | bytes 4000000 | tf_op jit(solution)/shard_map/pallas_call | solution.py:403
  (20 shorter events, 0.0 us)
Async XLA Ops:
  0.7 1.5 %copy-start.19 = (bf16[2048,474]{0,1:T(8,128)(2,1)S(1)}, bf16[2048,474]{0,1:T(8,128)(2,1)}, u32[]{:S(2)}) copy-start(bf16[2048,474]{0,1:T(8,128)(2,1)} %param.28) | copy-start | bytes 5824516
  2.2 1.0 %copy-start.20 = (bf16[512,512]{1,0:T(8,128)(2,1)S(1)}, bf16[512,512]{1,0:T(8,128)(2,1)}, u32[]{:S(2)}) copy-start(bf16[512,512]{1,0:T(8,128)(2,1)} %second_ref.1) | copy-start | bytes 1572868
  3.2 1.0 %copy-start.21 = (bf16[512,512]{1,0:T(8,128)(2,1)S(1)}, bf16[512,512]{1,0:T(8,128)(2,1)}, u32[]{:S(2)}) copy-start(bf16[512,512]{1,0:T(8,128)(2,1)} %send_weight_ref.1) | copy-start | bytes 1572868
  4.3 1.0 %copy-start.23 = (bf16[474,512]{1,0:T(8,128)(2,1)S(1)}, bf16[474,512]{1,0:T(8,128)(2,1)}, u32[]{:S(2)}) copy-start(bf16[474,512]{1,0:T(8,128)(2,1)} %first_ref.1) | copy-start | bytes 1456132
  5.3 0.7 %copy-start.29 = (f32[512]{0:T(512)S(1)}, f32[512]{0:T(512)}, u32[]{:S(2)}) copy-start(f32[512]{0:T(512)} %param.30) | copy-start | bytes 6148
  6.0 0.7 %copy-start.30 = (f32[512]{0:T(512)S(1)}, f32[512]{0:T(512)}, u32[]{:S(2)}) copy-start(f32[512]{0:T(512)} %param.33) | copy-start | bytes 6148
  6.7 5.4 %copy-start.24 = (f32[24,4,128]{2,1,0:T(4,128)S(1)}, f32[24,4,128]{2,1,0:T(4,128)}, u32[]{:S(2)}) copy-start(f32[24,4,128]{2,1,0:T(4,128)} %feat_ref.1) | copy-start | bytes 147460
  6.7 5.4 %copy-start.25 = (s32[24,128]{1,0:T(8,128)S(1)}, s32[24,128]{1,0:T(8,128)}, u32[]{:S(2)}) copy-start(s32[24,128]{1,0:T(8,128)} %send_ref.3) | copy-start | bytes 36868
  6.7 5.4 %copy-start.26 = (s32[24,128]{1,0:T(8,128)S(1)}, s32[24,128]{1,0:T(8,128)}, u32[]{:S(2)}) copy-start(s32[24,128]{1,0:T(8,128)} %recv_ref.2) | copy-start | bytes 36868
  6.7 5.5 %copy-start.27 = (bf16[4,512]{1,0:T(4,128)(2,1)S(1)}, bf16[4,512]{1,0:T(4,128)(2,1)}, u32[]{:S(2)}) copy-start(bf16[4,512]{1,0:T(4,128)(2,1)} %feat_weight_ref.1) | copy-start | bytes 12292
  6.7 5.5 %copy-start.28 = (s32[1024]{0:T(1024)S(1)}, s32[1024]{0:T(1024)}, u32[]{:S(2)}) copy-start(s32[1024]{0:T(1024)} %param.53) | copy-start | bytes 12292
  12.2 11.5 %copy-start.16 = (s32[4,128]{1,0:T(4,128)S(1)}, s32[4,128]{1,0:T(4,128)}, u32[]{:S(2)}) copy-start(s32[4,128]{1,0:T(4,128)} %send_ref.2) | copy-start | bytes 6148
  12.2 21.0 %copy-start.1 = (bf16[1024,512]{1,0:T(8,128)(2,1)S(1)}, bf16[1024,512]{1,0:T(8,128)(2,1)}, u32[]{:S(2)}) copy-start(bf16[1024,512]{1,0:T(8,128)(2,1)} %node_input_ref.1) | copy-start | bytes 3145732
  12.2 21.0 %copy-start.4 = (bf16[512,512]{1,0:T(8,128)(2,1)S(1)}, bf16[512,512]{1,0:T(8,128)(2,1)}, u32[]{:S(2)}) copy-start(bf16[512,512]{1,0:T(8,128)(2,1)} %edge_out_ref.1) | copy-start | bytes 1572868
  12.2 21.0 %copy-start.5 = (bf16[512,512]{1,0:T(8,128)(2,1)S(1)}, bf16[512,512]{1,0:T(8,128)(2,1)}, u32[]{:S(2)}) copy-start(bf16[512,512]{1,0:T(8,128)(2,1)} %node_out_ref.1) | copy-start | bytes 1572868
  12.2 21.0 %copy-start.6 = (bf16[512,512]{1,0:T(8,128)(2,1)S(1)}, bf16[512,512]{1,0:T(8,128)(2,1)}, u32[]{:S(2)}) copy-start(bf16[512,512]{1,0:T(8,128)(2,1)} %mesh_sender_ref.1) | copy-start | bytes 1572868
  12.2 21.0 %copy-start.14 = (bf16[64,512]{1,0:T(8,128)(2,1)S(1)}, bf16[64,512]{1,0:T(8,128)(2,1)}, u32[]{:S(2)}) copy-start(bf16[64,512]{1,0:T(8,128)(2,1)} %latent_ref.1) | copy-start | bytes 196612
  12.2 21.0 %copy-start.17 = (f32[512]{0:T(512)S(1)}, f32[512]{0:T(512)}, u32[]{:S(2)}) copy-start(f32[512]{0:T(512)} %param.37) | copy-start | bytes 6148
  12.2 21.0 %copy-start.18 = (f32[512]{0:T(512)S(1)}, f32[512]{0:T(512)}, u32[]{:S(2)}) copy-start(f32[512]{0:T(512)} %param.39) | copy-start | bytes 6148
  22.5 10.6 %collective-permute-start.1 = (bf16[64,512]{1,0:T(8,128)(2,1)S(1)}, bf16[64,512]{1,0:T(8,128)(2,1)S(1)}, u32[]{:S(2)}, u32[]{:S(2)}) collective-permute-start(bf16[64,512]{1,0:T(8,128)(2,1)S(1)} %get-tuple-element.14), channel_id=1, source_target_pairs={{0,1},{2,3},{4,5},{6,7},{8,9},{10,11},{12,13},{14,15},{1,0},{3,2},... | collective-permute-start | bytes 196616 | tf_op jit(solution)/shard_map/ppermute | solution.py:350
  23.0 10.1 %collective-permute-start = (bf16[64,512]{1,0:T(8,128)(2,1)S(1)}, bf16[64,512]{1,0:T(8,128)(2,1)S(1)}, u32[]{:S(2)}, u32[]{:S(2)}) collective-permute-start(bf16[64,512]{1,0:T(8,128)(2,1)S(1)} %get-tuple-element.17), channel_id=1, source_target_pairs={{1,2},{3,4},{5,6},{7,8},{9,10},{11,12},{13,14},{2,1},{4,3},{6,5},{... | collective-permute-start | bytes 196616 | tf_op jit(solution)/shard_map/ppermute | solution.py:349
  24.3 15.4 %all-to-all-start = ((s32[16,4,128]{2,1,0:T(4,128)}), s32[16,4,128]{2,1,0:T(4,128)S(1)}, u32[]{:S(2)}, u32[]{:S(2)}) async-start(s32[16,4,128]{2,1,0:T(4,128)} %bitcast.6), calls=%async_computation | async-start | bytes 65536 | tf_op jit(solution)/shard_map/all_to_all | solution.py:353
  34.2 0.6 %copy-start.9 = (bf16[64,512]{1,0:T(8,128)(2,1)}, bf16[64,512]{1,0:T(8,128)(2,1)S(1)}, u32[]{:S(2)}) copy-start(bf16[64,512]{1,0:T(8,128)(2,1)S(1)} %get-tuple-element.19.encoded_ref) | copy-start | bytes 196612
  41.3 8.4 %copy-start = (bf16[1024,512]{1,0:T(8,128)(2,1)S(1)}, bf16[1024,512]{1,0:T(8,128)(2,1)}, u32[]{:S(2)}) copy-start(bf16[1024,512]{1,0:T(8,128)(2,1)} %update_input_ref.3) | copy-start | bytes 3145732
  41.3 8.4 %copy-start.31 = (s32[4,128]{1,0:T(4,128)S(1)}, s32[4,128]{1,0:T(4,128)}, u32[]{:S(2)}) copy-start(s32[4,128]{1,0:T(4,128)} %recv_ref.3) | copy-start | bytes 6148
  41.3 8.4 %copy-start.32 = (f32[512]{0:T(512)S(1)}, f32[512]{0:T(512)}, u32[]{:S(2)}) copy-start(f32[512]{0:T(512)} %param.42) | copy-start | bytes 6148
  41.3 13.7 %all-to-all-start.1 = ((bf16[16,16,512]{2,1,0:T(8,128)(2,1)}), bf16[16,16,512]{2,1,0:T(8,128)(2,1)S(1)}, u32[]{:S(2)}, u32[]{:S(2)}) async-start(bf16[16,16,512]{2,1,0:T(8,128)(2,1)} %bitcast.10), calls=%async_computation.1 | async-start | bytes 524288 | tf_op jit(solution)/shard_map/all_to_all | solution.py:379
  45.0 4.8 %copy-start.10 = (bf16[64,512]{1,0:T(8,128)(2,1)S(1)}, bf16[64,512]{1,0:T(8,128)(2,1)}, u32[]{:S(2)}) copy-start(bf16[64,512]{1,0:T(8,128)(2,1)} %copy-done.9) | copy-start | bytes 196612
  45.0 4.8 %copy-start.22 = (bf16[512,512]{1,0:T(8,128)(2,1)S(1)}, bf16[512,512]{1,0:T(8,128)(2,1)}, u32[]{:S(2)}) copy-start(bf16[512,512]{1,0:T(8,128)(2,1)} %mesh_receiver_ref.1) | copy-start | bytes 1572868
  45.0 4.8 %copy-start.33 = (f32[512]{0:T(512)S(1)}, f32[512]{0:T(512)}, u32[]{:S(2)}) copy-start(f32[512]{0:T(512)} %param.45) | copy-start | bytes 6148
  49.0 0.7 %copy-start.7 = (bf16[512,256]{1,0:T(8,128)(2,1)}, bf16[512,256]{1,0:T(8,128)(2,1)S(1)}, u32[]{:S(2)}) copy-start(bf16[512,256]{1,0:T(8,128)(2,1)S(1)} %shard_map.262.wanted_ref) | copy-start | bytes 786436
  49.7 5.3 %copy-start.2 = (bf16[512,512]{1,0:T(8,128)(2,1)S(1)}, bf16[512,512]{1,0:T(8,128)(2,1)}, u32[]{:S(2)}) copy-start(bf16[512,512]{1,0:T(8,128)(2,1)} %message_out_ref.1) | copy-start | bytes 1572868
  49.7 5.3 %copy-start.3 = (bf16[512,512]{1,0:T(8,128)(2,1)S(1)}, bf16[512,512]{1,0:T(8,128)(2,1)}, u32[]{:S(2)}) copy-start(bf16[512,512]{1,0:T(8,128)(2,1)} %update_out_ref.1) | copy-start | bytes 1572868
  49.7 5.3 %copy-start.15 = (f32[512]{0:T(512)S(1)}, f32[512]{0:T(512)}, u32[]{:S(2)}) copy-start(f32[512]{0:T(512)} %param.47) | copy-start | bytes 6148
  50.5 0.6 %copy-start.12 = (bf16[64,512]{1,0:T(8,128)(2,1)}, bf16[64,512]{1,0:T(8,128)(2,1)S(1)}, u32[]{:S(2)}) copy-start(bf16[64,512]{1,0:T(8,128)(2,1)S(1)} %get-tuple-element.20.incoming_ref) | copy-start | bytes 196612
  55.0 1.0 %copy-start.8 = (bf16[512,256]{1,0:T(8,128)(2,1)S(1)}, bf16[512,256]{1,0:T(8,128)(2,1)}, u32[]{:S(2)}) copy-start(bf16[512,256]{1,0:T(8,128)(2,1)} %copy-done.7) | copy-start | bytes 786436
  55.9 0.8 %copy-start.11 = (bf16[64,512]{1,0:T(8,128)(2,1)S(1)}, bf16[64,512]{1,0:T(8,128)(2,1)}, u32[]{:S(2)}) copy-start(bf16[64,512]{1,0:T(8,128)(2,1)} %copy-done.9) | copy-start | bytes 196612
  56.8 0.8 %copy-start.13 = (bf16[64,512]{1,0:T(8,128)(2,1)S(1)}, bf16[64,512]{1,0:T(8,128)(2,1)}, u32[]{:S(2)}) copy-start(bf16[64,512]{1,0:T(8,128)(2,1)} %copy-done.12) | copy-start | bytes 196612

commit v3 on v2

--- a/solution.py
+++ b/solution.py
@@ -15,7 +15,9 @@
 LANES = 128
 VMEM = pltpu.VMEM
 SMEM = pltpu.SMEM
-PARAMS = pltpu.CompilerParams(vmem_limit_bytes=40 * 1024 * 1024)
+HBM = pltpu.HBM
+GRID_STEPS = 4
+MEBI = 1024 * 1024
 
 
 def mm(left, right):
@@ -56,31 +58,60 @@
 
 
 def grid_kernel(
+    grid_hbm,
+    first_hbm,
+    grid_bias_hbm,
+    second_hbm,
+    send_weight_hbm,
+    edge_bias_hbm,
+    table_ref,
     grid_ref,
     first_ref,
     grid_bias_ref,
     second_ref,
     send_weight_ref,
     edge_bias_ref,
-    table_ref,
+    sems,
 ):
     channels, grid_rows = grid_ref.shape
     width = second_ref.shape[1]
-    step_rows = 512
+    step_rows = grid_rows // GRID_STEPS
+    columns = [pl.ds(step * step_rows, step_rows) for step in range(GRID_STEPS)]
+    pairs = [
+        (first_hbm, first_ref),
+        (grid_bias_hbm, grid_bias_ref),
+        (grid_hbm.at[:, columns[0]], grid_ref.at[:, columns[0]]),
+        (second_hbm, second_ref),
+        (send_weight_hbm, send_weight_ref),
+        (edge_bias_hbm, edge_bias_ref),
+    ] + [(grid_hbm.at[:, part], grid_ref.at[:, part]) for part in columns[1:]]
+    copies = [
+        pltpu.make_async_copy(source, target, sems.at[at])
+        for at, (source, target) in enumerate(pairs)
+    ]
+    for copy in copies:
+        copy.start()
+    column = lambda ref: jnp.broadcast_to(0.5 * ref[...], (LANES, width)).T
+    wide = lambda value: jnp.concatenate([value] * (step_rows // LANES), axis=1)
+    for copy in copies[:2]:
+        copy.wait()
     first_t = (0.5 * first_ref[...].astype(F32)).T.astype(BF16)
-    second_t = second_ref[...].T
-    weight_t = (0.5 * send_weight_ref[...].astype(F32)).T.astype(BF16)
-    grid_bias = jnp.broadcast_to(0.5 * grid_bias_ref[...], (LANES, width)).T
-    edge_bias = jnp.broadcast_to(0.5 * edge_bias_ref[...], (LANES, width)).T
-    wide = lambda column: jnp.concatenate([column] * (step_rows // LANES), axis=1)
-    for start in range(0, grid_rows, step_rows):
-        half = mm(first_t, grid_ref[:, start : start + step_rows]) + wide(grid_bias)
-        value = mm(second_t, silu_half(half).astype(BF16))
+    grid_bias = column(grid_bias_ref)
+    for step, part in enumerate(columns):
+        copies[2 if step == 0 else 5 + step].wait()
+        half = mm(first_t, grid_ref[:, part]) + wide(grid_bias)
+        hidden = silu_half(half).astype(BF16)
+        if step == 0:
+            for copy in copies[3:6]:
+                copy.wait()
+            second_t = second_ref[...].T
+            weight_t = (0.5 * send_weight_ref[...].astype(F32)).T.astype(BF16)
+            edge_bias = column(edge_bias_ref)
+        value = mm(second_t, hidden)
         center = value - jnp.mean(value, axis=0, keepdims=True)
         spread = jnp.mean(center * center, axis=0, keepdims=True)
         code = (center * lax.rsqrt(spread + 1e-05)).astype(BF16)
-        part = mm(weight_t, code) + wide(edge_bias)
-        table_ref[:, start : start + step_rows] = part.astype(BF16)
+        table_ref[:, part] = (mm(weight_t, code) + wide(edge_bias)).astype(BF16)
 
 
 def edge_kernel(
@@ -172,9 +203,9 @@
         )
 
 
-def supply_kernel(place_ref, slot_ref, request_ref, code_ref, rows_ref):
-    owned = code_ref.shape[0]
-    devices = rows_ref.shape[0] // SEND_CAP
+def supply_kernel(place_ref, slot_ref, request_ref, supply_ref):
+    owned = supply_ref.shape[1]
+    devices = supply_ref.shape[0] // SEND_CAP
     per_device = request_ref.shape[0] // devices
     ids = ids_of_rows(slot_ref[...], place_ref[0] * owned, owned)
     lane = iota((owned, LANES), 1)
@@ -192,7 +223,7 @@
     supply = jnp.concatenate(
         [(rank[d : d + 1, :owned] == slots).astype(F32) for d in range(devices)], axis=0
     )
-    rows_ref[...] = mm(supply.astype(BF16), code_ref[...]).astype(BF16)
+    supply_ref[...] = supply.astype(BF16)
 
 
 def node_kernel(
@@ -206,8 +237,9 @@
     node_out_ref,
     node_gain_ref,
     mesh_sender_ref,
+    supply_ref,
     encoded_ref,
-    code_ref,
+    rows_ref,
 ):
     width = latent_ref.shape[1]
     latent = latent_ref[...]
@@ -218,7 +250,8 @@
     encoded = latent.astype(F32) + layer_norm(mm(hidden, node_out_ref[...])) * node_gain_ref[...]
     encoded = encoded.astype(BF16)
     encoded_ref[...] = encoded
-    code_ref[...] = mm(encoded, mesh_sender_ref[...]).astype(BF16)
+    sender_code = mm(encoded, mesh_sender_ref[...]).astype(BF16)
+    rows_ref[...] = mm(supply_ref[...], sender_code).astype(BF16)
 
 
 def receiver_kernel(
@@ -272,14 +305,14 @@
     out_ref[...] = (encoded_ref[...].astype(F32) + out).astype(BF16)
 
 
-def call(kernel, out_shape, spaces, scratch=(), flops=0, moved=0):
+def call(kernel, out_shape, spaces, scratch=(), flops=0, moved=0, vmem=8):
     return pl.pallas_call(
         kernel,
         out_shape=out_shape,
         in_specs=[pl.BlockSpec(memory_space=space) for space in spaces],
         out_specs=jax.tree.map(lambda _: pl.BlockSpec(memory_space=VMEM), out_shape),
         scratch_shapes=scratch,
-        compiler_params=PARAMS,
+        compiler_params=pltpu.CompilerParams(vmem_limit_bytes=vmem * MEBI),
         cost_estimate=pl.CostEstimate(flops=flops, bytes_accessed=moved, transcendentals=0),
     )
 
@@ -328,13 +361,25 @@
     slot = mesh_slot.reshape(1, -1)
     row = lambda vector: vector.reshape(1, -1)
 
+    requests = lax.all_to_all(jnp.tile(mesh_send, (devices, 1)), "bulk", 0, 0, tiled=True)
     table = call(
         grid_kernel,
         shape(width, grid_rows),
-        [VMEM] * 6,
+        [HBM] * 6,
+        scratch=[
+            pltpu.VMEM(grid_in.shape[::-1], BF16),
+            pltpu.VMEM(grid_first.shape, BF16),
+            pltpu.VMEM((1, width), F32),
+            pltpu.VMEM(grid_second.shape, BF16),
+            pltpu.VMEM(send_weight.shape, BF16),
+            pltpu.VMEM((1, width), F32),
+            pltpu.SemaphoreType.DMA((5 + GRID_STEPS,)),
+        ],
         flops=3_000_000_000,
         moved=4_000_000,
+        vmem=56,
     )(grid_in.T, grid_first, row(grid_bias), grid_second, send_weight, row(edge_bias))
+    table, requests = lax.optimization_barrier((table, requests))
     own, cross, chip = call(
         edge_kernel,
         (shape(owned, width, kind=F32), shape(owned, width), shape(owned, width)),
@@ -342,19 +387,25 @@
         scratch=[pltpu.VMEM((width, 3 * owned), F32)],
         flops=7_000_000_000,
         moved=4_000_000,
+        vmem=16,
     )(place, g2m_count, table, feat_weight, slot, g2m_send, g2m_recv, g2m_feat)
     crossing = [(d, d + 1) for d in range(1, devices - 1, 2)]
     within = [(d, d + 1) for d in range(0, devices, 2)]
     both = lambda pairs: pairs + [(b, a) for a, b in pairs]
     from_cross = lax.ppermute(cross, "bulk", both(crossing))
     from_chip = lax.ppermute(chip, "bulk", both(within))
-    asked = jnp.tile(mesh_send, (devices, 1))
-    asked, _ = lax.optimization_barrier((asked, chip))
-    requests = lax.all_to_all(asked, "bulk", 0, 0, tiled=True)
-    encoded, code = call(
+    requests, _ = lax.optimization_barrier((requests, own))
+    supply = call(
+        supply_kernel,
+        shape(places, owned),
+        [SMEM] + [VMEM] * 2,
+        flops=500_000_000,
+        moved=500_000,
+    )(place, slot, requests)
+    encoded, rows = call(
         node_kernel,
-        (shape(owned, width), shape(owned, width)),
-        [VMEM] * 10,
+        (shape(owned, width), shape(places, width)),
+        [VMEM] * 11,
         flops=500_000_000,
         moved=4_000_000,
     )(
@@ -368,15 +419,10 @@
         node_out,
         row(node_gain),
         mesh_sender,
-    )
-    rows = call(
-        supply_kernel,
-        shape(places, width),
-        [SMEM] + [VMEM] * 3,
-        flops=500_000_000,
-        moved=500_000,
-    )(place, slot, requests, code)
+        supply,
+    )
     piece = lax.all_to_all(rows, "bulk", 0, 0, tiled=True)
+    mesh_send, _ = lax.optimization_barrier((mesh_send, encoded))
     wanted = call(
         functools.partial(wanted_kernel, owned),
         shape(edges, places),

time: 60.1 us -> 59.6 us (level)
  starting transfers between devices: 13.6 us -> 18.4 us
  waiting for transfers between devices: 8.77 us -> 4.11 us
  local copies, waits for them, and re-layouts: 11.3 us -> 7.54 us
  Pallas kernels: 24.7 us -> 28 us
    all_to_all x1, waiting for transfers between devices: 4.93 us -> 0.01 us  [per_device(): lax.all_to_all(jnp.tile(mesh_send, (devices, 1)), 'bulk', 0, 0, tiled=True)]
    unnamed x68 -> x58, local copies, waits for them, and re-layouts: 10.7 us -> 6.24 us
    pallas_call x3, Pallas kernels: 7.91 us -> 11.3 us  [the longest x1 8.73 us: per_device(): call(grid_kernel, shape(width, grid_rows), [HBM] * 6, scratch=[pltpu.VMEM...]
    all_to_all x1, starting transfers between devices: 3.66 us -> 6.91 us  [per_device(): piece = lax.all_to_all(rows, 'bulk', 0, 0, tiled=True)]
    ppermute x1, starting transfers between devices: 0.52 us -> 3.35 us  [per_device(): from_chip = lax.ppermute(chip, 'bulk', both(within))]
    all_to_all x1, starting transfers between devices: 8.8 us -> 7.39 us  [per_device(): lax.all_to_all(jnp.tile(mesh_send, (devices, 1)), 'bulk', 0, 0, tiled=True)]
    another operation x1, local copies, waits for them, and re-layouts: 0.61 us -> 1.3 us  [per_device(): jnp.tile(mesh_send, (devices, 1))]
  transfers between devices with their start and end apart: 4 -> 4, of which waited for: 2 -> 2; matrix products, arithmetic and copies ran while one was open for 1% -> 0% of each run, Pallas kernels for 10% -> 24%
where the time goes in v3:
time: 59.6 us; the launch traced here: 59.1 us
  Pallas kernels  28 us (47%)
  starting transfers between devices  18.4 us (31%)
  local copies, waits for them, and re-layouts  7.54 us (13%)
  waiting for transfers between devices  4.11 us (7%)
  between operations  0.99 us (2%)
    pallas_call x1, Pallas kernels, per_device(): call(edge_kernel, (shape(owned, width, kind=F32), shape(owned, width), sh...  10.2 us
    pallas_call x1, Pallas kernels, per_device(): call(grid_kernel, shape(width, grid_rows), [HBM] * 6, scratch=[pltpu.VMEM...  8.73 us
    all_to_all x1, starting transfers between devices, per_device(): lax.all_to_all(jnp.tile(mesh_send, (devices, 1)), 'bulk', 0, 0, tiled=True)  7.39 us
    all_to_all x1, starting transfers between devices, per_device(): piece = lax.all_to_all(rows, 'bulk', 0, 0, tiled=True)  6.91 us
    unnamed x58, local copies, waits for them, and re-layouts  6.24 us
    pallas_call x1, Pallas kernels, per_device(): call(functools.partial(wanted_kernel, owned), shape(edges, places), [VMEM...  3.99 us
    all_to_all x1, waiting for transfers between devices, per_device(): piece = lax.all_to_all(rows, 'bulk', 0, 0, tiled=True)  3.88 us
    ppermute x1, starting transfers between devices, per_device(): from_chip = lax.ppermute(chip, 'bulk', both(within))  3.35 us
  transfers between devices with their start and end apart: 4, of which 2 were waited for; matrix products, arithmetic and copies ran while one was open for 0% of the time, Pallas kernels for 24%

profile of v3, /device:TPU:0, one launch (start us, length us, event | category | flops | bytes accessed | tf_op | source)
XLA Modules:
  0.0 59.1 jit_solution(13384507785942794935)
XLA Ops:
  0.0 1.3 %tile.2 = s32[16,4,128]{2,1,0:T(4,128)} broadcast(s32[4,128]{1,0:T(4,128)} %send_ref.2), dimensions={1,2} | broadcast | bytes 34816 | tf_op jit(solution)/shard_map/tile | solution.py:364
  1.3 7.4 %all-to-all-start = ((s32[16,4,128]{2,1,0:T(4,128)}), s32[16,4,128]{2,1,0:T(4,128)S(1)}, u32[]{:S(2)}, u32[]{:S(2)}) async-start(s32[16,4,128]{2,1,0:T(4,128)} %tile.2), calls=%async_computation | async-start | bytes 65536 | tf_op jit(solution)/shard_map/all_to_all | solution.py:364
  8.7 0.0 copy-start.20
  8.7 0.0 copy-start.21
  8.7 0.0 copy-start.22
  8.7 0.0 copy-start.23
  8.7 0.0 copy-start.24
  8.8 8.7 %shard_map.262.table_ref = bf16[512,2048]{1,0:T(8,128)(2,1)} custom-call(bf16[474,2048]{1,0:T(8,128)(2,1)} %bitcast.24, bf16[474,512]{1,0:T(8,128)(2,1)} %first_hbm.1, f32[1,512]{1,0:T(1,128)} %bitcast.25, bf16[512,512]{1,0:T(8,128)(2,1)} %second_hbm.1, bf16[512,512]{1,0:T(8,128)(2,1)} %send_weight_hbm.1, f32[1,512]{1,0:T(1,128)} %bitcast.26), custom_call_target="tpu_custom_call" | custom-call | flops 3000000000 | bytes 4000000 | tf_op jit(solution)/shard_map/pallas_call | solution.py:365
  18.1 0.0 all-to-all-done
  18.2 0.0 copy-done.20
  18.2 0.0 copy-done.21
  18.2 0.0 copy-done.22
  18.2 0.0 copy-done.23
  18.2 0.0 copy-done.24
  18.2 0.0 copy-start.28
  18.2 1.6 %copy-done.28 = bf16[512,2048]{1,0:T(8,128)(2,1)S(1)} copy-done((bf16[512,2048]{1,0:T(8,128)(2,1)S(1)}, bf16[512,2048]{1,0:T(8,128)(2,1)}, u32[]{:S(2)}) %copy-start.28) | copy-done | bytes 2097176
  19.8 0.0 copy-start.5
  19.8 0.0 copy-start.6
  19.8 0.0 copy-start.14
  19.8 0.0 copy-start.18
  19.8 10.2 %shard_map.263 = (f32[64,512]{1,0:T(8,128)S(1)}, bf16[64,512]{1,0:T(8,128)(2,1)S(1)}, bf16[64,512]{1,0:T(8,128)(2,1)S(1)}) custom-call(s32[1]{0:T(128)} %bitcast.1.place_ref, s32[1]{0:T(128)S(6)} %copy.29.count_ref, bf16[512,2048]{1,0:T(8,128)(2,1)S(1)} %copy-done.28, bf16[4,512]{1,0:T(4,128)(2,1)S(1)} %copy-done.23, s32[1,1024]{1,0:T(1,128)S(1)} %bitcast.18, ...), custom_call_target="tpu_custom_call" | custom-call | flops 7000000000 | bytes 4000000 | tf_op jit(solution)/shard_map/pallas_call | solution.py:383
  30.0 0.0 copy-start.1
  30.1 0.0 copy-start.4
  30.1 0.8 %collective-permute-start = (bf16[64,512]{1,0:T(8,128)(2,1)S(1)}, bf16[64,512]{1,0:T(8,128)(2,1)S(1)}, u32[]{:S(2)}, u32[]{:S(2)}) collective-permute-start(bf16[64,512]{1,0:T(8,128)(2,1)S(1)} %get-tuple-element.19), channel_id=1, source_target_pairs={{1,2},{3,4},{5,6},{7,8},{9,10},{11,12},{13,14},{2,1},{4,3},{6,5},{... | collective-permute-start | bytes 196616 | tf_op jit(solution)/shard_map/ppermute | solution.py:395
  30.9 3.3 %collective-permute-start.1 = (bf16[64,512]{1,0:T(8,128)(2,1)S(1)}, bf16[64,512]{1,0:T(8,128)(2,1)S(1)}, u32[]{:S(2)}, u32[]{:S(2)}) collective-permute-start(bf16[64,512]{1,0:T(8,128)(2,1)S(1)} %get-tuple-element.20), channel_id=1, source_target_pairs={{0,1},{2,3},{4,5},{6,7},{8,9},{10,11},{12,13},{14,15},{1,0},{3,2},... | collective-permute-start | bytes 196616 | tf_op jit(solution)/shard_map/ppermute | solution.py:396
  34.2 0.7 %shard_map.264.supply_ref = bf16[256,64]{1,0:T(8,128)(2,1)S(1)} custom-call(s32[1]{0:T(128)} %bitcast.1.place_ref, s32[1,1024]{1,0:T(1,128)S(1)} %bitcast.19, s32[64,128]{1,0:T(8,128)S(1)} %bitcast.14), custom_call_target="tpu_custom_call" | custom-call | flops 500000000 | bytes 500000 | tf_op jit(solution)/shard_map/pallas_call | solution.py:398
  34.9 0.0 copy-start.16
  34.9 0.0 collective-permute-done.from_cross_ref
  34.9 0.2 collective-permute-done.1.from_chip_ref
  35.1 0.0 copy-done.5
  35.1 0.0 copy-done.6
  35.1 0.0 copy-done.14
  35.1 0.0 copy-done.17
  35.1 0.0 copy-done.18
  35.1 0.0 copy-done.1
  35.1 0.0 copy-done.4
  35.2 1.9 %shard_map.265 = (bf16[64,512]{1,0:T(8,128)(2,1)S(1)}, bf16[256,512]{1,0:T(8,128)(2,1)}) custom-call(f32[64,512]{1,0:T(8,128)S(1)} %get-tuple-element.18.own_ref, bf16[64,512]{1,0:T(8,128)(2,1)S(1)} %collective-permute-done.from_cross_ref, bf16[64,512]{1,0:T(8,128)(2,1)S(1)} %collective-permute-done.1.from_chip_ref, bf16[64,512]{1,0:T(8,128)(2,1)S(1)} %copy-done.14, ...), custom_call_target="tpu_custom_call" | custom-call | flops 500000000 | bytes 4000000 | tf_op jit(solution)/shard_map/pallas_call | solution.py:405
  37.1 0.6 %copy-done.9 = bf16[64,512]{1,0:T(8,128)(2,1)} copy-done((bf16[64,512]{1,0:T(8,128)(2,1)}, bf16[64,512]{1,0:T(8,128)(2,1)S(1)}, u32[]{:S(2)}) %copy-start.9) | copy-done | bytes 65560
  37.7 6.9 %all-to-all-start.1 = ((bf16[16,16,512]{2,1,0:T(8,128)(2,1)}), bf16[16,16,512]{2,1,0:T(8,128)(2,1)S(1)}, u32[]{:S(2)}, u32[]{:S(2)}) async-start(bf16[16,16,512]{2,1,0:T(8,128)(2,1)} %bitcast.8), calls=%async_computation.1 | async-start | bytes 524288 | tf_op jit(solution)/shard_map/all_to_all | solution.py:424
  44.6 0.0 copy-start.10
  44.6 0.0 copy-start.19
  44.6 0.0 copy-start.27
  44.6 0.0 copy-done.16
  44.7 4.0 %shard_map.266.wanted_ref = bf16[512,256]{1,0:T(8,128)(2,1)S(1)} custom-call(s32[1,1024]{1,0:T(1,128)S(1)} %bitcast.20, s32[4,128]{1,0:T(4,128)S(1)} %copy-done.16), custom_call_target="tpu_custom_call" | custom-call | flops 1000000000 | bytes 500000 | tf_op jit(solution)/shard_map/pallas_call | solution.py:426
  48.7 0.0 copy-start.7
  48.7 0.7 %copy-done.7 = bf16[512,256]{1,0:T(8,128)(2,1)} copy-done((bf16[512,256]{1,0:T(8,128)(2,1)}, bf16[512,256]{1,0:T(8,128)(2,1)S(1)}, u32[]{:S(2)}) %copy-start.7) | copy-done | bytes 262168
  49.4 0.0 copy-done
  49.4 0.0 copy-done.25
  49.4 0.0 copy-done.26
  49.4 0.0 copy-done.10
  49.4 0.0 copy-done.19
  49.4 0.0 copy-done.27
  49.4 0.7 %shard_map.267 = (bf16[64,512]{1,0:T(8,128)(2,1)S(1)}, f32[512,512]{1,0:T(8,128)S(1)}, f32[64,512]{1,0:T(8,128)S(1)}) custom-call(s32[1]{0:T(128)} %bitcast.1.place_ref, s32[1,1024]{1,0:T(1,128)S(1)} %bitcast.21, s32[4,128]{1,0:T(4,128)S(1)} %copy-done.25, bf16[64,512]{1,0:T(8,128)(2,1)S(1)} %copy-done.10, bf16[512,512]{1,0:T(8,128)(2,1)S(1)} %copy-done.19, ...), custom_call_target="tpu_custom_call" | custom-call | flops 1000000000 | bytes 4000000 | tf_op jit(solution)/shard_map/pallas_call | solution.py:433
  50.1 0.0 copy-start.12
  50.2 0.6 %copy-done.12 = bf16[64,512]{1,0:T(8,128)(2,1)} copy-done((bf16[64,512]{1,0:T(8,128)(2,1)}, bf16[64,512]{1,0:T(8,128)(2,1)S(1)}, u32[]{:S(2)}) %copy-start.12) | copy-done | bytes 65560
  50.8 3.9 %all-to-all-done.1 = bf16[16,16,512]{2,1,0:T(8,128)(2,1)S(1)} async-done(((bf16[16,16,512]{2,1,0:T(8,128)(2,1)}), bf16[16,16,512]{2,1,0:T(8,128)(2,1)S(1)}, u32[]{:S(2)}, u32[]{:S(2)}) %all-to-all-start.1) | async-done | bytes 262176 | tf_op jit(solution)/shard_map/all_to_all | solution.py:424
  54.7 0.0 copy-done.2
  54.7 0.0 copy-done.3
  54.7 0.0 copy-done.15
  54.7 0.0 copy-start.8
  54.7 0.9 %copy-done.8 = bf16[512,256]{1,0:T(8,128)(2,1)S(1)} copy-done((bf16[512,256]{1,0:T(8,128)(2,1)S(1)}, bf16[512,256]{1,0:T(8,128)(2,1)}, u32[]{:S(2)}) %copy-start.8) | copy-done | bytes 262168
  55.6 0.8 %copy-done.11 = bf16[64,512]{1,0:T(8,128)(2,1)S(1)} copy-done((bf16[64,512]{1,0:T(8,128)(2,1)S(1)}, bf16[64,512]{1,0:T(8,128)(2,1)}, u32[]{:S(2)}) %copy-start.11) | copy-done | bytes 65560
  56.5 0.8 %copy-done.13 = bf16[64,512]{1,0:T(8,128)(2,1)S(1)} copy-done((bf16[64,512]{1,0:T(8,128)(2,1)S(1)}, bf16[64,512]{1,0:T(8,128)(2,1)}, u32[]{:S(2)}) %copy-start.13) | copy-done | bytes 65560
  57.3 1.8 %shard_map.268 = bf16[64,512]{1,0:T(8,128)(2,1)} custom-call(bf16[512,256]{1,0:T(8,128)(2,1)S(1)} %copy-done.8, bf16[256,512]{1,0:T(8,128)(2,1)S(1)} %bitcast.13, bf16[64,512]{1,0:T(8,128)(2,1)S(1)} %copy-done.13, f32[512,512]{1,0:T(8,128)S(1)} %get-tuple-element.27.receiver_ref, f32[64,512]{1,0:T(8,128)S(1)} %get-tuple-element.28.upper_ref, ...), custom_call_target="tpu_custom_call" | custom-call | flops 1000000000 | bytes 4000000 | tf_op jit(solution)/shard_map/pallas_call | solution.py:449
  (10 shorter events, 0.0 us)
Async XLA Ops:
  1.3 16.8 %all-to-all-start = ((s32[16,4,128]{2,1,0:T(4,128)}), s32[16,4,128]{2,1,0:T(4,128)S(1)}, u32[]{:S(2)}, u32[]{:S(2)}) async-start(s32[16,4,128]{2,1,0:T(4,128)} %tile.2), calls=%async_computation | async-start | bytes 65536 | tf_op jit(solution)/shard_map/all_to_all | solution.py:364
  8.7 9.5 %copy-start.20 = (f32[24,4,128]{2,1,0:T(4,128)S(1)}, f32[24,4,128]{2,1,0:T(4,128)}, u32[]{:S(2)}) copy-start(f32[24,4,128]{2,1,0:T(4,128)} %feat_ref.1) | copy-start | bytes 147460
  8.7 9.5 %copy-start.21 = (s32[24,128]{1,0:T(8,128)S(1)}, s32[24,128]{1,0:T(8,128)}, u32[]{:S(2)}) copy-start(s32[24,128]{1,0:T(8,128)} %send_ref.1) | copy-start | bytes 36868
  8.7 9.5 %copy-start.22 = (s32[24,128]{1,0:T(8,128)S(1)}, s32[24,128]{1,0:T(8,128)}, u32[]{:S(2)}) copy-start(s32[24,128]{1,0:T(8,128)} %recv_ref.2) | copy-start | bytes 36868
  8.7 9.5 %copy-start.23 = (bf16[4,512]{1,0:T(4,128)(2,1)S(1)}, bf16[4,512]{1,0:T(4,128)(2,1)}, u32[]{:S(2)}) copy-start(bf16[4,512]{1,0:T(4,128)(2,1)} %feat_weight_ref.1) | copy-start | bytes 12292
  8.7 9.5 %copy-start.24 = (s32[1024]{0:T(1024)S(1)}, s32[1024]{0:T(1024)}, u32[]{:S(2)}) copy-start(s32[1024]{0:T(1024)} %param.53) | copy-start | bytes 12292
  18.2 1.6 %copy-start.28 = (bf16[512,2048]{1,0:T(8,128)(2,1)S(1)}, bf16[512,2048]{1,0:T(8,128)(2,1)}, u32[]{:S(2)}) copy-start(bf16[512,2048]{1,0:T(8,128)(2,1)} %shard_map.262.table_ref) | copy-start | bytes 6291460
  19.8 15.3 %copy-start.5 = (bf16[512,512]{1,0:T(8,128)(2,1)S(1)}, bf16[512,512]{1,0:T(8,128)(2,1)}, u32[]{:S(2)}) copy-start(bf16[512,512]{1,0:T(8,128)(2,1)} %node_out_ref.1) | copy-start | bytes 1572868
  19.8 15.3 %copy-start.6 = (bf16[512,512]{1,0:T(8,128)(2,1)S(1)}, bf16[512,512]{1,0:T(8,128)(2,1)}, u32[]{:S(2)}) copy-start(bf16[512,512]{1,0:T(8,128)(2,1)} %mesh_sender_ref.1) | copy-start | bytes 1572868
  19.8 15.3 %copy-start.14 = (bf16[64,512]{1,0:T(8,128)(2,1)S(1)}, bf16[64,512]{1,0:T(8,128)(2,1)}, u32[]{:S(2)}) copy-start(bf16[64,512]{1,0:T(8,128)(2,1)} %latent_ref.1) | copy-start | bytes 196612
  19.8 15.3 %copy-start.17 = (f32[512]{0:T(512)S(1)}, f32[512]{0:T(512)}, u32[]{:S(2)}) copy-start(f32[512]{0:T(512)} %param.37) | copy-start | bytes 6148
  19.8 15.3 %copy-start.18 = (f32[512]{0:T(512)S(1)}, f32[512]{0:T(512)}, u32[]{:S(2)}) copy-start(f32[512]{0:T(512)} %param.39) | copy-start | bytes 6148
  30.0 5.1 %copy-start.1 = (bf16[1024,512]{1,0:T(8,128)(2,1)S(1)}, bf16[1024,512]{1,0:T(8,128)(2,1)}, u32[]{:S(2)}) copy-start(bf16[1024,512]{1,0:T(8,128)(2,1)} %node_input_ref.1) | copy-start | bytes 3145732
  30.1 5.1 %copy-start.4 = (bf16[512,512]{1,0:T(8,128)(2,1)S(1)}, bf16[512,512]{1,0:T(8,128)(2,1)}, u32[]{:S(2)}) copy-start(bf16[512,512]{1,0:T(8,128)(2,1)} %edge_out_ref.1) | copy-start | bytes 1572868
  30.1 4.8 %collective-permute-start = (bf16[64,512]{1,0:T(8,128)(2,1)S(1)}, bf16[64,512]{1,0:T(8,128)(2,1)S(1)}, u32[]{:S(2)}, u32[]{:S(2)}) collective-permute-start(bf16[64,512]{1,0:T(8,128)(2,1)S(1)} %get-tuple-element.19), channel_id=1, source_target_pairs={{1,2},{3,4},{5,6},{7,8},{9,10},{11,12},{13,14},{2,1},{4,3},{6,5},{... | collective-permute-start | bytes 196616 | tf_op jit(solution)/shard_map/ppermute | solution.py:395
  30.9 4.2 %collective-permute-start.1 = (bf16[64,512]{1,0:T(8,128)(2,1)S(1)}, bf16[64,512]{1,0:T(8,128)(2,1)S(1)}, u32[]{:S(2)}, u32[]{:S(2)}) collective-permute-start(bf16[64,512]{1,0:T(8,128)(2,1)S(1)} %get-tuple-element.20), channel_id=1, source_target_pairs={{0,1},{2,3},{4,5},{6,7},{8,9},{10,11},{12,13},{14,15},{1,0},{3,2},... | collective-permute-start | bytes 196616 | tf_op jit(solution)/shard_map/ppermute | solution.py:396
  34.9 9.8 %copy-start.16 = (s32[4,128]{1,0:T(4,128)S(1)}, s32[4,128]{1,0:T(4,128)}, u32[]{:S(2)}) copy-start(s32[4,128]{1,0:T(4,128)} %send_ref.2) | copy-start | bytes 6148
  37.0 0.6 %copy-start.9 = (bf16[64,512]{1,0:T(8,128)(2,1)}, bf16[64,512]{1,0:T(8,128)(2,1)S(1)}, u32[]{:S(2)}) copy-start(bf16[64,512]{1,0:T(8,128)(2,1)S(1)} %get-tuple-element.23.encoded_ref) | copy-start | bytes 196612
  37.7 11.7 %copy-start = (bf16[1024,512]{1,0:T(8,128)(2,1)S(1)}, bf16[1024,512]{1,0:T(8,128)(2,1)}, u32[]{:S(2)}) copy-start(bf16[1024,512]{1,0:T(8,128)(2,1)} %update_input_ref.3) | copy-start | bytes 3145732
  37.7 11.7 %copy-start.25 = (s32[4,128]{1,0:T(4,128)S(1)}, s32[4,128]{1,0:T(4,128)}, u32[]{:S(2)}) copy-start(s32[4,128]{1,0:T(4,128)} %recv_ref.3) | copy-start | bytes 6148
  37.7 11.7 %copy-start.26 = (f32[512]{0:T(512)S(1)}, f32[512]{0:T(512)}, u32[]{:S(2)}) copy-start(f32[512]{0:T(512)} %param.42) | copy-start | bytes 6148
  37.7 17.0 %all-to-all-start.1 = ((bf16[16,16,512]{2,1,0:T(8,128)(2,1)}), bf16[16,16,512]{2,1,0:T(8,128)(2,1)S(1)}, u32[]{:S(2)}, u32[]{:S(2)}) async-start(bf16[16,16,512]{2,1,0:T(8,128)(2,1)} %bitcast.8), calls=%async_computation.1 | async-start | bytes 524288 | tf_op jit(solution)/shard_map/all_to_all | solution.py:424
  44.6 4.8 %copy-start.10 = (bf16[64,512]{1,0:T(8,128)(2,1)S(1)}, bf16[64,512]{1,0:T(8,128)(2,1)}, u32[]{:S(2)}) copy-start(bf16[64,512]{1,0:T(8,128)(2,1)} %copy-done.9) | copy-start | bytes 196612
  44.6 4.8 %copy-start.19 = (bf16[512,512]{1,0:T(8,128)(2,1)S(1)}, bf16[512,512]{1,0:T(8,128)(2,1)}, u32[]{:S(2)}) copy-start(bf16[512,512]{1,0:T(8,128)(2,1)} %mesh_receiver_ref.1) | copy-start | bytes 1572868
  44.6 4.8 %copy-start.27 = (f32[512]{0:T(512)S(1)}, f32[512]{0:T(512)}, u32[]{:S(2)}) copy-start(f32[512]{0:T(512)} %param.45) | copy-start | bytes 6148
  48.7 0.7 %copy-start.7 = (bf16[512,256]{1,0:T(8,128)(2,1)}, bf16[512,256]{1,0:T(8,128)(2,1)S(1)}, u32[]{:S(2)}) copy-start(bf16[512,256]{1,0:T(8,128)(2,1)S(1)} %shard_map.266.wanted_ref) | copy-start | bytes 786436
  49.3 5.3 %copy-start.2 = (bf16[512,512]{1,0:T(8,128)(2,1)S(1)}, bf16[512,512]{1,0:T(8,128)(2,1)}, u32[]{:S(2)}) copy-start(bf16[512,512]{1,0:T(8,128)(2,1)} %message_out_ref.1) | copy-start | bytes 1572868
  49.3 5.3 %copy-start.3 = (bf16[512,512]{1,0:T(8,128)(2,1)S(1)}, bf16[512,512]{1,0:T(8,128)(2,1)}, u32[]{:S(2)}) copy-start(bf16[512,512]{1,0:T(8,128)(2,1)} %update_out_ref.1) | copy-start | bytes 1572868
  49.3 5.3 %copy-start.15 = (f32[512]{0:T(512)S(1)}, f32[512]{0:T(512)}, u32[]{:S(2)}) copy-start(f32[512]{0:T(512)} %param.47) | copy-start | bytes 6148
  50.1 0.6 %copy-start.12 = (bf16[64,512]{1,0:T(8,128)(2,1)}, bf16[64,512]{1,0:T(8,128)(2,1)S(1)}, u32[]{:S(2)}) copy-start(bf16[64,512]{1,0:T(8,128)(2,1)S(1)} %get-tuple-element.26.incoming_ref) | copy-start | bytes 196612
  54.7 1.0 %copy-start.8 = (bf16[512,256]{1,0:T(8,128)(2,1)S(1)}, bf16[512,256]{1,0:T(8,128)(2,1)}, u32[]{:S(2)}) copy-start(bf16[512,256]{1,0:T(8,128)(2,1)} %copy-done.7) | copy-start | bytes 786436
  55.6 0.8 %copy-start.11 = (bf16[64,512]{1,0:T(8,128)(2,1)S(1)}, bf16[64,512]{1,0:T(8,128)(2,1)}, u32[]{:S(2)}) copy-start(bf16[64,512]{1,0:T(8,128)(2,1)} %copy-done.9) | copy-start | bytes 196612
  56.5 0.8 %copy-start.13 = (bf16[64,512]{1,0:T(8,128)(2,1)S(1)}, bf16[64,512]{1,0:T(8,128)(2,1)}, u32[]{:S(2)}) copy-start(bf16[64,512]{1,0:T(8,128)(2,1)} %copy-done.12) | copy-start | bytes 196612

commit v4 on v3

--- a/solution.py
+++ b/solution.py
@@ -57,24 +57,47 @@
     return jnp.max(jnp.where(slot == rows, iota((count, nodes), 1), -1), axis=1, keepdims=True)
 
 
-def grid_kernel(
-    grid_hbm,
+def edge_kernel(
+    place_ref,
     first_hbm,
     grid_bias_hbm,
+    grid_hbm,
     second_hbm,
     send_weight_hbm,
     edge_bias_hbm,
-    table_ref,
-    grid_ref,
+    count_hbm,
+    slot_hbm,
+    feat_weight_hbm,
+    send_hbm,
+    recv_hbm,
+    feat_hbm,
+    mesh_send_hbm,
+    own_ref,
+    cross_ref,
+    chip_ref,
+    asked_ref,
     first_ref,
     grid_bias_ref,
+    grid_ref,
     second_ref,
     send_weight_ref,
     edge_bias_ref,
+    count_ref,
+    slot_ref,
+    feat_weight_ref,
+    send_ref,
+    recv_ref,
+    feat_ref,
+    mesh_send_ref,
+    table,
+    total,
     sems,
 ):
     channels, grid_rows = grid_ref.shape
     width = second_ref.shape[1]
+    blocks, block_edges = send_ref.shape
+    owned = own_ref.shape[0]
+    feats = feat_ref.shape[1]
     step_rows = grid_rows // GRID_STEPS
     columns = [pl.ds(step * step_rows, step_rows) for step in range(GRID_STEPS)]
     pairs = [
@@ -84,17 +107,29 @@
         (second_hbm, second_ref),
         (send_weight_hbm, send_weight_ref),
         (edge_bias_hbm, edge_bias_ref),
-    ] + [(grid_hbm.at[:, part], grid_ref.at[:, part]) for part in columns[1:]]
+    ]
+    pairs += [(grid_hbm.at[:, part], grid_ref.at[:, part]) for part in columns[1:]]
+    pairs += [
+        (slot_hbm, slot_ref),
+        (feat_weight_hbm, feat_weight_ref),
+        (send_hbm, send_ref),
+        (recv_hbm, recv_ref),
+        (feat_hbm, feat_ref),
+        (mesh_send_hbm, mesh_send_ref),
+        (count_hbm, count_ref),
+    ]
     copies = [
         pltpu.make_async_copy(source, target, sems.at[at])
         for at, (source, target) in enumerate(pairs)
     ]
-    for copy in copies:
+    for copy in copies[:3]:
         copy.start()
     column = lambda ref: jnp.broadcast_to(0.5 * ref[...], (LANES, width)).T
     wide = lambda value: jnp.concatenate([value] * (step_rows // LANES), axis=1)
     for copy in copies[:2]:
         copy.wait()
+    for copy in copies[3:]:
+        copy.start()
     first_t = (0.5 * first_ref[...].astype(F32)).T.astype(BF16)
     grid_bias = column(grid_bias_ref)
     for step, part in enumerate(columns):
@@ -111,57 +146,34 @@
         center = value - jnp.mean(value, axis=0, keepdims=True)
         spread = jnp.mean(center * center, axis=0, keepdims=True)
         code = (center * lax.rsqrt(spread + 1e-05)).astype(BF16)
-        table_ref[:, part] = (mm(weight_t, code) + wide(edge_bias)).astype(BF16)
-
-
-def edge_kernel(
-    place_ref,
-    count_ref,
-    table_ref,
-    feat_weight_ref,
-    slot_ref,
-    send_ref,
-    recv_ref,
-    feat_ref,
-    own_ref,
-    cross_ref,
-    chip_ref,
-    total,
-):
-    grid_rows = table_ref.shape[1]
-    width = table_ref.shape[0]
-    blocks, block_edges = send_ref.shape
-    owned = own_ref.shape[0]
-    feats = feat_ref.shape[1]
+        table[:, part] = (mm(weight_t, code) + wide(edge_bias)).astype(BF16)
+
+    for copy in copies[5 + GRID_STEPS :]:
+        copy.wait()
+    asked = mesh_send_ref[...]
+    for at in range(asked_ref.shape[0] // asked.shape[0]):
+        asked_ref[at * asked.shape[0] : (at + 1) * asked.shape[0], :] = asked
     place = place_ref[0]
-    used = count_ref[0]
+    used = count_ref[...]
     feat_weight = jnp.concatenate(
         [0.5 * feat_weight_ref[...].astype(F32), jnp.zeros((LANES - feats, width), F32)], axis=0
     )
     feat_weight = feat_weight.T.astype(BF16)[:, :feats]
     ids = ids_of_rows(slot_ref[...], (place - 1) * owned, 3 * owned)
     group = math.gcd(blocks, 4)
-    total[...] = jnp.zeros_like(total)
-
-    def edge_step(step, carry):
-        first = step * group
-        senders = jnp.concatenate([send_ref[pl.ds(first + b, 1), :] for b in range(group)], axis=1)
+    for first in range(0, blocks, group):
+        senders = jnp.concatenate([send_ref[b : b + 1, :] for b in range(first, first + group)], axis=1)
         picker = one_hot(senders, grid_rows)
-        feat = jnp.concatenate([feat_ref[first + b] for b in range(group)], axis=1)
-        half = mm(table_ref[...], picker) + mm(feat_weight, feat.astype(BF16))
+        feat = jnp.concatenate([feat_ref[b] for b in range(first, first + group)], axis=1)
+        half = mm(table[...], picker) + mm(feat_weight, feat.astype(BF16))
         hidden = silu_half(half).astype(BF16)
         receivers = jnp.concatenate(
-            [
-                jnp.where(first + b < used, recv_ref[pl.ds(first + b, 1), :], -2)
-                for b in range(group)
-            ],
+            [jnp.where(b < used, recv_ref[b : b + 1, :], -2) for b in range(first, first + group)],
             axis=1,
         )
         spread = (ids == receivers).astype(F32).astype(BF16)
-        total[...] += mm_nt(hidden, spread)
-        return carry
-
-    lax.fori_loop(0, blocks // group, edge_step, 0)
+        sums = mm_nt(hidden, spread)
+        total[...] = sums if first == 0 else total[...] + sums
     pad = -3 * owned % LANES
     sums = jnp.concatenate([total[...], jnp.zeros((width, pad), F32)], axis=1).T
     below, above = sums[:owned].astype(BF16), sums[2 * owned : 3 * owned].astype(BF16)
@@ -193,7 +205,7 @@
         found = jnp.where(spot == iota((chunk, places), 1), ids, -1)
         return jnp.maximum(best, jnp.max(found, axis=0, keepdims=True))
 
-    best = lax.fori_loop(0, nodes // chunk, find, jnp.full((1, places), -1, I32))
+    best = lax.fori_loop(0, nodes // chunk, find, jnp.full((1, places), -1, I32), unroll=2)
     best = best.astype(F32)
     for b in range(blocks):
         senders = jnp.broadcast_to(send_ref[b : b + 1, :].astype(F32), (block_edges, block_edges)).T
@@ -264,7 +276,9 @@
     update_input_ref,
     update_bias_ref,
     incoming_ref,
-    receiver_ref,
+    pick_ref,
+    high_ref,
+    low_ref,
     upper_ref,
 ):
     owned, width = encoded_ref.shape
@@ -273,13 +287,13 @@
     incoming = jnp.concatenate(
         [(ids == recv_ref[b : b + 1, :]).astype(F32) for b in range(blocks)], axis=1
     )
-    pick = incoming.T.astype(BF16)
+    pick_ref[...] = incoming.T.astype(BF16)
     incoming_ref[...] = incoming.astype(BF16)
     encoded = encoded_ref[...]
     receiver = mm(encoded, mesh_receiver_ref[...]) + message_bias_ref[...]
     high = receiver.astype(BF16)
-    low = (receiver - high.astype(F32)).astype(BF16)
-    receiver_ref[...] = mm(pick, high) + mm(pick, low)
+    high_ref[...] = high
+    low_ref[...] = (receiver - high.astype(F32)).astype(BF16)
     upper_ref[...] = mm(encoded, update_input_ref[:width]) + update_bias_ref[...]
 
 
@@ -287,7 +301,9 @@
     wanted_ref,
     piece_ref,
     incoming_ref,
-    receiver_ref,
+    pick_ref,
+    high_ref,
+    low_ref,
     upper_ref,
     encoded_ref,
     message_out_ref,
@@ -297,7 +313,8 @@
     out_ref,
 ):
     width = encoded_ref.shape[1]
-    message = silu(mm(wanted_ref[...], piece_ref[...]) + receiver_ref[...]).astype(BF16)
+    receiver = mm(pick_ref[...], high_ref[...]) + mm(pick_ref[...], low_ref[...])
+    message = silu(mm(wanted_ref[...], piece_ref[...]) + receiver).astype(BF16)
     message_sum = mm(incoming_ref[...], message).astype(BF16)
     update = mm(message_sum, message_out_ref[...]).astype(BF16)
     hidden = silu(upper_ref[...] + mm(update, update_input_ref[width:])).astype(BF16)
@@ -361,40 +378,46 @@
     slot = mesh_slot.reshape(1, -1)
     row = lambda vector: vector.reshape(1, -1)
 
-    requests = lax.all_to_all(jnp.tile(mesh_send, (devices, 1)), "bulk", 0, 0, tiled=True)
-    table = call(
-        grid_kernel,
-        shape(width, grid_rows),
-        [HBM] * 6,
-        scratch=[
-            pltpu.VMEM(grid_in.shape[::-1], BF16),
-            pltpu.VMEM(grid_first.shape, BF16),
-            pltpu.VMEM((1, width), F32),
-            pltpu.VMEM(grid_second.shape, BF16),
-            pltpu.VMEM(send_weight.shape, BF16),
-            pltpu.VMEM((1, width), F32),
-            pltpu.SemaphoreType.DMA((5 + GRID_STEPS,)),
+    operands = (
+        grid_first,
+        row(grid_bias),
+        grid_in.T,
+        grid_second,
+        send_weight,
+        row(edge_bias),
+        g2m_count.reshape(1, 1),
+        slot,
+        feat_weight,
+        g2m_send,
+        g2m_recv,
+        g2m_feat,
+        mesh_send,
+    )
+    own, cross, chip, asked = call(
+        edge_kernel,
+        (
+            shape(owned, width, kind=F32),
+            shape(owned, width),
+            shape(owned, width),
+            shape(devices * mesh_send.shape[0], mesh_send.shape[1], kind=I32),
+        ),
+        [SMEM] + [HBM] * len(operands),
+        scratch=[VMEM(value.shape, value.dtype) for value in operands]
+        + [
+            pltpu.VMEM((width, grid_rows), BF16),
+            pltpu.VMEM((width, 3 * owned), F32),
+            pltpu.SemaphoreType.DMA((len(operands) - 1 + GRID_STEPS,)),
         ],
-        flops=3_000_000_000,
+        flops=10_000_000_000,
         moved=4_000_000,
         vmem=56,
-    )(grid_in.T, grid_first, row(grid_bias), grid_second, send_weight, row(edge_bias))
-    table, requests = lax.optimization_barrier((table, requests))
-    own, cross, chip = call(
-        edge_kernel,
-        (shape(owned, width, kind=F32), shape(owned, width), shape(owned, width)),
-        [SMEM, SMEM] + [VMEM] * 6,
-        scratch=[pltpu.VMEM((width, 3 * owned), F32)],
-        flops=7_000_000_000,
-        moved=4_000_000,
-        vmem=16,
-    )(place, g2m_count, table, feat_weight, slot, g2m_send, g2m_recv, g2m_feat)
+    )(place, *operands)
+    requests = lax.all_to_all(asked, "bulk", 0, 0, tiled=True)
     crossing = [(d, d + 1) for d in range(1, devices - 1, 2)]
     within = [(d, d + 1) for d in range(0, devices, 2)]
     both = lambda pairs: pairs + [(b, a) for a, b in pairs]
     from_cross = lax.ppermute(cross, "bulk", both(crossing))
     from_chip = lax.ppermute(chip, "bulk", both(within))
-    requests, _ = lax.optimization_barrier((requests, own))
     supply = call(
         supply_kernel,
         shape(places, owned),
@@ -430,9 +453,15 @@
         flops=1_000_000_000,
         moved=500_000,
     )(slot, mesh_send)
-    incoming, receiver, upper = call(
+    incoming, pick, high, low, upper = call(
         receiver_kernel,
-        (shape(owned, edges), shape(edges, width, kind=F32), shape(owned, width, kind=F32)),
+        (
+            shape(owned, edges),
+            shape(edges, owned),
+            shape(owned, width),
+            shape(owned, width),
+            shape(owned, width, kind=F32),
+        ),
         [SMEM] + [VMEM] * 7,
         flops=1_000_000_000,
         moved=4_000_000,
@@ -449,14 +478,16 @@
     return call(
         message_kernel,
         shape(owned, width),
-        [VMEM] * 10,
+        [VMEM] * 12,
         flops=1_000_000_000,
         moved=4_000_000,
     )(
         wanted,
         piece,
         incoming,
-        receiver,
+        pick,
+        high,
+        low,
         upper,
         encoded,
         message_out,

time: 59.6 us -> 58.1 us (0.975)
  local copies, waits for them, and re-layouts: 7.54 us -> 0.1 us
  waiting for transfers between devices: 4.11 us -> 9.64 us
  Pallas kernels: 28 us -> 30.9 us
  starting transfers between devices: 18.4 us -> 16.1 us
    pallas_call x1, Pallas kernels: 10.2 us -> 23.5 us  [per_device(): call(edge_kernel, (shape(owned, width, kind=F32), shape(owned, width), sh...]
    pallas_call x3 -> x2, Pallas kernels: 11.3 us -> 2.38 us  [the longest x1 2.05 us: per_device(): call(message_kernel, shape(owned, width), [VMEM] * 12, flops=1000000000,...]
    unnamed x58 -> x36, local copies, waits for them, and re-layouts: 6.24 us -> 0.1 us
    all_to_all x1, waiting for transfers between devices: 3.88 us -> 7.01 us  [per_device(): piece = lax.all_to_all(rows, 'bulk', 0, 0, tiled=True)]
    all_to_all x1, waiting for transfers between devices: 0.01 us -> 2.62 us  [per_device(): requests = lax.all_to_all(asked, 'bulk', 0, 0, tiled=True)]
    all_to_all x1, starting transfers between devices: 6.91 us -> 4.57 us  [per_device(): piece = lax.all_to_all(rows, 'bulk', 0, 0, tiled=True)]
    pallas_call x1, Pallas kernels: 3.99 us -> 2.53 us  [per_device(): call(functools.partial(wanted_kernel, owned), shape(edges, places), [VMEM...]
    another operation x1 -> x0, local copies, waits for them, and re-layouts: 1.3 us -> none  [per_device(): jnp.tile(mesh_send, (devices, 1))]
  transfers between devices with their start and end apart: 4 -> 4, of which waited for: 2 -> 2; matrix products, arithmetic and copies ran while one was open for 0% -> 0% of each run, Pallas kernels for 24% -> 6%
where the time goes in v4:
time: 58.1 us; the launch traced here: 57.8 us
  Pallas kernels  30.9 us (53%)
  starting transfers between devices  16.1 us (28%)
  waiting for transfers between devices  9.64 us (17%)
  between operations  0.98 us (2%)
    pallas_call x1, Pallas kernels, per_device(): call(edge_kernel, (shape(owned, width, kind=F32), shape(owned, width), sh...  23.5 us
    all_to_all x1, starting transfers between devices, per_device(): requests = lax.all_to_all(asked, 'bulk', 0, 0, tiled=True)  7.53 us
    all_to_all x1, waiting for transfers between devices, per_device(): piece = lax.all_to_all(rows, 'bulk', 0, 0, tiled=True)  7.01 us
    all_to_all x1, starting transfers between devices, per_device(): piece = lax.all_to_all(rows, 'bulk', 0, 0, tiled=True)  4.57 us
    ppermute x1, starting transfers between devices, per_device(): from_chip = lax.ppermute(chip, 'bulk', both(within))  3.34 us
    all_to_all x1, waiting for transfers between devices, per_device(): requests = lax.all_to_all(asked, 'bulk', 0, 0, tiled=True)  2.62 us
    pallas_call x1, Pallas kernels, per_device(): call(functools.partial(wanted_kernel, owned), shape(edges, places), [VMEM...  2.53 us
    pallas_call x1, Pallas kernels, per_device(): call(message_kernel, shape(owned, width), [VMEM] * 12, flops=1000000000,...  2.05 us
  transfers between devices with their start and end apart: 4, of which 2 were waited for; matrix products, arithmetic and copies ran while one was open for 0% of the time, Pallas kernels for 6%

profile of v4, /device:TPU:0, one launch (start us, length us, event | category | flops | bytes accessed | tf_op | source)
XLA Modules:
  0.0 57.8 jit_solution(16835041488840239387)
XLA Ops:
  0.7 0.0 copy-start.12
  0.7 0.0 copy-start.2
  0.7 0.0 copy-start.3
  0.7 0.0 copy-start.6
  0.7 0.0 copy-start.7
  0.7 23.5 %shard_map.262 = (f32[64,512]{1,0:T(8,128)}, bf16[64,512]{1,0:T(8,128)(2,1)}, bf16[64,512]{1,0:T(8,128)(2,1)}, s32[64,128]{1,0:T(8,128)}) custom-call(s32[1]{0:T(128)} %bitcast.1.place_ref, bf16[474,512]{1,0:T(8,128)(2,1)} %first_hbm.1, f32[1,512]{1,0:T(1,128)} %bitcast.29, bf16[474,2048]{1,0:T(8,128)(2,1)} %bitcast.28, bf16[512,512]{1,0:T(8,128)(2,1)} %second_hbm.1, ...), custom_call_target="tpu_custom_call" | custom-call | flops 10000000000 | bytes 4000000 | tf_op jit(solution)/shard_map/pallas_call | solution.py:396
  24.2 0.0 copy-start
  24.2 0.0 copy-start.1
  24.2 0.0 copy-start.4
  24.2 0.0 copy-start.5
  24.2 7.5 %all-to-all-start = ((s32[16,4,128]{2,1,0:T(4,128)}), s32[16,4,128]{2,1,0:T(4,128)S(1)}, u32[]{:S(2)}, u32[]{:S(2)}) async-start(s32[16,4,128]{2,1,0:T(4,128)} %bitcast.27), calls=%async_computation | async-start | bytes 65536 | tf_op jit(solution)/shard_map/all_to_all | solution.py:415
  31.8 0.7 %collective-permute-start = (bf16[64,512]{1,0:T(8,128)(2,1)}, bf16[64,512]{1,0:T(8,128)(2,1)S(1)}, u32[]{:S(2)}, u32[]{:S(2)}) collective-permute-start(bf16[64,512]{1,0:T(8,128)(2,1)} %get-tuple-element.18), channel_id=1, source_target_pairs={{1,2},{3,4},{5,6},{7,8},{9,10},{11,12},{13,14},{2,1},{4,3},{6,5},{... | collective-permute-start | bytes 196616 | tf_op jit(solution)/shard_map/ppermute | solution.py:419
  32.5 3.3 %collective-permute-start.1 = (bf16[64,512]{1,0:T(8,128)(2,1)}, bf16[64,512]{1,0:T(8,128)(2,1)S(1)}, u32[]{:S(2)}, u32[]{:S(2)}) collective-permute-start(bf16[64,512]{1,0:T(8,128)(2,1)} %get-tuple-element.19), channel_id=1, source_target_pairs={{0,1},{2,3},{4,5},{6,7},{8,9},{10,11},{12,13},{14,15},{1,0},{3,2},... | collective-permute-start | bytes 196616 | tf_op jit(solution)/shard_map/ppermute | solution.py:420
  35.8 2.6 %all-to-all-done = s32[16,4,128]{2,1,0:T(4,128)S(1)} async-done(((s32[16,4,128]{2,1,0:T(4,128)}), s32[16,4,128]{2,1,0:T(4,128)S(1)}, u32[]{:S(2)}, u32[]{:S(2)}) %all-to-all-start) | async-done | bytes 32800 | tf_op jit(solution)/shard_map/all_to_all | solution.py:415
  38.4 0.0 copy-done.12
  38.4 0.7 %shard_map.263.supply_ref = bf16[256,64]{1,0:T(8,128)(2,1)S(1)} custom-call(s32[1]{0:T(128)} %bitcast.1.place_ref, s32[1,1024]{1,0:T(1,128)S(1)} %bitcast.21, s32[64,128]{1,0:T(8,128)S(1)} %bitcast.17), custom_call_target="tpu_custom_call" | custom-call | flops 500000000 | bytes 500000 | tf_op jit(solution)/shard_map/pallas_call | solution.py:421
  39.1 0.0 copy-start.13
  39.1 0.0 collective-permute-done.from_cross_ref
  39.1 0.0 collective-permute-done.1.from_chip_ref
  39.1 0.0 copy-done.2
  39.1 0.0 copy-done.3
  39.1 0.0 copy-done.6
  39.1 0.0 copy-done.7
  39.2 0.0 copy-done
  39.2 0.0 copy-done.1
  39.2 0.0 copy-done.4
  39.2 0.0 copy-done.5
  39.2 1.9 %shard_map.264 = (bf16[64,512]{1,0:T(8,128)(2,1)S(1)}, bf16[256,512]{1,0:T(8,128)(2,1)}) custom-call(f32[64,512]{1,0:T(8,128)S(1)} %copy-done.4, bf16[64,512]{1,0:T(8,128)(2,1)S(1)} %collective-permute-done.from_cross_ref, bf16[64,512]{1,0:T(8,128)(2,1)S(1)} %collective-permute-done.1.from_chip_ref, bf16[64,512]{1,0:T(8,128)(2,1)S(1)} %copy-done.5, ...), custom_call_target="tpu_custom_call" | custom-call | flops 500000000 | bytes 4000000 | tf_op jit(solution)/shard_map/pallas_call | solution.py:428
  41.1 4.6 %all-to-all-start.1 = ((bf16[16,16,512]{2,1,0:T(8,128)(2,1)}), bf16[16,16,512]{2,1,0:T(8,128)(2,1)S(1)}, u32[]{:S(2)}, u32[]{:S(2)}) async-start(bf16[16,16,512]{2,1,0:T(8,128)(2,1)} %bitcast.10), calls=%async_computation.1 | async-start | bytes 524288 | tf_op jit(solution)/shard_map/all_to_all | solution.py:447
  45.6 0.0 copy-start.8
  45.7 0.0 copy-start.9
  45.7 0.0 copy-start.14
  45.7 0.0 copy-start.15
  45.7 0.0 copy-start.16
  45.7 0.0 copy-done.13
  45.7 2.5 %shard_map.265.wanted_ref = bf16[512,256]{1,0:T(8,128)(2,1)S(1)} custom-call(s32[1,1024]{1,0:T(1,128)S(1)} %bitcast.22, s32[4,128]{1,0:T(4,128)S(1)} %copy-done.13), custom_call_target="tpu_custom_call" | custom-call | flops 1000000000 | bytes 500000 | tf_op jit(solution)/shard_map/pallas_call | solution.py:449
  48.3 0.0 copy-start.10
  48.3 0.0 copy-start.11
  48.3 0.0 copy-start.17
  48.3 0.0 copy-done.8
  48.3 0.0 copy-done.9
  48.3 0.0 copy-done.14
  48.3 0.0 copy-done.15
  48.3 0.0 copy-done.16
  48.3 0.3 shard_map.266
  48.7 7.0 %all-to-all-done.1 = bf16[16,16,512]{2,1,0:T(8,128)(2,1)S(1)} async-done(((bf16[16,16,512]{2,1,0:T(8,128)(2,1)}), bf16[16,16,512]{2,1,0:T(8,128)(2,1)S(1)}, u32[]{:S(2)}, u32[]{:S(2)}) %all-to-all-start.1) | async-done | bytes 262176 | tf_op jit(solution)/shard_map/all_to_all | solution.py:447
  55.7 0.0 copy-done.10
  55.7 0.0 copy-done.11
  55.7 0.0 copy-done.17
  55.7 2.1 %shard_map.267 = bf16[64,512]{1,0:T(8,128)(2,1)} custom-call(bf16[512,256]{1,0:T(8,128)(2,1)S(1)} %shard_map.265.wanted_ref, bf16[256,512]{1,0:T(8,128)(2,1)S(1)} %bitcast.16, bf16[64,512]{1,0:T(8,128)(2,1)S(1)} %get-tuple-element.24.incoming_ref, bf16[512,64]{1,0:T(8,128)(2,1)S(1)} %get-tuple-element.25.pick_ref, ...), custom_call_target="tpu_custom_call" | custom-call | flops 1000000000 | bytes 4000000 | tf_op jit(solution)/shard_map/pallas_call | solution.py:478
Async XLA Ops:
  0.7 37.8 %copy-start.12 = (s32[1024]{0:T(1024)S(1)}, s32[1024]{0:T(1024)}, u32[]{:S(2)}) copy-start(s32[1024]{0:T(1024)} %param.53) | copy-start | bytes 12292
  0.7 38.5 %copy-start.2 = (bf16[512,512]{1,0:T(8,128)(2,1)S(1)}, bf16[512,512]{1,0:T(8,128)(2,1)}, u32[]{:S(2)}) copy-start(bf16[512,512]{1,0:T(8,128)(2,1)} %node_out_ref.1) | copy-start | bytes 1572868
  0.7 38.5 %copy-start.3 = (bf16[512,512]{1,0:T(8,128)(2,1)S(1)}, bf16[512,512]{1,0:T(8,128)(2,1)}, u32[]{:S(2)}) copy-start(bf16[512,512]{1,0:T(8,128)(2,1)} %mesh_sender_ref.1) | copy-start | bytes 1572868
  0.7 38.5 %copy-start.6 = (f32[512]{0:T(512)S(1)}, f32[512]{0:T(512)}, u32[]{:S(2)}) copy-start(f32[512]{0:T(512)} %param.37) | copy-start | bytes 6148
  0.7 38.5 %copy-start.7 = (f32[512]{0:T(512)S(1)}, f32[512]{0:T(512)}, u32[]{:S(2)}) copy-start(f32[512]{0:T(512)} %param.39) | copy-start | bytes 6148
  24.2 15.0 %copy-start = (bf16[1024,512]{1,0:T(8,128)(2,1)S(1)}, bf16[1024,512]{1,0:T(8,128)(2,1)}, u32[]{:S(2)}) copy-start(bf16[1024,512]{1,0:T(8,128)(2,1)} %node_input_ref.1) | copy-start | bytes 3145732
  24.2 15.0 %copy-start.1 = (bf16[512,512]{1,0:T(8,128)(2,1)S(1)}, bf16[512,512]{1,0:T(8,128)(2,1)}, u32[]{:S(2)}) copy-start(bf16[512,512]{1,0:T(8,128)(2,1)} %edge_out_ref.1) | copy-start | bytes 1572868
  24.2 15.0 %copy-start.4 = (f32[64,512]{1,0:T(8,128)S(1)}, f32[64,512]{1,0:T(8,128)}, u32[]{:S(2)}) copy-start(f32[64,512]{1,0:T(8,128)} %get-tuple-element.17.own_ref) | copy-start | bytes 393220
  24.2 15.0 %copy-start.5 = (bf16[64,512]{1,0:T(8,128)(2,1)S(1)}, bf16[64,512]{1,0:T(8,128)(2,1)}, u32[]{:S(2)}) copy-start(bf16[64,512]{1,0:T(8,128)(2,1)} %latent_ref.1) | copy-start | bytes 196612
  24.2 14.2 %all-to-all-start = ((s32[16,4,128]{2,1,0:T(4,128)}), s32[16,4,128]{2,1,0:T(4,128)S(1)}, u32[]{:S(2)}, u32[]{:S(2)}) async-start(s32[16,4,128]{2,1,0:T(4,128)} %bitcast.27), calls=%async_computation | async-start | bytes 65536 | tf_op jit(solution)/shard_map/all_to_all | solution.py:415
  31.8 7.3 %collective-permute-start = (bf16[64,512]{1,0:T(8,128)(2,1)}, bf16[64,512]{1,0:T(8,128)(2,1)S(1)}, u32[]{:S(2)}, u32[]{:S(2)}) collective-permute-start(bf16[64,512]{1,0:T(8,128)(2,1)} %get-tuple-element.18), channel_id=1, source_target_pairs={{1,2},{3,4},{5,6},{7,8},{9,10},{11,12},{13,14},{2,1},{4,3},{6,5},{... | collective-permute-start | bytes 196616 | tf_op jit(solution)/shard_map/ppermute | solution.py:419
  32.5 6.7 %collective-permute-start.1 = (bf16[64,512]{1,0:T(8,128)(2,1)}, bf16[64,512]{1,0:T(8,128)(2,1)S(1)}, u32[]{:S(2)}, u32[]{:S(2)}) collective-permute-start(bf16[64,512]{1,0:T(8,128)(2,1)} %get-tuple-element.19), channel_id=1, source_target_pairs={{0,1},{2,3},{4,5},{6,7},{8,9},{10,11},{12,13},{14,15},{1,0},{3,2},... | collective-permute-start | bytes 196616 | tf_op jit(solution)/shard_map/ppermute | solution.py:420
  39.1 6.6 %copy-start.13 = (s32[4,128]{1,0:T(4,128)S(1)}, s32[4,128]{1,0:T(4,128)}, u32[]{:S(2)}) copy-start(s32[4,128]{1,0:T(4,128)} %send_ref) | copy-start | bytes 6148
  41.1 14.6 %all-to-all-start.1 = ((bf16[16,16,512]{2,1,0:T(8,128)(2,1)}), bf16[16,16,512]{2,1,0:T(8,128)(2,1)S(1)}, u32[]{:S(2)}, u32[]{:S(2)}) async-start(bf16[16,16,512]{2,1,0:T(8,128)(2,1)} %bitcast.10), calls=%async_computation.1 | async-start | bytes 524288 | tf_op jit(solution)/shard_map/all_to_all | solution.py:447
  45.6 2.7 %copy-start.8 = (bf16[1024,512]{1,0:T(8,128)(2,1)S(1)}, bf16[1024,512]{1,0:T(8,128)(2,1)}, u32[]{:S(2)}) copy-start(bf16[1024,512]{1,0:T(8,128)(2,1)} %update_input_ref.3) | copy-start | bytes 3145732
  45.7 2.6 %copy-start.9 = (bf16[512,512]{1,0:T(8,128)(2,1)S(1)}, bf16[512,512]{1,0:T(8,128)(2,1)}, u32[]{:S(2)}) copy-start(bf16[512,512]{1,0:T(8,128)(2,1)} %mesh_receiver_ref.1) | copy-start | bytes 1572868
  45.7 2.6 %copy-start.14 = (s32[4,128]{1,0:T(4,128)S(1)}, s32[4,128]{1,0:T(4,128)}, u32[]{:S(2)}) copy-start(s32[4,128]{1,0:T(4,128)} %recv_ref.1) | copy-start | bytes 6148
  45.7 2.6 %copy-start.15 = (f32[512]{0:T(512)S(1)}, f32[512]{0:T(512)}, u32[]{:S(2)}) copy-start(f32[512]{0:T(512)} %param.42) | copy-start | bytes 6148
  45.7 2.6 %copy-start.16 = (f32[512]{0:T(512)S(1)}, f32[512]{0:T(512)}, u32[]{:S(2)}) copy-start(f32[512]{0:T(512)} %param.45) | copy-start | bytes 6148
  48.3 7.4 %copy-start.10 = (bf16[512,512]{1,0:T(8,128)(2,1)S(1)}, bf16[512,512]{1,0:T(8,128)(2,1)}, u32[]{:S(2)}) copy-start(bf16[512,512]{1,0:T(8,128)(2,1)} %message_out_ref.1) | copy-start | bytes 1572868
  48.3 7.4 %copy-start.11 = (bf16[512,512]{1,0:T(8,128)(2,1)S(1)}, bf16[512,512]{1,0:T(8,128)(2,1)}, u32[]{:S(2)}) copy-start(bf16[512,512]{1,0:T(8,128)(2,1)} %update_out_ref.1) | copy-start | bytes 1572868
  48.3 7.4 %copy-start.17 = (f32[512]{0:T(512)S(1)}, f32[512]{0:T(512)}, u32[]{:S(2)}) copy-start(f32[512]{0:T(512)} %param.47) | copy-start | bytes 6148

commit v5 on v4

--- a/solution.py
+++ b/solution.py
@@ -71,11 +71,9 @@
     send_hbm,
     recv_hbm,
     feat_hbm,
-    mesh_send_hbm,
     own_ref,
     cross_ref,
     chip_ref,
-    asked_ref,
     first_ref,
     grid_bias_ref,
     grid_ref,
@@ -88,7 +86,6 @@
     send_ref,
     recv_ref,
     feat_ref,
-    mesh_send_ref,
     table,
     total,
     sems,
@@ -115,7 +112,6 @@
         (send_hbm, send_ref),
         (recv_hbm, recv_ref),
         (feat_hbm, feat_ref),
-        (mesh_send_hbm, mesh_send_ref),
         (count_hbm, count_ref),
     ]
     copies = [
@@ -150,9 +146,6 @@
 
     for copy in copies[5 + GRID_STEPS :]:
         copy.wait()
-    asked = mesh_send_ref[...]
-    for at in range(asked_ref.shape[0] // asked.shape[0]):
-        asked_ref[at * asked.shape[0] : (at + 1) * asked.shape[0], :] = asked
     place = place_ref[0]
     used = count_ref[...]
     feat_weight = jnp.concatenate(
@@ -161,19 +154,21 @@
     feat_weight = feat_weight.T.astype(BF16)[:, :feats]
     ids = ids_of_rows(slot_ref[...], (place - 1) * owned, 3 * owned)
     group = math.gcd(blocks, 4)
-    for first in range(0, blocks, group):
-        senders = jnp.concatenate([send_ref[b : b + 1, :] for b in range(first, first + group)], axis=1)
+    total[...] = jnp.zeros_like(total)
+
+    def edge_step(step, carry):
+        here = [step * group + b for b in range(group)]
+        senders = jnp.concatenate([send_ref[pl.ds(b, 1), :] for b in here], axis=1)
         picker = one_hot(senders, grid_rows)
-        feat = jnp.concatenate([feat_ref[b] for b in range(first, first + group)], axis=1)
+        feat = jnp.concatenate([feat_ref[b] for b in here], axis=1)
         half = mm(table[...], picker) + mm(feat_weight, feat.astype(BF16))
         hidden = silu_half(half).astype(BF16)
-        receivers = jnp.concatenate(
-            [jnp.where(b < used, recv_ref[b : b + 1, :], -2) for b in range(first, first + group)],
-            axis=1,
-        )
-        spread = (ids == receivers).astype(F32).astype(BF16)
-        sums = mm_nt(hidden, spread)
-        total[...] = sums if first == 0 else total[...] + sums
+        receivers = [jnp.where(b < used, recv_ref[pl.ds(b, 1), :], -2) for b in here]
+        spread = (ids == jnp.concatenate(receivers, axis=1)).astype(F32).astype(BF16)
+        total[...] += mm_nt(hidden, spread)
+        return carry
+
+    lax.fori_loop(0, blocks // group, edge_step, 0)
     pad = -3 * owned % LANES
     sums = jnp.concatenate([total[...], jnp.zeros((width, pad), F32)], axis=1).T
     below, above = sums[:owned].astype(BF16), sums[2 * owned : 3 * owned].astype(BF16)
@@ -378,6 +373,7 @@
     slot = mesh_slot.reshape(1, -1)
     row = lambda vector: vector.reshape(1, -1)
 
+    requests = lax.all_to_all(jnp.tile(mesh_send, (devices, 1)), "bulk", 0, 0, tiled=True)
     operands = (
         grid_first,
         row(grid_bias),
@@ -391,15 +387,13 @@
         g2m_send,
         g2m_recv,
         g2m_feat,
-        mesh_send,
-    )
-    own, cross, chip, asked = call(
+    )
+    own, cross, chip = call(
         edge_kernel,
         (
             shape(owned, width, kind=F32),
             shape(owned, width),
             shape(owned, width),
-            shape(devices * mesh_send.shape[0], mesh_send.shape[1], kind=I32),
         ),
         [SMEM] + [HBM] * len(operands),
         scratch=[VMEM(value.shape, value.dtype) for value in operands]
@@ -412,7 +406,7 @@
         moved=4_000_000,
         vmem=56,
     )(place, *operands)
-    requests = lax.all_to_all(asked, "bulk", 0, 0, tiled=True)
+    requests, _ = lax.optimization_barrier((requests, own))
     crossing = [(d, d + 1) for d in range(1, devices - 1, 2)]
     within = [(d, d + 1) for d in range(0, devices, 2)]
     both = lambda pairs: pairs + [(b, a) for a, b in pairs]

time: 58.1 us -> 55.7 us (0.959)
  Pallas kernels: 30.9 us -> 26.3 us
  waiting for transfers between devices: 9.64 us -> 7.44 us
  local copies, waits for them, and re-layouts: 0.1 us -> 2.3 us
  starting transfers between devices: 16.1 us -> 18.3 us
    pallas_call x1, Pallas kernels: 23.5 us -> 18.9 us  [per_device(): call(edge_kernel, (shape(owned, width, kind=F32), shape(owned, width), sh...]
    all_to_all x1, waiting for transfers between devices: 2.62 us -> 0.01 us  [per_device(): lax.all_to_all(jnp.tile(mesh_send, (devices, 1)), 'bulk', 0, 0, tiled=True)]
    all_to_all x1, starting transfers between devices: 4.57 us -> 6.79 us  [per_device(): piece = lax.all_to_all(rows, 'bulk', 0, 0, tiled=True)]
    another operation x0 -> x1, local copies, waits for them, and re-layouts: none -> 1.3 us  [per_device(): jnp.tile(mesh_send, (devices, 1))]
    unnamed x36, local copies, waits for them, and re-layouts: 0.1 us -> 1 us
  transfers between devices with their start and end apart: 4 -> 4, of which waited for: 2 -> 2; matrix products, arithmetic and copies ran while one was open for 0% -> 0% of each run, Pallas kernels for 6% -> 41%
where the time goes in v5:
time: 55.7 us; the launch traced here: 55.3 us
  Pallas kernels  26.3 us (47%)
  starting transfers between devices  18.3 us (33%)
  waiting for transfers between devices  7.44 us (13%)
  local copies, waits for them, and re-layouts  2.3 us (4%)
  between operations  0.94 us (2%)
    pallas_call x1, Pallas kernels, per_device(): call(edge_kernel, (shape(owned, width, kind=F32), shape(owned, width), sh...  18.9 us
    all_to_all x1, starting transfers between devices, per_device(): lax.all_to_all(jnp.tile(mesh_send, (devices, 1)), 'bulk', 0, 0, tiled=True)  7.39 us
    all_to_all x1, waiting for transfers between devices, per_device(): piece = lax.all_to_all(rows, 'bulk', 0, 0, tiled=True)  7.01 us
    all_to_all x1, starting transfers between devices, per_device(): piece = lax.all_to_all(rows, 'bulk', 0, 0, tiled=True)  6.79 us
    ppermute x1, starting transfers between devices, per_device(): from_chip = lax.ppermute(chip, 'bulk', both(within))  3.36 us
    pallas_call x1, Pallas kernels, per_device(): call(functools.partial(wanted_kernel, owned), shape(edges, places), [VMEM...  2.53 us
    pallas_call x1, Pallas kernels, per_device(): call(message_kernel, shape(owned, width), [VMEM] * 12, flops=1000000000,...  2.05 us
    pallas_call x1, Pallas kernels, per_device(): call(node_kernel, (shape(owned, width), shape(places, width)), [VMEM] * 1...  1.87 us
  transfers between devices with their start and end apart: 4, of which 2 were waited for; matrix products, arithmetic and copies ran while one was open for 0% of the time, Pallas kernels for 41%

profile of v5, /device:TPU:0, one launch (start us, length us, event | category | flops | bytes accessed | tf_op | source)
XLA Modules:
  0.0 55.3 jit_solution(6009078497530288065)
XLA Ops:
  0.0 1.3 %tile.2 = s32[16,4,128]{2,1,0:T(4,128)} broadcast(s32[4,128]{1,0:T(4,128)} %send_ref), dimensions={1,2} | broadcast | bytes 34816 | tf_op jit(solution)/shard_map/tile | solution.py:376
  1.3 7.4 %all-to-all-start = ((s32[16,4,128]{2,1,0:T(4,128)}), s32[16,4,128]{2,1,0:T(4,128)S(1)}, u32[]{:S(2)}, u32[]{:S(2)}) async-start(s32[16,4,128]{2,1,0:T(4,128)} %tile.2), calls=%async_computation | async-start | bytes 65536 | tf_op jit(solution)/shard_map/all_to_all | solution.py:376
  9.3 0.0 copy-start.13
  9.4 0.0 copy-start.2
  9.4 0.0 copy-start.3
  9.4 0.0 copy-start.5
  9.4 0.0 copy-start.7
  9.4 0.0 copy-start.8
  9.4 18.9 %shard_map.262 = (f32[64,512]{1,0:T(8,128)}, bf16[64,512]{1,0:T(8,128)(2,1)}, bf16[64,512]{1,0:T(8,128)(2,1)}) custom-call(s32[1]{0:T(128)} %bitcast.1.place_ref, bf16[474,512]{1,0:T(8,128)(2,1)} %first_hbm.1, f32[1,512]{1,0:T(1,128)} %bitcast.27, bf16[474,2048]{1,0:T(8,128)(2,1)} %bitcast.26, bf16[512,512]{1,0:T(8,128)(2,1)} %second_hbm.1, ...), custom_call_target="tpu_custom_call" | custom-call | flops 10000000000 | bytes 4000000 | tf_op jit(solution)/shard_map/pallas_call | solution.py:391
  28.3 0.0 copy-start
  28.3 0.0 copy-start.1
  28.4 0.8 %collective-permute-start = (bf16[64,512]{1,0:T(8,128)(2,1)}, bf16[64,512]{1,0:T(8,128)(2,1)S(1)}, u32[]{:S(2)}, u32[]{:S(2)}) collective-permute-start(bf16[64,512]{1,0:T(8,128)(2,1)} %get-tuple-element.18), channel_id=1, source_target_pairs={{1,2},{3,4},{5,6},{7,8},{9,10},{11,12},{13,14},{2,1},{4,3},{6,5},{... | collective-permute-start | bytes 196616 | tf_op jit(solution)/shard_map/ppermute | solution.py:413
  29.2 3.4 %collective-permute-start.1 = (bf16[64,512]{1,0:T(8,128)(2,1)}, bf16[64,512]{1,0:T(8,128)(2,1)S(1)}, u32[]{:S(2)}, u32[]{:S(2)}) collective-permute-start(bf16[64,512]{1,0:T(8,128)(2,1)} %get-tuple-element.19), channel_id=1, source_target_pairs={{0,1},{2,3},{4,5},{6,7},{8,9},{10,11},{12,13},{14,15},{1,0},{3,2},... | collective-permute-start | bytes 196616 | tf_op jit(solution)/shard_map/ppermute | solution.py:414
  32.5 0.0 all-to-all-done
  32.5 0.0 copy-done.13
  32.5 0.7 %shard_map.263.supply_ref = bf16[256,64]{1,0:T(8,128)(2,1)S(1)} custom-call(s32[1]{0:T(128)} %bitcast.1.place_ref, s32[1,1024]{1,0:T(1,128)S(1)} %bitcast.20, s32[64,128]{1,0:T(8,128)S(1)} %bitcast.16), custom_call_target="tpu_custom_call" | custom-call | flops 500000000 | bytes 500000 | tf_op jit(solution)/shard_map/pallas_call | solution.py:415
  33.2 0.0 copy-start.6
  33.2 0.0 collective-permute-done.from_cross_ref
  33.2 0.4 collective-permute-done.1.from_chip_ref
  33.6 0.0 copy-done.2
  33.6 0.0 copy-done.3
  33.6 0.0 copy-done.5
  33.6 0.0 copy-done.7
  33.6 0.0 copy-done.8
  33.7 0.0 copy-done
  33.7 0.0 copy-done.1
  33.7 0.0 copy-start.4
  33.7 0.9 %copy-done.4 = f32[64,512]{1,0:T(8,128)S(1)} copy-done((f32[64,512]{1,0:T(8,128)S(1)}, f32[64,512]{1,0:T(8,128)}, u32[]{:S(2)}) %copy-start.4) | copy-done | bytes 131096
  34.6 1.9 %shard_map.264 = (bf16[64,512]{1,0:T(8,128)(2,1)S(1)}, bf16[256,512]{1,0:T(8,128)(2,1)}) custom-call(f32[64,512]{1,0:T(8,128)S(1)} %copy-done.4, bf16[64,512]{1,0:T(8,128)(2,1)S(1)} %collective-permute-done.from_cross_ref, bf16[64,512]{1,0:T(8,128)(2,1)S(1)} %collective-permute-done.1.from_chip_ref, bf16[64,512]{1,0:T(8,128)(2,1)S(1)} %copy-done.5, ...), custom_call_target="tpu_custom_call" | custom-call | flops 500000000 | bytes 4000000 | tf_op jit(solution)/shard_map/pallas_call | solution.py:422
  36.4 6.8 %all-to-all-start.1 = ((bf16[16,16,512]{2,1,0:T(8,128)(2,1)}), bf16[16,16,512]{2,1,0:T(8,128)(2,1)S(1)}, u32[]{:S(2)}, u32[]{:S(2)}) async-start(bf16[16,16,512]{2,1,0:T(8,128)(2,1)} %bitcast.9), calls=%async_computation.1 | async-start | bytes 524288 | tf_op jit(solution)/shard_map/all_to_all | solution.py:441
  43.2 0.0 copy-start.9
  43.3 0.0 copy-start.10
  43.3 0.0 copy-start.14
  43.3 0.0 copy-start.15
  43.3 0.0 copy-start.16
  43.3 0.0 copy-done.6
  43.3 2.5 %shard_map.265.wanted_ref = bf16[512,256]{1,0:T(8,128)(2,1)S(1)} custom-call(s32[1,1024]{1,0:T(1,128)S(1)} %bitcast.21, s32[4,128]{1,0:T(4,128)S(1)} %copy-done.6), custom_call_target="tpu_custom_call" | custom-call | flops 1000000000 | bytes 500000 | tf_op jit(solution)/shard_map/pallas_call | solution.py:443
  45.9 0.0 copy-start.11
  45.9 0.0 copy-start.12
  45.9 0.0 copy-start.17
  45.9 0.0 copy-done.9
  45.9 0.0 copy-done.10
  45.9 0.0 copy-done.14
  45.9 0.0 copy-done.15
  45.9 0.0 copy-done.16
  45.9 0.3 shard_map.266
  46.3 7.0 %all-to-all-done.1 = bf16[16,16,512]{2,1,0:T(8,128)(2,1)S(1)} async-done(((bf16[16,16,512]{2,1,0:T(8,128)(2,1)}), bf16[16,16,512]{2,1,0:T(8,128)(2,1)S(1)}, u32[]{:S(2)}, u32[]{:S(2)}) %all-to-all-start.1) | async-done | bytes 262176 | tf_op jit(solution)/shard_map/all_to_all | solution.py:441
  53.3 0.0 copy-done.11
  53.3 0.0 copy-done.12
  53.3 0.0 copy-done.17
  53.3 2.0 %shard_map.267 = bf16[64,512]{1,0:T(8,128)(2,1)} custom-call(bf16[512,256]{1,0:T(8,128)(2,1)S(1)} %shard_map.265.wanted_ref, bf16[256,512]{1,0:T(8,128)(2,1)S(1)} %bitcast.15, bf16[64,512]{1,0:T(8,128)(2,1)S(1)} %get-tuple-element.24.incoming_ref, bf16[512,64]{1,0:T(8,128)(2,1)S(1)} %get-tuple-element.25.pick_ref, ...), custom_call_target="tpu_custom_call" | custom-call | flops 1000000000 | bytes 4000000 | tf_op jit(solution)/shard_map/pallas_call | solution.py:472
Async XLA Ops:
  1.3 31.2 %all-to-all-start = ((s32[16,4,128]{2,1,0:T(4,128)}), s32[16,4,128]{2,1,0:T(4,128)S(1)}, u32[]{:S(2)}, u32[]{:S(2)}) async-start(s32[16,4,128]{2,1,0:T(4,128)} %tile.2), calls=%async_computation | async-start | bytes 65536 | tf_op jit(solution)/shard_map/all_to_all | solution.py:376
  9.3 23.2 %copy-start.13 = (s32[1024]{0:T(1024)S(1)}, s32[1024]{0:T(1024)}, u32[]{:S(2)}) copy-start(s32[1024]{0:T(1024)} %param.53) | copy-start | bytes 12292
  9.4 24.3 %copy-start.2 = (bf16[512,512]{1,0:T(8,128)(2,1)S(1)}, bf16[512,512]{1,0:T(8,128)(2,1)}, u32[]{:S(2)}) copy-start(bf16[512,512]{1,0:T(8,128)(2,1)} %node_out_ref.1) | copy-start | bytes 1572868
  9.4 24.3 %copy-start.3 = (bf16[512,512]{1,0:T(8,128)(2,1)S(1)}, bf16[512,512]{1,0:T(8,128)(2,1)}, u32[]{:S(2)}) copy-start(bf16[512,512]{1,0:T(8,128)(2,1)} %mesh_sender_ref.1) | copy-start | bytes 1572868
  9.4 24.3 %copy-start.5 = (bf16[64,512]{1,0:T(8,128)(2,1)S(1)}, bf16[64,512]{1,0:T(8,128)(2,1)}, u32[]{:S(2)}) copy-start(bf16[64,512]{1,0:T(8,128)(2,1)} %latent_ref.1) | copy-start | bytes 196612
  9.4 24.2 %copy-start.7 = (f32[512]{0:T(512)S(1)}, f32[512]{0:T(512)}, u32[]{:S(2)}) copy-start(f32[512]{0:T(512)} %param.37) | copy-start | bytes 6148
  9.4 24.2 %copy-start.8 = (f32[512]{0:T(512)S(1)}, f32[512]{0:T(512)}, u32[]{:S(2)}) copy-start(f32[512]{0:T(512)} %param.39) | copy-start | bytes 6148
  28.3 5.3 %copy-start = (bf16[1024,512]{1,0:T(8,128)(2,1)S(1)}, bf16[1024,512]{1,0:T(8,128)(2,1)}, u32[]{:S(2)}) copy-start(bf16[1024,512]{1,0:T(8,128)(2,1)} %node_input_ref.1) | copy-start | bytes 3145732
  28.3 5.3 %copy-start.1 = (bf16[512,512]{1,0:T(8,128)(2,1)S(1)}, bf16[512,512]{1,0:T(8,128)(2,1)}, u32[]{:S(2)}) copy-start(bf16[512,512]{1,0:T(8,128)(2,1)} %edge_out_ref.1) | copy-start | bytes 1572868
  28.4 4.8 %collective-permute-start = (bf16[64,512]{1,0:T(8,128)(2,1)}, bf16[64,512]{1,0:T(8,128)(2,1)S(1)}, u32[]{:S(2)}, u32[]{:S(2)}) collective-permute-start(bf16[64,512]{1,0:T(8,128)(2,1)} %get-tuple-element.18), channel_id=1, source_target_pairs={{1,2},{3,4},{5,6},{7,8},{9,10},{11,12},{13,14},{2,1},{4,3},{6,5},{... | collective-permute-start | bytes 196616 | tf_op jit(solution)/shard_map/ppermute | solution.py:413
  29.2 4.5 %collective-permute-start.1 = (bf16[64,512]{1,0:T(8,128)(2,1)}, bf16[64,512]{1,0:T(8,128)(2,1)S(1)}, u32[]{:S(2)}, u32[]{:S(2)}) collective-permute-start(bf16[64,512]{1,0:T(8,128)(2,1)} %get-tuple-element.19), channel_id=1, source_target_pairs={{0,1},{2,3},{4,5},{6,7},{8,9},{10,11},{12,13},{14,15},{1,0},{3,2},... | collective-permute-start | bytes 196616 | tf_op jit(solution)/shard_map/ppermute | solution.py:414
  33.2 10.1 %copy-start.6 = (s32[4,128]{1,0:T(4,128)S(1)}, s32[4,128]{1,0:T(4,128)}, u32[]{:S(2)}) copy-start(s32[4,128]{1,0:T(4,128)} %send_ref) | copy-start | bytes 6148
  33.7 0.9 %copy-start.4 = (f32[64,512]{1,0:T(8,128)S(1)}, f32[64,512]{1,0:T(8,128)}, u32[]{:S(2)}) copy-start(f32[64,512]{1,0:T(8,128)} %get-tuple-element.17.own_ref) | copy-start | bytes 393220
  36.4 16.8 %all-to-all-start.1 = ((bf16[16,16,512]{2,1,0:T(8,128)(2,1)}), bf16[16,16,512]{2,1,0:T(8,128)(2,1)S(1)}, u32[]{:S(2)}, u32[]{:S(2)}) async-start(bf16[16,16,512]{2,1,0:T(8,128)(2,1)} %bitcast.9), calls=%async_computation.1 | async-start | bytes 524288 | tf_op jit(solution)/shard_map/all_to_all | solution.py:441
  43.2 2.6 %copy-start.9 = (bf16[1024,512]{1,0:T(8,128)(2,1)S(1)}, bf16[1024,512]{1,0:T(8,128)(2,1)}, u32[]{:S(2)}) copy-start(bf16[1024,512]{1,0:T(8,128)(2,1)} %update_input_ref.3) | copy-start | bytes 3145732
  43.3 2.6 %copy-start.10 = (bf16[512,512]{1,0:T(8,128)(2,1)S(1)}, bf16[512,512]{1,0:T(8,128)(2,1)}, u32[]{:S(2)}) copy-start(bf16[512,512]{1,0:T(8,128)(2,1)} %mesh_receiver_ref.1) | copy-start | bytes 1572868
  43.3 2.6 %copy-start.14 = (s32[4,128]{1,0:T(4,128)S(1)}, s32[4,128]{1,0:T(4,128)}, u32[]{:S(2)}) copy-start(s32[4,128]{1,0:T(4,128)} %recv_ref.1) | copy-start | bytes 6148
  43.3 2.6 %copy-start.15 = (f32[512]{0:T(512)S(1)}, f32[512]{0:T(512)}, u32[]{:S(2)}) copy-start(f32[512]{0:T(512)} %param.42) | copy-start | bytes 6148
  43.3 2.6 %copy-start.16 = (f32[512]{0:T(512)S(1)}, f32[512]{0:T(512)}, u32[]{:S(2)}) copy-start(f32[512]{0:T(512)} %param.45) | copy-start | bytes 6148
  45.9 7.4 %copy-start.11 = (bf16[512,512]{1,0:T(8,128)(2,1)S(1)}, bf16[512,512]{1,0:T(8,128)(2,1)}, u32[]{:S(2)}) copy-start(bf16[512,512]{1,0:T(8,128)(2,1)} %message_out_ref.1) | copy-start | bytes 1572868
  45.9 7.4 %copy-start.12 = (bf16[512,512]{1,0:T(8,128)(2,1)S(1)}, bf16[512,512]{1,0:T(8,128)(2,1)}, u32[]{:S(2)}) copy-start(bf16[512,512]{1,0:T(8,128)(2,1)} %update_out_ref.1) | copy-start | bytes 1572868
  45.9 7.4 %copy-start.17 = (f32[512]{0:T(512)S(1)}, f32[512]{0:T(512)}, u32[]{:S(2)}) copy-start(f32[512]{0:T(512)} %param.47) | copy-start | bytes 6148

commit v6 on v5

--- a/solution.py
+++ b/solution.py
@@ -60,33 +60,38 @@
 def edge_kernel(
     place_ref,
     first_hbm,
-    grid_bias_hbm,
     grid_hbm,
     second_hbm,
     send_weight_hbm,
+    grid_bias_hbm,
     edge_bias_hbm,
-    count_hbm,
     slot_hbm,
     feat_weight_hbm,
     send_hbm,
     recv_hbm,
     feat_hbm,
+    count_hbm,
     own_ref,
     cross_ref,
     chip_ref,
     first_ref,
-    grid_bias_ref,
     grid_ref,
     second_ref,
     send_weight_ref,
+    grid_bias_ref,
     edge_bias_ref,
-    count_ref,
     slot_ref,
     feat_weight_ref,
     send_ref,
     recv_ref,
     feat_ref,
+    count_ref,
     table,
+    first_t,
+    second_t,
+    weight_t,
+    grid_column,
+    edge_column,
     total,
     sems,
 ):
@@ -96,17 +101,17 @@
     owned = own_ref.shape[0]
     feats = feat_ref.shape[1]
     step_rows = grid_rows // GRID_STEPS
-    columns = [pl.ds(step * step_rows, step_rows) for step in range(GRID_STEPS)]
+
+    def grid_copy(step):
+        part = pl.ds(pl.multiple_of(step * step_rows, step_rows), step_rows)
+        return pltpu.make_async_copy(grid_hbm.at[:, part], grid_ref.at[:, part], sems.at[step])
+
     pairs = [
         (first_hbm, first_ref),
-        (grid_bias_hbm, grid_bias_ref),
-        (grid_hbm.at[:, columns[0]], grid_ref.at[:, columns[0]]),
         (second_hbm, second_ref),
         (send_weight_hbm, send_weight_ref),
+        (grid_bias_hbm, grid_bias_ref),
         (edge_bias_hbm, edge_bias_ref),
-    ]
-    pairs += [(grid_hbm.at[:, part], grid_ref.at[:, part]) for part in columns[1:]]
-    pairs += [
         (slot_hbm, slot_ref),
         (feat_weight_hbm, feat_weight_ref),
         (send_hbm, send_ref),
@@ -115,54 +120,59 @@
         (count_hbm, count_ref),
     ]
     copies = [
-        pltpu.make_async_copy(source, target, sems.at[at])
+        pltpu.make_async_copy(source, target, sems.at[GRID_STEPS + at])
         for at, (source, target) in enumerate(pairs)
     ]
-    for copy in copies[:3]:
+    for copy in copies[:5]:
         copy.start()
-    column = lambda ref: jnp.broadcast_to(0.5 * ref[...], (LANES, width)).T
-    wide = lambda value: jnp.concatenate([value] * (step_rows // LANES), axis=1)
-    for copy in copies[:2]:
-        copy.wait()
-    for copy in copies[3:]:
+    for step in range(GRID_STEPS):
+        grid_copy(step).start()
+    for copy in copies[5:]:
         copy.start()
-    first_t = (0.5 * first_ref[...].astype(F32)).T.astype(BF16)
-    grid_bias = column(grid_bias_ref)
-    for step, part in enumerate(columns):
-        copies[2 if step == 0 else 5 + step].wait()
-        half = mm(first_t, grid_ref[:, part]) + wide(grid_bias)
-        hidden = silu_half(half).astype(BF16)
-        if step == 0:
-            for copy in copies[3:6]:
-                copy.wait()
-            second_t = second_ref[...].T
-            weight_t = (0.5 * send_weight_ref[...].astype(F32)).T.astype(BF16)
-            edge_bias = column(edge_bias_ref)
-        value = mm(second_t, hidden)
+    copies[0].wait()
+    first_t[...] = (0.5 * first_ref[...].astype(F32)).T.astype(BF16)
+    copies[1].wait()
+    second_t[...] = second_ref[...].T
+    copies[2].wait()
+    weight_t[...] = (0.5 * send_weight_ref[...].astype(F32)).T.astype(BF16)
+    copies[3].wait()
+    grid_column[...] = jnp.broadcast_to(0.5 * grid_bias_ref[...], (LANES, width)).T
+    copies[4].wait()
+    edge_column[...] = jnp.broadcast_to(0.5 * edge_bias_ref[...], (LANES, width)).T
+    wide = lambda ref: jnp.concatenate([ref[...]] * (step_rows // LANES), axis=1)
+
+    def grid_step(step, carry):
+        part = pl.ds(pl.multiple_of(step * step_rows, step_rows), step_rows)
+        grid_copy(step).wait()
+        hidden = silu_half(mm(first_t[...], grid_ref[:, part]) + wide(grid_column)).astype(BF16)
+        value = mm(second_t[...], hidden)
         center = value - jnp.mean(value, axis=0, keepdims=True)
         spread = jnp.mean(center * center, axis=0, keepdims=True)
         code = (center * lax.rsqrt(spread + 1e-05)).astype(BF16)
-        table[:, part] = (mm(weight_t, code) + wide(edge_bias)).astype(BF16)
-
-    for copy in copies[5 + GRID_STEPS :]:
+        table[:, part] = (mm(weight_t[...], code) + wide(edge_column)).astype(BF16)
+        return carry
+
+    lax.fori_loop(0, GRID_STEPS, grid_step, 0)
+    for copy in copies[5:]:
         copy.wait()
     place = place_ref[0]
     used = count_ref[...]
     feat_weight = jnp.concatenate(
         [0.5 * feat_weight_ref[...].astype(F32), jnp.zeros((LANES - feats, width), F32)], axis=0
     )
-    feat_weight = feat_weight.T.astype(BF16)[:, :feats]
+    table[:, grid_rows:] = feat_weight.T.astype(BF16)
     ids = ids_of_rows(slot_ref[...], (place - 1) * owned, 3 * owned)
     group = math.gcd(blocks, 4)
+    blank = jnp.zeros((LANES - feats, group * block_edges), F32)
     total[...] = jnp.zeros_like(total)
 
     def edge_step(step, carry):
         here = [step * group + b for b in range(group)]
         senders = jnp.concatenate([send_ref[pl.ds(b, 1), :] for b in here], axis=1)
-        picker = one_hot(senders, grid_rows)
         feat = jnp.concatenate([feat_ref[b] for b in here], axis=1)
-        half = mm(table[...], picker) + mm(feat_weight, feat.astype(BF16))
-        hidden = silu_half(half).astype(BF16)
+        feat = jnp.concatenate([feat, blank], axis=0).astype(BF16)
+        picker = jnp.concatenate([one_hot(senders, grid_rows), feat], axis=0)
+        hidden = silu_half(mm(table[...], picker)).astype(BF16)
         receivers = [jnp.where(b < used, recv_ref[pl.ds(b, 1), :], -2) for b in here]
         spread = (ids == jnp.concatenate(receivers, axis=1)).astype(F32).astype(BF16)
         total[...] += mm_nt(hidden, spread)
@@ -210,7 +220,7 @@
         )
 
 
-def supply_kernel(place_ref, slot_ref, request_ref, supply_ref):
+def supply_kernel(blocks, place_ref, slot_ref, request_ref, supply_ref):
     owned = supply_ref.shape[1]
     devices = supply_ref.shape[0] // SEND_CAP
     per_device = request_ref.shape[0] // devices
@@ -219,7 +229,7 @@
     used = jnp.zeros((owned, LANES), F32)
     for d in range(devices):
         hit = jnp.zeros((owned, request_ref.shape[1]), F32)
-        for b in range(per_device):
+        for b in range(blocks):
             at = d * per_device + b
             hit = jnp.maximum(hit, (ids == request_ref[at : at + 1, :]).astype(F32))
         used = jnp.where(lane == d, jnp.max(hit, axis=1, keepdims=True), used)
@@ -327,6 +337,10 @@
         compiler_params=pltpu.CompilerParams(vmem_limit_bytes=vmem * MEBI),
         cost_estimate=pl.CostEstimate(flops=flops, bytes_accessed=moved, transcendentals=0),
     )
+
+
+def hold(value):
+    return value if value.size == 1 else pltpu.with_memory_space_constraint(value, HBM)
 
 
 def shape(*sizes, kind=BF16):
@@ -376,36 +390,37 @@
     requests = lax.all_to_all(jnp.tile(mesh_send, (devices, 1)), "bulk", 0, 0, tiled=True)
     operands = (
         grid_first,
-        row(grid_bias),
         grid_in.T,
         grid_second,
         send_weight,
+        row(grid_bias),
         row(edge_bias),
-        g2m_count.reshape(1, 1),
         slot,
         feat_weight,
         g2m_send,
         g2m_recv,
         g2m_feat,
+        g2m_count.reshape(1, 1),
     )
     own, cross, chip = call(
         edge_kernel,
-        (
-            shape(owned, width, kind=F32),
-            shape(owned, width),
-            shape(owned, width),
-        ),
+        (shape(owned, width, kind=F32), shape(owned, width), shape(owned, width)),
         [SMEM] + [HBM] * len(operands),
         scratch=[VMEM(value.shape, value.dtype) for value in operands]
         + [
-            pltpu.VMEM((width, grid_rows), BF16),
+            pltpu.VMEM((width, grid_rows + LANES), BF16),
+            pltpu.VMEM((width, grid_first.shape[0]), BF16),
+            pltpu.VMEM((width, width), BF16),
+            pltpu.VMEM((width, width), BF16),
+            pltpu.VMEM((width, LANES), F32),
+            pltpu.VMEM((width, LANES), F32),
             pltpu.VMEM((width, 3 * owned), F32),
             pltpu.SemaphoreType.DMA((len(operands) - 1 + GRID_STEPS,)),
         ],
         flops=10_000_000_000,
         moved=4_000_000,
-        vmem=56,
-    )(place, *operands)
+        vmem=32,
+    )(place, *[hold(value) for value in operands])
     requests, _ = lax.optimization_barrier((requests, own))
     crossing = [(d, d + 1) for d in range(1, devices - 1, 2)]
     within = [(d, d + 1) for d in range(0, devices, 2)]
@@ -413,7 +428,7 @@
     from_cross = lax.ppermute(cross, "bulk", both(crossing))
     from_chip = lax.ppermute(chip, "bulk", both(within))
     supply = call(
-        supply_kernel,
+        functools.partial(supply_kernel, mesh_send.shape[0]),
         shape(places, owned),
         [SMEM] + [VMEM] * 2,
         flops=500_000_000,

time: 55.7 us -> 54 us (0.969)
  local copies, waits for them, and re-layouts: 2.3 us -> 1.41 us
    unnamed x36 -> x34, local copies, waits for them, and re-layouts: 1 us -> 0.11 us
    pallas_call x1, Pallas kernels: 18.9 us -> 18.3 us  [per_device(): call(edge_kernel, (shape(owned, width, kind=F32), shape(owned, width), sh...]
where the time goes in v6:
time: 54 us; the launch traced here: 53.7 us
  Pallas kernels  25.8 us (48%)
  starting transfers between devices  18.3 us (34%)
  waiting for transfers between devices  7.23 us (13%)
  local copies, waits for them, and re-layouts  1.41 us (3%)
  between operations  0.93 us (2%)
    pallas_call x1, Pallas kernels, per_device(): call(edge_kernel, (shape(owned, width, kind=F32), shape(owned, width), sh...  18.3 us
    all_to_all x1, starting transfers between devices, per_device(): lax.all_to_all(jnp.tile(mesh_send, (devices, 1)), 'bulk', 0, 0, tiled=True)  7.39 us
    all_to_all x1, waiting for transfers between devices, per_device(): piece = lax.all_to_all(rows, 'bulk', 0, 0, tiled=True)  7.02 us
    all_to_all x1, starting transfers between devices, per_device(): piece = lax.all_to_all(rows, 'bulk', 0, 0, tiled=True)  6.8 us
    ppermute x1, starting transfers between devices, per_device(): from_chip = lax.ppermute(chip, 'bulk', both(within))  3.35 us
    pallas_call x1, Pallas kernels, per_device(): call(functools.partial(wanted_kernel, owned), shape(edges, places), [VMEM...  2.53 us
    pallas_call x1, Pallas kernels, per_device(): call(message_kernel, shape(owned, width), [VMEM] * 12, flops=1000000000,...  2.05 us
    pallas_call x1, Pallas kernels, per_device(): call(node_kernel, (shape(owned, width), shape(places, width)), [VMEM] * 1...  1.87 us
  transfers between devices with their start and end apart: 4, of which 2 were waited for; matrix products, arithmetic and copies ran while one was open for 0% of the time, Pallas kernels for 41%

profile of v6, /device:TPU:0, one launch (start us, length us, event | category | flops | bytes accessed | tf_op | source)
XLA Modules:
  0.0 53.7 jit_solution(945995926437288457)
XLA Ops:
  0.0 1.3 %tile.2 = s32[16,4,128]{2,1,0:T(4,128)} broadcast(s32[4,128]{1,0:T(4,128)} %send_ref), dimensions={1,2} | broadcast | bytes 34816 | tf_op jit(solution)/shard_map/tile | solution.py:390
  1.3 7.4 %all-to-all-start = ((s32[16,4,128]{2,1,0:T(4,128)}), s32[16,4,128]{2,1,0:T(4,128)S(1)}, u32[]{:S(2)}, u32[]{:S(2)}) async-start(s32[16,4,128]{2,1,0:T(4,128)} %tile.2), calls=%async_computation | async-start | bytes 65536 | tf_op jit(solution)/shard_map/all_to_all | solution.py:390
  9.3 0.0 copy-start.12
  9.4 0.0 copy-start.2
  9.4 0.0 copy-start.3
  9.4 0.0 copy-start.4
  9.4 0.0 copy-start.6
  9.4 0.0 copy-start.7
  9.4 18.3 %shard_map.262 = (f32[64,512]{1,0:T(8,128)S(1)}, bf16[64,512]{1,0:T(8,128)(2,1)S(1)}, bf16[64,512]{1,0:T(8,128)(2,1)S(1)}) custom-call(s32[1]{0:T(128)} %bitcast.1.place_ref, bf16[474,512]{1,0:T(8,128)(2,1)} %first_hbm.1, bf16[474,2048]{1,0:T(8,128)(2,1)} %bitcast.26, bf16[512,512]{1,0:T(8,128)(2,1)} %second_hbm.1, bf16[512,512]{1,0:T(8,128)(2,1)} %send_weight_hbm.1, ...), custom_call_target="tpu_custom_call" | custom-call | flops 10000000000 | bytes 4000000 | tf_op jit(solution)/shard_map/pallas_call | solution.py:405
  27.8 0.0 copy-start
  27.8 0.0 copy-start.1
  27.8 0.8 %collective-permute-start = (bf16[64,512]{1,0:T(8,128)(2,1)S(1)}, bf16[64,512]{1,0:T(8,128)(2,1)S(1)}, u32[]{:S(2)}, u32[]{:S(2)}) collective-permute-start(bf16[64,512]{1,0:T(8,128)(2,1)S(1)} %get-tuple-element.18), channel_id=1, source_target_pairs={{1,2},{3,4},{5,6},{7,8},{9,10},{11,12},{13,14},{2,1},{4,3},{6,5},{... | collective-permute-start | bytes 196616 | tf_op jit(solution)/shard_map/ppermute | solution.py:428
  28.6 3.4 %collective-permute-start.1 = (bf16[64,512]{1,0:T(8,128)(2,1)S(1)}, bf16[64,512]{1,0:T(8,128)(2,1)S(1)}, u32[]{:S(2)}, u32[]{:S(2)}) collective-permute-start(bf16[64,512]{1,0:T(8,128)(2,1)S(1)} %get-tuple-element.19), channel_id=1, source_target_pairs={{0,1},{2,3},{4,5},{6,7},{8,9},{10,11},{12,13},{14,15},{1,0},{3,2},... | collective-permute-start | bytes 196616 | tf_op jit(solution)/shard_map/ppermute | solution.py:429
  31.9 0.0 all-to-all-done
  31.9 0.0 copy-done.12
  31.9 0.7 %shard_map.263.supply_ref = bf16[256,64]{1,0:T(8,128)(2,1)S(1)} custom-call(s32[1]{0:T(128)} %bitcast.1.place_ref, s32[1,1024]{1,0:T(1,128)S(1)} %bitcast.20, s32[64,128]{1,0:T(8,128)S(1)} %bitcast.16), custom_call_target="tpu_custom_call" | custom-call | flops 500000000 | bytes 500000 | tf_op jit(solution)/shard_map/pallas_call | solution.py:430
  32.6 0.0 copy-start.5
  32.6 0.0 collective-permute-done.from_cross_ref
  32.6 0.2 collective-permute-done.1.from_chip_ref
  32.8 0.0 copy-done.2
  32.8 0.0 copy-done.3
  32.8 0.0 copy-done.4
  32.8 0.0 copy-done.6
  32.9 0.0 copy-done.7
  32.9 0.0 copy-done
  32.9 0.0 copy-done.1
  32.9 1.9 %shard_map.264 = (bf16[64,512]{1,0:T(8,128)(2,1)S(1)}, bf16[256,512]{1,0:T(8,128)(2,1)}) custom-call(f32[64,512]{1,0:T(8,128)S(1)} %get-tuple-element.17.own_ref, bf16[64,512]{1,0:T(8,128)(2,1)S(1)} %collective-permute-done.from_cross_ref, bf16[64,512]{1,0:T(8,128)(2,1)S(1)} %collective-permute-done.1.from_chip_ref, bf16[64,512]{1,0:T(8,128)(2,1)S(1)} %copy-done.4, ...), custom_call_target="tpu_custom_call" | custom-call | flops 500000000 | bytes 4000000 | tf_op jit(solution)/shard_map/pallas_call | solution.py:437
  34.8 6.8 %all-to-all-start.1 = ((bf16[16,16,512]{2,1,0:T(8,128)(2,1)}), bf16[16,16,512]{2,1,0:T(8,128)(2,1)S(1)}, u32[]{:S(2)}, u32[]{:S(2)}) async-start(bf16[16,16,512]{2,1,0:T(8,128)(2,1)} %bitcast.9), calls=%async_computation.1 | async-start | bytes 524288 | tf_op jit(solution)/shard_map/all_to_all | solution.py:456
  41.6 0.0 copy-start.8
  41.6 0.0 copy-start.9
  41.6 0.0 copy-start.13
  41.6 0.0 copy-start.14
  41.6 0.0 copy-start.15
  41.6 0.0 copy-done.5
  41.6 2.5 %shard_map.265.wanted_ref = bf16[512,256]{1,0:T(8,128)(2,1)S(1)} custom-call(s32[1,1024]{1,0:T(1,128)S(1)} %bitcast.21, s32[4,128]{1,0:T(4,128)S(1)} %copy-done.5), custom_call_target="tpu_custom_call" | custom-call | flops 1000000000 | bytes 500000 | tf_op jit(solution)/shard_map/pallas_call | solution.py:458
  44.2 0.0 copy-start.10
  44.2 0.0 copy-start.11
  44.2 0.0 copy-start.16
  44.2 0.0 copy-done.8
  44.2 0.0 copy-done.9
  44.2 0.0 copy-done.13
  44.2 0.0 copy-done.14
  44.3 0.0 copy-done.15
  44.3 0.3 shard_map.266
  44.6 7.0 %all-to-all-done.1 = bf16[16,16,512]{2,1,0:T(8,128)(2,1)S(1)} async-done(((bf16[16,16,512]{2,1,0:T(8,128)(2,1)}), bf16[16,16,512]{2,1,0:T(8,128)(2,1)S(1)}, u32[]{:S(2)}, u32[]{:S(2)}) %all-to-all-start.1) | async-done | bytes 262176 | tf_op jit(solution)/shard_map/all_to_all | solution.py:456
  51.6 0.0 copy-done.10
  51.6 0.0 copy-done.11
  51.6 0.0 copy-done.16
  51.6 2.0 %shard_map.267 = bf16[64,512]{1,0:T(8,128)(2,1)} custom-call(bf16[512,256]{1,0:T(8,128)(2,1)S(1)} %shard_map.265.wanted_ref, bf16[256,512]{1,0:T(8,128)(2,1)S(1)} %bitcast.15, bf16[64,512]{1,0:T(8,128)(2,1)S(1)} %get-tuple-element.24.incoming_ref, bf16[512,64]{1,0:T(8,128)(2,1)S(1)} %get-tuple-element.25.pick_ref, ...), custom_call_target="tpu_custom_call" | custom-call | flops 1000000000 | bytes 4000000 | tf_op jit(solution)/shard_map/pallas_call | solution.py:487
Async XLA Ops:
  1.3 30.6 %all-to-all-start = ((s32[16,4,128]{2,1,0:T(4,128)}), s32[16,4,128]{2,1,0:T(4,128)S(1)}, u32[]{:S(2)}, u32[]{:S(2)}) async-start(s32[16,4,128]{2,1,0:T(4,128)} %tile.2), calls=%async_computation | async-start | bytes 65536 | tf_op jit(solution)/shard_map/all_to_all | solution.py:390
  9.3 22.6 %copy-start.12 = (s32[1024]{0:T(1024)S(1)}, s32[1024]{0:T(1024)}, u32[]{:S(2)}) copy-start(s32[1024]{0:T(1024)} %param.53) | copy-start | bytes 12292
  9.4 23.5 %copy-start.2 = (bf16[512,512]{1,0:T(8,128)(2,1)S(1)}, bf16[512,512]{1,0:T(8,128)(2,1)}, u32[]{:S(2)}) copy-start(bf16[512,512]{1,0:T(8,128)(2,1)} %node_out_ref.1) | copy-start | bytes 1572868
  9.4 23.5 %copy-start.3 = (bf16[512,512]{1,0:T(8,128)(2,1)S(1)}, bf16[512,512]{1,0:T(8,128)(2,1)}, u32[]{:S(2)}) copy-start(bf16[512,512]{1,0:T(8,128)(2,1)} %mesh_sender_ref.1) | copy-start | bytes 1572868
  9.4 23.5 %copy-start.4 = (bf16[64,512]{1,0:T(8,128)(2,1)S(1)}, bf16[64,512]{1,0:T(8,128)(2,1)}, u32[]{:S(2)}) copy-start(bf16[64,512]{1,0:T(8,128)(2,1)} %latent_ref.1) | copy-start | bytes 196612
  9.4 23.5 %copy-start.6 = (f32[512]{0:T(512)S(1)}, f32[512]{0:T(512)}, u32[]{:S(2)}) copy-start(f32[512]{0:T(512)} %param.37) | copy-start | bytes 6148
  9.4 23.4 %copy-start.7 = (f32[512]{0:T(512)S(1)}, f32[512]{0:T(512)}, u32[]{:S(2)}) copy-start(f32[512]{0:T(512)} %param.39) | copy-start | bytes 6148
  27.8 5.1 %copy-start = (bf16[1024,512]{1,0:T(8,128)(2,1)S(1)}, bf16[1024,512]{1,0:T(8,128)(2,1)}, u32[]{:S(2)}) copy-start(bf16[1024,512]{1,0:T(8,128)(2,1)} %node_input_ref.1) | copy-start | bytes 3145732
  27.8 5.1 %copy-start.1 = (bf16[512,512]{1,0:T(8,128)(2,1)S(1)}, bf16[512,512]{1,0:T(8,128)(2,1)}, u32[]{:S(2)}) copy-start(bf16[512,512]{1,0:T(8,128)(2,1)} %edge_out_ref.1) | copy-start | bytes 1572868
  27.8 4.8 %collective-permute-start = (bf16[64,512]{1,0:T(8,128)(2,1)S(1)}, bf16[64,512]{1,0:T(8,128)(2,1)S(1)}, u32[]{:S(2)}, u32[]{:S(2)}) collective-permute-start(bf16[64,512]{1,0:T(8,128)(2,1)S(1)} %get-tuple-element.18), channel_id=1, source_target_pairs={{1,2},{3,4},{5,6},{7,8},{9,10},{11,12},{13,14},{2,1},{4,3},{6,5},{... | collective-permute-start | bytes 196616 | tf_op jit(solution)/shard_map/ppermute | solution.py:428
  28.6 4.3 %collective-permute-start.1 = (bf16[64,512]{1,0:T(8,128)(2,1)S(1)}, bf16[64,512]{1,0:T(8,128)(2,1)S(1)}, u32[]{:S(2)}, u32[]{:S(2)}) collective-permute-start(bf16[64,512]{1,0:T(8,128)(2,1)S(1)} %get-tuple-element.19), channel_id=1, source_target_pairs={{0,1},{2,3},{4,5},{6,7},{8,9},{10,11},{12,13},{14,15},{1,0},{3,2},... | collective-permute-start | bytes 196616 | tf_op jit(solution)/shard_map/ppermute | solution.py:429
  32.6 9.0 %copy-start.5 = (s32[4,128]{1,0:T(4,128)S(1)}, s32[4,128]{1,0:T(4,128)}, u32[]{:S(2)}) copy-start(s32[4,128]{1,0:T(4,128)} %send_ref) | copy-start | bytes 6148
  34.8 16.9 %all-to-all-start.1 = ((bf16[16,16,512]{2,1,0:T(8,128)(2,1)}), bf16[16,16,512]{2,1,0:T(8,128)(2,1)S(1)}, u32[]{:S(2)}, u32[]{:S(2)}) async-start(bf16[16,16,512]{2,1,0:T(8,128)(2,1)} %bitcast.9), calls=%async_computation.1 | async-start | bytes 524288 | tf_op jit(solution)/shard_map/all_to_all | solution.py:456
  41.6 2.6 %copy-start.8 = (bf16[1024,512]{1,0:T(8,128)(2,1)S(1)}, bf16[1024,512]{1,0:T(8,128)(2,1)}, u32[]{:S(2)}) copy-start(bf16[1024,512]{1,0:T(8,128)(2,1)} %update_input_ref.3) | copy-start | bytes 3145732
  41.6 2.6 %copy-start.9 = (bf16[512,512]{1,0:T(8,128)(2,1)S(1)}, bf16[512,512]{1,0:T(8,128)(2,1)}, u32[]{:S(2)}) copy-start(bf16[512,512]{1,0:T(8,128)(2,1)} %mesh_receiver_ref.1) | copy-start | bytes 1572868
  41.6 2.6 %copy-start.13 = (s32[4,128]{1,0:T(4,128)S(1)}, s32[4,128]{1,0:T(4,128)}, u32[]{:S(2)}) copy-start(s32[4,128]{1,0:T(4,128)} %recv_ref.1) | copy-start | bytes 6148
  41.6 2.6 %copy-start.14 = (f32[512]{0:T(512)S(1)}, f32[512]{0:T(512)}, u32[]{:S(2)}) copy-start(f32[512]{0:T(512)} %param.42) | copy-start | bytes 6148
  41.6 2.6 %copy-start.15 = (f32[512]{0:T(512)S(1)}, f32[512]{0:T(512)}, u32[]{:S(2)}) copy-start(f32[512]{0:T(512)} %param.45) | copy-start | bytes 6148
  44.2 7.4 %copy-start.10 = (bf16[512,512]{1,0:T(8,128)(2,1)S(1)}, bf16[512,512]{1,0:T(8,128)(2,1)}, u32[]{:S(2)}) copy-start(bf16[512,512]{1,0:T(8,128)(2,1)} %message_out_ref.1) | copy-start | bytes 1572868
  44.2 7.4 %copy-start.11 = (bf16[512,512]{1,0:T(8,128)(2,1)S(1)}, bf16[512,512]{1,0:T(8,128)(2,1)}, u32[]{:S(2)}) copy-start(bf16[512,512]{1,0:T(8,128)(2,1)} %update_out_ref.1) | copy-start | bytes 1572868
  44.2 7.4 %copy-start.16 = (f32[512]{0:T(512)S(1)}, f32[512]{0:T(512)}, u32[]{:S(2)}) copy-start(f32[512]{0:T(512)} %param.47) | copy-start | bytes 6148

commit v7 on v6

--- a/solution.py
+++ b/solution.py
@@ -86,17 +86,17 @@
     recv_ref,
     feat_ref,
     count_ref,
+    starts,
     table,
-    first_t,
-    second_t,
-    weight_t,
-    grid_column,
-    edge_column,
+    even_rows,
+    odd_rows,
+    hidden_ref,
     total,
     sems,
 ):
     channels, grid_rows = grid_ref.shape
     width = second_ref.shape[1]
+    pieces = width // LANES
     blocks, block_edges = send_ref.shape
     owned = own_ref.shape[0]
     feats = feat_ref.shape[1]
@@ -112,78 +112,113 @@
         (send_weight_hbm, send_weight_ref),
         (grid_bias_hbm, grid_bias_ref),
         (edge_bias_hbm, edge_bias_ref),
+        (send_hbm, send_ref),
         (slot_hbm, slot_ref),
         (feat_weight_hbm, feat_weight_ref),
-        (send_hbm, send_ref),
         (recv_hbm, recv_ref),
         (feat_hbm, feat_ref),
         (count_hbm, count_ref),
+        (send_ref, starts),
     ]
     copies = [
         pltpu.make_async_copy(source, target, sems.at[GRID_STEPS + at])
         for at, (source, target) in enumerate(pairs)
     ]
-    for copy in copies[:5]:
+    copies[0].start()
+    grid_copy(0).start()
+    for copy in copies[1:6]:
         copy.start()
-    for step in range(GRID_STEPS):
+    for step in range(1, GRID_STEPS):
         grid_copy(step).start()
-    for copy in copies[5:]:
+    for copy in copies[6:-1]:
         copy.start()
     copies[0].wait()
-    first_t[...] = (0.5 * first_ref[...].astype(F32)).T.astype(BF16)
-    copies[1].wait()
-    second_t[...] = second_ref[...].T
-    copies[2].wait()
-    weight_t[...] = (0.5 * send_weight_ref[...].astype(F32)).T.astype(BF16)
-    copies[3].wait()
-    grid_column[...] = jnp.broadcast_to(0.5 * grid_bias_ref[...], (LANES, width)).T
-    copies[4].wait()
-    edge_column[...] = jnp.broadcast_to(0.5 * edge_bias_ref[...], (LANES, width)).T
-    wide = lambda ref: jnp.concatenate([ref[...]] * (step_rows // LANES), axis=1)
+    first_ref[...] = first_ref[...] * 0.5
+    for copy in copies[1:6]:
+        copy.wait()
+    send_weight_ref[...] = send_weight_ref[...] * 0.5
+    grid_bias = 0.5 * grid_bias_ref[...]
+    edge_bias = 0.5 * edge_bias_ref[...]
+    senders = send_ref[...]
+    send_ref[...] = (senders // 8) * (8 * pieces) + senders % 8
+    copies[-1].start()
 
     def grid_step(step, carry):
         part = pl.ds(pl.multiple_of(step * step_rows, step_rows), step_rows)
         grid_copy(step).wait()
-        hidden = silu_half(mm(first_t[...], grid_ref[:, part]) + wide(grid_column)).astype(BF16)
-        value = mm(second_t[...], hidden)
-        center = value - jnp.mean(value, axis=0, keepdims=True)
-        spread = jnp.mean(center * center, axis=0, keepdims=True)
-        code = (center * lax.rsqrt(spread + 1e-05)).astype(BF16)
-        table[:, part] = (mm(weight_t[...], code) + wide(edge_column)).astype(BF16)
+        value = grid_ref[:, part].T
+        hidden = silu_half(mm(value, first_ref[...]) + grid_bias).astype(BF16)
+        code = layer_norm(mm(hidden, second_ref[...])).astype(BF16)
+        row = (mm(code, send_weight_ref[...]) + edge_bias).astype(BF16).astype(F32)
+        first = pl.multiple_of(step * (step_rows * pieces), step_rows * pieces)
+        for group in range(step_rows // 8):
+            for piece in range(pieces):
+                at = (group * pieces + piece) * 8
+                table[pl.ds(first + at, 8), :] = row[
+                    group * 8 : group * 8 + 8, piece * LANES : (piece + 1) * LANES
+                ]
         return carry
 
     lax.fori_loop(0, GRID_STEPS, grid_step, 0)
-    for copy in copies[5:]:
+    for copy in copies[6:]:
         copy.wait()
     place = place_ref[0]
     used = count_ref[...]
-    feat_weight = jnp.concatenate(
-        [0.5 * feat_weight_ref[...].astype(F32), jnp.zeros((LANES - feats, width), F32)], axis=0
-    )
-    table[:, grid_rows:] = feat_weight.T.astype(BF16)
+    feat_weight = 0.5 * feat_weight_ref[...].astype(F32)
+    feat_weight = jnp.concatenate([feat_weight, jnp.zeros((8 - feats, width), F32)], axis=0)
+    feat_weight = feat_weight.astype(BF16)
     ids = ids_of_rows(slot_ref[...], (place - 1) * owned, 3 * owned)
-    group = math.gcd(blocks, 4)
-    blank = jnp.zeros((LANES - feats, group * block_edges), F32)
+    group = 2 if blocks % 4 == 0 else 1
+    chunks = blocks // group
+    part_rows = 64
     total[...] = jnp.zeros_like(total)
 
-    def edge_step(step, carry):
-        here = [step * group + b for b in range(group)]
-        senders = jnp.concatenate([send_ref[pl.ds(b, 1), :] for b in here], axis=1)
+    def gather(chunk, edges, target):
+        for edge in edges:
+            start = starts[chunk * group + edge // block_edges, edge % block_edges]
+            target[pl.ds(edge // 8 * (8 * pieces) + edge % 8, pieces, stride=8), :] = table[
+                pl.ds(start, pieces, stride=8), :
+            ]
+
+    def rows_of(source, first, count):
+        return jnp.concatenate(
+            [
+                jnp.concatenate(
+                    [
+                        source[pl.ds((at * pieces + piece) * 8, 8), :]
+                        for at in range(first // 8, (first + count) // 8)
+                    ],
+                    axis=0,
+                )
+                for piece in range(pieces)
+            ],
+            axis=1,
+        )
+
+    def work(chunk, source, target):
+        here = [chunk * group + b for b in range(group)]
         feat = jnp.concatenate([feat_ref[b] for b in here], axis=1)
-        feat = jnp.concatenate([feat, blank], axis=0).astype(BF16)
-        picker = jnp.concatenate([one_hot(senders, grid_rows), feat], axis=0)
-        hidden = silu_half(mm(table[...], picker)).astype(BF16)
+        feat = jnp.concatenate([feat, jnp.zeros((8 - feats, feat.shape[1]), F32)], axis=0)
+        extra = mm(feat.T.astype(BF16), feat_weight)
+        after = jnp.minimum(chunk + 1, chunks - 1)
+        for first in range(0, group * block_edges, part_rows):
+            gather(after, range(first, first + part_rows), target)
+            half = rows_of(source, first, part_rows) + extra[first : first + part_rows]
+            hidden_ref[first : first + part_rows, :] = silu_half(half).astype(BF16)
         receivers = [jnp.where(b < used, recv_ref[pl.ds(b, 1), :], -2) for b in here]
         spread = (ids == jnp.concatenate(receivers, axis=1)).astype(F32).astype(BF16)
-        total[...] += mm_nt(hidden, spread)
+        total[...] += mm(spread, hidden_ref[...])
+
+    def edge_step(step, carry):
+        work(2 * step, even_rows, odd_rows)
+        work(2 * step + 1, odd_rows, even_rows)
         return carry
 
-    lax.fori_loop(0, blocks // group, edge_step, 0)
-    pad = -3 * owned % LANES
-    sums = jnp.concatenate([total[...], jnp.zeros((width, pad), F32)], axis=1).T
-    below, above = sums[:owned].astype(BF16), sums[2 * owned : 3 * owned].astype(BF16)
-    own_ref[...] = sums[owned : 2 * owned]
+    gather(0, range(group * block_edges), even_rows)
+    lax.fori_loop(0, chunks // 2, edge_step, 0)
     odd = place % 2 == 1
+    below, above = total[:owned].astype(BF16), total[2 * owned :].astype(BF16)
+    own_ref[...] = total[owned : 2 * owned]
     cross_ref[...] = jnp.where(odd, above, below)
     chip_ref[...] = jnp.where(odd, below, above)
 
@@ -408,14 +443,13 @@
         [SMEM] + [HBM] * len(operands),
         scratch=[VMEM(value.shape, value.dtype) for value in operands]
         + [
-            pltpu.VMEM((width, grid_rows + LANES), BF16),
-            pltpu.VMEM((width, grid_first.shape[0]), BF16),
-            pltpu.VMEM((width, width), BF16),
-            pltpu.VMEM((width, width), BF16),
-            pltpu.VMEM((width, LANES), F32),
-            pltpu.VMEM((width, LANES), F32),
-            pltpu.VMEM((width, 3 * owned), F32),
-            pltpu.SemaphoreType.DMA((len(operands) - 1 + GRID_STEPS,)),
+            SMEM(g2m_send.shape, I32),
+            VMEM((grid_rows * (width // LANES), LANES), F32),
+            VMEM((2 * g2m_send.shape[1] * (width // LANES), LANES), F32),
+            VMEM((2 * g2m_send.shape[1] * (width // LANES), LANES), F32),
+            VMEM((2 * g2m_send.shape[1], width), BF16),
+            VMEM((3 * owned, width), F32),
+            pltpu.SemaphoreType.DMA((len(operands) + GRID_STEPS,)),
         ],
         flops=10_000_000_000,
         moved=4_000_000,

time: 54 us -> 48.7 us (0.902)
  Pallas kernels: 25.8 us -> 20.5 us
    pallas_call x1, Pallas kernels: 18.3 us -> 13 us  [per_device(): call(edge_kernel, (shape(owned, width, kind=F32), shape(owned, width), sh...]
  transfers between devices with their start and end apart: 4 -> 4, of which waited for: 2 -> 2; matrix products, arithmetic and copies ran while one was open for 0% -> 0% of each run, Pallas kernels for 41% -> 34%
where the time goes in v7:
time: 48.7 us; the launch traced here: 48.4 us
  Pallas kernels  20.5 us (42%)
  starting transfers between devices  18.3 us (38%)
  waiting for transfers between devices  7.23 us (15%)
  local copies, waits for them, and re-layouts  1.41 us (3%)
  between operations  0.93 us (2%)
    pallas_call x1, Pallas kernels, per_device(): call(edge_kernel, (shape(owned, width, kind=F32), shape(owned, width), sh...  13 us
    all_to_all x1, starting transfers between devices, per_device(): lax.all_to_all(jnp.tile(mesh_send, (devices, 1)), 'bulk', 0, 0, tiled=True)  7.39 us
    all_to_all x1, waiting for transfers between devices, per_device(): piece = lax.all_to_all(rows, 'bulk', 0, 0, tiled=True)  7.01 us
    all_to_all x1, starting transfers between devices, per_device(): piece = lax.all_to_all(rows, 'bulk', 0, 0, tiled=True)  6.8 us
    ppermute x1, starting transfers between devices, per_device(): from_chip = lax.ppermute(chip, 'bulk', both(within))  3.35 us
    pallas_call x1, Pallas kernels, per_device(): call(functools.partial(wanted_kernel, owned), shape(edges, places), [VMEM...  2.53 us
    pallas_call x1, Pallas kernels, per_device(): call(message_kernel, shape(owned, width), [VMEM] * 12, flops=1000000000,...  2.04 us
    pallas_call x1, Pallas kernels, per_device(): call(node_kernel, (shape(owned, width), shape(places, width)), [VMEM] * 1...  1.87 us
  transfers between devices with their start and end apart: 4, of which 2 were waited for; matrix products, arithmetic and copies ran while one was open for 0% of the time, Pallas kernels for 34%

profile of v7, /device:TPU:0, one launch (start us, length us, event | category | flops | bytes accessed | tf_op | source)
XLA Modules:
  0.0 48.4 jit_solution(18161905666405706327)
XLA Ops:
  0.0 1.3 %tile.2 = s32[16,4,128]{2,1,0:T(4,128)} broadcast(s32[4,128]{1,0:T(4,128)} %send_ref), dimensions={1,2} | broadcast | bytes 34816 | tf_op jit(solution)/shard_map/tile | solution.py:425
  1.3 7.4 %all-to-all-start = ((s32[16,4,128]{2,1,0:T(4,128)}), s32[16,4,128]{2,1,0:T(4,128)S(1)}, u32[]{:S(2)}, u32[]{:S(2)}) async-start(s32[16,4,128]{2,1,0:T(4,128)} %tile.2), calls=%async_computation | async-start | bytes 65536 | tf_op jit(solution)/shard_map/all_to_all | solution.py:425
  9.3 0.0 copy-start.12
  9.4 0.0 copy-start.2
  9.4 0.0 copy-start.3
  9.4 0.0 copy-start.4
  9.4 0.0 copy-start.6
  9.4 0.0 copy-start.7
  9.4 13.0 %shard_map.262 = (f32[64,512]{1,0:T(8,128)S(1)}, bf16[64,512]{1,0:T(8,128)(2,1)S(1)}, bf16[64,512]{1,0:T(8,128)(2,1)S(1)}) custom-call(s32[1]{0:T(128)} %bitcast.1.place_ref, bf16[474,512]{1,0:T(8,128)(2,1)} %first_hbm.1, bf16[474,2048]{1,0:T(8,128)(2,1)} %bitcast.26, bf16[512,512]{1,0:T(8,128)(2,1)} %second_hbm.1, bf16[512,512]{1,0:T(8,128)(2,1)} %send_weight_hbm.1, ...), custom_call_target="tpu_custom_call" | custom-call | flops 10000000000 | bytes 4000000 | tf_op jit(solution)/shard_map/pallas_call | solution.py:440
  22.5 0.0 copy-start
  22.5 0.0 copy-start.1
  22.5 0.8 %collective-permute-start = (bf16[64,512]{1,0:T(8,128)(2,1)S(1)}, bf16[64,512]{1,0:T(8,128)(2,1)S(1)}, u32[]{:S(2)}, u32[]{:S(2)}) collective-permute-start(bf16[64,512]{1,0:T(8,128)(2,1)S(1)} %get-tuple-element.18), channel_id=1, source_target_pairs={{1,2},{3,4},{5,6},{7,8},{9,10},{11,12},{13,14},{2,1},{4,3},{6,5},{... | collective-permute-start | bytes 196616 | tf_op jit(solution)/shard_map/ppermute | solution.py:462
  23.3 3.3 %collective-permute-start.1 = (bf16[64,512]{1,0:T(8,128)(2,1)S(1)}, bf16[64,512]{1,0:T(8,128)(2,1)S(1)}, u32[]{:S(2)}, u32[]{:S(2)}) collective-permute-start(bf16[64,512]{1,0:T(8,128)(2,1)S(1)} %get-tuple-element.19), channel_id=1, source_target_pairs={{0,1},{2,3},{4,5},{6,7},{8,9},{10,11},{12,13},{14,15},{1,0},{3,2},... | collective-permute-start | bytes 196616 | tf_op jit(solution)/shard_map/ppermute | solution.py:463
  26.6 0.0 all-to-all-done
  26.6 0.0 copy-done.12
  26.6 0.7 %shard_map.263.supply_ref = bf16[256,64]{1,0:T(8,128)(2,1)S(1)} custom-call(s32[1]{0:T(128)} %bitcast.1.place_ref, s32[1,1024]{1,0:T(1,128)S(1)} %bitcast.20, s32[64,128]{1,0:T(8,128)S(1)} %bitcast.16), custom_call_target="tpu_custom_call" | custom-call | flops 500000000 | bytes 500000 | tf_op jit(solution)/shard_map/pallas_call | solution.py:464
  27.3 0.0 copy-start.5
  27.3 0.0 collective-permute-done.from_cross_ref
  27.3 0.2 collective-permute-done.1.from_chip_ref
  27.5 0.0 copy-done.2
  27.5 0.0 copy-done.3
  27.5 0.0 copy-done.4
  27.5 0.0 copy-done.6
  27.6 0.0 copy-done.7
  27.6 0.0 copy-done
  27.6 0.0 copy-done.1
  27.6 1.9 %shard_map.264 = (bf16[64,512]{1,0:T(8,128)(2,1)S(1)}, bf16[256,512]{1,0:T(8,128)(2,1)}) custom-call(f32[64,512]{1,0:T(8,128)S(1)} %get-tuple-element.17.own_ref, bf16[64,512]{1,0:T(8,128)(2,1)S(1)} %collective-permute-done.from_cross_ref, bf16[64,512]{1,0:T(8,128)(2,1)S(1)} %collective-permute-done.1.from_chip_ref, bf16[64,512]{1,0:T(8,128)(2,1)S(1)} %copy-done.4, ...), custom_call_target="tpu_custom_call" | custom-call | flops 500000000 | bytes 4000000 | tf_op jit(solution)/shard_map/pallas_call | solution.py:471
  29.5 6.8 %all-to-all-start.1 = ((bf16[16,16,512]{2,1,0:T(8,128)(2,1)}), bf16[16,16,512]{2,1,0:T(8,128)(2,1)S(1)}, u32[]{:S(2)}, u32[]{:S(2)}) async-start(bf16[16,16,512]{2,1,0:T(8,128)(2,1)} %bitcast.9), calls=%async_computation.1 | async-start | bytes 524288 | tf_op jit(solution)/shard_map/all_to_all | solution.py:490
  36.3 0.0 copy-start.8
  36.3 0.0 copy-start.9
  36.3 0.0 copy-start.13
  36.3 0.0 copy-start.14
  36.3 0.0 copy-start.15
  36.3 0.0 copy-done.5
  36.3 2.5 %shard_map.265.wanted_ref = bf16[512,256]{1,0:T(8,128)(2,1)S(1)} custom-call(s32[1,1024]{1,0:T(1,128)S(1)} %bitcast.21, s32[4,128]{1,0:T(4,128)S(1)} %copy-done.5), custom_call_target="tpu_custom_call" | custom-call | flops 1000000000 | bytes 500000 | tf_op jit(solution)/shard_map/pallas_call | solution.py:492
  38.9 0.0 copy-start.10
  38.9 0.0 copy-start.11
  38.9 0.0 copy-start.16
  38.9 0.0 copy-done.8
  38.9 0.0 copy-done.9
  38.9 0.0 copy-done.13
  38.9 0.0 copy-done.14
  38.9 0.0 copy-done.15
  39.0 0.3 shard_map.266
  39.3 7.0 %all-to-all-done.1 = bf16[16,16,512]{2,1,0:T(8,128)(2,1)S(1)} async-done(((bf16[16,16,512]{2,1,0:T(8,128)(2,1)}), bf16[16,16,512]{2,1,0:T(8,128)(2,1)S(1)}, u32[]{:S(2)}, u32[]{:S(2)}) %all-to-all-start.1) | async-done | bytes 262176 | tf_op jit(solution)/shard_map/all_to_all | solution.py:490
  46.3 0.0 copy-done.10
  46.3 0.0 copy-done.11
  46.3 0.0 copy-done.16
  46.3 2.0 %shard_map.267 = bf16[64,512]{1,0:T(8,128)(2,1)} custom-call(bf16[512,256]{1,0:T(8,128)(2,1)S(1)} %shard_map.265.wanted_ref, bf16[256,512]{1,0:T(8,128)(2,1)S(1)} %bitcast.15, bf16[64,512]{1,0:T(8,128)(2,1)S(1)} %get-tuple-element.24.incoming_ref, bf16[512,64]{1,0:T(8,128)(2,1)S(1)} %get-tuple-element.25.pick_ref, ...), custom_call_target="tpu_custom_call" | custom-call | flops 1000000000 | bytes 4000000 | tf_op jit(solution)/shard_map/pallas_call | solution.py:521
Async XLA Ops:
  1.3 25.3 %all-to-all-start = ((s32[16,4,128]{2,1,0:T(4,128)}), s32[16,4,128]{2,1,0:T(4,128)S(1)}, u32[]{:S(2)}, u32[]{:S(2)}) async-start(s32[16,4,128]{2,1,0:T(4,128)} %tile.2), calls=%async_computation | async-start | bytes 65536 | tf_op jit(solution)/shard_map/all_to_all | solution.py:425
  9.3 17.3 %copy-start.12 = (s32[1024]{0:T(1024)S(1)}, s32[1024]{0:T(1024)}, u32[]{:S(2)}) copy-start(s32[1024]{0:T(1024)} %param.53) | copy-start | bytes 12292
  9.4 18.2 %copy-start.2 = (bf16[512,512]{1,0:T(8,128)(2,1)S(1)}, bf16[512,512]{1,0:T(8,128)(2,1)}, u32[]{:S(2)}) copy-start(bf16[512,512]{1,0:T(8,128)(2,1)} %node_out_ref.1) | copy-start | bytes 1572868
  9.4 18.2 %copy-start.3 = (bf16[512,512]{1,0:T(8,128)(2,1)S(1)}, bf16[512,512]{1,0:T(8,128)(2,1)}, u32[]{:S(2)}) copy-start(bf16[512,512]{1,0:T(8,128)(2,1)} %mesh_sender_ref.1) | copy-start | bytes 1572868
  9.4 18.2 %copy-start.4 = (bf16[64,512]{1,0:T(8,128)(2,1)S(1)}, bf16[64,512]{1,0:T(8,128)(2,1)}, u32[]{:S(2)}) copy-start(bf16[64,512]{1,0:T(8,128)(2,1)} %latent_ref.1) | copy-start | bytes 196612
  9.4 18.2 %copy-start.6 = (f32[512]{0:T(512)S(1)}, f32[512]{0:T(512)}, u32[]{:S(2)}) copy-start(f32[512]{0:T(512)} %param.37) | copy-start | bytes 6148
  9.4 18.1 %copy-start.7 = (f32[512]{0:T(512)S(1)}, f32[512]{0:T(512)}, u32[]{:S(2)}) copy-start(f32[512]{0:T(512)} %param.39) | copy-start | bytes 6148
  22.5 5.1 %copy-start = (bf16[1024,512]{1,0:T(8,128)(2,1)S(1)}, bf16[1024,512]{1,0:T(8,128)(2,1)}, u32[]{:S(2)}) copy-start(bf16[1024,512]{1,0:T(8,128)(2,1)} %node_input_ref.1) | copy-start | bytes 3145732
  22.5 5.1 %copy-start.1 = (bf16[512,512]{1,0:T(8,128)(2,1)S(1)}, bf16[512,512]{1,0:T(8,128)(2,1)}, u32[]{:S(2)}) copy-start(bf16[512,512]{1,0:T(8,128)(2,1)} %edge_out_ref.1) | copy-start | bytes 1572868
  22.5 4.8 %collective-permute-start = (bf16[64,512]{1,0:T(8,128)(2,1)S(1)}, bf16[64,512]{1,0:T(8,128)(2,1)S(1)}, u32[]{:S(2)}, u32[]{:S(2)}) collective-permute-start(bf16[64,512]{1,0:T(8,128)(2,1)S(1)} %get-tuple-element.18), channel_id=1, source_target_pairs={{1,2},{3,4},{5,6},{7,8},{9,10},{11,12},{13,14},{2,1},{4,3},{6,5},{... | collective-permute-start | bytes 196616 | tf_op jit(solution)/shard_map/ppermute | solution.py:462
  23.3 4.2 %collective-permute-start.1 = (bf16[64,512]{1,0:T(8,128)(2,1)S(1)}, bf16[64,512]{1,0:T(8,128)(2,1)S(1)}, u32[]{:S(2)}, u32[]{:S(2)}) collective-permute-start(bf16[64,512]{1,0:T(8,128)(2,1)S(1)} %get-tuple-element.19), channel_id=1, source_target_pairs={{0,1},{2,3},{4,5},{6,7},{8,9},{10,11},{12,13},{14,15},{1,0},{3,2},... | collective-permute-start | bytes 196616 | tf_op jit(solution)/shard_map/ppermute | solution.py:463
  27.3 9.0 %copy-start.5 = (s32[4,128]{1,0:T(4,128)S(1)}, s32[4,128]{1,0:T(4,128)}, u32[]{:S(2)}) copy-start(s32[4,128]{1,0:T(4,128)} %send_ref) | copy-start | bytes 6148
  29.5 16.9 %all-to-all-start.1 = ((bf16[16,16,512]{2,1,0:T(8,128)(2,1)}), bf16[16,16,512]{2,1,0:T(8,128)(2,1)S(1)}, u32[]{:S(2)}, u32[]{:S(2)}) async-start(bf16[16,16,512]{2,1,0:T(8,128)(2,1)} %bitcast.9), calls=%async_computation.1 | async-start | bytes 524288 | tf_op jit(solution)/shard_map/all_to_all | solution.py:490
  36.3 2.6 %copy-start.8 = (bf16[1024,512]{1,0:T(8,128)(2,1)S(1)}, bf16[1024,512]{1,0:T(8,128)(2,1)}, u32[]{:S(2)}) copy-start(bf16[1024,512]{1,0:T(8,128)(2,1)} %update_input_ref.3) | copy-start | bytes 3145732
  36.3 2.6 %copy-start.9 = (bf16[512,512]{1,0:T(8,128)(2,1)S(1)}, bf16[512,512]{1,0:T(8,128)(2,1)}, u32[]{:S(2)}) copy-start(bf16[512,512]{1,0:T(8,128)(2,1)} %mesh_receiver_ref.1) | copy-start | bytes 1572868
  36.3 2.6 %copy-start.13 = (s32[4,128]{1,0:T(4,128)S(1)}, s32[4,128]{1,0:T(4,128)}, u32[]{:S(2)}) copy-start(s32[4,128]{1,0:T(4,128)} %recv_ref.1) | copy-start | bytes 6148
  36.3 2.6 %copy-start.14 = (f32[512]{0:T(512)S(1)}, f32[512]{0:T(512)}, u32[]{:S(2)}) copy-start(f32[512]{0:T(512)} %param.42) | copy-start | bytes 6148
  36.3 2.6 %copy-start.15 = (f32[512]{0:T(512)S(1)}, f32[512]{0:T(512)}, u32[]{:S(2)}) copy-start(f32[512]{0:T(512)} %param.45) | copy-start | bytes 6148
  38.9 7.4 %copy-start.10 = (bf16[512,512]{1,0:T(8,128)(2,1)S(1)}, bf16[512,512]{1,0:T(8,128)(2,1)}, u32[]{:S(2)}) copy-start(bf16[512,512]{1,0:T(8,128)(2,1)} %message_out_ref.1) | copy-start | bytes 1572868
  38.9 7.4 %copy-start.11 = (bf16[512,512]{1,0:T(8,128)(2,1)S(1)}, bf16[512,512]{1,0:T(8,128)(2,1)}, u32[]{:S(2)}) copy-start(bf16[512,512]{1,0:T(8,128)(2,1)} %update_out_ref.1) | copy-start | bytes 1572868
  38.9 7.4 %copy-start.16 = (f32[512]{0:T(512)S(1)}, f32[512]{0:T(512)}, u32[]{:S(2)}) copy-start(f32[512]{0:T(512)} %param.47) | copy-start | bytes 6148

commit v8 on v7

--- a/solution.py
+++ b/solution.py
@@ -91,6 +91,7 @@
     even_rows,
     odd_rows,
     hidden_ref,
+    ids_ref,
     total,
     sems,
 ):
@@ -124,54 +125,67 @@
         pltpu.make_async_copy(source, target, sems.at[GRID_STEPS + at])
         for at, (source, target) in enumerate(pairs)
     ]
-    copies[0].start()
+    first_copy, second_copy, send_weight_copy, grid_bias_copy, edge_bias_copy, send_copy = copies[:6]
+    slot_copy, starts_copy = copies[6], copies[-1]
+    first_copy.start()
     grid_copy(0).start()
-    for copy in copies[1:6]:
+    for copy in copies[1:-1]:
         copy.start()
     for step in range(1, GRID_STEPS):
         grid_copy(step).start()
-    for copy in copies[6:-1]:
-        copy.start()
-    copies[0].wait()
+    send_copy.wait()
+    senders = send_ref[...]
+    send_ref[...] = (senders // 8) * (8 * pieces) + senders % 8
+    starts_copy.start()
+    slot_copy.wait()
+    place = place_ref[0]
+    ids_ref[...] = jnp.broadcast_to(
+        ids_of_rows(slot_ref[...], (place - 1) * owned, 3 * owned), ids_ref.shape
+    )
+    total[...] = jnp.zeros_like(total)
+    first_copy.wait()
     first_ref[...] = first_ref[...] * 0.5
-    for copy in copies[1:6]:
-        copy.wait()
+    second_copy.wait()
+    send_weight_copy.wait()
     send_weight_ref[...] = send_weight_ref[...] * 0.5
+    grid_bias_copy.wait()
+    edge_bias_copy.wait()
     grid_bias = 0.5 * grid_bias_ref[...]
     edge_bias = 0.5 * edge_bias_ref[...]
-    senders = send_ref[...]
-    send_ref[...] = (senders // 8) * (8 * pieces) + senders % 8
-    copies[-1].start()
+    half_rows = step_rows // 2
 
     def grid_step(step, carry):
-        part = pl.ds(pl.multiple_of(step * step_rows, step_rows), step_rows)
         grid_copy(step).wait()
-        value = grid_ref[:, part].T
-        hidden = silu_half(mm(value, first_ref[...]) + grid_bias).astype(BF16)
-        code = layer_norm(mm(hidden, second_ref[...])).astype(BF16)
-        row = (mm(code, send_weight_ref[...]) + edge_bias).astype(BF16).astype(F32)
-        first = pl.multiple_of(step * (step_rows * pieces), step_rows * pieces)
-        for group in range(step_rows // 8):
-            for piece in range(pieces):
-                at = (group * pieces + piece) * 8
-                table[pl.ds(first + at, 8), :] = row[
-                    group * 8 : group * 8 + 8, piece * LANES : (piece + 1) * LANES
-                ]
+        first = pl.multiple_of(step * step_rows, step_rows)
+        values = [
+            mm(grid_ref[:, pl.ds(first + at, half_rows)].T, first_ref[...])
+            for at in (0, half_rows)
+        ]
+        values = [silu_half(value + grid_bias).astype(BF16) for value in values]
+        values = [mm(value, second_ref[...]) for value in values]
+        values = [layer_norm(value).astype(BF16) for value in values]
+        values = [mm(value, send_weight_ref[...]) for value in values]
+        for half, value in enumerate(values):
+            row = (value + edge_bias).astype(BF16).astype(F32)
+            base = pl.multiple_of((first + half * half_rows) * pieces, half_rows * pieces)
+            for group in range(half_rows // 8):
+                for piece in range(pieces):
+                    at = (group * pieces + piece) * 8
+                    table[pl.ds(base + at, 8), :] = row[
+                        group * 8 : group * 8 + 8, piece * LANES : (piece + 1) * LANES
+                    ]
         return carry
 
     lax.fori_loop(0, GRID_STEPS, grid_step, 0)
-    for copy in copies[6:]:
+    for copy in copies[7:]:
         copy.wait()
-    place = place_ref[0]
     used = count_ref[...]
     feat_weight = 0.5 * feat_weight_ref[...].astype(F32)
     feat_weight = jnp.concatenate([feat_weight, jnp.zeros((8 - feats, width), F32)], axis=0)
     feat_weight = feat_weight.astype(BF16)
-    ids = ids_of_rows(slot_ref[...], (place - 1) * owned, 3 * owned)
     group = 2 if blocks % 4 == 0 else 1
     chunks = blocks // group
     part_rows = 64
-    total[...] = jnp.zeros_like(total)
 
     def gather(chunk, edges, target):
         for edge in edges:
@@ -206,7 +220,8 @@
             half = rows_of(source, first, part_rows) + extra[first : first + part_rows]
             hidden_ref[first : first + part_rows, :] = silu_half(half).astype(BF16)
         receivers = [jnp.where(b < used, recv_ref[pl.ds(b, 1), :], -2) for b in here]
-        spread = (ids == jnp.concatenate(receivers, axis=1)).astype(F32).astype(BF16)
+        spread = jnp.concatenate([(ids_ref[...] == row).astype(F32) for row in receivers], axis=1)
+        spread = spread.astype(BF16)
         total[...] += mm(spread, hidden_ref[...])
 
     def edge_step(step, carry):
@@ -317,8 +332,7 @@
     update_bias_ref,
     incoming_ref,
     pick_ref,
-    high_ref,
-    low_ref,
+    parts_ref,
     upper_ref,
 ):
     owned, width = encoded_ref.shape
@@ -327,13 +341,14 @@
     incoming = jnp.concatenate(
         [(ids == recv_ref[b : b + 1, :]).astype(F32) for b in range(blocks)], axis=1
     )
-    pick_ref[...] = incoming.T.astype(BF16)
+    pick = incoming.T.astype(BF16)
+    pick_ref[...] = jnp.concatenate([pick, pick], axis=1)
     incoming_ref[...] = incoming.astype(BF16)
     encoded = encoded_ref[...]
     receiver = mm(encoded, mesh_receiver_ref[...]) + message_bias_ref[...]
     high = receiver.astype(BF16)
-    high_ref[...] = high
-    low_ref[...] = (receiver - high.astype(F32)).astype(BF16)
+    parts_ref[:owned, :] = high
+    parts_ref[owned:, :] = (receiver - high.astype(F32)).astype(BF16)
     upper_ref[...] = mm(encoded, update_input_ref[:width]) + update_bias_ref[...]
 
 
@@ -342,8 +357,7 @@
     piece_ref,
     incoming_ref,
     pick_ref,
-    high_ref,
-    low_ref,
+    parts_ref,
     upper_ref,
     encoded_ref,
     message_out_ref,
@@ -353,8 +367,9 @@
     out_ref,
 ):
     width = encoded_ref.shape[1]
-    receiver = mm(pick_ref[...], high_ref[...]) + mm(pick_ref[...], low_ref[...])
-    message = silu(mm(wanted_ref[...], piece_ref[...]) + receiver).astype(BF16)
+    chosen = jnp.concatenate([wanted_ref[...], pick_ref[...]], axis=1)
+    codes = jnp.concatenate([piece_ref[...], parts_ref[...]], axis=0)
+    message = silu(mm(chosen, codes)).astype(BF16)
     message_sum = mm(incoming_ref[...], message).astype(BF16)
     update = mm(message_sum, message_out_ref[...]).astype(BF16)
     hidden = silu(upper_ref[...] + mm(update, update_input_ref[width:])).astype(BF16)
@@ -448,6 +463,7 @@
             VMEM((2 * g2m_send.shape[1] * (width // LANES), LANES), F32),
             VMEM((2 * g2m_send.shape[1] * (width // LANES), LANES), F32),
             VMEM((2 * g2m_send.shape[1], width), BF16),
+            VMEM((3 * owned, LANES), I32),
             VMEM((3 * owned, width), F32),
             pltpu.SemaphoreType.DMA((len(operands) + GRID_STEPS,)),
         ],
@@ -487,6 +503,7 @@
         mesh_sender,
         supply,
     )
+    rows = pltpu.with_memory_space_constraint(rows, VMEM)
     piece = lax.all_to_all(rows, "bulk", 0, 0, tiled=True)
     mesh_send, _ = lax.optimization_barrier((mesh_send, encoded))
     wanted = call(
@@ -496,13 +513,12 @@
         flops=1_000_000_000,
         moved=500_000,
     )(slot, mesh_send)
-    incoming, pick, high, low, upper = call(
+    incoming, pick, parts, upper = call(
         receiver_kernel,
         (
             shape(owned, edges),
-            shape(edges, owned),
-            shape(owned, width),
-            shape(owned, width),
+            shape(edges, 2 * owned),
+            shape(2 * owned, width),
             shape(owned, width, kind=F32),
         ),
         [SMEM] + [VMEM] * 7,
@@ -521,7 +537,7 @@
     return call(
         message_kernel,
         shape(owned, width),
-        [VMEM] * 12,
+        [VMEM] * 11,
         flops=1_000_000_000,
         moved=4_000_000,
     )(
@@ -529,8 +545,7 @@
         piece,
         incoming,
         pick,
-        high,
-        low,
+        parts,
         upper,
         encoded,
         message_out,

time: 48.7 us -> 48.8 us (level)
  transfers between devices with their start and end apart: 4 -> 4, of which waited for: 2 -> 2; matrix products, arithmetic and copies ran while one was open for 0% -> 0% of each run, Pallas kernels for 34% -> 35%
where the time goes in v8:
time: 48.8 us; the launch traced here: 48.4 us
  Pallas kernels  20.6 us (42%)
  starting transfers between devices  18.3 us (38%)
  waiting for transfers between devices  7.16 us (15%)
  local copies, waits for them, and re-layouts  1.41 us (3%)
  between operations  0.93 us (2%)
    pallas_call x1, Pallas kernels, per_device(): call(edge_kernel, (shape(owned, width, kind=F32), shape(owned, width), sh...  13.2 us
    all_to_all x1, starting transfers between devices, per_device(): lax.all_to_all(jnp.tile(mesh_send, (devices, 1)), 'bulk', 0, 0, tiled=True)  7.39 us
    all_to_all x1, waiting for transfers between devices, per_device(): piece = lax.all_to_all(rows, 'bulk', 0, 0, tiled=True)  6.94 us
    all_to_all x1, starting transfers between devices, per_device(): piece = lax.all_to_all(rows, 'bulk', 0, 0, tiled=True)  6.78 us
    ppermute x1, starting transfers between devices, per_device(): from_chip = lax.ppermute(chip, 'bulk', both(within))  3.37 us
    pallas_call x1, Pallas kernels, per_device(): call(functools.partial(wanted_kernel, owned), shape(edges, places), [VMEM...  2.53 us
    pallas_call x1, Pallas kernels, per_device(): call(message_kernel, shape(owned, width), [VMEM] * 11, flops=1000000000,...  1.94 us
    pallas_call x1, Pallas kernels, per_device(): call(node_kernel, (shape(owned, width), shape(places, width)), [VMEM] * 1...  1.87 us
  transfers between devices with their start and end apart: 4, of which 2 were waited for; matrix products, arithmetic and copies ran while one was open for 0% of the time, Pallas kernels for 35%

profile of v8, /device:TPU:0, one launch (start us, length us, event | category | flops | bytes accessed | tf_op | source)
XLA Modules:
  0.0 48.4 jit_solution(3821947366484407924)
XLA Ops:
  0.0 1.3 %tile.2 = s32[16,4,128]{2,1,0:T(4,128)} broadcast(s32[4,128]{1,0:T(4,128)} %send_ref), dimensions={1,2} | broadcast | bytes 34816 | tf_op jit(solution)/shard_map/tile | solution.py:440
  1.3 7.4 %all-to-all-start = ((s32[16,4,128]{2,1,0:T(4,128)}), s32[16,4,128]{2,1,0:T(4,128)S(1)}, u32[]{:S(2)}, u32[]{:S(2)}) async-start(s32[16,4,128]{2,1,0:T(4,128)} %tile.2), calls=%async_computation | async-start | bytes 65536 | tf_op jit(solution)/shard_map/all_to_all | solution.py:440
  9.3 0.0 copy-start.12
  9.4 0.0 copy-start.2
  9.4 0.0 copy-start.3
  9.4 0.0 copy-start.4
  9.4 0.0 copy-start.6
  9.4 0.0 copy-start.7
  9.4 13.2 %shard_map.262 = (f32[64,512]{1,0:T(8,128)S(1)}, bf16[64,512]{1,0:T(8,128)(2,1)S(1)}, bf16[64,512]{1,0:T(8,128)(2,1)S(1)}) custom-call(s32[1]{0:T(128)} %bitcast.1.place_ref, bf16[474,512]{1,0:T(8,128)(2,1)} %first_hbm.1, bf16[474,2048]{1,0:T(8,128)(2,1)} %bitcast.26, bf16[512,512]{1,0:T(8,128)(2,1)} %second_hbm.1, bf16[512,512]{1,0:T(8,128)(2,1)} %send_weight_hbm.1, ...), custom_call_target="tpu_custom_call" | custom-call | flops 10000000000 | bytes 4000000 | tf_op jit(solution)/shard_map/pallas_call | solution.py:455
  22.6 0.0 copy-start
  22.7 0.0 copy-start.1
  22.7 0.8 %collective-permute-start = (bf16[64,512]{1,0:T(8,128)(2,1)S(1)}, bf16[64,512]{1,0:T(8,128)(2,1)S(1)}, u32[]{:S(2)}, u32[]{:S(2)}) collective-permute-start(bf16[64,512]{1,0:T(8,128)(2,1)S(1)} %get-tuple-element.17), channel_id=1, source_target_pairs={{1,2},{3,4},{5,6},{7,8},{9,10},{11,12},{13,14},{2,1},{4,3},{6,5},{... | collective-permute-start | bytes 196616 | tf_op jit(solution)/shard_map/ppermute | solution.py:478
  23.5 3.4 %collective-permute-start.1 = (bf16[64,512]{1,0:T(8,128)(2,1)S(1)}, bf16[64,512]{1,0:T(8,128)(2,1)S(1)}, u32[]{:S(2)}, u32[]{:S(2)}) collective-permute-start(bf16[64,512]{1,0:T(8,128)(2,1)S(1)} %get-tuple-element.18), channel_id=1, source_target_pairs={{0,1},{2,3},{4,5},{6,7},{8,9},{10,11},{12,13},{14,15},{1,0},{3,2},... | collective-permute-start | bytes 196616 | tf_op jit(solution)/shard_map/ppermute | solution.py:479
  26.8 0.0 all-to-all-done
  26.8 0.0 copy-done.12
  26.8 0.7 %shard_map.263.supply_ref = bf16[256,64]{1,0:T(8,128)(2,1)S(1)} custom-call(s32[1]{0:T(128)} %bitcast.1.place_ref, s32[1,1024]{1,0:T(1,128)S(1)} %bitcast.20, s32[64,128]{1,0:T(8,128)S(1)} %bitcast.16), custom_call_target="tpu_custom_call" | custom-call | flops 500000000 | bytes 500000 | tf_op jit(solution)/shard_map/pallas_call | solution.py:480
  27.5 0.0 copy-start.5
  27.5 0.0 collective-permute-done.from_cross_ref
  27.5 0.2 collective-permute-done.1.from_chip_ref
  27.7 0.0 copy-done.2
  27.7 0.0 copy-done.3
  27.8 0.0 copy-done.4
  27.8 0.0 copy-done.6
  27.8 0.0 copy-done.7
  27.8 0.0 copy-done
  27.8 0.0 copy-done.1
  27.8 1.9 %shard_map.264 = (bf16[64,512]{1,0:T(8,128)(2,1)S(1)}, bf16[256,512]{1,0:T(8,128)(2,1)}) custom-call(f32[64,512]{1,0:T(8,128)S(1)} %get-tuple-element.16.own_ref, bf16[64,512]{1,0:T(8,128)(2,1)S(1)} %collective-permute-done.from_cross_ref, bf16[64,512]{1,0:T(8,128)(2,1)S(1)} %collective-permute-done.1.from_chip_ref, bf16[64,512]{1,0:T(8,128)(2,1)S(1)} %copy-done.4, ...), custom_call_target="tpu_custom_call" | custom-call | flops 500000000 | bytes 4000000 | tf_op jit(solution)/shard_map/pallas_call | solution.py:487
  29.7 6.8 %all-to-all-start.1 = ((bf16[16,16,512]{2,1,0:T(8,128)(2,1)}), bf16[16,16,512]{2,1,0:T(8,128)(2,1)S(1)}, u32[]{:S(2)}, u32[]{:S(2)}) async-start(bf16[16,16,512]{2,1,0:T(8,128)(2,1)} %bitcast.9), calls=%async_computation.1 | async-start | bytes 524288 | tf_op jit(solution)/shard_map/all_to_all | solution.py:507
  36.4 0.0 copy-start.8
  36.5 0.0 copy-start.9
  36.5 0.0 copy-start.13
  36.5 0.0 copy-start.14
  36.5 0.0 copy-start.15
  36.5 0.0 copy-done.5
  36.5 2.5 %shard_map.265.wanted_ref = bf16[512,256]{1,0:T(8,128)(2,1)S(1)} custom-call(s32[1,1024]{1,0:T(1,128)S(1)} %bitcast.21, s32[4,128]{1,0:T(4,128)S(1)} %copy-done.5), custom_call_target="tpu_custom_call" | custom-call | flops 1000000000 | bytes 500000 | tf_op jit(solution)/shard_map/pallas_call | solution.py:509
  39.1 0.0 copy-start.10
  39.1 0.0 copy-start.11
  39.1 0.0 copy-start.16
  39.1 0.0 copy-done.8
  39.1 0.0 copy-done.9
  39.1 0.0 copy-done.13
  39.1 0.0 copy-done.14
  39.1 0.0 copy-done.15
  39.1 0.4 shard_map.266
  39.6 6.9 %all-to-all-done.1 = bf16[16,16,512]{2,1,0:T(8,128)(2,1)S(1)} async-done(((bf16[16,16,512]{2,1,0:T(8,128)(2,1)}), bf16[16,16,512]{2,1,0:T(8,128)(2,1)S(1)}, u32[]{:S(2)}, u32[]{:S(2)}) %all-to-all-start.1) | async-done | bytes 262176 | tf_op jit(solution)/shard_map/all_to_all | solution.py:507
  46.5 0.0 copy-done.10
  46.5 0.0 copy-done.11
  46.5 0.0 copy-done.16
  46.5 1.9 %shard_map.267 = bf16[64,512]{1,0:T(8,128)(2,1)} custom-call(bf16[512,256]{1,0:T(8,128)(2,1)S(1)} %shard_map.265.wanted_ref, bf16[256,512]{1,0:T(8,128)(2,1)S(1)} %bitcast.15, bf16[64,512]{1,0:T(8,128)(2,1)S(1)} %get-tuple-element.23.incoming_ref, bf16[512,128]{1,0:T(8,128)(2,1)S(1)} %get-tuple-element.24.pick_ref, ...), custom_call_target="tpu_custom_call" | custom-call | flops 1000000000 | bytes 4000000 | tf_op jit(solution)/shard_map/pallas_call | solution.py:537
Async XLA Ops:
  1.3 25.5 %all-to-all-start = ((s32[16,4,128]{2,1,0:T(4,128)}), s32[16,4,128]{2,1,0:T(4,128)S(1)}, u32[]{:S(2)}, u32[]{:S(2)}) async-start(s32[16,4,128]{2,1,0:T(4,128)} %tile.2), calls=%async_computation | async-start | bytes 65536 | tf_op jit(solution)/shard_map/all_to_all | solution.py:440
  9.3 17.5 %copy-start.12 = (s32[1024]{0:T(1024)S(1)}, s32[1024]{0:T(1024)}, u32[]{:S(2)}) copy-start(s32[1024]{0:T(1024)} %param.53) | copy-start | bytes 12292
  9.4 18.4 %copy-start.2 = (bf16[512,512]{1,0:T(8,128)(2,1)S(1)}, bf16[512,512]{1,0:T(8,128)(2,1)}, u32[]{:S(2)}) copy-start(bf16[512,512]{1,0:T(8,128)(2,1)} %node_out_ref.1) | copy-start | bytes 1572868
  9.4 18.4 %copy-start.3 = (bf16[512,512]{1,0:T(8,128)(2,1)S(1)}, bf16[512,512]{1,0:T(8,128)(2,1)}, u32[]{:S(2)}) copy-start(bf16[512,512]{1,0:T(8,128)(2,1)} %mesh_sender_ref.1) | copy-start | bytes 1572868
  9.4 18.4 %copy-start.4 = (bf16[64,512]{1,0:T(8,128)(2,1)S(1)}, bf16[64,512]{1,0:T(8,128)(2,1)}, u32[]{:S(2)}) copy-start(bf16[64,512]{1,0:T(8,128)(2,1)} %latent_ref.1) | copy-start | bytes 196612
  9.4 18.4 %copy-start.6 = (f32[512]{0:T(512)S(1)}, f32[512]{0:T(512)}, u32[]{:S(2)}) copy-start(f32[512]{0:T(512)} %param.37) | copy-start | bytes 6148
  9.4 18.4 %copy-start.7 = (f32[512]{0:T(512)S(1)}, f32[512]{0:T(512)}, u32[]{:S(2)}) copy-start(f32[512]{0:T(512)} %param.39) | copy-start | bytes 6148
  22.6 5.1 %copy-start = (bf16[1024,512]{1,0:T(8,128)(2,1)S(1)}, bf16[1024,512]{1,0:T(8,128)(2,1)}, u32[]{:S(2)}) copy-start(bf16[1024,512]{1,0:T(8,128)(2,1)} %node_input_ref.1) | copy-start | bytes 3145732
  22.7 5.1 %copy-start.1 = (bf16[512,512]{1,0:T(8,128)(2,1)S(1)}, bf16[512,512]{1,0:T(8,128)(2,1)}, u32[]{:S(2)}) copy-start(bf16[512,512]{1,0:T(8,128)(2,1)} %edge_out_ref.1) | copy-start | bytes 1572868
  22.7 4.9 %collective-permute-start = (bf16[64,512]{1,0:T(8,128)(2,1)S(1)}, bf16[64,512]{1,0:T(8,128)(2,1)S(1)}, u32[]{:S(2)}, u32[]{:S(2)}) collective-permute-start(bf16[64,512]{1,0:T(8,128)(2,1)S(1)} %get-tuple-element.17), channel_id=1, source_target_pairs={{1,2},{3,4},{5,6},{7,8},{9,10},{11,12},{13,14},{2,1},{4,3},{6,5},{... | collective-permute-start | bytes 196616 | tf_op jit(solution)/shard_map/ppermute | solution.py:478
  23.5 4.3 %collective-permute-start.1 = (bf16[64,512]{1,0:T(8,128)(2,1)S(1)}, bf16[64,512]{1,0:T(8,128)(2,1)S(1)}, u32[]{:S(2)}, u32[]{:S(2)}) collective-permute-start(bf16[64,512]{1,0:T(8,128)(2,1)S(1)} %get-tuple-element.18), channel_id=1, source_target_pairs={{0,1},{2,3},{4,5},{6,7},{8,9},{10,11},{12,13},{14,15},{1,0},{3,2},... | collective-permute-start | bytes 196616 | tf_op jit(solution)/shard_map/ppermute | solution.py:479
  27.5 9.0 %copy-start.5 = (s32[4,128]{1,0:T(4,128)S(1)}, s32[4,128]{1,0:T(4,128)}, u32[]{:S(2)}) copy-start(s32[4,128]{1,0:T(4,128)} %send_ref) | copy-start | bytes 6148
  29.7 16.8 %all-to-all-start.1 = ((bf16[16,16,512]{2,1,0:T(8,128)(2,1)}), bf16[16,16,512]{2,1,0:T(8,128)(2,1)S(1)}, u32[]{:S(2)}, u32[]{:S(2)}) async-start(bf16[16,16,512]{2,1,0:T(8,128)(2,1)} %bitcast.9), calls=%async_computation.1 | async-start | bytes 524288 | tf_op jit(solution)/shard_map/all_to_all | solution.py:507
  36.4 2.6 %copy-start.8 = (bf16[1024,512]{1,0:T(8,128)(2,1)S(1)}, bf16[1024,512]{1,0:T(8,128)(2,1)}, u32[]{:S(2)}) copy-start(bf16[1024,512]{1,0:T(8,128)(2,1)} %update_input_ref.3) | copy-start | bytes 3145732
  36.5 2.6 %copy-start.9 = (bf16[512,512]{1,0:T(8,128)(2,1)S(1)}, bf16[512,512]{1,0:T(8,128)(2,1)}, u32[]{:S(2)}) copy-start(bf16[512,512]{1,0:T(8,128)(2,1)} %mesh_receiver_ref.1) | copy-start | bytes 1572868
  36.5 2.6 %copy-start.13 = (s32[4,128]{1,0:T(4,128)S(1)}, s32[4,128]{1,0:T(4,128)}, u32[]{:S(2)}) copy-start(s32[4,128]{1,0:T(4,128)} %recv_ref.1) | copy-start | bytes 6148
  36.5 2.6 %copy-start.14 = (f32[512]{0:T(512)S(1)}, f32[512]{0:T(512)}, u32[]{:S(2)}) copy-start(f32[512]{0:T(512)} %param.42) | copy-start | bytes 6148
  36.5 2.6 %copy-start.15 = (f32[512]{0:T(512)S(1)}, f32[512]{0:T(512)}, u32[]{:S(2)}) copy-start(f32[512]{0:T(512)} %param.45) | copy-start | bytes 6148
  39.1 7.4 %copy-start.10 = (bf16[512,512]{1,0:T(8,128)(2,1)S(1)}, bf16[512,512]{1,0:T(8,128)(2,1)}, u32[]{:S(2)}) copy-start(bf16[512,512]{1,0:T(8,128)(2,1)} %message_out_ref.1) | copy-start | bytes 1572868
  39.1 7.4 %copy-start.11 = (bf16[512,512]{1,0:T(8,128)(2,1)S(1)}, bf16[512,512]{1,0:T(8,128)(2,1)}, u32[]{:S(2)}) copy-start(bf16[512,512]{1,0:T(8,128)(2,1)} %update_out_ref.1) | copy-start | bytes 1572868
  39.1 7.4 %copy-start.16 = (f32[512]{0:T(512)S(1)}, f32[512]{0:T(512)}, u32[]{:S(2)}) copy-start(f32[512]{0:T(512)} %param.47) | copy-start | bytes 6148

commit v9 on v8

--- a/solution.py
+++ b/solution.py
@@ -36,9 +36,9 @@
     return silu_half(0.5 * value)
 
 
-def layer_norm(value):
-    center = value - jnp.mean(value, axis=-1, keepdims=True)
-    spread = jnp.mean(center * center, axis=-1, keepdims=True)
+def layer_norm(value, axis=-1):
+    center = value - jnp.mean(value, axis=axis, keepdims=True)
+    spread = jnp.mean(center * center, axis=axis, keepdims=True)
     return center * lax.rsqrt(spread + 1e-05)
 
 
@@ -87,6 +87,9 @@
     feat_ref,
     count_ref,
     starts,
+    first_t,
+    second_t,
+    grid_column,
     table,
     even_rows,
     odd_rows,
@@ -144,26 +147,27 @@
     )
     total[...] = jnp.zeros_like(total)
     first_copy.wait()
-    first_ref[...] = first_ref[...] * 0.5
+    first_t[...] = (first_ref[...] * 0.5).T
     second_copy.wait()
+    second_t[...] = second_ref[...].T
+    grid_bias_copy.wait()
+    grid_column[...] = jnp.broadcast_to(0.5 * grid_bias_ref[...], (LANES, width)).T
     send_weight_copy.wait()
     send_weight_ref[...] = send_weight_ref[...] * 0.5
-    grid_bias_copy.wait()
     edge_bias_copy.wait()
-    grid_bias = 0.5 * grid_bias_ref[...]
     edge_bias = 0.5 * edge_bias_ref[...]
     half_rows = step_rows // 2
 
     def grid_step(step, carry):
         grid_copy(step).wait()
         first = pl.multiple_of(step * step_rows, step_rows)
+        bias = jnp.concatenate([grid_column[...]] * (half_rows // LANES), axis=1)
         values = [
-            mm(grid_ref[:, pl.ds(first + at, half_rows)].T, first_ref[...])
-            for at in (0, half_rows)
+            mm(first_t[...], grid_ref[:, pl.ds(first + at, half_rows)]) for at in (0, half_rows)
         ]
-        values = [silu_half(value + grid_bias).astype(BF16) for value in values]
-        values = [mm(value, second_ref[...]) for value in values]
-        values = [layer_norm(value).astype(BF16) for value in values]
+        values = [silu_half(value + bias).astype(BF16) for value in values]
+        values = [mm(second_t[...], value) for value in values]
+        values = [layer_norm(value, 0).astype(BF16).T for value in values]
         values = [mm(value, send_weight_ref[...]) for value in values]
         for half, value in enumerate(values):
             row = (value + edge_bias).astype(BF16).astype(F32)
@@ -459,6 +463,9 @@
         scratch=[VMEM(value.shape, value.dtype) for value in operands]
         + [
             SMEM(g2m_send.shape, I32),
+            VMEM(grid_first.shape[::-1], BF16),
+            VMEM(grid_second.shape, BF16),
+            VMEM((width, LANES), F32),
             VMEM((grid_rows * (width // LANES), LANES), F32),
             VMEM((2 * g2m_send.shape[1] * (width // LANES), LANES), F32),
             VMEM((2 * g2m_send.shape[1] * (width // LANES), LANES), F32),

time: 48.8 us -> 49.9 us (1.023)
  Pallas kernels: 20.6 us -> 21.7 us
    pallas_call x1, Pallas kernels: 13.2 us -> 14.3 us  [per_device(): call(edge_kernel, (shape(owned, width, kind=F32), shape(owned, width), sh...]
  transfers between devices with their start and end apart: 4 -> 4, of which waited for: 2 -> 2; matrix products, arithmetic and copies ran while one was open for 0% -> 0% of each run, Pallas kernels for 35% -> 36%
where the time goes in v9:
time: 49.9 us; the launch traced here: 49.6 us
  Pallas kernels  21.7 us (43%)
  starting transfers between devices  18.3 us (37%)
  waiting for transfers between devices  7.16 us (14%)
  local copies, waits for them, and re-layouts  1.41 us (3%)
  between operations  0.93 us (2%)
    pallas_call x1, Pallas kernels, per_device(): call(edge_kernel, (shape(owned, width, kind=F32), shape(owned, width), sh...  14.3 us
    all_to_all x1, starting transfers between devices, per_device(): lax.all_to_all(jnp.tile(mesh_send, (devices, 1)), 'bulk', 0, 0, tiled=True)  7.39 us
    all_to_all x1, waiting for transfers between devices, per_device(): piece = lax.all_to_all(rows, 'bulk', 0, 0, tiled=True)  6.94 us
    all_to_all x1, starting transfers between devices, per_device(): piece = lax.all_to_all(rows, 'bulk', 0, 0, tiled=True)  6.79 us
    ppermute x1, starting transfers between devices, per_device(): from_chip = lax.ppermute(chip, 'bulk', both(within))  3.36 us
    pallas_call x1, Pallas kernels, per_device(): call(functools.partial(wanted_kernel, owned), shape(edges, places), [VMEM...  2.53 us
    pallas_call x1, Pallas kernels, per_device(): call(message_kernel, shape(owned, width), [VMEM] * 11, flops=1000000000,...  1.93 us
    pallas_call x1, Pallas kernels, per_device(): call(node_kernel, (shape(owned, width), shape(places, width)), [VMEM] * 1...  1.87 us
  transfers between devices with their start and end apart: 4, of which 2 were waited for; matrix products, arithmetic and copies ran while one was open for 0% of the time, Pallas kernels for 36%

profile of v9, /device:TPU:0, one launch (start us, length us, event | category | flops | bytes accessed | tf_op | source)
XLA Modules:
  0.0 49.6 jit_solution(14296798912047870798)
XLA Ops:
  0.0 1.3 %tile.2 = s32[16,4,128]{2,1,0:T(4,128)} broadcast(s32[4,128]{1,0:T(4,128)} %send_ref), dimensions={1,2} | broadcast | bytes 34816 | tf_op jit(solution)/shard_map/tile | solution.py:444
  1.3 7.4 %all-to-all-start = ((s32[16,4,128]{2,1,0:T(4,128)}), s32[16,4,128]{2,1,0:T(4,128)S(1)}, u32[]{:S(2)}, u32[]{:S(2)}) async-start(s32[16,4,128]{2,1,0:T(4,128)} %tile.2), calls=%async_computation | async-start | bytes 65536 | tf_op jit(solution)/shard_map/all_to_all | solution.py:444
  9.3 0.0 copy-start.12
  9.4 0.0 copy-start.2
  9.4 0.0 copy-start.3
  9.4 0.0 copy-start.4
  9.4 0.0 copy-start.6
  9.4 0.0 copy-start.7
  9.4 14.3 %shard_map.262 = (f32[64,512]{1,0:T(8,128)S(1)}, bf16[64,512]{1,0:T(8,128)(2,1)S(1)}, bf16[64,512]{1,0:T(8,128)(2,1)S(1)}) custom-call(s32[1]{0:T(128)} %bitcast.1.place_ref, bf16[474,512]{1,0:T(8,128)(2,1)} %first_hbm.1, bf16[474,2048]{1,0:T(8,128)(2,1)} %bitcast.26, bf16[512,512]{1,0:T(8,128)(2,1)} %second_hbm.1, bf16[512,512]{1,0:T(8,128)(2,1)} %send_weight_hbm.1, ...), custom_call_target="tpu_custom_call" | custom-call | flops 10000000000 | bytes 4000000 | tf_op jit(solution)/shard_map/pallas_call | solution.py:459
  23.8 0.0 copy-start
  23.8 0.0 copy-start.1
  23.8 0.8 %collective-permute-start = (bf16[64,512]{1,0:T(8,128)(2,1)S(1)}, bf16[64,512]{1,0:T(8,128)(2,1)S(1)}, u32[]{:S(2)}, u32[]{:S(2)}) collective-permute-start(bf16[64,512]{1,0:T(8,128)(2,1)S(1)} %get-tuple-element.17), channel_id=1, source_target_pairs={{1,2},{3,4},{5,6},{7,8},{9,10},{11,12},{13,14},{2,1},{4,3},{6,5},{... | collective-permute-start | bytes 196616 | tf_op jit(solution)/shard_map/ppermute | solution.py:485
  24.6 3.4 %collective-permute-start.1 = (bf16[64,512]{1,0:T(8,128)(2,1)S(1)}, bf16[64,512]{1,0:T(8,128)(2,1)S(1)}, u32[]{:S(2)}, u32[]{:S(2)}) collective-permute-start(bf16[64,512]{1,0:T(8,128)(2,1)S(1)} %get-tuple-element.18), channel_id=1, source_target_pairs={{0,1},{2,3},{4,5},{6,7},{8,9},{10,11},{12,13},{14,15},{1,0},{3,2},... | collective-permute-start | bytes 196616 | tf_op jit(solution)/shard_map/ppermute | solution.py:486
  28.0 0.0 all-to-all-done
  28.0 0.0 copy-done.12
  28.0 0.7 %shard_map.263.supply_ref = bf16[256,64]{1,0:T(8,128)(2,1)S(1)} custom-call(s32[1]{0:T(128)} %bitcast.1.place_ref, s32[1,1024]{1,0:T(1,128)S(1)} %bitcast.20, s32[64,128]{1,0:T(8,128)S(1)} %bitcast.16), custom_call_target="tpu_custom_call" | custom-call | flops 500000000 | bytes 500000 | tf_op jit(solution)/shard_map/pallas_call | solution.py:487
  28.6 0.0 copy-start.5
  28.6 0.0 collective-permute-done.from_cross_ref
  28.6 0.2 collective-permute-done.1.from_chip_ref
  28.9 0.0 copy-done.2
  28.9 0.0 copy-done.3
  28.9 0.0 copy-done.4
  28.9 0.0 copy-done.6
  28.9 0.0 copy-done.7
  28.9 0.0 copy-done
  28.9 0.0 copy-done.1
  28.9 1.9 %shard_map.264 = (bf16[64,512]{1,0:T(8,128)(2,1)S(1)}, bf16[256,512]{1,0:T(8,128)(2,1)}) custom-call(f32[64,512]{1,0:T(8,128)S(1)} %get-tuple-element.16.own_ref, bf16[64,512]{1,0:T(8,128)(2,1)S(1)} %collective-permute-done.from_cross_ref, bf16[64,512]{1,0:T(8,128)(2,1)S(1)} %collective-permute-done.1.from_chip_ref, bf16[64,512]{1,0:T(8,128)(2,1)S(1)} %copy-done.4, ...), custom_call_target="tpu_custom_call" | custom-call | flops 500000000 | bytes 4000000 | tf_op jit(solution)/shard_map/pallas_call | solution.py:494
  30.8 6.8 %all-to-all-start.1 = ((bf16[16,16,512]{2,1,0:T(8,128)(2,1)}), bf16[16,16,512]{2,1,0:T(8,128)(2,1)S(1)}, u32[]{:S(2)}, u32[]{:S(2)}) async-start(bf16[16,16,512]{2,1,0:T(8,128)(2,1)} %bitcast.9), calls=%async_computation.1 | async-start | bytes 524288 | tf_op jit(solution)/shard_map/all_to_all | solution.py:514
  37.6 0.0 copy-start.8
  37.6 0.0 copy-start.9
  37.6 0.0 copy-start.13
  37.6 0.0 copy-start.14
  37.6 0.0 copy-start.15
  37.6 0.0 copy-done.5
  37.6 2.5 %shard_map.265.wanted_ref = bf16[512,256]{1,0:T(8,128)(2,1)S(1)} custom-call(s32[1,1024]{1,0:T(1,128)S(1)} %bitcast.21, s32[4,128]{1,0:T(4,128)S(1)} %copy-done.5), custom_call_target="tpu_custom_call" | custom-call | flops 1000000000 | bytes 500000 | tf_op jit(solution)/shard_map/pallas_call | solution.py:516
  40.2 0.0 copy-start.10
  40.2 0.0 copy-start.11
  40.2 0.0 copy-start.16
  40.2 0.0 copy-done.8
  40.2 0.0 copy-done.9
  40.2 0.0 copy-done.13
  40.2 0.0 copy-done.14
  40.3 0.0 copy-done.15
  40.3 0.4 shard_map.266
  40.7 6.9 %all-to-all-done.1 = bf16[16,16,512]{2,1,0:T(8,128)(2,1)S(1)} async-done(((bf16[16,16,512]{2,1,0:T(8,128)(2,1)}), bf16[16,16,512]{2,1,0:T(8,128)(2,1)S(1)}, u32[]{:S(2)}, u32[]{:S(2)}) %all-to-all-start.1) | async-done | bytes 262176 | tf_op jit(solution)/shard_map/all_to_all | solution.py:514
  47.6 0.0 copy-done.10
  47.6 0.0 copy-done.11
  47.6 0.0 copy-done.16
  47.6 1.9 %shard_map.267 = bf16[64,512]{1,0:T(8,128)(2,1)} custom-call(bf16[512,256]{1,0:T(8,128)(2,1)S(1)} %shard_map.265.wanted_ref, bf16[256,512]{1,0:T(8,128)(2,1)S(1)} %bitcast.15, bf16[64,512]{1,0:T(8,128)(2,1)S(1)} %get-tuple-element.23.incoming_ref, bf16[512,128]{1,0:T(8,128)(2,1)S(1)} %get-tuple-element.24.pick_ref, ...), custom_call_target="tpu_custom_call" | custom-call | flops 1000000000 | bytes 4000000 | tf_op jit(solution)/shard_map/pallas_call | solution.py:544
Async XLA Ops:
  1.3 26.7 %all-to-all-start = ((s32[16,4,128]{2,1,0:T(4,128)}), s32[16,4,128]{2,1,0:T(4,128)S(1)}, u32[]{:S(2)}, u32[]{:S(2)}) async-start(s32[16,4,128]{2,1,0:T(4,128)} %tile.2), calls=%async_computation | async-start | bytes 65536 | tf_op jit(solution)/shard_map/all_to_all | solution.py:444
  9.3 18.6 %copy-start.12 = (s32[1024]{0:T(1024)S(1)}, s32[1024]{0:T(1024)}, u32[]{:S(2)}) copy-start(s32[1024]{0:T(1024)} %param.53) | copy-start | bytes 12292
  9.4 19.5 %copy-start.2 = (bf16[512,512]{1,0:T(8,128)(2,1)S(1)}, bf16[512,512]{1,0:T(8,128)(2,1)}, u32[]{:S(2)}) copy-start(bf16[512,512]{1,0:T(8,128)(2,1)} %node_out_ref.1) | copy-start | bytes 1572868
  9.4 19.5 %copy-start.3 = (bf16[512,512]{1,0:T(8,128)(2,1)S(1)}, bf16[512,512]{1,0:T(8,128)(2,1)}, u32[]{:S(2)}) copy-start(bf16[512,512]{1,0:T(8,128)(2,1)} %mesh_sender_ref.1) | copy-start | bytes 1572868
  9.4 19.5 %copy-start.4 = (bf16[64,512]{1,0:T(8,128)(2,1)S(1)}, bf16[64,512]{1,0:T(8,128)(2,1)}, u32[]{:S(2)}) copy-start(bf16[64,512]{1,0:T(8,128)(2,1)} %latent_ref.1) | copy-start | bytes 196612
  9.4 19.5 %copy-start.6 = (f32[512]{0:T(512)S(1)}, f32[512]{0:T(512)}, u32[]{:S(2)}) copy-start(f32[512]{0:T(512)} %param.37) | copy-start | bytes 6148
  9.4 19.5 %copy-start.7 = (f32[512]{0:T(512)S(1)}, f32[512]{0:T(512)}, u32[]{:S(2)}) copy-start(f32[512]{0:T(512)} %param.39) | copy-start | bytes 6148
  23.8 5.1 %copy-start = (bf16[1024,512]{1,0:T(8,128)(2,1)S(1)}, bf16[1024,512]{1,0:T(8,128)(2,1)}, u32[]{:S(2)}) copy-start(bf16[1024,512]{1,0:T(8,128)(2,1)} %node_input_ref.1) | copy-start | bytes 3145732
  23.8 5.1 %copy-start.1 = (bf16[512,512]{1,0:T(8,128)(2,1)S(1)}, bf16[512,512]{1,0:T(8,128)(2,1)}, u32[]{:S(2)}) copy-start(bf16[512,512]{1,0:T(8,128)(2,1)} %edge_out_ref.1) | copy-start | bytes 1572868
  23.8 4.8 %collective-permute-start = (bf16[64,512]{1,0:T(8,128)(2,1)S(1)}, bf16[64,512]{1,0:T(8,128)(2,1)S(1)}, u32[]{:S(2)}, u32[]{:S(2)}) collective-permute-start(bf16[64,512]{1,0:T(8,128)(2,1)S(1)} %get-tuple-element.17), channel_id=1, source_target_pairs={{1,2},{3,4},{5,6},{7,8},{9,10},{11,12},{13,14},{2,1},{4,3},{6,5},{... | collective-permute-start | bytes 196616 | tf_op jit(solution)/shard_map/ppermute | solution.py:485
  24.6 4.3 %collective-permute-start.1 = (bf16[64,512]{1,0:T(8,128)(2,1)S(1)}, bf16[64,512]{1,0:T(8,128)(2,1)S(1)}, u32[]{:S(2)}, u32[]{:S(2)}) collective-permute-start(bf16[64,512]{1,0:T(8,128)(2,1)S(1)} %get-tuple-element.18), channel_id=1, source_target_pairs={{0,1},{2,3},{4,5},{6,7},{8,9},{10,11},{12,13},{14,15},{1,0},{3,2},... | collective-permute-start | bytes 196616 | tf_op jit(solution)/shard_map/ppermute | solution.py:486
  28.6 9.0 %copy-start.5 = (s32[4,128]{1,0:T(4,128)S(1)}, s32[4,128]{1,0:T(4,128)}, u32[]{:S(2)}) copy-start(s32[4,128]{1,0:T(4,128)} %send_ref) | copy-start | bytes 6148
  30.8 16.8 %all-to-all-start.1 = ((bf16[16,16,512]{2,1,0:T(8,128)(2,1)}), bf16[16,16,512]{2,1,0:T(8,128)(2,1)S(1)}, u32[]{:S(2)}, u32[]{:S(2)}) async-start(bf16[16,16,512]{2,1,0:T(8,128)(2,1)} %bitcast.9), calls=%async_computation.1 | async-start | bytes 524288 | tf_op jit(solution)/shard_map/all_to_all | solution.py:514
  37.6 2.6 %copy-start.8 = (bf16[1024,512]{1,0:T(8,128)(2,1)S(1)}, bf16[1024,512]{1,0:T(8,128)(2,1)}, u32[]{:S(2)}) copy-start(bf16[1024,512]{1,0:T(8,128)(2,1)} %update_input_ref.3) | copy-start | bytes 3145732
  37.6 2.6 %copy-start.9 = (bf16[512,512]{1,0:T(8,128)(2,1)S(1)}, bf16[512,512]{1,0:T(8,128)(2,1)}, u32[]{:S(2)}) copy-start(bf16[512,512]{1,0:T(8,128)(2,1)} %mesh_receiver_ref.1) | copy-start | bytes 1572868
  37.6 2.6 %copy-start.13 = (s32[4,128]{1,0:T(4,128)S(1)}, s32[4,128]{1,0:T(4,128)}, u32[]{:S(2)}) copy-start(s32[4,128]{1,0:T(4,128)} %recv_ref.1) | copy-start | bytes 6148
  37.6 2.6 %copy-start.14 = (f32[512]{0:T(512)S(1)}, f32[512]{0:T(512)}, u32[]{:S(2)}) copy-start(f32[512]{0:T(512)} %param.42) | copy-start | bytes 6148
  37.6 2.6 %copy-start.15 = (f32[512]{0:T(512)S(1)}, f32[512]{0:T(512)}, u32[]{:S(2)}) copy-start(f32[512]{0:T(512)} %param.45) | copy-start | bytes 6148
  40.2 7.4 %copy-start.10 = (bf16[512,512]{1,0:T(8,128)(2,1)S(1)}, bf16[512,512]{1,0:T(8,128)(2,1)}, u32[]{:S(2)}) copy-start(bf16[512,512]{1,0:T(8,128)(2,1)} %message_out_ref.1) | copy-start | bytes 1572868
  40.2 7.4 %copy-start.11 = (bf16[512,512]{1,0:T(8,128)(2,1)S(1)}, bf16[512,512]{1,0:T(8,128)(2,1)}, u32[]{:S(2)}) copy-start(bf16[512,512]{1,0:T(8,128)(2,1)} %update_out_ref.1) | copy-start | bytes 1572868
  40.2 7.4 %copy-start.16 = (f32[512]{0:T(512)S(1)}, f32[512]{0:T(512)}, u32[]{:S(2)}) copy-start(f32[512]{0:T(512)} %param.47) | copy-start | bytes 6148

commit v10 on v8

--- a/solution.py
+++ b/solution.py
@@ -51,18 +51,63 @@
     return jnp.where(hit, jnp.ones((), BF16), jnp.zeros((), BF16))
 
 
+def sending_order(devices):
+    quarter = devices // 4
+    members = list(range(devices))
+    return members[: 2 * quarter] + members[3 * quarter :] + members[2 * quarter : 3 * quarter]
+
+
 def ids_of_rows(slot, first, count):
     nodes = slot.shape[1]
     rows = iota((count, nodes), 0) + first
     return jnp.max(jnp.where(slot == rows, iota((count, nodes), 1), -1), axis=1, keepdims=True)
 
 
-def edge_kernel(
-    place_ref,
+def opening_kernel(
+    mesh_send_hbm,
     first_hbm,
     grid_hbm,
     second_hbm,
     send_weight_hbm,
+    asked_ref,
+    first_ref,
+    grid_ref,
+    second_ref,
+    send_weight_ref,
+    mesh_send_ref,
+    sems,
+):
+    pairs = [
+        (mesh_send_hbm, mesh_send_ref),
+        (first_hbm, first_ref),
+        (send_weight_hbm, send_weight_ref),
+        (second_hbm, second_ref),
+        (grid_hbm.at[:, : grid_ref.shape[1]], grid_ref),
+    ]
+    copies = [
+        pltpu.make_async_copy(source, target, sems.at[at])
+        for at, (source, target) in enumerate(pairs)
+    ]
+    for copy in copies:
+        copy.start()
+    copies[0].wait()
+    rows = mesh_send_ref.shape[0]
+    for at in range(asked_ref.shape[0] // rows):
+        asked_ref[at * rows : (at + 1) * rows, :] = mesh_send_ref[...]
+    for copy, ref in zip(copies[1:3], (first_ref, send_weight_ref)):
+        copy.wait()
+        ref[...] = ref[...] * 0.5
+    for copy in copies[3:]:
+        copy.wait()
+
+
+def edge_kernel(
+    place_ref,
+    first_ref,
+    opening_ref,
+    second_ref,
+    send_weight_ref,
+    grid_hbm,
     grid_bias_hbm,
     edge_bias_hbm,
     slot_hbm,
@@ -74,10 +119,7 @@
     own_ref,
     cross_ref,
     chip_ref,
-    first_ref,
     grid_ref,
-    second_ref,
-    send_weight_ref,
     grid_bias_ref,
     edge_bias_ref,
     slot_ref,
@@ -108,9 +150,6 @@
         return pltpu.make_async_copy(grid_hbm.at[:, part], grid_ref.at[:, part], sems.at[step])
 
     pairs = [
-        (first_hbm, first_ref),
-        (second_hbm, second_ref),
-        (send_weight_hbm, send_weight_ref),
         (grid_bias_hbm, grid_bias_ref),
         (edge_bias_hbm, edge_bias_ref),
         (send_hbm, send_ref),
@@ -125,14 +164,13 @@
         pltpu.make_async_copy(source, target, sems.at[GRID_STEPS + at])
         for at, (source, target) in enumerate(pairs)
     ]
-    first_copy, second_copy, send_weight_copy, grid_bias_copy, edge_bias_copy, send_copy = copies[:6]
-    slot_copy, starts_copy = copies[6], copies[-1]
-    first_copy.start()
-    grid_copy(0).start()
-    for copy in copies[1:-1]:
+    grid_bias_copy, edge_bias_copy, send_copy, slot_copy = copies[:4]
+    starts_copy = copies[-1]
+    for copy in copies[:-1]:
         copy.start()
     for step in range(1, GRID_STEPS):
         grid_copy(step).start()
+    grid_ref[:, :step_rows] = opening_ref[...]
     send_copy.wait()
     senders = send_ref[...]
     send_ref[...] = (senders // 8) * (8 * pieces) + senders % 8
@@ -143,11 +181,6 @@
         ids_of_rows(slot_ref[...], (place - 1) * owned, 3 * owned), ids_ref.shape
     )
     total[...] = jnp.zeros_like(total)
-    first_copy.wait()
-    first_ref[...] = first_ref[...] * 0.5
-    second_copy.wait()
-    send_weight_copy.wait()
-    send_weight_ref[...] = send_weight_ref[...] * 0.5
     grid_bias_copy.wait()
     edge_bias_copy.wait()
     grid_bias = 0.5 * grid_bias_ref[...]
@@ -155,7 +188,10 @@
     half_rows = step_rows // 2
 
     def grid_step(step, carry):
-        grid_copy(step).wait()
+        @pl.when(step > 0)
+        def _():
+            grid_copy(step).wait()
+
         first = pl.multiple_of(step * step_rows, step_rows)
         values = [
             mm(grid_ref[:, pl.ds(first + at, half_rows)].T, first_ref[...])
@@ -177,7 +213,7 @@
         return carry
 
     lax.fori_loop(0, GRID_STEPS, grid_step, 0)
-    for copy in copies[7:]:
+    for copy in copies[4:]:
         copy.wait()
     used = count_ref[...]
     feat_weight = 0.5 * feat_weight_ref[...].astype(F32)
@@ -262,6 +298,13 @@
 
     best = lax.fori_loop(0, nodes // chunk, find, jnp.full((1, places), -1, I32), unroll=2)
     best = best.astype(F32)
+    best = jnp.concatenate(
+        [
+            best[:, owner * SEND_CAP : (owner + 1) * SEND_CAP]
+            for owner in sending_order(places // SEND_CAP)
+        ],
+        axis=1,
+    )
     for b in range(blocks):
         senders = jnp.broadcast_to(send_ref[b : b + 1, :].astype(F32), (block_edges, block_edges)).T
         senders = jnp.concatenate([senders] * (places // LANES), axis=1)
@@ -288,7 +331,7 @@
     rank = jnp.concatenate([rank, jnp.full((LANES - owned, LANES), -1.0, F32)], axis=0).T
     slots = iota((SEND_CAP, owned), 0).astype(F32)
     supply = jnp.concatenate(
-        [(rank[d : d + 1, :owned] == slots).astype(F32) for d in range(devices)], axis=0
+        [(rank[d : d + 1, :owned] == slots).astype(F32) for d in sending_order(devices)], axis=0
     )
     supply_ref[...] = supply.astype(BF16)
 
@@ -437,12 +480,31 @@
     slot = mesh_slot.reshape(1, -1)
     row = lambda vector: vector.reshape(1, -1)
 
-    requests = lax.all_to_all(jnp.tile(mesh_send, (devices, 1)), "bulk", 0, 0, tiled=True)
+    grid_turned = pltpu.with_memory_space_constraint(grid_in.T, HBM)
+    asked, *opened = call(
+        opening_kernel,
+        (
+            shape(devices * mesh_send.shape[0], mesh_send.shape[1], kind=I32),
+            shape(*grid_first.shape),
+            shape(grid_in.shape[1], grid_rows // GRID_STEPS),
+            shape(*grid_second.shape),
+            shape(*send_weight.shape),
+        ),
+        [HBM] * 5,
+        scratch=[VMEM(mesh_send.shape, I32), pltpu.SemaphoreType.DMA((5,))],
+        flops=1_000_000,
+        moved=3_000_000,
+    )(
+        hold(mesh_send),
+        hold(grid_first),
+        grid_turned,
+        hold(grid_second),
+        hold(send_weight),
+    )
+    requests = lax.all_to_all(asked, "bulk", 0, 0, tiled=True)
+    opened = [pltpu.with_memory_space_constraint(value, VMEM) for value in opened]
     operands = (
-        grid_first,
-        grid_in.T,
-        grid_second,
-        send_weight,
+        grid_turned,
         row(grid_bias),
         row(edge_bias),
         slot,
@@ -455,7 +517,7 @@
     own, cross, chip = call(
         edge_kernel,
         (shape(owned, width, kind=F32), shape(owned, width), shape(owned, width)),
-        [SMEM] + [HBM] * len(operands),
+        [SMEM] + [VMEM] * 4 + [HBM] * len(operands),
         scratch=[VMEM(value.shape, value.dtype) for value in operands]
         + [
             SMEM(g2m_send.shape, I32),
@@ -470,7 +532,7 @@
         flops=10_000_000_000,
         moved=4_000_000,
         vmem=32,
-    )(place, *[hold(value) for value in operands])
+    )(place, *opened, grid_turned, *[hold(value) for value in operands[1:]])
     requests, _ = lax.optimization_barrier((requests, own))
     crossing = [(d, d + 1) for d in range(1, devices - 1, 2)]
     within = [(d, d + 1) for d in range(0, devices, 2)]
@@ -503,8 +565,8 @@
         mesh_sender,
         supply,
     )
-    rows = pltpu.with_memory_space_constraint(rows, VMEM)
-    piece = lax.all_to_all(rows, "bulk", 0, 0, tiled=True)
+    members = [sending_order(devices)]
+    piece = lax.all_to_all(rows, "bulk", 0, 0, axis_index_groups=members, tiled=True)
     mesh_send, _ = lax.optimization_barrier((mesh_send, encoded))
     wanted = call(
         functools.partial(wanted_kernel, owned),

time: 48.8 us -> 49.9 us (1.023)
  Pallas kernels: 20.6 us -> 22.3 us
  local copies, waits for them, and re-layouts: 1.41 us -> 0.11 us
    pallas_call x0 -> x1, Pallas kernels: none -> 2.16 us  [per_device(): call(opening_kernel, (shape(devices * mesh_send.shape[0], mesh_send.shape...]
    another operation x1 -> x0, local copies, waits for them, and re-layouts: 1.3 us -> none  [per_device(): jnp.tile(mesh_send, (devices, 1))]
    pallas_call x1, Pallas kernels: 13.2 us -> 12.7 us  [per_device(): call(edge_kernel, (shape(owned, width, kind=F32), shape(owned, width), sh...]
  transfers between devices with their start and end apart: 4 -> 4, of which waited for: 2 -> 2; matrix products, arithmetic and copies ran while one was open for 0% -> 0% of each run, Pallas kernels for 35% -> 33%
where the time goes in v10:
time: 49.9 us; the launch traced here: 49.5 us
  Pallas kernels  22.3 us (45%)
  starting transfers between devices  18.6 us (37%)
  waiting for transfers between devices  7.64 us (15%)
  between operations  0.94 us (2%)
    pallas_call x1, Pallas kernels, per_device(): call(edge_kernel, (shape(owned, width, kind=F32), shape(owned, width), sh...  12.7 us
    all_to_all x1, waiting for transfers between devices, per_device(): lax.all_to_all(rows, 'bulk', 0, 0, axis_index_groups=members, tiled=True)  7.42 us
    all_to_all x1, starting transfers between devices, per_device(): requests = lax.all_to_all(asked, 'bulk', 0, 0, tiled=True)  7.4 us
    all_to_all x1, starting transfers between devices, per_device(): lax.all_to_all(rows, 'bulk', 0, 0, axis_index_groups=members, tiled=True)  7.01 us
    ppermute x1, starting transfers between devices, per_device(): from_chip = lax.ppermute(chip, 'bulk', both(within))  3.35 us
    pallas_call x1, Pallas kernels, per_device(): call(functools.partial(wanted_kernel, owned), shape(edges, places), [VMEM...  2.56 us
    pallas_call x1, Pallas kernels, per_device(): call(opening_kernel, (shape(devices * mesh_send.shape[0], mesh_send.shape...  2.16 us
    pallas_call x1, Pallas kernels, per_device(): call(message_kernel, shape(owned, width), [VMEM] * 11, flops=1000000000,...  1.93 us
  transfers between devices with their start and end apart: 4, of which 2 were waited for; matrix products, arithmetic and copies ran while one was open for 0% of the time, Pallas kernels for 33%

profile of v10, /device:TPU:0, one launch (start us, length us, event | category | flops | bytes accessed | tf_op | source)
XLA Modules:
  0.0 49.5 jit_solution(9279215364766213795)
XLA Ops:
  0.0 2.2 %shard_map.262 = (s32[64,128]{1,0:T(8,128)}, bf16[474,512]{1,0:T(8,128)(2,1)S(1)}, bf16[474,512]{1,0:T(8,128)(2,1)S(1)}, bf16[512,512]{1,0:T(8,128)(2,1)S(1)}, bf16[512,512]{1,0:T(8,128)(2,1)S(1)}) custom-call(s32[4,128]{1,0:T(4,128)} %send_ref, bf16[474,512]{1,0:T(8,128)(2,1)} %first_hbm.1, bf16[474,2048]{1,0:T(8,128)(2,1)} %bitcast.27, ...), custom_call_target="tpu_custom_call" | custom-call | flops 1000000 | bytes 3000000 | tf_op jit(solution)/shard_map/pallas_call | solution.py:484
  2.2 7.4 %all-to-all-start = ((s32[16,4,128]{2,1,0:T(4,128)}), s32[16,4,128]{2,1,0:T(4,128)S(1)}, u32[]{:S(2)}, u32[]{:S(2)}) async-start(s32[16,4,128]{2,1,0:T(4,128)} %bitcast.8), calls=%async_computation | async-start | bytes 65536 | tf_op jit(solution)/shard_map/all_to_all | solution.py:504
  10.2 0.0 copy-start.12
  10.2 0.0 copy-start.2
  10.3 0.0 copy-start.3
  10.3 0.0 copy-start.4
  10.3 0.0 copy-start.6
  10.3 0.0 copy-start.7
  10.3 12.7 %shard_map.263 = (f32[64,512]{1,0:T(8,128)S(1)}, bf16[64,512]{1,0:T(8,128)(2,1)}, bf16[64,512]{1,0:T(8,128)(2,1)S(1)}) custom-call(s32[1]{0:T(128)} %bitcast.1.place_ref, bf16[474,512]{1,0:T(8,128)(2,1)S(1)} %get-tuple-element.21.first_ref, bf16[474,512]{1,0:T(8,128)(2,1)S(1)} %get-tuple-element.22.opening_ref, ...), custom_call_target="tpu_custom_call" | custom-call | flops 10000000000 | bytes 4000000 | tf_op jit(solution)/shard_map/pallas_call | solution.py:517
  23.0 0.0 copy-start
  23.0 0.0 copy-start.1
  23.0 0.8 %collective-permute-start = (bf16[64,512]{1,0:T(8,128)(2,1)}, bf16[64,512]{1,0:T(8,128)(2,1)S(1)}, u32[]{:S(2)}, u32[]{:S(2)}) collective-permute-start(bf16[64,512]{1,0:T(8,128)(2,1)} %get-tuple-element.26), channel_id=1, source_target_pairs={{1,2},{3,4},{5,6},{7,8},{9,10},{11,12},{13,14},{2,1},{4,3},{6,5},{... | collective-permute-start | bytes 196616 | tf_op jit(solution)/shard_map/ppermute | solution.py:540
  23.8 3.4 %collective-permute-start.1 = (bf16[64,512]{1,0:T(8,128)(2,1)S(1)}, bf16[64,512]{1,0:T(8,128)(2,1)S(1)}, u32[]{:S(2)}, u32[]{:S(2)}) collective-permute-start(bf16[64,512]{1,0:T(8,128)(2,1)S(1)} %get-tuple-element.27), channel_id=1, source_target_pairs={{0,1},{2,3},{4,5},{6,7},{8,9},{10,11},{12,13},{14,15},{1,0},{3,2},... | collective-permute-start | bytes 196616 | tf_op jit(solution)/shard_map/ppermute | solution.py:541
  27.2 0.0 all-to-all-done
  27.2 0.0 copy-done.12
  27.2 0.7 %shard_map.264.supply_ref = bf16[256,64]{1,0:T(8,128)(2,1)S(1)} custom-call(s32[1]{0:T(128)} %bitcast.1.place_ref, s32[1,1024]{1,0:T(1,128)S(1)} %bitcast.21, s32[64,128]{1,0:T(8,128)S(1)} %bitcast.17), custom_call_target="tpu_custom_call" | custom-call | flops 500000000 | bytes 500000 | tf_op jit(solution)/shard_map/pallas_call | solution.py:542
  27.9 0.0 copy-start.5
  27.9 0.0 collective-permute-done.from_cross_ref
  27.9 0.2 collective-permute-done.1.from_chip_ref
  28.1 0.0 copy-done.2
  28.1 0.0 copy-done.3
  28.1 0.0 copy-done.4
  28.1 0.0 copy-done.6
  28.1 0.0 copy-done.7
  28.1 0.0 copy-done
  28.1 0.0 copy-done.1
  28.1 1.9 %shard_map.265 = (bf16[64,512]{1,0:T(8,128)(2,1)S(1)}, bf16[256,512]{1,0:T(8,128)(2,1)}) custom-call(f32[64,512]{1,0:T(8,128)S(1)} %get-tuple-element.25.own_ref, bf16[64,512]{1,0:T(8,128)(2,1)S(1)} %collective-permute-done.from_cross_ref, bf16[64,512]{1,0:T(8,128)(2,1)S(1)} %collective-permute-done.1.from_chip_ref, bf16[64,512]{1,0:T(8,128)(2,1)S(1)} %copy-done.4, ...), custom_call_target="tpu_custom_call" | custom-call | flops 500000000 | bytes 4000000 | tf_op jit(solution)/shard_map/pallas_call | solution.py:549
  30.0 7.0 %all-to-all-start.1 = ((bf16[16,16,512]{2,1,0:T(8,128)(2,1)}), bf16[16,16,512]{2,1,0:T(8,128)(2,1)S(1)}, u32[]{:S(2)}, u32[]{:S(2)}) async-start(bf16[16,16,512]{2,1,0:T(8,128)(2,1)} %bitcast.10), calls=%async_computation.1 | async-start | bytes 524288 | tf_op jit(solution)/shard_map/all_to_all | solution.py:569
  37.0 0.0 copy-start.8
  37.0 0.0 copy-start.9
  37.0 0.0 copy-start.13
  37.1 0.0 copy-start.14
  37.1 0.0 copy-start.15
  37.1 0.0 copy-done.5
  37.1 2.6 %shard_map.266.wanted_ref = bf16[512,256]{1,0:T(8,128)(2,1)S(1)} custom-call(s32[1,1024]{1,0:T(1,128)S(1)} %bitcast.22, s32[4,128]{1,0:T(4,128)S(1)} %copy-done.5), custom_call_target="tpu_custom_call" | custom-call | flops 1000000000 | bytes 500000 | tf_op jit(solution)/shard_map/pallas_call | solution.py:571
  39.7 0.0 copy-start.10
  39.7 0.0 copy-start.11
  39.7 0.0 copy-start.16
  39.7 0.0 copy-done.8
  39.7 0.0 copy-done.9
  39.7 0.0 copy-done.13
  39.7 0.0 copy-done.14
  39.7 0.0 copy-done.15
  39.7 0.4 shard_map.267
  40.1 7.4 %all-to-all-done.1 = bf16[16,16,512]{2,1,0:T(8,128)(2,1)S(1)} async-done(((bf16[16,16,512]{2,1,0:T(8,128)(2,1)}), bf16[16,16,512]{2,1,0:T(8,128)(2,1)S(1)}, u32[]{:S(2)}, u32[]{:S(2)}) %all-to-all-start.1) | async-done | bytes 262176 | tf_op jit(solution)/shard_map/all_to_all | solution.py:569
  47.6 0.0 copy-done.10
  47.6 0.0 copy-done.11
  47.6 0.0 copy-done.16
  47.6 1.9 %shard_map.268 = bf16[64,512]{1,0:T(8,128)(2,1)} custom-call(bf16[512,256]{1,0:T(8,128)(2,1)S(1)} %shard_map.266.wanted_ref, bf16[256,512]{1,0:T(8,128)(2,1)S(1)} %bitcast.16, bf16[64,512]{1,0:T(8,128)(2,1)S(1)} %get-tuple-element.33.incoming_ref, bf16[512,128]{1,0:T(8,128)(2,1)S(1)} %get-tuple-element.34.pick_ref, ...), custom_call_target="tpu_custom_call" | custom-call | flops 1000000000 | bytes 4000000 | tf_op jit(solution)/shard_map/pallas_call | solution.py:599
Async XLA Ops:
  2.2 25.0 %all-to-all-start = ((s32[16,4,128]{2,1,0:T(4,128)}), s32[16,4,128]{2,1,0:T(4,128)S(1)}, u32[]{:S(2)}, u32[]{:S(2)}) async-start(s32[16,4,128]{2,1,0:T(4,128)} %bitcast.8), calls=%async_computation | async-start | bytes 65536 | tf_op jit(solution)/shard_map/all_to_all | solution.py:504
  10.2 17.0 %copy-start.12 = (s32[1024]{0:T(1024)S(1)}, s32[1024]{0:T(1024)}, u32[]{:S(2)}) copy-start(s32[1024]{0:T(1024)} %param.53) | copy-start | bytes 12292
  10.2 17.9 %copy-start.2 = (bf16[512,512]{1,0:T(8,128)(2,1)S(1)}, bf16[512,512]{1,0:T(8,128)(2,1)}, u32[]{:S(2)}) copy-start(bf16[512,512]{1,0:T(8,128)(2,1)} %node_out_ref.1) | copy-start | bytes 1572868
  10.3 17.8 %copy-start.3 = (bf16[512,512]{1,0:T(8,128)(2,1)S(1)}, bf16[512,512]{1,0:T(8,128)(2,1)}, u32[]{:S(2)}) copy-start(bf16[512,512]{1,0:T(8,128)(2,1)} %mesh_sender_ref.1) | copy-start | bytes 1572868
  10.3 17.8 %copy-start.4 = (bf16[64,512]{1,0:T(8,128)(2,1)S(1)}, bf16[64,512]{1,0:T(8,128)(2,1)}, u32[]{:S(2)}) copy-start(bf16[64,512]{1,0:T(8,128)(2,1)} %latent_ref.1) | copy-start | bytes 196612
  10.3 17.8 %copy-start.6 = (f32[512]{0:T(512)S(1)}, f32[512]{0:T(512)}, u32[]{:S(2)}) copy-start(f32[512]{0:T(512)} %param.37) | copy-start | bytes 6148
  10.3 17.8 %copy-start.7 = (f32[512]{0:T(512)S(1)}, f32[512]{0:T(512)}, u32[]{:S(2)}) copy-start(f32[512]{0:T(512)} %param.39) | copy-start | bytes 6148
  23.0 5.1 %copy-start = (bf16[1024,512]{1,0:T(8,128)(2,1)S(1)}, bf16[1024,512]{1,0:T(8,128)(2,1)}, u32[]{:S(2)}) copy-start(bf16[1024,512]{1,0:T(8,128)(2,1)} %node_input_ref.1) | copy-start | bytes 3145732
  23.0 5.1 %copy-start.1 = (bf16[512,512]{1,0:T(8,128)(2,1)S(1)}, bf16[512,512]{1,0:T(8,128)(2,1)}, u32[]{:S(2)}) copy-start(bf16[512,512]{1,0:T(8,128)(2,1)} %edge_out_ref.1) | copy-start | bytes 1572868
  23.0 4.8 %collective-permute-start = (bf16[64,512]{1,0:T(8,128)(2,1)}, bf16[64,512]{1,0:T(8,128)(2,1)S(1)}, u32[]{:S(2)}, u32[]{:S(2)}) collective-permute-start(bf16[64,512]{1,0:T(8,128)(2,1)} %get-tuple-element.26), channel_id=1, source_target_pairs={{1,2},{3,4},{5,6},{7,8},{9,10},{11,12},{13,14},{2,1},{4,3},{6,5},{... | collective-permute-start | bytes 196616 | tf_op jit(solution)/shard_map/ppermute | solution.py:540
  23.8 4.3 %collective-permute-start.1 = (bf16[64,512]{1,0:T(8,128)(2,1)S(1)}, bf16[64,512]{1,0:T(8,128)(2,1)S(1)}, u32[]{:S(2)}, u32[]{:S(2)}) collective-permute-start(bf16[64,512]{1,0:T(8,128)(2,1)S(1)} %get-tuple-element.27), channel_id=1, source_target_pairs={{0,1},{2,3},{4,5},{6,7},{8,9},{10,11},{12,13},{14,15},{1,0},{3,2},... | collective-permute-start | bytes 196616 | tf_op jit(solution)/shard_map/ppermute | solution.py:541
  27.9 9.2 %copy-start.5 = (s32[4,128]{1,0:T(4,128)S(1)}, s32[4,128]{1,0:T(4,128)}, u32[]{:S(2)}) copy-start(s32[4,128]{1,0:T(4,128)} %send_ref) | copy-start | bytes 6148
  30.0 17.6 %all-to-all-start.1 = ((bf16[16,16,512]{2,1,0:T(8,128)(2,1)}), bf16[16,16,512]{2,1,0:T(8,128)(2,1)S(1)}, u32[]{:S(2)}, u32[]{:S(2)}) async-start(bf16[16,16,512]{2,1,0:T(8,128)(2,1)} %bitcast.10), calls=%async_computation.1 | async-start | bytes 524288 | tf_op jit(solution)/shard_map/all_to_all | solution.py:569
  37.0 2.7 %copy-start.8 = (bf16[1024,512]{1,0:T(8,128)(2,1)S(1)}, bf16[1024,512]{1,0:T(8,128)(2,1)}, u32[]{:S(2)}) copy-start(bf16[1024,512]{1,0:T(8,128)(2,1)} %update_input_ref.3) | copy-start | bytes 3145732
  37.0 2.7 %copy-start.9 = (bf16[512,512]{1,0:T(8,128)(2,1)S(1)}, bf16[512,512]{1,0:T(8,128)(2,1)}, u32[]{:S(2)}) copy-start(bf16[512,512]{1,0:T(8,128)(2,1)} %mesh_receiver_ref.1) | copy-start | bytes 1572868
  37.0 2.7 %copy-start.13 = (s32[4,128]{1,0:T(4,128)S(1)}, s32[4,128]{1,0:T(4,128)}, u32[]{:S(2)}) copy-start(s32[4,128]{1,0:T(4,128)} %recv_ref.1) | copy-start | bytes 6148
  37.1 2.7 %copy-start.14 = (f32[512]{0:T(512)S(1)}, f32[512]{0:T(512)}, u32[]{:S(2)}) copy-start(f32[512]{0:T(512)} %param.42) | copy-start | bytes 6148
  37.1 2.7 %copy-start.15 = (f32[512]{0:T(512)S(1)}, f32[512]{0:T(512)}, u32[]{:S(2)}) copy-start(f32[512]{0:T(512)} %param.45) | copy-start | bytes 6148
  39.7 7.9 %copy-start.10 = (bf16[512,512]{1,0:T(8,128)(2,1)S(1)}, bf16[512,512]{1,0:T(8,128)(2,1)}, u32[]{:S(2)}) copy-start(bf16[512,512]{1,0:T(8,128)(2,1)} %message_out_ref.1) | copy-start | bytes 1572868
  39.7 7.9 %copy-start.11 = (bf16[512,512]{1,0:T(8,128)(2,1)S(1)}, bf16[512,512]{1,0:T(8,128)(2,1)}, u32[]{:S(2)}) copy-start(bf16[512,512]{1,0:T(8,128)(2,1)} %update_out_ref.1) | copy-start | bytes 1572868
  39.7 7.9 %copy-start.16 = (f32[512]{0:T(512)S(1)}, f32[512]{0:T(512)}, u32[]{:S(2)}) copy-start(f32[512]{0:T(512)} %param.47) | copy-start | bytes 6148

commit v11 on v8

--- a/solution.py
+++ b/solution.py
@@ -17,6 +17,8 @@
 SMEM = pltpu.SMEM
 HBM = pltpu.HBM
 GRID_STEPS = 4
+STEP_ROWS = 256
+BATCH = 16
 MEBI = 1024 * 1024
 
 
@@ -152,47 +154,46 @@
     edge_bias_copy.wait()
     grid_bias = 0.5 * grid_bias_ref[...]
     edge_bias = 0.5 * edge_bias_ref[...]
-    half_rows = step_rows // 2
-
     def grid_step(step, carry):
-        grid_copy(step).wait()
-        first = pl.multiple_of(step * step_rows, step_rows)
-        values = [
-            mm(grid_ref[:, pl.ds(first + at, half_rows)].T, first_ref[...])
-            for at in (0, half_rows)
-        ]
-        values = [silu_half(value + grid_bias).astype(BF16) for value in values]
-        values = [mm(value, second_ref[...]) for value in values]
-        values = [layer_norm(value).astype(BF16) for value in values]
-        values = [mm(value, send_weight_ref[...]) for value in values]
-        for half, value in enumerate(values):
-            row = (value + edge_bias).astype(BF16).astype(F32)
-            base = pl.multiple_of((first + half * half_rows) * pieces, half_rows * pieces)
-            for group in range(half_rows // 8):
-                for piece in range(pieces):
-                    at = (group * pieces + piece) * 8
-                    table[pl.ds(base + at, 8), :] = row[
-                        group * 8 : group * 8 + 8, piece * LANES : (piece + 1) * LANES
-                    ]
+        first = pl.multiple_of(step * STEP_ROWS, STEP_ROWS)
+        per_copy = step_rows // STEP_ROWS
+
+        @pl.when(step % per_copy == 0)
+        def _():
+            grid_copy(step // per_copy).wait()
+
+        value = mm(grid_ref[:, pl.ds(first, STEP_ROWS)].T, first_ref[...])
+        value = silu_half(value + grid_bias).astype(BF16)
+        value = layer_norm(mm(value, second_ref[...])).astype(BF16)
+        row = mm(value, send_weight_ref[...]) + edge_bias
+        row = row.astype(BF16).astype(F32)
+        base = pl.multiple_of(first * pieces, STEP_ROWS * pieces)
+        for group in range(STEP_ROWS // 8):
+            for piece in range(pieces):
+                at = (group * pieces + piece) * 8
+                table[pl.ds(base + at, 8), :] = row[
+                    group * 8 : group * 8 + 8, piece * LANES : (piece + 1) * LANES
+                ]
         return carry
 
-    lax.fori_loop(0, GRID_STEPS, grid_step, 0)
+    lax.fori_loop(0, grid_rows // STEP_ROWS, grid_step, 0)
     for copy in copies[7:]:
         copy.wait()
     used = count_ref[...]
     feat_weight = 0.5 * feat_weight_ref[...].astype(F32)
     feat_weight = jnp.concatenate([feat_weight, jnp.zeros((8 - feats, width), F32)], axis=0)
     feat_weight = feat_weight.astype(BF16)
-    group = 2 if blocks % 4 == 0 else 1
+    group = 1
     chunks = blocks // group
     part_rows = 64
 
     def gather(chunk, edges, target):
-        for edge in edges:
-            start = starts[chunk * group + edge // block_edges, edge % block_edges]
-            target[pl.ds(edge // 8 * (8 * pieces) + edge % 8, pieces, stride=8), :] = table[
-                pl.ds(start, pieces, stride=8), :
-            ]
+        for batch in range(0, len(edges), BATCH):
+            some = edges[batch : batch + BATCH]
+            places = [starts[chunk * group + e // block_edges, e % block_edges] for e in some]
+            rows = [table[pl.ds(place, pieces, stride=8), :] for place in places]
+            for e, row in zip(some, rows):
+                target[pl.ds(e // 8 * (8 * pieces) + e % 8, pieces, stride=8), :] = row
 
     def rows_of(source, first, count):
         return jnp.concatenate(
@@ -460,9 +461,9 @@
         + [
             SMEM(g2m_send.shape, I32),
             VMEM((grid_rows * (width // LANES), LANES), F32),
-            VMEM((2 * g2m_send.shape[1] * (width // LANES), LANES), F32),
-            VMEM((2 * g2m_send.shape[1] * (width // LANES), LANES), F32),
-            VMEM((2 * g2m_send.shape[1], width), BF16),
+            VMEM((g2m_send.shape[1] * (width // LANES), LANES), F32),
+            VMEM((g2m_send.shape[1] * (width // LANES), LANES), F32),
+            VMEM((g2m_send.shape[1], width), BF16),
             VMEM((3 * owned, LANES), I32),
             VMEM((3 * owned, width), F32),
             pltpu.SemaphoreType.DMA((len(operands) + GRID_STEPS,)),
@@ -503,7 +504,6 @@
         mesh_sender,
         supply,
     )
-    rows = pltpu.with_memory_space_constraint(rows, VMEM)
     piece = lax.all_to_all(rows, "bulk", 0, 0, tiled=True)
     mesh_send, _ = lax.optimization_barrier((mesh_send, encoded))
     wanted = call(

time: 48.8 us -> 54.5 us (1.12)
  Pallas kernels: 20.6 us -> 26.3 us
    pallas_call x1, Pallas kernels: 13.2 us -> 18.9 us  [per_device(): call(edge_kernel, (shape(owned, width, kind=F32), shape(owned, width), sh...]
  transfers between devices with their start and end apart: 4 -> 4, of which waited for: 2 -> 2; matrix products, arithmetic and copies ran while one was open for 0% -> 0% of each run, Pallas kernels for 35% -> 42%
where the time goes in v11:
time: 54.5 us; the launch traced here: 54.1 us
  Pallas kernels  26.3 us (48%)
  starting transfers between devices  18.3 us (34%)
  waiting for transfers between devices  7.16 us (13%)
  local copies, waits for them, and re-layouts  1.41 us (3%)
  between operations  0.93 us (2%)
    pallas_call x1, Pallas kernels, per_device(): call(edge_kernel, (shape(owned, width, kind=F32), shape(owned, width), sh...  18.9 us
    all_to_all x1, starting transfers between devices, per_device(): lax.all_to_all(jnp.tile(mesh_send, (devices, 1)), 'bulk', 0, 0, tiled=True)  7.39 us
    all_to_all x1, waiting for transfers between devices, per_device(): piece = lax.all_to_all(rows, 'bulk', 0, 0, tiled=True)  6.94 us
    all_to_all x1, starting transfers between devices, per_device(): piece = lax.all_to_all(rows, 'bulk', 0, 0, tiled=True)  6.83 us
    ppermute x1, starting transfers between devices, per_device(): from_chip = lax.ppermute(chip, 'bulk', both(within))  3.33 us
    pallas_call x1, Pallas kernels, per_device(): call(functools.partial(wanted_kernel, owned), shape(edges, places), [VMEM...  2.53 us
    pallas_call x1, Pallas kernels, per_device(): call(message_kernel, shape(owned, width), [VMEM] * 11, flops=1000000000,...  1.93 us
    pallas_call x1, Pallas kernels, per_device(): call(node_kernel, (shape(owned, width), shape(places, width)), [VMEM] * 1...  1.87 us
  transfers between devices with their start and end apart: 4, of which 2 were waited for; matrix products, arithmetic and copies ran while one was open for 0% of the time, Pallas kernels for 42%

profile of v11, /device:TPU:0, one launch (start us, length us, event | category | flops | bytes accessed | tf_op | source)
XLA Modules:
  0.0 54.1 jit_solution(6115963566831644291)
XLA Ops:
  0.0 1.3 %tile.2 = s32[16,4,128]{2,1,0:T(4,128)} broadcast(s32[4,128]{1,0:T(4,128)} %send_ref), dimensions={1,2} | broadcast | bytes 34816 | tf_op jit(solution)/shard_map/tile | solution.py:441
  1.3 7.4 %all-to-all-start = ((s32[16,4,128]{2,1,0:T(4,128)}), s32[16,4,128]{2,1,0:T(4,128)S(1)}, u32[]{:S(2)}, u32[]{:S(2)}) async-start(s32[16,4,128]{2,1,0:T(4,128)} %tile.2), calls=%async_computation | async-start | bytes 65536 | tf_op jit(solution)/shard_map/all_to_all | solution.py:441
  9.3 0.0 copy-start.12
  9.4 0.0 copy-start.2
  9.4 0.0 copy-start.3
  9.4 0.0 copy-start.4
  9.4 0.0 copy-start.6
  9.4 0.0 copy-start.7
  9.4 18.9 %shard_map.262 = (f32[64,512]{1,0:T(8,128)S(1)}, bf16[64,512]{1,0:T(8,128)(2,1)S(1)}, bf16[64,512]{1,0:T(8,128)(2,1)S(1)}) custom-call(s32[1]{0:T(128)} %bitcast.1.place_ref, bf16[474,512]{1,0:T(8,128)(2,1)} %first_hbm.1, bf16[474,2048]{1,0:T(8,128)(2,1)} %bitcast.26, bf16[512,512]{1,0:T(8,128)(2,1)} %second_hbm.1, bf16[512,512]{1,0:T(8,128)(2,1)} %send_weight_hbm.1, ...), custom_call_target="tpu_custom_call" | custom-call | flops 10000000000 | bytes 4000000 | tf_op jit(solution)/shard_map/pallas_call | solution.py:456
  28.3 0.0 copy-start
  28.3 0.0 copy-start.1
  28.4 0.8 %collective-permute-start = (bf16[64,512]{1,0:T(8,128)(2,1)S(1)}, bf16[64,512]{1,0:T(8,128)(2,1)S(1)}, u32[]{:S(2)}, u32[]{:S(2)}) collective-permute-start(bf16[64,512]{1,0:T(8,128)(2,1)S(1)} %get-tuple-element.17), channel_id=1, source_target_pairs={{1,2},{3,4},{5,6},{7,8},{9,10},{11,12},{13,14},{2,1},{4,3},{6,5},{... | collective-permute-start | bytes 196616 | tf_op jit(solution)/shard_map/ppermute | solution.py:479
  29.2 3.3 %collective-permute-start.1 = (bf16[64,512]{1,0:T(8,128)(2,1)S(1)}, bf16[64,512]{1,0:T(8,128)(2,1)S(1)}, u32[]{:S(2)}, u32[]{:S(2)}) collective-permute-start(bf16[64,512]{1,0:T(8,128)(2,1)S(1)} %get-tuple-element.18), channel_id=1, source_target_pairs={{0,1},{2,3},{4,5},{6,7},{8,9},{10,11},{12,13},{14,15},{1,0},{3,2},... | collective-permute-start | bytes 196616 | tf_op jit(solution)/shard_map/ppermute | solution.py:480
  32.5 0.0 all-to-all-done
  32.5 0.0 copy-done.12
  32.5 0.7 %shard_map.263.supply_ref = bf16[256,64]{1,0:T(8,128)(2,1)S(1)} custom-call(s32[1]{0:T(128)} %bitcast.1.place_ref, s32[1,1024]{1,0:T(1,128)S(1)} %bitcast.20, s32[64,128]{1,0:T(8,128)S(1)} %bitcast.16), custom_call_target="tpu_custom_call" | custom-call | flops 500000000 | bytes 500000 | tf_op jit(solution)/shard_map/pallas_call | solution.py:481
  33.2 0.0 copy-start.5
  33.2 0.0 collective-permute-done.from_cross_ref
  33.2 0.2 collective-permute-done.1.from_chip_ref
  33.4 0.0 copy-done.2
  33.4 0.0 copy-done.3
  33.4 0.0 copy-done.4
  33.4 0.0 copy-done.6
  33.4 0.0 copy-done.7
  33.4 0.0 copy-done
  33.4 0.0 copy-done.1
  33.4 1.9 %shard_map.264 = (bf16[64,512]{1,0:T(8,128)(2,1)S(1)}, bf16[256,512]{1,0:T(8,128)(2,1)}) custom-call(f32[64,512]{1,0:T(8,128)S(1)} %get-tuple-element.16.own_ref, bf16[64,512]{1,0:T(8,128)(2,1)S(1)} %collective-permute-done.from_cross_ref, bf16[64,512]{1,0:T(8,128)(2,1)S(1)} %collective-permute-done.1.from_chip_ref, bf16[64,512]{1,0:T(8,128)(2,1)S(1)} %copy-done.4, ...), custom_call_target="tpu_custom_call" | custom-call | flops 500000000 | bytes 4000000 | tf_op jit(solution)/shard_map/pallas_call | solution.py:488
  35.3 6.8 %all-to-all-start.1 = ((bf16[16,16,512]{2,1,0:T(8,128)(2,1)}), bf16[16,16,512]{2,1,0:T(8,128)(2,1)S(1)}, u32[]{:S(2)}, u32[]{:S(2)}) async-start(bf16[16,16,512]{2,1,0:T(8,128)(2,1)} %bitcast.9), calls=%async_computation.1 | async-start | bytes 524288 | tf_op jit(solution)/shard_map/all_to_all | solution.py:507
  42.1 0.0 copy-start.8
  42.1 0.0 copy-start.9
  42.2 0.0 copy-start.13
  42.2 0.0 copy-start.14
  42.2 0.0 copy-start.15
  42.2 0.0 copy-done.5
  42.2 2.5 %shard_map.265.wanted_ref = bf16[512,256]{1,0:T(8,128)(2,1)S(1)} custom-call(s32[1,1024]{1,0:T(1,128)S(1)} %bitcast.21, s32[4,128]{1,0:T(4,128)S(1)} %copy-done.5), custom_call_target="tpu_custom_call" | custom-call | flops 1000000000 | bytes 500000 | tf_op jit(solution)/shard_map/pallas_call | solution.py:509
  44.7 0.0 copy-start.10
  44.8 0.0 copy-start.11
  44.8 0.0 copy-start.16
  44.8 0.0 copy-done.8
  44.8 0.0 copy-done.9
  44.8 0.0 copy-done.13
  44.8 0.0 copy-done.14
  44.8 0.0 copy-done.15
  44.8 0.4 shard_map.266
  45.2 6.9 %all-to-all-done.1 = bf16[16,16,512]{2,1,0:T(8,128)(2,1)S(1)} async-done(((bf16[16,16,512]{2,1,0:T(8,128)(2,1)}), bf16[16,16,512]{2,1,0:T(8,128)(2,1)S(1)}, u32[]{:S(2)}, u32[]{:S(2)}) %all-to-all-start.1) | async-done | bytes 262176 | tf_op jit(solution)/shard_map/all_to_all | solution.py:507
  52.2 0.0 copy-done.10
  52.2 0.0 copy-done.11
  52.2 0.0 copy-done.16
  52.2 1.9 %shard_map.267 = bf16[64,512]{1,0:T(8,128)(2,1)} custom-call(bf16[512,256]{1,0:T(8,128)(2,1)S(1)} %shard_map.265.wanted_ref, bf16[256,512]{1,0:T(8,128)(2,1)S(1)} %bitcast.15, bf16[64,512]{1,0:T(8,128)(2,1)S(1)} %get-tuple-element.23.incoming_ref, bf16[512,128]{1,0:T(8,128)(2,1)S(1)} %get-tuple-element.24.pick_ref, ...), custom_call_target="tpu_custom_call" | custom-call | flops 1000000000 | bytes 4000000 | tf_op jit(solution)/shard_map/pallas_call | solution.py:537
Async XLA Ops:
  1.3 31.2 %all-to-all-start = ((s32[16,4,128]{2,1,0:T(4,128)}), s32[16,4,128]{2,1,0:T(4,128)S(1)}, u32[]{:S(2)}, u32[]{:S(2)}) async-start(s32[16,4,128]{2,1,0:T(4,128)} %tile.2), calls=%async_computation | async-start | bytes 65536 | tf_op jit(solution)/shard_map/all_to_all | solution.py:441
  9.3 23.1 %copy-start.12 = (s32[1024]{0:T(1024)S(1)}, s32[1024]{0:T(1024)}, u32[]{:S(2)}) copy-start(s32[1024]{0:T(1024)} %param.53) | copy-start | bytes 12292
  9.4 24.0 %copy-start.2 = (bf16[512,512]{1,0:T(8,128)(2,1)S(1)}, bf16[512,512]{1,0:T(8,128)(2,1)}, u32[]{:S(2)}) copy-start(bf16[512,512]{1,0:T(8,128)(2,1)} %node_out_ref.1) | copy-start | bytes 1572868
  9.4 24.0 %copy-start.3 = (bf16[512,512]{1,0:T(8,128)(2,1)S(1)}, bf16[512,512]{1,0:T(8,128)(2,1)}, u32[]{:S(2)}) copy-start(bf16[512,512]{1,0:T(8,128)(2,1)} %mesh_sender_ref.1) | copy-start | bytes 1572868
  9.4 24.0 %copy-start.4 = (bf16[64,512]{1,0:T(8,128)(2,1)S(1)}, bf16[64,512]{1,0:T(8,128)(2,1)}, u32[]{:S(2)}) copy-start(bf16[64,512]{1,0:T(8,128)(2,1)} %latent_ref.1) | copy-start | bytes 196612
  9.4 24.0 %copy-start.6 = (f32[512]{0:T(512)S(1)}, f32[512]{0:T(512)}, u32[]{:S(2)}) copy-start(f32[512]{0:T(512)} %param.37) | copy-start | bytes 6148
  9.4 24.0 %copy-start.7 = (f32[512]{0:T(512)S(1)}, f32[512]{0:T(512)}, u32[]{:S(2)}) copy-start(f32[512]{0:T(512)} %param.39) | copy-start | bytes 6148
  28.3 5.1 %copy-start = (bf16[1024,512]{1,0:T(8,128)(2,1)S(1)}, bf16[1024,512]{1,0:T(8,128)(2,1)}, u32[]{:S(2)}) copy-start(bf16[1024,512]{1,0:T(8,128)(2,1)} %node_input_ref.1) | copy-start | bytes 3145732
  28.3 5.1 %copy-start.1 = (bf16[512,512]{1,0:T(8,128)(2,1)S(1)}, bf16[512,512]{1,0:T(8,128)(2,1)}, u32[]{:S(2)}) copy-start(bf16[512,512]{1,0:T(8,128)(2,1)} %edge_out_ref.1) | copy-start | bytes 1572868
  28.4 4.8 %collective-permute-start = (bf16[64,512]{1,0:T(8,128)(2,1)S(1)}, bf16[64,512]{1,0:T(8,128)(2,1)S(1)}, u32[]{:S(2)}, u32[]{:S(2)}) collective-permute-start(bf16[64,512]{1,0:T(8,128)(2,1)S(1)} %get-tuple-element.17), channel_id=1, source_target_pairs={{1,2},{3,4},{5,6},{7,8},{9,10},{11,12},{13,14},{2,1},{4,3},{6,5},{... | collective-permute-start | bytes 196616 | tf_op jit(solution)/shard_map/ppermute | solution.py:479
  29.2 4.2 %collective-permute-start.1 = (bf16[64,512]{1,0:T(8,128)(2,1)S(1)}, bf16[64,512]{1,0:T(8,128)(2,1)S(1)}, u32[]{:S(2)}, u32[]{:S(2)}) collective-permute-start(bf16[64,512]{1,0:T(8,128)(2,1)S(1)} %get-tuple-element.18), channel_id=1, source_target_pairs={{0,1},{2,3},{4,5},{6,7},{8,9},{10,11},{12,13},{14,15},{1,0},{3,2},... | collective-permute-start | bytes 196616 | tf_op jit(solution)/shard_map/ppermute | solution.py:480
  33.2 9.0 %copy-start.5 = (s32[4,128]{1,0:T(4,128)S(1)}, s32[4,128]{1,0:T(4,128)}, u32[]{:S(2)}) copy-start(s32[4,128]{1,0:T(4,128)} %send_ref) | copy-start | bytes 6148
  35.3 16.9 %all-to-all-start.1 = ((bf16[16,16,512]{2,1,0:T(8,128)(2,1)}), bf16[16,16,512]{2,1,0:T(8,128)(2,1)S(1)}, u32[]{:S(2)}, u32[]{:S(2)}) async-start(bf16[16,16,512]{2,1,0:T(8,128)(2,1)} %bitcast.9), calls=%async_computation.1 | async-start | bytes 524288 | tf_op jit(solution)/shard_map/all_to_all | solution.py:507
  42.1 2.6 %copy-start.8 = (bf16[1024,512]{1,0:T(8,128)(2,1)S(1)}, bf16[1024,512]{1,0:T(8,128)(2,1)}, u32[]{:S(2)}) copy-start(bf16[1024,512]{1,0:T(8,128)(2,1)} %update_input_ref.3) | copy-start | bytes 3145732
  42.1 2.6 %copy-start.9 = (bf16[512,512]{1,0:T(8,128)(2,1)S(1)}, bf16[512,512]{1,0:T(8,128)(2,1)}, u32[]{:S(2)}) copy-start(bf16[512,512]{1,0:T(8,128)(2,1)} %mesh_receiver_ref.1) | copy-start | bytes 1572868
  42.2 2.6 %copy-start.13 = (s32[4,128]{1,0:T(4,128)S(1)}, s32[4,128]{1,0:T(4,128)}, u32[]{:S(2)}) copy-start(s32[4,128]{1,0:T(4,128)} %recv_ref.1) | copy-start | bytes 6148
  42.2 2.6 %copy-start.14 = (f32[512]{0:T(512)S(1)}, f32[512]{0:T(512)}, u32[]{:S(2)}) copy-start(f32[512]{0:T(512)} %param.42) | copy-start | bytes 6148
  42.2 2.6 %copy-start.15 = (f32[512]{0:T(512)S(1)}, f32[512]{0:T(512)}, u32[]{:S(2)}) copy-start(f32[512]{0:T(512)} %param.45) | copy-start | bytes 6148
  44.7 7.4 %copy-start.10 = (bf16[512,512]{1,0:T(8,128)(2,1)S(1)}, bf16[512,512]{1,0:T(8,128)(2,1)}, u32[]{:S(2)}) copy-start(bf16[512,512]{1,0:T(8,128)(2,1)} %message_out_ref.1) | copy-start | bytes 1572868
  44.8 7.4 %copy-start.11 = (bf16[512,512]{1,0:T(8,128)(2,1)S(1)}, bf16[512,512]{1,0:T(8,128)(2,1)}, u32[]{:S(2)}) copy-start(bf16[512,512]{1,0:T(8,128)(2,1)} %update_out_ref.1) | copy-start | bytes 1572868
  44.8 7.4 %copy-start.16 = (f32[512]{0:T(512)S(1)}, f32[512]{0:T(512)}, u32[]{:S(2)}) copy-start(f32[512]{0:T(512)} %param.47) | copy-start | bytes 6148

commit v12 on v8

--- a/solution.py
+++ b/solution.py
@@ -16,7 +16,8 @@
 VMEM = pltpu.VMEM
 SMEM = pltpu.SMEM
 HBM = pltpu.HBM
-GRID_STEPS = 4
+GRID_STEPS = 2
+CHUNK_BLOCKS = 4
 MEBI = 1024 * 1024
 
 
@@ -183,7 +184,7 @@
     feat_weight = 0.5 * feat_weight_ref[...].astype(F32)
     feat_weight = jnp.concatenate([feat_weight, jnp.zeros((8 - feats, width), F32)], axis=0)
     feat_weight = feat_weight.astype(BF16)
-    group = 2 if blocks % 4 == 0 else 1
+    group = CHUNK_BLOCKS
     chunks = blocks // group
     part_rows = 64
 
@@ -460,9 +461,9 @@
         + [
             SMEM(g2m_send.shape, I32),
             VMEM((grid_rows * (width // LANES), LANES), F32),
-            VMEM((2 * g2m_send.shape[1] * (width // LANES), LANES), F32),
-            VMEM((2 * g2m_send.shape[1] * (width // LANES), LANES), F32),
-            VMEM((2 * g2m_send.shape[1], width), BF16),
+            VMEM((CHUNK_BLOCKS * g2m_send.shape[1] * (width // LANES), LANES), F32),
+            VMEM((CHUNK_BLOCKS * g2m_send.shape[1] * (width // LANES), LANES), F32),
+            VMEM((CHUNK_BLOCKS * g2m_send.shape[1], width), BF16),
             VMEM((3 * owned, LANES), I32),
             VMEM((3 * owned, width), F32),
             pltpu.SemaphoreType.DMA((len(operands) + GRID_STEPS,)),
@@ -503,7 +504,6 @@
         mesh_sender,
         supply,
     )
-    rows = pltpu.with_memory_space_constraint(rows, VMEM)
     piece = lax.all_to_all(rows, "bulk", 0, 0, tiled=True)
     mesh_send, _ = lax.optimization_barrier((mesh_send, encoded))
     wanted = call(

time: 48.8 us -> 46.9 us (0.961)
  Pallas kernels: 20.6 us -> 18.8 us
    pallas_call x1, Pallas kernels: 13.2 us -> 11.4 us  [per_device(): call(edge_kernel, (shape(owned, width, kind=F32), shape(owned, width), sh...]
  transfers between devices with their start and end apart: 4 -> 4, of which waited for: 2 -> 2; matrix products, arithmetic and copies ran while one was open for 0% -> 0% of each run, Pallas kernels for 35% -> 32%
where the time goes in v12:
time: 46.9 us; the launch traced here: 46.6 us
  Pallas kernels  18.8 us (40%)
  starting transfers between devices  18.3 us (39%)
  waiting for transfers between devices  7.16 us (15%)
  local copies, waits for them, and re-layouts  1.41 us (3%)
  between operations  0.93 us (2%)
    pallas_call x1, Pallas kernels, per_device(): call(edge_kernel, (shape(owned, width, kind=F32), shape(owned, width), sh...  11.4 us
    all_to_all x1, starting transfers between devices, per_device(): lax.all_to_all(jnp.tile(mesh_send, (devices, 1)), 'bulk', 0, 0, tiled=True)  7.39 us
    all_to_all x1, waiting for transfers between devices, per_device(): piece = lax.all_to_all(rows, 'bulk', 0, 0, tiled=True)  6.94 us
    all_to_all x1, starting transfers between devices, per_device(): piece = lax.all_to_all(rows, 'bulk', 0, 0, tiled=True)  6.77 us
    ppermute x1, starting transfers between devices, per_device(): from_chip = lax.ppermute(chip, 'bulk', both(within))  3.37 us
    pallas_call x1, Pallas kernels, per_device(): call(functools.partial(wanted_kernel, owned), shape(edges, places), [VMEM...  2.53 us
    pallas_call x1, Pallas kernels, per_device(): call(message_kernel, shape(owned, width), [VMEM] * 11, flops=1000000000,...  1.93 us
    pallas_call x1, Pallas kernels, per_device(): call(node_kernel, (shape(owned, width), shape(places, width)), [VMEM] * 1...  1.87 us
  transfers between devices with their start and end apart: 4, of which 2 were waited for; matrix products, arithmetic and copies ran while one was open for 0% of the time, Pallas kernels for 32%

profile of v12, /device:TPU:0, one launch (start us, length us, event | category | flops | bytes accessed | tf_op | source)
XLA Modules:
  0.0 46.6 jit_solution(10250269538405845441)
XLA Ops:
  0.0 1.3 %tile.2 = s32[16,4,128]{2,1,0:T(4,128)} broadcast(s32[4,128]{1,0:T(4,128)} %send_ref), dimensions={1,2} | broadcast | bytes 34816 | tf_op jit(solution)/shard_map/tile | solution.py:441
  1.3 7.4 %all-to-all-start = ((s32[16,4,128]{2,1,0:T(4,128)}), s32[16,4,128]{2,1,0:T(4,128)S(1)}, u32[]{:S(2)}, u32[]{:S(2)}) async-start(s32[16,4,128]{2,1,0:T(4,128)} %tile.2), calls=%async_computation | async-start | bytes 65536 | tf_op jit(solution)/shard_map/all_to_all | solution.py:441
  9.3 0.0 copy-start.12
  9.4 0.0 copy-start.2
  9.4 0.0 copy-start.3
  9.4 0.0 copy-start.4
  9.4 0.0 copy-start.6
  9.4 0.0 copy-start.7
  9.4 11.4 %shard_map.262 = (f32[64,512]{1,0:T(8,128)S(1)}, bf16[64,512]{1,0:T(8,128)(2,1)S(1)}, bf16[64,512]{1,0:T(8,128)(2,1)S(1)}) custom-call(s32[1]{0:T(128)} %bitcast.1.place_ref, bf16[474,512]{1,0:T(8,128)(2,1)} %first_hbm.1, bf16[474,2048]{1,0:T(8,128)(2,1)} %bitcast.26, bf16[512,512]{1,0:T(8,128)(2,1)} %second_hbm.1, bf16[512,512]{1,0:T(8,128)(2,1)} %send_weight_hbm.1, ...), custom_call_target="tpu_custom_call" | custom-call | flops 10000000000 | bytes 4000000 | tf_op jit(solution)/shard_map/pallas_call | solution.py:456
  20.8 0.0 copy-start
  20.8 0.0 copy-start.1
  20.9 0.8 %collective-permute-start = (bf16[64,512]{1,0:T(8,128)(2,1)S(1)}, bf16[64,512]{1,0:T(8,128)(2,1)S(1)}, u32[]{:S(2)}, u32[]{:S(2)}) collective-permute-start(bf16[64,512]{1,0:T(8,128)(2,1)S(1)} %get-tuple-element.17), channel_id=1, source_target_pairs={{1,2},{3,4},{5,6},{7,8},{9,10},{11,12},{13,14},{2,1},{4,3},{6,5},{... | collective-permute-start | bytes 196616 | tf_op jit(solution)/shard_map/ppermute | solution.py:479
  21.7 3.4 %collective-permute-start.1 = (bf16[64,512]{1,0:T(8,128)(2,1)S(1)}, bf16[64,512]{1,0:T(8,128)(2,1)S(1)}, u32[]{:S(2)}, u32[]{:S(2)}) collective-permute-start(bf16[64,512]{1,0:T(8,128)(2,1)S(1)} %get-tuple-element.18), channel_id=1, source_target_pairs={{0,1},{2,3},{4,5},{6,7},{8,9},{10,11},{12,13},{14,15},{1,0},{3,2},... | collective-permute-start | bytes 196616 | tf_op jit(solution)/shard_map/ppermute | solution.py:480
  25.0 0.0 all-to-all-done
  25.0 0.0 copy-done.12
  25.0 0.7 %shard_map.263.supply_ref = bf16[256,64]{1,0:T(8,128)(2,1)S(1)} custom-call(s32[1]{0:T(128)} %bitcast.1.place_ref, s32[1,1024]{1,0:T(1,128)S(1)} %bitcast.20, s32[64,128]{1,0:T(8,128)S(1)} %bitcast.16), custom_call_target="tpu_custom_call" | custom-call | flops 500000000 | bytes 500000 | tf_op jit(solution)/shard_map/pallas_call | solution.py:481
  25.7 0.0 copy-start.5
  25.7 0.0 collective-permute-done.from_cross_ref
  25.7 0.2 collective-permute-done.1.from_chip_ref
  25.9 0.0 copy-done.2
  25.9 0.0 copy-done.3
  25.9 0.0 copy-done.4
  25.9 0.0 copy-done.6
  25.9 0.0 copy-done.7
  26.0 0.0 copy-done
  26.0 0.0 copy-done.1
  26.0 1.9 %shard_map.264 = (bf16[64,512]{1,0:T(8,128)(2,1)S(1)}, bf16[256,512]{1,0:T(8,128)(2,1)}) custom-call(f32[64,512]{1,0:T(8,128)S(1)} %get-tuple-element.16.own_ref, bf16[64,512]{1,0:T(8,128)(2,1)S(1)} %collective-permute-done.from_cross_ref, bf16[64,512]{1,0:T(8,128)(2,1)S(1)} %collective-permute-done.1.from_chip_ref, bf16[64,512]{1,0:T(8,128)(2,1)S(1)} %copy-done.4, ...), custom_call_target="tpu_custom_call" | custom-call | flops 500000000 | bytes 4000000 | tf_op jit(solution)/shard_map/pallas_call | solution.py:488
  27.8 6.8 %all-to-all-start.1 = ((bf16[16,16,512]{2,1,0:T(8,128)(2,1)}), bf16[16,16,512]{2,1,0:T(8,128)(2,1)S(1)}, u32[]{:S(2)}, u32[]{:S(2)}) async-start(bf16[16,16,512]{2,1,0:T(8,128)(2,1)} %bitcast.9), calls=%async_computation.1 | async-start | bytes 524288 | tf_op jit(solution)/shard_map/all_to_all | solution.py:507
  34.6 0.0 copy-start.8
  34.6 0.0 copy-start.9
  34.6 0.0 copy-start.13
  34.7 0.0 copy-start.14
  34.7 0.0 copy-start.15
  34.7 0.0 copy-done.5
  34.7 2.5 %shard_map.265.wanted_ref = bf16[512,256]{1,0:T(8,128)(2,1)S(1)} custom-call(s32[1,1024]{1,0:T(1,128)S(1)} %bitcast.21, s32[4,128]{1,0:T(4,128)S(1)} %copy-done.5), custom_call_target="tpu_custom_call" | custom-call | flops 1000000000 | bytes 500000 | tf_op jit(solution)/shard_map/pallas_call | solution.py:509
  37.2 0.0 copy-start.10
  37.2 0.0 copy-start.11
  37.3 0.0 copy-start.16
  37.3 0.0 copy-done.8
  37.3 0.0 copy-done.9
  37.3 0.0 copy-done.13
  37.3 0.0 copy-done.14
  37.3 0.0 copy-done.15
  37.3 0.4 shard_map.266
  37.7 6.9 %all-to-all-done.1 = bf16[16,16,512]{2,1,0:T(8,128)(2,1)S(1)} async-done(((bf16[16,16,512]{2,1,0:T(8,128)(2,1)}), bf16[16,16,512]{2,1,0:T(8,128)(2,1)S(1)}, u32[]{:S(2)}, u32[]{:S(2)}) %all-to-all-start.1) | async-done | bytes 262176 | tf_op jit(solution)/shard_map/all_to_all | solution.py:507
  44.7 0.0 copy-done.10
  44.7 0.0 copy-done.11
  44.7 0.0 copy-done.16
  44.7 1.9 %shard_map.267 = bf16[64,512]{1,0:T(8,128)(2,1)} custom-call(bf16[512,256]{1,0:T(8,128)(2,1)S(1)} %shard_map.265.wanted_ref, bf16[256,512]{1,0:T(8,128)(2,1)S(1)} %bitcast.15, bf16[64,512]{1,0:T(8,128)(2,1)S(1)} %get-tuple-element.23.incoming_ref, bf16[512,128]{1,0:T(8,128)(2,1)S(1)} %get-tuple-element.24.pick_ref, ...), custom_call_target="tpu_custom_call" | custom-call | flops 1000000000 | bytes 4000000 | tf_op jit(solution)/shard_map/pallas_call | solution.py:537
Async XLA Ops:
  1.3 23.7 %all-to-all-start = ((s32[16,4,128]{2,1,0:T(4,128)}), s32[16,4,128]{2,1,0:T(4,128)S(1)}, u32[]{:S(2)}, u32[]{:S(2)}) async-start(s32[16,4,128]{2,1,0:T(4,128)} %tile.2), calls=%async_computation | async-start | bytes 65536 | tf_op jit(solution)/shard_map/all_to_all | solution.py:441
  9.3 15.7 %copy-start.12 = (s32[1024]{0:T(1024)S(1)}, s32[1024]{0:T(1024)}, u32[]{:S(2)}) copy-start(s32[1024]{0:T(1024)} %param.53) | copy-start | bytes 12292
  9.4 16.6 %copy-start.2 = (bf16[512,512]{1,0:T(8,128)(2,1)S(1)}, bf16[512,512]{1,0:T(8,128)(2,1)}, u32[]{:S(2)}) copy-start(bf16[512,512]{1,0:T(8,128)(2,1)} %node_out_ref.1) | copy-start | bytes 1572868
  9.4 16.6 %copy-start.3 = (bf16[512,512]{1,0:T(8,128)(2,1)S(1)}, bf16[512,512]{1,0:T(8,128)(2,1)}, u32[]{:S(2)}) copy-start(bf16[512,512]{1,0:T(8,128)(2,1)} %mesh_sender_ref.1) | copy-start | bytes 1572868
  9.4 16.6 %copy-start.4 = (bf16[64,512]{1,0:T(8,128)(2,1)S(1)}, bf16[64,512]{1,0:T(8,128)(2,1)}, u32[]{:S(2)}) copy-start(bf16[64,512]{1,0:T(8,128)(2,1)} %latent_ref.1) | copy-start | bytes 196612
  9.4 16.6 %copy-start.6 = (f32[512]{0:T(512)S(1)}, f32[512]{0:T(512)}, u32[]{:S(2)}) copy-start(f32[512]{0:T(512)} %param.37) | copy-start | bytes 6148
  9.4 16.5 %copy-start.7 = (f32[512]{0:T(512)S(1)}, f32[512]{0:T(512)}, u32[]{:S(2)}) copy-start(f32[512]{0:T(512)} %param.39) | copy-start | bytes 6148
  20.8 5.1 %copy-start = (bf16[1024,512]{1,0:T(8,128)(2,1)S(1)}, bf16[1024,512]{1,0:T(8,128)(2,1)}, u32[]{:S(2)}) copy-start(bf16[1024,512]{1,0:T(8,128)(2,1)} %node_input_ref.1) | copy-start | bytes 3145732
  20.8 5.1 %copy-start.1 = (bf16[512,512]{1,0:T(8,128)(2,1)S(1)}, bf16[512,512]{1,0:T(8,128)(2,1)}, u32[]{:S(2)}) copy-start(bf16[512,512]{1,0:T(8,128)(2,1)} %edge_out_ref.1) | copy-start | bytes 1572868
  20.9 4.9 %collective-permute-start = (bf16[64,512]{1,0:T(8,128)(2,1)S(1)}, bf16[64,512]{1,0:T(8,128)(2,1)S(1)}, u32[]{:S(2)}, u32[]{:S(2)}) collective-permute-start(bf16[64,512]{1,0:T(8,128)(2,1)S(1)} %get-tuple-element.17), channel_id=1, source_target_pairs={{1,2},{3,4},{5,6},{7,8},{9,10},{11,12},{13,14},{2,1},{4,3},{6,5},{... | collective-permute-start | bytes 196616 | tf_op jit(solution)/shard_map/ppermute | solution.py:479
  21.7 4.3 %collective-permute-start.1 = (bf16[64,512]{1,0:T(8,128)(2,1)S(1)}, bf16[64,512]{1,0:T(8,128)(2,1)S(1)}, u32[]{:S(2)}, u32[]{:S(2)}) collective-permute-start(bf16[64,512]{1,0:T(8,128)(2,1)S(1)} %get-tuple-element.18), channel_id=1, source_target_pairs={{0,1},{2,3},{4,5},{6,7},{8,9},{10,11},{12,13},{14,15},{1,0},{3,2},... | collective-permute-start | bytes 196616 | tf_op jit(solution)/shard_map/ppermute | solution.py:480
  25.7 9.0 %copy-start.5 = (s32[4,128]{1,0:T(4,128)S(1)}, s32[4,128]{1,0:T(4,128)}, u32[]{:S(2)}) copy-start(s32[4,128]{1,0:T(4,128)} %send_ref) | copy-start | bytes 6148
  27.8 16.8 %all-to-all-start.1 = ((bf16[16,16,512]{2,1,0:T(8,128)(2,1)}), bf16[16,16,512]{2,1,0:T(8,128)(2,1)S(1)}, u32[]{:S(2)}, u32[]{:S(2)}) async-start(bf16[16,16,512]{2,1,0:T(8,128)(2,1)} %bitcast.9), calls=%async_computation.1 | async-start | bytes 524288 | tf_op jit(solution)/shard_map/all_to_all | solution.py:507
  34.6 2.6 %copy-start.8 = (bf16[1024,512]{1,0:T(8,128)(2,1)S(1)}, bf16[1024,512]{1,0:T(8,128)(2,1)}, u32[]{:S(2)}) copy-start(bf16[1024,512]{1,0:T(8,128)(2,1)} %update_input_ref.3) | copy-start | bytes 3145732
  34.6 2.6 %copy-start.9 = (bf16[512,512]{1,0:T(8,128)(2,1)S(1)}, bf16[512,512]{1,0:T(8,128)(2,1)}, u32[]{:S(2)}) copy-start(bf16[512,512]{1,0:T(8,128)(2,1)} %mesh_receiver_ref.1) | copy-start | bytes 1572868
  34.6 2.6 %copy-start.13 = (s32[4,128]{1,0:T(4,128)S(1)}, s32[4,128]{1,0:T(4,128)}, u32[]{:S(2)}) copy-start(s32[4,128]{1,0:T(4,128)} %recv_ref.1) | copy-start | bytes 6148
  34.7 2.6 %copy-start.14 = (f32[512]{0:T(512)S(1)}, f32[512]{0:T(512)}, u32[]{:S(2)}) copy-start(f32[512]{0:T(512)} %param.42) | copy-start | bytes 6148
  34.7 2.6 %copy-start.15 = (f32[512]{0:T(512)S(1)}, f32[512]{0:T(512)}, u32[]{:S(2)}) copy-start(f32[512]{0:T(512)} %param.45) | copy-start | bytes 6148
  37.2 7.4 %copy-start.10 = (bf16[512,512]{1,0:T(8,128)(2,1)S(1)}, bf16[512,512]{1,0:T(8,128)(2,1)}, u32[]{:S(2)}) copy-start(bf16[512,512]{1,0:T(8,128)(2,1)} %message_out_ref.1) | copy-start | bytes 1572868
  37.2 7.4 %copy-start.11 = (bf16[512,512]{1,0:T(8,128)(2,1)S(1)}, bf16[512,512]{1,0:T(8,128)(2,1)}, u32[]{:S(2)}) copy-start(bf16[512,512]{1,0:T(8,128)(2,1)} %update_out_ref.1) | copy-start | bytes 1572868
  37.3 7.4 %copy-start.16 = (f32[512]{0:T(512)S(1)}, f32[512]{0:T(512)}, u32[]{:S(2)}) copy-start(f32[512]{0:T(512)} %param.47) | copy-start | bytes 6148

commit v13 on v12

--- a/solution.py
+++ b/solution.py
@@ -91,7 +91,8 @@
     table,
     even_rows,
     odd_rows,
-    hidden_ref,
+    even_hidden,
+    odd_hidden,
     ids_ref,
     total,
     sems,
@@ -210,28 +211,33 @@
             axis=1,
         )
 
-    def work(chunk, source, target):
+    def add_sums(chunk, hidden):
+        here = [chunk * group + b for b in range(group)]
+        receivers = [jnp.where(b < used, recv_ref[pl.ds(b, 1), :], -2) for b in here]
+        spread = jnp.concatenate([(ids_ref[...] == row).astype(F32) for row in receivers], axis=1)
+        total[...] += mm(spread.astype(BF16), hidden[...])
+
+    def work(chunk, source, target, hidden, hidden_before):
         here = [chunk * group + b for b in range(group)]
         feat = jnp.concatenate([feat_ref[b] for b in here], axis=1)
         feat = jnp.concatenate([feat, jnp.zeros((8 - feats, feat.shape[1]), F32)], axis=0)
         extra = mm(feat.T.astype(BF16), feat_weight)
+        add_sums(jnp.maximum(chunk - 1, 0), hidden_before)
         after = jnp.minimum(chunk + 1, chunks - 1)
         for first in range(0, group * block_edges, part_rows):
             gather(after, range(first, first + part_rows), target)
             half = rows_of(source, first, part_rows) + extra[first : first + part_rows]
-            hidden_ref[first : first + part_rows, :] = silu_half(half).astype(BF16)
-        receivers = [jnp.where(b < used, recv_ref[pl.ds(b, 1), :], -2) for b in here]
-        spread = jnp.concatenate([(ids_ref[...] == row).astype(F32) for row in receivers], axis=1)
-        spread = spread.astype(BF16)
-        total[...] += mm(spread, hidden_ref[...])
+            hidden[first : first + part_rows, :] = silu_half(half).astype(BF16)
 
     def edge_step(step, carry):
-        work(2 * step, even_rows, odd_rows)
-        work(2 * step + 1, odd_rows, even_rows)
+        work(2 * step, even_rows, odd_rows, even_hidden, odd_hidden)
+        work(2 * step + 1, odd_rows, even_rows, odd_hidden, even_hidden)
         return carry
 
+    odd_hidden[...] = jnp.zeros_like(odd_hidden)
     gather(0, range(group * block_edges), even_rows)
     lax.fori_loop(0, chunks // 2, edge_step, 0)
+    add_sums(chunks - 1, odd_hidden)
     odd = place % 2 == 1
     below, above = total[:owned].astype(BF16), total[2 * owned :].astype(BF16)
     own_ref[...] = total[owned : 2 * owned]
@@ -463,6 +469,7 @@
             VMEM((grid_rows * (width // LANES), LANES), F32),
             VMEM((CHUNK_BLOCKS * g2m_send.shape[1] * (width // LANES), LANES), F32),
             VMEM((CHUNK_BLOCKS * g2m_send.shape[1] * (width // LANES), LANES), F32),
+            VMEM((CHUNK_BLOCKS * g2m_send.shape[1], width), BF16),
             VMEM((CHUNK_BLOCKS * g2m_send.shape[1], width), BF16),
             VMEM((3 * owned, LANES), I32),
             VMEM((3 * owned, width), F32),

time: 46.9 us -> 46.9 us (level)
  no operation moved by 1% of the time
where the time goes in v13:
time: 46.9 us; the launch traced here: 46.6 us
  Pallas kernels  18.8 us (40%)
  starting transfers between devices  18.3 us (39%)
  waiting for transfers between devices  7.16 us (15%)
  local copies, waits for them, and re-layouts  1.41 us (3%)
  between operations  0.93 us (2%)
    pallas_call x1, Pallas kernels, per_device(): call(edge_kernel, (shape(owned, width, kind=F32), shape(owned, width), sh...  11.4 us
    all_to_all x1, starting transfers between devices, per_device(): lax.all_to_all(jnp.tile(mesh_send, (devices, 1)), 'bulk', 0, 0, tiled=True)  7.39 us
    all_to_all x1, waiting for transfers between devices, per_device(): piece = lax.all_to_all(rows, 'bulk', 0, 0, tiled=True)  6.94 us
    all_to_all x1, starting transfers between devices, per_device(): piece = lax.all_to_all(rows, 'bulk', 0, 0, tiled=True)  6.78 us
    ppermute x1, starting transfers between devices, per_device(): from_chip = lax.ppermute(chip, 'bulk', both(within))  3.35 us
    pallas_call x1, Pallas kernels, per_device(): call(functools.partial(wanted_kernel, owned), shape(edges, places), [VMEM...  2.53 us
    pallas_call x1, Pallas kernels, per_device(): call(message_kernel, shape(owned, width), [VMEM] * 11, flops=1000000000,...  1.93 us
    pallas_call x1, Pallas kernels, per_device(): call(node_kernel, (shape(owned, width), shape(places, width)), [VMEM] * 1...  1.88 us
  transfers between devices with their start and end apart: 4, of which 2 were waited for; matrix products, arithmetic and copies ran while one was open for 0% of the time, Pallas kernels for 32%

profile of v13, /device:TPU:0, one launch (start us, length us, event | category | flops | bytes accessed | tf_op | source)
XLA Modules:
  0.0 46.6 jit_solution(17764538697423316792)
XLA Ops:
  0.0 1.3 %tile.2 = s32[16,4,128]{2,1,0:T(4,128)} broadcast(s32[4,128]{1,0:T(4,128)} %send_ref), dimensions={1,2} | broadcast | bytes 34816 | tf_op jit(solution)/shard_map/tile | solution.py:447
  1.3 7.4 %all-to-all-start = ((s32[16,4,128]{2,1,0:T(4,128)}), s32[16,4,128]{2,1,0:T(4,128)S(1)}, u32[]{:S(2)}, u32[]{:S(2)}) async-start(s32[16,4,128]{2,1,0:T(4,128)} %tile.2), calls=%async_computation | async-start | bytes 65536 | tf_op jit(solution)/shard_map/all_to_all | solution.py:447
  9.3 0.0 copy-start.12
  9.4 0.0 copy-start.2
  9.4 0.0 copy-start.3
  9.4 0.0 copy-start.4
  9.4 0.0 copy-start.6
  9.4 0.0 copy-start.7
  9.4 11.4 %shard_map.262 = (f32[64,512]{1,0:T(8,128)S(1)}, bf16[64,512]{1,0:T(8,128)(2,1)S(1)}, bf16[64,512]{1,0:T(8,128)(2,1)S(1)}) custom-call(s32[1]{0:T(128)} %bitcast.1.place_ref, bf16[474,512]{1,0:T(8,128)(2,1)} %first_hbm.1, bf16[474,2048]{1,0:T(8,128)(2,1)} %bitcast.26, bf16[512,512]{1,0:T(8,128)(2,1)} %second_hbm.1, bf16[512,512]{1,0:T(8,128)(2,1)} %send_weight_hbm.1, ...), custom_call_target="tpu_custom_call" | custom-call | flops 10000000000 | bytes 4000000 | tf_op jit(solution)/shard_map/pallas_call | solution.py:462
  20.8 0.0 copy-start
  20.8 0.0 copy-start.1
  20.8 0.8 %collective-permute-start = (bf16[64,512]{1,0:T(8,128)(2,1)S(1)}, bf16[64,512]{1,0:T(8,128)(2,1)S(1)}, u32[]{:S(2)}, u32[]{:S(2)}) collective-permute-start(bf16[64,512]{1,0:T(8,128)(2,1)S(1)} %get-tuple-element.17), channel_id=1, source_target_pairs={{1,2},{3,4},{5,6},{7,8},{9,10},{11,12},{13,14},{2,1},{4,3},{6,5},{... | collective-permute-start | bytes 196616 | tf_op jit(solution)/shard_map/ppermute | solution.py:486
  21.6 3.3 %collective-permute-start.1 = (bf16[64,512]{1,0:T(8,128)(2,1)S(1)}, bf16[64,512]{1,0:T(8,128)(2,1)S(1)}, u32[]{:S(2)}, u32[]{:S(2)}) collective-permute-start(bf16[64,512]{1,0:T(8,128)(2,1)S(1)} %get-tuple-element.18), channel_id=1, source_target_pairs={{0,1},{2,3},{4,5},{6,7},{8,9},{10,11},{12,13},{14,15},{1,0},{3,2},... | collective-permute-start | bytes 196616 | tf_op jit(solution)/shard_map/ppermute | solution.py:487
  25.0 0.0 all-to-all-done
  25.0 0.0 copy-done.12
  25.0 0.7 %shard_map.263.supply_ref = bf16[256,64]{1,0:T(8,128)(2,1)S(1)} custom-call(s32[1]{0:T(128)} %bitcast.1.place_ref, s32[1,1024]{1,0:T(1,128)S(1)} %bitcast.20, s32[64,128]{1,0:T(8,128)S(1)} %bitcast.16), custom_call_target="tpu_custom_call" | custom-call | flops 500000000 | bytes 500000 | tf_op jit(solution)/shard_map/pallas_call | solution.py:488
  25.6 0.0 copy-start.5
  25.6 0.0 collective-permute-done.from_cross_ref
  25.7 0.2 collective-permute-done.1.from_chip_ref
  25.9 0.0 copy-done.2
  25.9 0.0 copy-done.3
  25.9 0.0 copy-done.4
  25.9 0.0 copy-done.6
  25.9 0.0 copy-done.7
  25.9 0.0 copy-done
  25.9 0.0 copy-done.1
  25.9 1.9 %shard_map.264 = (bf16[64,512]{1,0:T(8,128)(2,1)S(1)}, bf16[256,512]{1,0:T(8,128)(2,1)}) custom-call(f32[64,512]{1,0:T(8,128)S(1)} %get-tuple-element.16.own_ref, bf16[64,512]{1,0:T(8,128)(2,1)S(1)} %collective-permute-done.from_cross_ref, bf16[64,512]{1,0:T(8,128)(2,1)S(1)} %collective-permute-done.1.from_chip_ref, bf16[64,512]{1,0:T(8,128)(2,1)S(1)} %copy-done.4, ...), custom_call_target="tpu_custom_call" | custom-call | flops 500000000 | bytes 4000000 | tf_op jit(solution)/shard_map/pallas_call | solution.py:495
  27.8 6.8 %all-to-all-start.1 = ((bf16[16,16,512]{2,1,0:T(8,128)(2,1)}), bf16[16,16,512]{2,1,0:T(8,128)(2,1)S(1)}, u32[]{:S(2)}, u32[]{:S(2)}) async-start(bf16[16,16,512]{2,1,0:T(8,128)(2,1)} %bitcast.9), calls=%async_computation.1 | async-start | bytes 524288 | tf_op jit(solution)/shard_map/all_to_all | solution.py:514
  34.6 0.0 copy-start.8
  34.6 0.0 copy-start.9
  34.6 0.0 copy-start.13
  34.6 0.0 copy-start.14
  34.6 0.0 copy-start.15
  34.6 0.0 copy-done.5
  34.6 2.5 %shard_map.265.wanted_ref = bf16[512,256]{1,0:T(8,128)(2,1)S(1)} custom-call(s32[1,1024]{1,0:T(1,128)S(1)} %bitcast.21, s32[4,128]{1,0:T(4,128)S(1)} %copy-done.5), custom_call_target="tpu_custom_call" | custom-call | flops 1000000000 | bytes 500000 | tf_op jit(solution)/shard_map/pallas_call | solution.py:516
  37.2 0.0 copy-start.10
  37.2 0.0 copy-start.11
  37.2 0.0 copy-start.16
  37.2 0.0 copy-done.8
  37.2 0.0 copy-done.9
  37.2 0.0 copy-done.13
  37.3 0.0 copy-done.14
  37.3 0.0 copy-done.15
  37.3 0.4 shard_map.266
  37.7 6.9 %all-to-all-done.1 = bf16[16,16,512]{2,1,0:T(8,128)(2,1)S(1)} async-done(((bf16[16,16,512]{2,1,0:T(8,128)(2,1)}), bf16[16,16,512]{2,1,0:T(8,128)(2,1)S(1)}, u32[]{:S(2)}, u32[]{:S(2)}) %all-to-all-start.1) | async-done | bytes 262176 | tf_op jit(solution)/shard_map/all_to_all | solution.py:514
  44.6 0.0 copy-done.10
  44.6 0.0 copy-done.11
  44.6 0.0 copy-done.16
  44.6 1.9 %shard_map.267 = bf16[64,512]{1,0:T(8,128)(2,1)} custom-call(bf16[512,256]{1,0:T(8,128)(2,1)S(1)} %shard_map.265.wanted_ref, bf16[256,512]{1,0:T(8,128)(2,1)S(1)} %bitcast.15, bf16[64,512]{1,0:T(8,128)(2,1)S(1)} %get-tuple-element.23.incoming_ref, bf16[512,128]{1,0:T(8,128)(2,1)S(1)} %get-tuple-element.24.pick_ref, ...), custom_call_target="tpu_custom_call" | custom-call | flops 1000000000 | bytes 4000000 | tf_op jit(solution)/shard_map/pallas_call | solution.py:544
Async XLA Ops:
  1.3 23.7 %all-to-all-start = ((s32[16,4,128]{2,1,0:T(4,128)}), s32[16,4,128]{2,1,0:T(4,128)S(1)}, u32[]{:S(2)}, u32[]{:S(2)}) async-start(s32[16,4,128]{2,1,0:T(4,128)} %tile.2), calls=%async_computation | async-start | bytes 65536 | tf_op jit(solution)/shard_map/all_to_all | solution.py:447
  9.3 15.6 %copy-start.12 = (s32[1024]{0:T(1024)S(1)}, s32[1024]{0:T(1024)}, u32[]{:S(2)}) copy-start(s32[1024]{0:T(1024)} %param.53) | copy-start | bytes 12292
  9.4 16.5 %copy-start.2 = (bf16[512,512]{1,0:T(8,128)(2,1)S(1)}, bf16[512,512]{1,0:T(8,128)(2,1)}, u32[]{:S(2)}) copy-start(bf16[512,512]{1,0:T(8,128)(2,1)} %node_out_ref.1) | copy-start | bytes 1572868
  9.4 16.5 %copy-start.3 = (bf16[512,512]{1,0:T(8,128)(2,1)S(1)}, bf16[512,512]{1,0:T(8,128)(2,1)}, u32[]{:S(2)}) copy-start(bf16[512,512]{1,0:T(8,128)(2,1)} %mesh_sender_ref.1) | copy-start | bytes 1572868
  9.4 16.5 %copy-start.4 = (bf16[64,512]{1,0:T(8,128)(2,1)S(1)}, bf16[64,512]{1,0:T(8,128)(2,1)}, u32[]{:S(2)}) copy-start(bf16[64,512]{1,0:T(8,128)(2,1)} %latent_ref.1) | copy-start | bytes 196612
  9.4 16.5 %copy-start.6 = (f32[512]{0:T(512)S(1)}, f32[512]{0:T(512)}, u32[]{:S(2)}) copy-start(f32[512]{0:T(512)} %param.37) | copy-start | bytes 6148
  9.4 16.5 %copy-start.7 = (f32[512]{0:T(512)S(1)}, f32[512]{0:T(512)}, u32[]{:S(2)}) copy-start(f32[512]{0:T(512)} %param.39) | copy-start | bytes 6148
  20.8 5.1 %copy-start = (bf16[1024,512]{1,0:T(8,128)(2,1)S(1)}, bf16[1024,512]{1,0:T(8,128)(2,1)}, u32[]{:S(2)}) copy-start(bf16[1024,512]{1,0:T(8,128)(2,1)} %node_input_ref.1) | copy-start | bytes 3145732
  20.8 5.1 %copy-start.1 = (bf16[512,512]{1,0:T(8,128)(2,1)S(1)}, bf16[512,512]{1,0:T(8,128)(2,1)}, u32[]{:S(2)}) copy-start(bf16[512,512]{1,0:T(8,128)(2,1)} %edge_out_ref.1) | copy-start | bytes 1572868
  20.8 4.8 %collective-permute-start = (bf16[64,512]{1,0:T(8,128)(2,1)S(1)}, bf16[64,512]{1,0:T(8,128)(2,1)S(1)}, u32[]{:S(2)}, u32[]{:S(2)}) collective-permute-start(bf16[64,512]{1,0:T(8,128)(2,1)S(1)} %get-tuple-element.17), channel_id=1, source_target_pairs={{1,2},{3,4},{5,6},{7,8},{9,10},{11,12},{13,14},{2,1},{4,3},{6,5},{... | collective-permute-start | bytes 196616 | tf_op jit(solution)/shard_map/ppermute | solution.py:486
  21.6 4.2 %collective-permute-start.1 = (bf16[64,512]{1,0:T(8,128)(2,1)S(1)}, bf16[64,512]{1,0:T(8,128)(2,1)S(1)}, u32[]{:S(2)}, u32[]{:S(2)}) collective-permute-start(bf16[64,512]{1,0:T(8,128)(2,1)S(1)} %get-tuple-element.18), channel_id=1, source_target_pairs={{0,1},{2,3},{4,5},{6,7},{8,9},{10,11},{12,13},{14,15},{1,0},{3,2},... | collective-permute-start | bytes 196616 | tf_op jit(solution)/shard_map/ppermute | solution.py:487
  25.6 9.0 %copy-start.5 = (s32[4,128]{1,0:T(4,128)S(1)}, s32[4,128]{1,0:T(4,128)}, u32[]{:S(2)}) copy-start(s32[4,128]{1,0:T(4,128)} %send_ref) | copy-start | bytes 6148
  27.8 16.8 %all-to-all-start.1 = ((bf16[16,16,512]{2,1,0:T(8,128)(2,1)}), bf16[16,16,512]{2,1,0:T(8,128)(2,1)S(1)}, u32[]{:S(2)}, u32[]{:S(2)}) async-start(bf16[16,16,512]{2,1,0:T(8,128)(2,1)} %bitcast.9), calls=%async_computation.1 | async-start | bytes 524288 | tf_op jit(solution)/shard_map/all_to_all | solution.py:514
  34.6 2.6 %copy-start.8 = (bf16[1024,512]{1,0:T(8,128)(2,1)S(1)}, bf16[1024,512]{1,0:T(8,128)(2,1)}, u32[]{:S(2)}) copy-start(bf16[1024,512]{1,0:T(8,128)(2,1)} %update_input_ref.3) | copy-start | bytes 3145732
  34.6 2.6 %copy-start.9 = (bf16[512,512]{1,0:T(8,128)(2,1)S(1)}, bf16[512,512]{1,0:T(8,128)(2,1)}, u32[]{:S(2)}) copy-start(bf16[512,512]{1,0:T(8,128)(2,1)} %mesh_receiver_ref.1) | copy-start | bytes 1572868
  34.6 2.6 %copy-start.13 = (s32[4,128]{1,0:T(4,128)S(1)}, s32[4,128]{1,0:T(4,128)}, u32[]{:S(2)}) copy-start(s32[4,128]{1,0:T(4,128)} %recv_ref.1) | copy-start | bytes 6148
  34.6 2.6 %copy-start.14 = (f32[512]{0:T(512)S(1)}, f32[512]{0:T(512)}, u32[]{:S(2)}) copy-start(f32[512]{0:T(512)} %param.42) | copy-start | bytes 6148
  34.6 2.6 %copy-start.15 = (f32[512]{0:T(512)S(1)}, f32[512]{0:T(512)}, u32[]{:S(2)}) copy-start(f32[512]{0:T(512)} %param.45) | copy-start | bytes 6148
  37.2 7.4 %copy-start.10 = (bf16[512,512]{1,0:T(8,128)(2,1)S(1)}, bf16[512,512]{1,0:T(8,128)(2,1)}, u32[]{:S(2)}) copy-start(bf16[512,512]{1,0:T(8,128)(2,1)} %message_out_ref.1) | copy-start | bytes 1572868
  37.2 7.4 %copy-start.11 = (bf16[512,512]{1,0:T(8,128)(2,1)S(1)}, bf16[512,512]{1,0:T(8,128)(2,1)}, u32[]{:S(2)}) copy-start(bf16[512,512]{1,0:T(8,128)(2,1)} %update_out_ref.1) | copy-start | bytes 1572868
  37.2 7.4 %copy-start.16 = (f32[512]{0:T(512)S(1)}, f32[512]{0:T(512)}, u32[]{:S(2)}) copy-start(f32[512]{0:T(512)} %param.47) | copy-start | bytes 6148

commit v14 on v13

--- a/solution.py
+++ b/solution.py
@@ -56,6 +56,18 @@
     nodes = slot.shape[1]
     rows = iota((count, nodes), 0) + first
     return jnp.max(jnp.where(slot == rows, iota((count, nodes), 1), -1), axis=1, keepdims=True)
+
+
+def asking_kernel(mesh_send_hbm, asked_hbm, sems):
+    rows = mesh_send_hbm.shape[0]
+    copies = [
+        pltpu.make_async_copy(mesh_send_hbm, asked_hbm.at[pl.ds(at * rows, rows), :], sems.at[at])
+        for at in range(asked_hbm.shape[0] // rows)
+    ]
+    for copy in copies:
+        copy.start()
+    for copy in copies:
+        copy.wait()
 
 
 def edge_kernel(
@@ -154,31 +166,23 @@
     edge_bias_copy.wait()
     grid_bias = 0.5 * grid_bias_ref[...]
     edge_bias = 0.5 * edge_bias_ref[...]
-    half_rows = step_rows // 2
-
-    def grid_step(step, carry):
+    values = []
+    for step in range(GRID_STEPS):
         grid_copy(step).wait()
-        first = pl.multiple_of(step * step_rows, step_rows)
-        values = [
-            mm(grid_ref[:, pl.ds(first + at, half_rows)].T, first_ref[...])
-            for at in (0, half_rows)
-        ]
-        values = [silu_half(value + grid_bias).astype(BF16) for value in values]
-        values = [mm(value, second_ref[...]) for value in values]
-        values = [layer_norm(value).astype(BF16) for value in values]
-        values = [mm(value, send_weight_ref[...]) for value in values]
-        for half, value in enumerate(values):
-            row = (value + edge_bias).astype(BF16).astype(F32)
-            base = pl.multiple_of((first + half * half_rows) * pieces, half_rows * pieces)
-            for group in range(half_rows // 8):
-                for piece in range(pieces):
-                    at = (group * pieces + piece) * 8
-                    table[pl.ds(base + at, 8), :] = row[
-                        group * 8 : group * 8 + 8, piece * LANES : (piece + 1) * LANES
-                    ]
-        return carry
-
-    lax.fori_loop(0, GRID_STEPS, grid_step, 0)
+        value = grid_ref[:, step * step_rows : (step + 1) * step_rows].T
+        values.append(mm(value, first_ref[...]))
+    values = [silu_half(value + grid_bias).astype(BF16) for value in values]
+    values = [mm(value, second_ref[...]) for value in values]
+    values = [layer_norm(value).astype(BF16) for value in values]
+    values = [mm(value, send_weight_ref[...]) for value in values]
+    for step, value in enumerate(values):
+        row = (value + edge_bias).astype(BF16).astype(F32)
+        for group in range(step_rows // 8):
+            for piece in range(pieces):
+                at = ((step * step_rows // 8 + group) * pieces + piece) * 8
+                table[at : at + 8, :] = row[
+                    group * 8 : group * 8 + 8, piece * LANES : (piece + 1) * LANES
+                ]
     for copy in copies[7:]:
         copy.wait()
     used = count_ref[...]
@@ -277,7 +281,22 @@
         )
 
 
-def supply_kernel(blocks, place_ref, slot_ref, request_ref, supply_ref):
+def supply_kernel(
+    blocks,
+    place_ref,
+    slot_ref,
+    request_ref,
+    latent_ref,
+    edge_out_ref,
+    node_input_ref,
+    node_bias_ref,
+    supply_ref,
+    upper_ref,
+    lower_ref,
+):
+    width = latent_ref.shape[1]
+    upper_ref[...] = mm(latent_ref[...], node_input_ref[:width]) + node_bias_ref[...]
+    lower_ref[...] = mm(edge_out_ref[...], node_input_ref[width:]).astype(BF16)
     owned = supply_ref.shape[1]
     devices = supply_ref.shape[0] // SEND_CAP
     per_device = request_ref.shape[0] // devices
@@ -305,9 +324,8 @@
     from_cross_ref,
     from_chip_ref,
     latent_ref,
-    edge_out_ref,
-    node_input_ref,
-    node_bias_ref,
+    upper_ref,
+    lower_ref,
     node_out_ref,
     node_gain_ref,
     mesh_sender_ref,
@@ -315,12 +333,9 @@
     encoded_ref,
     rows_ref,
 ):
-    width = latent_ref.shape[1]
     latent = latent_ref[...]
     node_sum = own_ref[...] + from_cross_ref[...].astype(F32) + from_chip_ref[...].astype(F32)
-    aggregate = mm(node_sum.astype(BF16), edge_out_ref[...]).astype(BF16)
-    hidden = mm(latent, node_input_ref[:width]) + mm(aggregate, node_input_ref[width:])
-    hidden = silu(hidden + node_bias_ref[...]).astype(BF16)
+    hidden = silu(upper_ref[...] + mm(node_sum.astype(BF16), lower_ref[...])).astype(BF16)
     encoded = latent.astype(F32) + layer_norm(mm(hidden, node_out_ref[...])) * node_gain_ref[...]
     encoded = encoded.astype(BF16)
     encoded_ref[...] = encoded
@@ -335,12 +350,14 @@
     encoded_ref,
     mesh_receiver_ref,
     message_bias_ref,
+    message_out_ref,
     update_input_ref,
     update_bias_ref,
     incoming_ref,
     pick_ref,
     parts_ref,
     upper_ref,
+    lower_ref,
 ):
     owned, width = encoded_ref.shape
     blocks = recv_ref.shape[0]
@@ -357,6 +374,7 @@
     parts_ref[:owned, :] = high
     parts_ref[owned:, :] = (receiver - high.astype(F32)).astype(BF16)
     upper_ref[...] = mm(encoded, update_input_ref[:width]) + update_bias_ref[...]
+    lower_ref[...] = mm(message_out_ref[...], update_input_ref[width:]).astype(BF16)
 
 
 def message_kernel(
@@ -366,30 +384,27 @@
     pick_ref,
     parts_ref,
     upper_ref,
+    lower_ref,
     encoded_ref,
-    message_out_ref,
-    update_input_ref,
     update_out_ref,
     update_gain_ref,
     out_ref,
 ):
-    width = encoded_ref.shape[1]
     chosen = jnp.concatenate([wanted_ref[...], pick_ref[...]], axis=1)
     codes = jnp.concatenate([piece_ref[...], parts_ref[...]], axis=0)
     message = silu(mm(chosen, codes)).astype(BF16)
     message_sum = mm(incoming_ref[...], message).astype(BF16)
-    update = mm(message_sum, message_out_ref[...]).astype(BF16)
-    hidden = silu(upper_ref[...] + mm(update, update_input_ref[width:])).astype(BF16)
+    hidden = silu(upper_ref[...] + mm(message_sum, lower_ref[...])).astype(BF16)
     out = layer_norm(mm(hidden, update_out_ref[...])) * update_gain_ref[...]
     out_ref[...] = (encoded_ref[...].astype(F32) + out).astype(BF16)
 
 
-def call(kernel, out_shape, spaces, scratch=(), flops=0, moved=0, vmem=8):
+def call(kernel, out_shape, spaces, scratch=(), flops=0, moved=0, vmem=8, out_space=VMEM):
     return pl.pallas_call(
         kernel,
         out_shape=out_shape,
         in_specs=[pl.BlockSpec(memory_space=space) for space in spaces],
-        out_specs=jax.tree.map(lambda _: pl.BlockSpec(memory_space=VMEM), out_shape),
+        out_specs=jax.tree.map(lambda _: pl.BlockSpec(memory_space=out_space), out_shape),
         scratch_shapes=scratch,
         compiler_params=pltpu.CompilerParams(vmem_limit_bytes=vmem * MEBI),
         cost_estimate=pl.CostEstimate(flops=flops, bytes_accessed=moved, transcendentals=0),
@@ -444,7 +459,16 @@
     slot = mesh_slot.reshape(1, -1)
     row = lambda vector: vector.reshape(1, -1)
 
-    requests = lax.all_to_all(jnp.tile(mesh_send, (devices, 1)), "bulk", 0, 0, tiled=True)
+    asked = call(
+        asking_kernel,
+        shape(devices * mesh_send.shape[0], mesh_send.shape[1], kind=I32),
+        [HBM],
+        scratch=[pltpu.SemaphoreType.DMA((devices,))],
+        moved=100_000,
+        out_space=HBM,
+    )(hold(mesh_send))
+    asked, first_place = lax.optimization_barrier((asked, place))
+    requests = lax.all_to_all(asked, "bulk", 0, 0, tiled=True)
     operands = (
         grid_first,
         grid_in.T,
@@ -478,24 +502,24 @@
         flops=10_000_000_000,
         moved=4_000_000,
         vmem=32,
-    )(place, *[hold(value) for value in operands])
+    )(first_place, *[hold(value) for value in operands])
     requests, _ = lax.optimization_barrier((requests, own))
     crossing = [(d, d + 1) for d in range(1, devices - 1, 2)]
     within = [(d, d + 1) for d in range(0, devices, 2)]
     both = lambda pairs: pairs + [(b, a) for a, b in pairs]
     from_cross = lax.ppermute(cross, "bulk", both(crossing))
     from_chip = lax.ppermute(chip, "bulk", both(within))
-    supply = call(
+    supply, upper, lower = call(
         functools.partial(supply_kernel, mesh_send.shape[0]),
-        shape(places, owned),
-        [SMEM] + [VMEM] * 2,
+        (shape(places, owned), shape(owned, width, kind=F32), shape(width, width)),
+        [SMEM] + [VMEM] * 6,
         flops=500_000_000,
         moved=500_000,
-    )(place, slot, requests)
+    )(place, slot, requests, mesh_latent, edge_out, node_input, row(node_bias))
     encoded, rows = call(
         node_kernel,
         (shape(owned, width), shape(places, width)),
-        [VMEM] * 11,
+        [VMEM] * 10,
         flops=500_000_000,
         moved=4_000_000,
     )(
@@ -503,9 +527,8 @@
         from_cross,
         from_chip,
         mesh_latent,
-        edge_out,
-        node_input,
-        row(node_bias),
+        upper,
+        lower,
         node_out,
         row(node_gain),
         mesh_sender,
@@ -520,15 +543,16 @@
         flops=1_000_000_000,
         moved=500_000,
     )(slot, mesh_send)
-    incoming, pick, parts, upper = call(
+    incoming, pick, parts, upper, lower = call(
         receiver_kernel,
         (
             shape(owned, edges),
             shape(edges, 2 * owned),
             shape(2 * owned, width),
             shape(owned, width, kind=F32),
+            shape(width, width),
         ),
-        [SMEM] + [VMEM] * 7,
+        [SMEM] + [VMEM] * 8,
         flops=1_000_000_000,
         moved=4_000_000,
     )(
@@ -538,13 +562,14 @@
         encoded,
         mesh_receiver,
         row(message_bias),
+        message_out,
         update_input,
         row(update_bias),
     )
     return call(
         message_kernel,
         shape(owned, width),
-        [VMEM] * 11,
+        [VMEM] * 10,
         flops=1_000_000_000,
         moved=4_000_000,
     )(
@@ -554,9 +579,8 @@
         pick,
         parts,
         upper,
+        lower,
         encoded,
-        message_out,
-        update_input,
         update_out,
         row(update_gain),
     )

time: 46.9 us -> 47.1 us (level)
  Pallas kernels: 18.8 us -> 20.6 us
  local copies, waits for them, and re-layouts: 1.41 us -> 0.11 us
    pallas_call x2 -> x3, Pallas kernels: 2.59 us -> 4.72 us  [the longest x1 2.24 us: per_device(): call(asking_kernel, shape(devices * mesh_send.shape[0], mesh_send.shape[1...]
    another operation x1 -> x0, local copies, waits for them, and re-layouts: 1.3 us -> none  [per_device(): jnp.tile(mesh_send, (devices, 1))]
where the time goes in v14:
time: 47.1 us; the launch traced here: 46.8 us
  Pallas kernels  20.6 us (44%)
  starting transfers between devices  18.3 us (39%)
  waiting for transfers between devices  6.83 us (15%)
  between operations  0.94 us (2%)
    pallas_call x1, Pallas kernels, per_device(): call(edge_kernel, (shape(owned, width, kind=F32), shape(owned, width), sh...  11.1 us
    all_to_all x1, starting transfers between devices, per_device(): requests = lax.all_to_all(asked, 'bulk', 0, 0, tiled=True)  7.4 us
    all_to_all x1, starting transfers between devices, per_device(): piece = lax.all_to_all(rows, 'bulk', 0, 0, tiled=True)  6.79 us
    all_to_all x1, waiting for transfers between devices, per_device(): piece = lax.all_to_all(rows, 'bulk', 0, 0, tiled=True)  6.71 us
    ppermute x1, starting transfers between devices, per_device(): from_chip = lax.ppermute(chip, 'bulk', both(within))  3.36 us
    pallas_call x1, Pallas kernels, per_device(): call(functools.partial(wanted_kernel, owned), shape(edges, places), [VMEM...  2.53 us
    pallas_call x1, Pallas kernels, per_device(): call(asking_kernel, shape(devices * mesh_send.shape[0], mesh_send.shape[1...  2.24 us
    pallas_call x1, Pallas kernels, per_device(): call(message_kernel, shape(owned, width), [VMEM] * 10, flops=1000000000,...  1.77 us
  transfers between devices with their start and end apart: 4, of which 2 were waited for; matrix products, arithmetic and copies ran while one was open for 0% of the time, Pallas kernels for 32%

profile of v14, /device:TPU:0, one launch (start us, length us, event | category | flops | bytes accessed | tf_op | source)
XLA Modules:
  0.0 46.8 jit_solution(1454045491275612607)
XLA Ops:
  0.0 2.2 %shard_map.262 = s32[64,128]{1,0:T(8,128)} custom-call(s32[4,128]{1,0:T(4,128)} %send_ref), custom_call_target="tpu_custom_call" | custom-call | bytes 100000 | tf_op jit(solution)/shard_map/pallas_call | solution.py:462
  2.2 7.4 %all-to-all-start = ((s32[16,4,128]{2,1,0:T(4,128)}), s32[16,4,128]{2,1,0:T(4,128)S(1)}, u32[]{:S(2)}, u32[]{:S(2)}) async-start(s32[16,4,128]{2,1,0:T(4,128)} %bitcast.6), calls=%async_computation | async-start | bytes 65536 | tf_op jit(solution)/shard_map/all_to_all | solution.py:471
  10.3 0.0 copy-start.2
  10.3 0.0 copy-start.5
  10.3 0.0 copy-start.7
  10.3 0.0 copy-start.11
  10.3 0.0 copy-start.12
  10.4 0.0 copy-start.3
  10.4 11.1 %shard_map.263 = (f32[64,512]{1,0:T(8,128)S(1)}, bf16[64,512]{1,0:T(8,128)(2,1)S(1)}, bf16[64,512]{1,0:T(8,128)(2,1)S(1)}) custom-call(s32[1]{0:T(128)} %bitcast.1.place_ref, bf16[474,512]{1,0:T(8,128)(2,1)} %first_hbm.1, bf16[474,2048]{1,0:T(8,128)(2,1)} %bitcast.27, bf16[512,512]{1,0:T(8,128)(2,1)} %second_hbm.1, bf16[512,512]{1,0:T(8,128)(2,1)} %send_weight_hbm.1, ...), custom_call_target="tpu_custom_call" | custom-call | flops 10000000000 | bytes 4000000 | tf_op jit(solution)/shard_map/pallas_call | solution.py:486
  21.4 0.0 copy-start
  21.5 0.0 copy-start.1
  21.5 0.8 %collective-permute-start = (bf16[64,512]{1,0:T(8,128)(2,1)S(1)}, bf16[64,512]{1,0:T(8,128)(2,1)S(1)}, u32[]{:S(2)}, u32[]{:S(2)}) collective-permute-start(bf16[64,512]{1,0:T(8,128)(2,1)S(1)} %get-tuple-element.24), channel_id=1, source_target_pairs={{1,2},{3,4},{5,6},{7,8},{9,10},{11,12},{13,14},{2,1},{4,3},{6,5},{... | collective-permute-start | bytes 196616 | tf_op jit(solution)/shard_map/ppermute | solution.py:510
  22.3 3.4 %collective-permute-start.1 = (bf16[64,512]{1,0:T(8,128)(2,1)S(1)}, bf16[64,512]{1,0:T(8,128)(2,1)S(1)}, u32[]{:S(2)}, u32[]{:S(2)}) collective-permute-start(bf16[64,512]{1,0:T(8,128)(2,1)S(1)} %get-tuple-element.25), channel_id=1, source_target_pairs={{0,1},{2,3},{4,5},{6,7},{8,9},{10,11},{12,13},{14,15},{1,0},{3,2},... | collective-permute-start | bytes 196616 | tf_op jit(solution)/shard_map/ppermute | solution.py:511
  25.6 0.0 all-to-all-done
  25.6 0.0 copy-done.2
  25.6 0.0 copy-done.5
  25.6 0.0 copy-done.7
  25.6 0.0 copy-done.11
  25.7 0.0 copy-done.12
  25.7 0.0 copy-start.4
  25.7 0.7 %shard_map.264 = (bf16[256,64]{1,0:T(8,128)(2,1)S(1)}, f32[64,512]{1,0:T(8,128)S(1)}, bf16[512,512]{1,0:T(8,128)(2,1)S(1)}) custom-call(s32[1]{0:T(128)} %bitcast.1.place_ref, s32[1,1024]{1,0:T(1,128)S(1)} %bitcast.20, s32[64,128]{1,0:T(8,128)S(1)} %bitcast.17, bf16[64,512]{1,0:T(8,128)(2,1)S(1)} %copy-done.2, bf16[512,512]{1,0:T(8,128)(2,1)S(1)} %copy-done.7, ...), custom_call_target="tpu_custom_call" | custom-call | flops 500000000 | bytes 500000 | tf_op jit(solution)/shard_map/pallas_call | solution.py:512
  26.4 0.0 collective-permute-done.from_cross_ref
  26.4 0.1 collective-permute-done.1.from_chip_ref
  26.5 0.0 copy-done.3
  26.5 0.0 copy-done
  26.5 0.0 copy-done.1
  26.5 1.6 %shard_map.265 = (bf16[64,512]{1,0:T(8,128)(2,1)S(1)}, bf16[256,512]{1,0:T(8,128)(2,1)}) custom-call(f32[64,512]{1,0:T(8,128)S(1)} %get-tuple-element.23.own_ref, bf16[64,512]{1,0:T(8,128)(2,1)S(1)} %collective-permute-done.from_cross_ref, bf16[64,512]{1,0:T(8,128)(2,1)S(1)} %collective-permute-done.1.from_chip_ref, bf16[64,512]{1,0:T(8,128)(2,1)S(1)} %copy-done.2, ...), custom_call_target="tpu_custom_call" | custom-call | flops 500000000 | bytes 4000000 | tf_op jit(solution)/shard_map/pallas_call | solution.py:519
  28.2 6.8 %all-to-all-start.1 = ((bf16[16,16,512]{2,1,0:T(8,128)(2,1)}), bf16[16,16,512]{2,1,0:T(8,128)(2,1)S(1)}, u32[]{:S(2)}, u32[]{:S(2)}) async-start(bf16[16,16,512]{2,1,0:T(8,128)(2,1)} %bitcast.10), calls=%async_computation.1 | async-start | bytes 524288 | tf_op jit(solution)/shard_map/all_to_all | solution.py:537
  35.0 0.0 copy-start.6
  35.0 0.0 copy-start.8
  35.0 0.0 copy-start.9
  35.0 0.0 copy-start.13
  35.0 0.0 copy-start.14
  35.0 0.0 copy-start.15
  35.0 0.0 copy-done.4
  35.0 2.5 %shard_map.266.wanted_ref = bf16[512,256]{1,0:T(8,128)(2,1)S(1)} custom-call(s32[1,1024]{1,0:T(1,128)S(1)} %bitcast.21, s32[4,128]{1,0:T(4,128)S(1)} %copy-done.4), custom_call_target="tpu_custom_call" | custom-call | flops 1000000000 | bytes 500000 | tf_op jit(solution)/shard_map/pallas_call | solution.py:539
  37.6 0.0 copy-start.10
  37.6 0.0 copy-start.16
  37.6 0.0 copy-done.6
  37.6 0.0 copy-done.8
  37.6 0.0 copy-done.9
  37.6 0.0 copy-done.13
  37.6 0.0 copy-done.14
  37.7 0.0 copy-done.15
  37.7 0.6 %shard_map.267 = (bf16[64,512]{1,0:T(8,128)(2,1)S(1)}, bf16[512,128]{1,0:T(8,128)(2,1)S(1)}, bf16[128,512]{1,0:T(8,128)(2,1)S(1)}, f32[64,512]{1,0:T(8,128)S(1)}, bf16[512,512]{1,0:T(8,128)(2,1)S(1)}) custom-call(s32[1]{0:T(128)} %bitcast.1.place_ref, s32[1,1024]{1,0:T(1,128)S(1)} %bitcast.22, s32[4,128]{1,0:T(4,128)S(1)} %copy-done.13, ...), custom_call_target="tpu_custom_call" | custom-call | flops 1000000000 | bytes 4000000 | tf_op jit(solution)/shard_map/pallas_call | solution.py:546
  38.3 6.7 %all-to-all-done.1 = bf16[16,16,512]{2,1,0:T(8,128)(2,1)S(1)} async-done(((bf16[16,16,512]{2,1,0:T(8,128)(2,1)}), bf16[16,16,512]{2,1,0:T(8,128)(2,1)S(1)}, u32[]{:S(2)}, u32[]{:S(2)}) %all-to-all-start.1) | async-done | bytes 262176 | tf_op jit(solution)/shard_map/all_to_all | solution.py:537
  45.0 0.0 copy-done.10
  45.0 0.0 copy-done.16
  45.0 1.8 %shard_map.268 = bf16[64,512]{1,0:T(8,128)(2,1)} custom-call(bf16[512,256]{1,0:T(8,128)(2,1)S(1)} %shard_map.266.wanted_ref, bf16[256,512]{1,0:T(8,128)(2,1)S(1)} %bitcast.16, bf16[64,512]{1,0:T(8,128)(2,1)S(1)} %get-tuple-element.34.incoming_ref, bf16[512,128]{1,0:T(8,128)(2,1)S(1)} %get-tuple-element.35.pick_ref, ...), custom_call_target="tpu_custom_call" | custom-call | flops 1000000000 | bytes 4000000 | tf_op jit(solution)/shard_map/pallas_call | solution.py:569
Async XLA Ops:
  2.2 23.4 %all-to-all-start = ((s32[16,4,128]{2,1,0:T(4,128)}), s32[16,4,128]{2,1,0:T(4,128)S(1)}, u32[]{:S(2)}, u32[]{:S(2)}) async-start(s32[16,4,128]{2,1,0:T(4,128)} %bitcast.6), calls=%async_computation | async-start | bytes 65536 | tf_op jit(solution)/shard_map/all_to_all | solution.py:471
  10.3 15.3 %copy-start.2 = (bf16[64,512]{1,0:T(8,128)(2,1)S(1)}, bf16[64,512]{1,0:T(8,128)(2,1)}, u32[]{:S(2)}) copy-start(bf16[64,512]{1,0:T(8,128)(2,1)} %latent_ref.3) | copy-start | bytes 196612
  10.3 15.3 %copy-start.5 = (bf16[1024,512]{1,0:T(8,128)(2,1)S(1)}, bf16[1024,512]{1,0:T(8,128)(2,1)}, u32[]{:S(2)}) copy-start(bf16[1024,512]{1,0:T(8,128)(2,1)} %node_input_ref.1) | copy-start | bytes 3145732
  10.3 15.3 %copy-start.7 = (bf16[512,512]{1,0:T(8,128)(2,1)S(1)}, bf16[512,512]{1,0:T(8,128)(2,1)}, u32[]{:S(2)}) copy-start(bf16[512,512]{1,0:T(8,128)(2,1)} %edge_out_ref.1) | copy-start | bytes 1572868
  10.3 15.3 %copy-start.11 = (s32[1024]{0:T(1024)S(1)}, s32[1024]{0:T(1024)}, u32[]{:S(2)}) copy-start(s32[1024]{0:T(1024)} %param.53) | copy-start | bytes 12292
  10.3 15.3 %copy-start.12 = (f32[512]{0:T(512)S(1)}, f32[512]{0:T(512)}, u32[]{:S(2)}) copy-start(f32[512]{0:T(512)} %param.37) | copy-start | bytes 6148
  10.4 16.2 %copy-start.3 = (f32[512]{0:T(512)S(1)}, f32[512]{0:T(512)}, u32[]{:S(2)}) copy-start(f32[512]{0:T(512)} %param.39) | copy-start | bytes 6148
  21.4 5.1 %copy-start = (bf16[512,512]{1,0:T(8,128)(2,1)S(1)}, bf16[512,512]{1,0:T(8,128)(2,1)}, u32[]{:S(2)}) copy-start(bf16[512,512]{1,0:T(8,128)(2,1)} %node_out_ref.1) | copy-start | bytes 1572868
  21.5 5.1 %copy-start.1 = (bf16[512,512]{1,0:T(8,128)(2,1)S(1)}, bf16[512,512]{1,0:T(8,128)(2,1)}, u32[]{:S(2)}) copy-start(bf16[512,512]{1,0:T(8,128)(2,1)} %mesh_sender_ref.1) | copy-start | bytes 1572868
  21.5 4.9 %collective-permute-start = (bf16[64,512]{1,0:T(8,128)(2,1)S(1)}, bf16[64,512]{1,0:T(8,128)(2,1)S(1)}, u32[]{:S(2)}, u32[]{:S(2)}) collective-permute-start(bf16[64,512]{1,0:T(8,128)(2,1)S(1)} %get-tuple-element.24), channel_id=1, source_target_pairs={{1,2},{3,4},{5,6},{7,8},{9,10},{11,12},{13,14},{2,1},{4,3},{6,5},{... | collective-permute-start | bytes 196616 | tf_op jit(solution)/shard_map/ppermute | solution.py:510
  22.3 4.3 %collective-permute-start.1 = (bf16[64,512]{1,0:T(8,128)(2,1)S(1)}, bf16[64,512]{1,0:T(8,128)(2,1)S(1)}, u32[]{:S(2)}, u32[]{:S(2)}) collective-permute-start(bf16[64,512]{1,0:T(8,128)(2,1)S(1)} %get-tuple-element.25), channel_id=1, source_target_pairs={{0,1},{2,3},{4,5},{6,7},{8,9},{10,11},{12,13},{14,15},{1,0},{3,2},... | collective-permute-start | bytes 196616 | tf_op jit(solution)/shard_map/ppermute | solution.py:511
  25.7 9.4 %copy-start.4 = (s32[4,128]{1,0:T(4,128)S(1)}, s32[4,128]{1,0:T(4,128)}, u32[]{:S(2)}) copy-start(s32[4,128]{1,0:T(4,128)} %send_ref) | copy-start | bytes 6148
  28.2 16.8 %all-to-all-start.1 = ((bf16[16,16,512]{2,1,0:T(8,128)(2,1)}), bf16[16,16,512]{2,1,0:T(8,128)(2,1)S(1)}, u32[]{:S(2)}, u32[]{:S(2)}) async-start(bf16[16,16,512]{2,1,0:T(8,128)(2,1)} %bitcast.10), calls=%async_computation.1 | async-start | bytes 524288 | tf_op jit(solution)/shard_map/all_to_all | solution.py:537
  35.0 2.6 %copy-start.6 = (bf16[1024,512]{1,0:T(8,128)(2,1)S(1)}, bf16[1024,512]{1,0:T(8,128)(2,1)}, u32[]{:S(2)}) copy-start(bf16[1024,512]{1,0:T(8,128)(2,1)} %update_input_ref.1) | copy-start | bytes 3145732
  35.0 2.6 %copy-start.8 = (bf16[512,512]{1,0:T(8,128)(2,1)S(1)}, bf16[512,512]{1,0:T(8,128)(2,1)}, u32[]{:S(2)}) copy-start(bf16[512,512]{1,0:T(8,128)(2,1)} %mesh_receiver_ref.1) | copy-start | bytes 1572868
  35.0 2.6 %copy-start.9 = (bf16[512,512]{1,0:T(8,128)(2,1)S(1)}, bf16[512,512]{1,0:T(8,128)(2,1)}, u32[]{:S(2)}) copy-start(bf16[512,512]{1,0:T(8,128)(2,1)} %message_out_ref.1) | copy-start | bytes 1572868
  35.0 2.6 %copy-start.13 = (s32[4,128]{1,0:T(4,128)S(1)}, s32[4,128]{1,0:T(4,128)}, u32[]{:S(2)}) copy-start(s32[4,128]{1,0:T(4,128)} %recv_ref.1) | copy-start | bytes 6148
  35.0 2.6 %copy-start.14 = (f32[512]{0:T(512)S(1)}, f32[512]{0:T(512)}, u32[]{:S(2)}) copy-start(f32[512]{0:T(512)} %param.42) | copy-start | bytes 6148
  35.0 2.6 %copy-start.15 = (f32[512]{0:T(512)S(1)}, f32[512]{0:T(512)}, u32[]{:S(2)}) copy-start(f32[512]{0:T(512)} %param.45) | copy-start | bytes 6148
  37.6 7.4 %copy-start.10 = (bf16[512,512]{1,0:T(8,128)(2,1)S(1)}, bf16[512,512]{1,0:T(8,128)(2,1)}, u32[]{:S(2)}) copy-start(bf16[512,512]{1,0:T(8,128)(2,1)} %update_out_ref.1) | copy-start | bytes 1572868
  37.6 7.4 %copy-start.16 = (f32[512]{0:T(512)S(1)}, f32[512]{0:T(512)}, u32[]{:S(2)}) copy-start(f32[512]{0:T(512)} %param.47) | copy-start | bytes 6148

commit v15 on v14

--- a/solution.py
+++ b/solution.py
@@ -18,6 +18,8 @@
 HBM = pltpu.HBM
 GRID_STEPS = 2
 CHUNK_BLOCKS = 4
+ROW_PITCH = 5
+PIECE_PITCH = 2
 MEBI = 1024 * 1024
 
 
@@ -56,18 +58,6 @@
     nodes = slot.shape[1]
     rows = iota((count, nodes), 0) + first
     return jnp.max(jnp.where(slot == rows, iota((count, nodes), 1), -1), axis=1, keepdims=True)
-
-
-def asking_kernel(mesh_send_hbm, asked_hbm, sems):
-    rows = mesh_send_hbm.shape[0]
-    copies = [
-        pltpu.make_async_copy(mesh_send_hbm, asked_hbm.at[pl.ds(at * rows, rows), :], sems.at[at])
-        for at in range(asked_hbm.shape[0] // rows)
-    ]
-    for copy in copies:
-        copy.start()
-    for copy in copies:
-        copy.wait()
 
 
 def edge_kernel(
@@ -149,7 +139,7 @@
         grid_copy(step).start()
     send_copy.wait()
     senders = send_ref[...]
-    send_ref[...] = (senders // 8) * (8 * pieces) + senders % 8
+    send_ref[...] = senders * ROW_PITCH
     starts_copy.start()
     slot_copy.wait()
     place = place_ref[0]
@@ -179,8 +169,8 @@
         row = (value + edge_bias).astype(BF16).astype(F32)
         for group in range(step_rows // 8):
             for piece in range(pieces):
-                at = ((step * step_rows // 8 + group) * pieces + piece) * 8
-                table[at : at + 8, :] = row[
+                at = (step * step_rows + group * 8) * ROW_PITCH + piece * PIECE_PITCH
+                table[pl.ds(at, 8, stride=ROW_PITCH), :] = row[
                     group * 8 : group * 8 + 8, piece * LANES : (piece + 1) * LANES
                 ]
     for copy in copies[7:]:
@@ -196,8 +186,8 @@
     def gather(chunk, edges, target):
         for edge in edges:
             start = starts[chunk * group + edge // block_edges, edge % block_edges]
-            target[pl.ds(edge // 8 * (8 * pieces) + edge % 8, pieces, stride=8), :] = table[
-                pl.ds(start, pieces, stride=8), :
+            target[pl.ds(edge * ROW_PITCH, pieces, stride=PIECE_PITCH), :] = table[
+                pl.ds(start, pieces, stride=PIECE_PITCH), :
             ]
 
     def rows_of(source, first, count):
@@ -205,7 +195,7 @@
             [
                 jnp.concatenate(
                     [
-                        source[pl.ds((at * pieces + piece) * 8, 8), :]
+                        source[pl.ds(at * 8 * ROW_PITCH + piece * PIECE_PITCH, 8, stride=ROW_PITCH), :]
                         for at in range(first // 8, (first + count) // 8)
                     ],
                     axis=0,
@@ -399,12 +389,12 @@
     out_ref[...] = (encoded_ref[...].astype(F32) + out).astype(BF16)
 
 
-def call(kernel, out_shape, spaces, scratch=(), flops=0, moved=0, vmem=8, out_space=VMEM):
+def call(kernel, out_shape, spaces, scratch=(), flops=0, moved=0, vmem=8):
     return pl.pallas_call(
         kernel,
         out_shape=out_shape,
         in_specs=[pl.BlockSpec(memory_space=space) for space in spaces],
-        out_specs=jax.tree.map(lambda _: pl.BlockSpec(memory_space=out_space), out_shape),
+        out_specs=jax.tree.map(lambda _: pl.BlockSpec(memory_space=VMEM), out_shape),
         scratch_shapes=scratch,
         compiler_params=pltpu.CompilerParams(vmem_limit_bytes=vmem * MEBI),
         cost_estimate=pl.CostEstimate(flops=flops, bytes_accessed=moved, transcendentals=0),
@@ -459,16 +449,7 @@
     slot = mesh_slot.reshape(1, -1)
     row = lambda vector: vector.reshape(1, -1)
 
-    asked = call(
-        asking_kernel,
-        shape(devices * mesh_send.shape[0], mesh_send.shape[1], kind=I32),
-        [HBM],
-        scratch=[pltpu.SemaphoreType.DMA((devices,))],
-        moved=100_000,
-        out_space=HBM,
-    )(hold(mesh_send))
-    asked, first_place = lax.optimization_barrier((asked, place))
-    requests = lax.all_to_all(asked, "bulk", 0, 0, tiled=True)
+    requests = lax.all_to_all(jnp.tile(mesh_send, (devices, 1)), "bulk", 0, 0, tiled=True)
     operands = (
         grid_first,
         grid_in.T,
@@ -490,9 +471,9 @@
         scratch=[VMEM(value.shape, value.dtype) for value in operands]
         + [
             SMEM(g2m_send.shape, I32),
-            VMEM((grid_rows * (width // LANES), LANES), F32),
-            VMEM((CHUNK_BLOCKS * g2m_send.shape[1] * (width // LANES), LANES), F32),
-            VMEM((CHUNK_BLOCKS * g2m_send.shape[1] * (width // LANES), LANES), F32),
+            VMEM((grid_rows * ROW_PITCH + 8, LANES), F32),
+            VMEM((CHUNK_BLOCKS * g2m_send.shape[1] * ROW_PITCH + 8, LANES), F32),
+            VMEM((CHUNK_BLOCKS * g2m_send.shape[1] * ROW_PITCH + 8, LANES), F32),
             VMEM((CHUNK_BLOCKS * g2m_send.shape[1], width), BF16),
             VMEM((CHUNK_BLOCKS * g2m_send.shape[1], width), BF16),
             VMEM((3 * owned, LANES), I32),
@@ -502,7 +483,7 @@
         flops=10_000_000_000,
         moved=4_000_000,
         vmem=32,
-    )(first_place, *[hold(value) for value in operands])
+    )(place, *[hold(value) for value in operands])
     requests, _ = lax.optimization_barrier((requests, own))
     crossing = [(d, d + 1) for d in range(1, devices - 1, 2)]
     within = [(d, d + 1) for d in range(0, devices, 2)]

time: 47.1 us -> 46.5 us (0.987)
  Pallas kernels: 20.6 us -> 18.7 us
  local copies, waits for them, and re-layouts: 0.11 us -> 1.41 us
    pallas_call x1 -> x0, Pallas kernels: 2.24 us -> none  [per_device(): call(asking_kernel, shape(devices * mesh_send.shape[0], mesh_send.shape[1...]
    another operation x0 -> x1, local copies, waits for them, and re-layouts: none -> 1.3 us  [per_device(): jnp.tile(mesh_send, (devices, 1))]
  transfers between devices with their start and end apart: 4 -> 4, of which waited for: 2 -> 2; matrix products, arithmetic and copies ran while one was open for 0% -> 0% of each run, Pallas kernels for 32% -> 33%
where the time goes in v15:
time: 46.5 us; the launch traced here: 46.2 us
  Pallas kernels  18.7 us (40%)
  starting transfers between devices  18.3 us (39%)
  waiting for transfers between devices  6.83 us (15%)
  local copies, waits for them, and re-layouts  1.41 us (3%)
  between operations  0.94 us (2%)
    pallas_call x1, Pallas kernels, per_device(): call(edge_kernel, (shape(owned, width, kind=F32), shape(owned, width), sh...  11.4 us
    all_to_all x1, starting transfers between devices, per_device(): lax.all_to_all(jnp.tile(mesh_send, (devices, 1)), 'bulk', 0, 0, tiled=True)  7.39 us
    all_to_all x1, starting transfers between devices, per_device(): piece = lax.all_to_all(rows, 'bulk', 0, 0, tiled=True)  6.79 us
    all_to_all x1, waiting for transfers between devices, per_device(): piece = lax.all_to_all(rows, 'bulk', 0, 0, tiled=True)  6.71 us
    ppermute x1, starting transfers between devices, per_device(): from_chip = lax.ppermute(chip, 'bulk', both(within))  3.33 us
    pallas_call x1, Pallas kernels, per_device(): call(functools.partial(wanted_kernel, owned), shape(edges, places), [VMEM...  2.53 us
    pallas_call x1, Pallas kernels, per_device(): call(message_kernel, shape(owned, width), [VMEM] * 10, flops=1000000000,...  1.77 us
    pallas_call x1, Pallas kernels, per_device(): call(node_kernel, (shape(owned, width), shape(places, width)), [VMEM] * 1...  1.62 us
  transfers between devices with their start and end apart: 4, of which 2 were waited for; matrix products, arithmetic and copies ran while one was open for 0% of the time, Pallas kernels for 33%

profile of v15, /device:TPU:0, one launch (start us, length us, event | category | flops | bytes accessed | tf_op | source)
XLA Modules:
  0.0 46.2 jit_solution(17960015020226317773)
XLA Ops:
  0.0 1.3 %tile.2 = s32[16,4,128]{2,1,0:T(4,128)} broadcast(s32[4,128]{1,0:T(4,128)} %send_ref), dimensions={1,2} | broadcast | bytes 34816 | tf_op jit(solution)/shard_map/tile | solution.py:452
  1.3 7.4 %all-to-all-start = ((s32[16,4,128]{2,1,0:T(4,128)}), s32[16,4,128]{2,1,0:T(4,128)S(1)}, u32[]{:S(2)}, u32[]{:S(2)}) async-start(s32[16,4,128]{2,1,0:T(4,128)} %tile.2), calls=%async_computation | async-start | bytes 65536 | tf_op jit(solution)/shard_map/all_to_all | solution.py:452
  9.3 0.0 copy-start.2
  9.4 0.0 copy-start.5
  9.4 0.0 copy-start.7
  9.4 0.0 copy-start.11
  9.4 0.0 copy-start.12
  9.4 0.0 copy-start.3
  9.4 11.4 %shard_map.262 = (f32[64,512]{1,0:T(8,128)S(1)}, bf16[64,512]{1,0:T(8,128)(2,1)S(1)}, bf16[64,512]{1,0:T(8,128)(2,1)S(1)}) custom-call(s32[1]{0:T(128)} %bitcast.1.place_ref, bf16[474,512]{1,0:T(8,128)(2,1)} %first_hbm.1, bf16[474,2048]{1,0:T(8,128)(2,1)} %bitcast.26, bf16[512,512]{1,0:T(8,128)(2,1)} %second_hbm.1, bf16[512,512]{1,0:T(8,128)(2,1)} %send_weight_hbm.1, ...), custom_call_target="tpu_custom_call" | custom-call | flops 10000000000 | bytes 4000000 | tf_op jit(solution)/shard_map/pallas_call | solution.py:467
  20.8 0.0 copy-start
  20.9 0.0 copy-start.1
  20.9 0.8 %collective-permute-start = (bf16[64,512]{1,0:T(8,128)(2,1)S(1)}, bf16[64,512]{1,0:T(8,128)(2,1)S(1)}, u32[]{:S(2)}, u32[]{:S(2)}) collective-permute-start(bf16[64,512]{1,0:T(8,128)(2,1)S(1)} %get-tuple-element.21), channel_id=1, source_target_pairs={{1,2},{3,4},{5,6},{7,8},{9,10},{11,12},{13,14},{2,1},{4,3},{6,5},{... | collective-permute-start | bytes 196616 | tf_op jit(solution)/shard_map/ppermute | solution.py:491
  21.7 3.3 %collective-permute-start.1 = (bf16[64,512]{1,0:T(8,128)(2,1)S(1)}, bf16[64,512]{1,0:T(8,128)(2,1)S(1)}, u32[]{:S(2)}, u32[]{:S(2)}) collective-permute-start(bf16[64,512]{1,0:T(8,128)(2,1)S(1)} %get-tuple-element.22), channel_id=1, source_target_pairs={{0,1},{2,3},{4,5},{6,7},{8,9},{10,11},{12,13},{14,15},{1,0},{3,2},... | collective-permute-start | bytes 196616 | tf_op jit(solution)/shard_map/ppermute | solution.py:492
  25.0 0.0 all-to-all-done
  25.0 0.0 copy-done.2
  25.0 0.0 copy-done.5
  25.0 0.0 copy-done.7
  25.0 0.0 copy-done.11
  25.0 0.0 copy-done.12
  25.0 0.0 copy-start.4
  25.1 0.7 %shard_map.263 = (bf16[256,64]{1,0:T(8,128)(2,1)S(1)}, f32[64,512]{1,0:T(8,128)S(1)}, bf16[512,512]{1,0:T(8,128)(2,1)S(1)}) custom-call(s32[1]{0:T(128)} %bitcast.1.place_ref, s32[1,1024]{1,0:T(1,128)S(1)} %bitcast.19, s32[64,128]{1,0:T(8,128)S(1)} %bitcast.16, bf16[64,512]{1,0:T(8,128)(2,1)S(1)} %copy-done.2, bf16[512,512]{1,0:T(8,128)(2,1)S(1)} %copy-done.7, ...), custom_call_target="tpu_custom_call" | custom-call | flops 500000000 | bytes 500000 | tf_op jit(solution)/shard_map/pallas_call | solution.py:493
  25.8 0.0 collective-permute-done.from_cross_ref
  25.8 0.1 collective-permute-done.1.from_chip_ref
  25.9 0.0 copy-done.3
  25.9 0.0 copy-done
  25.9 0.0 copy-done.1
  25.9 1.6 %shard_map.264 = (bf16[64,512]{1,0:T(8,128)(2,1)S(1)}, bf16[256,512]{1,0:T(8,128)(2,1)}) custom-call(f32[64,512]{1,0:T(8,128)S(1)} %get-tuple-element.20.own_ref, bf16[64,512]{1,0:T(8,128)(2,1)S(1)} %collective-permute-done.from_cross_ref, bf16[64,512]{1,0:T(8,128)(2,1)S(1)} %collective-permute-done.1.from_chip_ref, bf16[64,512]{1,0:T(8,128)(2,1)S(1)} %copy-done.2, ...), custom_call_target="tpu_custom_call" | custom-call | flops 500000000 | bytes 4000000 | tf_op jit(solution)/shard_map/pallas_call | solution.py:500
  27.5 6.8 %all-to-all-start.1 = ((bf16[16,16,512]{2,1,0:T(8,128)(2,1)}), bf16[16,16,512]{2,1,0:T(8,128)(2,1)S(1)}, u32[]{:S(2)}, u32[]{:S(2)}) async-start(bf16[16,16,512]{2,1,0:T(8,128)(2,1)} %bitcast.9), calls=%async_computation.1 | async-start | bytes 524288 | tf_op jit(solution)/shard_map/all_to_all | solution.py:518
  34.3 0.0 copy-start.6
  34.3 0.0 copy-start.8
  34.3 0.0 copy-start.9
  34.4 0.0 copy-start.13
  34.4 0.0 copy-start.14
  34.4 0.0 copy-start.15
  34.4 0.0 copy-done.4
  34.4 2.5 %shard_map.265.wanted_ref = bf16[512,256]{1,0:T(8,128)(2,1)S(1)} custom-call(s32[1,1024]{1,0:T(1,128)S(1)} %bitcast.20, s32[4,128]{1,0:T(4,128)S(1)} %copy-done.4), custom_call_target="tpu_custom_call" | custom-call | flops 1000000000 | bytes 500000 | tf_op jit(solution)/shard_map/pallas_call | solution.py:520
  36.9 0.0 copy-start.10
  37.0 0.0 copy-start.16
  37.0 0.0 copy-done.6
  37.0 0.0 copy-done.8
  37.0 0.0 copy-done.9
  37.0 0.0 copy-done.13
  37.0 0.0 copy-done.14
  37.0 0.0 copy-done.15
  37.0 0.6 %shard_map.266 = (bf16[64,512]{1,0:T(8,128)(2,1)S(1)}, bf16[512,128]{1,0:T(8,128)(2,1)S(1)}, bf16[128,512]{1,0:T(8,128)(2,1)S(1)}, f32[64,512]{1,0:T(8,128)S(1)}, bf16[512,512]{1,0:T(8,128)(2,1)S(1)}) custom-call(s32[1]{0:T(128)} %bitcast.1.place_ref, s32[1,1024]{1,0:T(1,128)S(1)} %bitcast.21, s32[4,128]{1,0:T(4,128)S(1)} %copy-done.13, ...), custom_call_target="tpu_custom_call" | custom-call | flops 1000000000 | bytes 4000000 | tf_op jit(solution)/shard_map/pallas_call | solution.py:527
  37.7 6.7 %all-to-all-done.1 = bf16[16,16,512]{2,1,0:T(8,128)(2,1)S(1)} async-done(((bf16[16,16,512]{2,1,0:T(8,128)(2,1)}), bf16[16,16,512]{2,1,0:T(8,128)(2,1)S(1)}, u32[]{:S(2)}, u32[]{:S(2)}) %all-to-all-start.1) | async-done | bytes 262176 | tf_op jit(solution)/shard_map/all_to_all | solution.py:518
  44.4 0.0 copy-done.10
  44.4 0.0 copy-done.16
  44.4 1.8 %shard_map.267 = bf16[64,512]{1,0:T(8,128)(2,1)} custom-call(bf16[512,256]{1,0:T(8,128)(2,1)S(1)} %shard_map.265.wanted_ref, bf16[256,512]{1,0:T(8,128)(2,1)S(1)} %bitcast.15, bf16[64,512]{1,0:T(8,128)(2,1)S(1)} %get-tuple-element.30.incoming_ref, bf16[512,128]{1,0:T(8,128)(2,1)S(1)} %get-tuple-element.31.pick_ref, ...), custom_call_target="tpu_custom_call" | custom-call | flops 1000000000 | bytes 4000000 | tf_op jit(solution)/shard_map/pallas_call | solution.py:550
Async XLA Ops:
  1.3 23.7 %all-to-all-start = ((s32[16,4,128]{2,1,0:T(4,128)}), s32[16,4,128]{2,1,0:T(4,128)S(1)}, u32[]{:S(2)}, u32[]{:S(2)}) async-start(s32[16,4,128]{2,1,0:T(4,128)} %tile.2), calls=%async_computation | async-start | bytes 65536 | tf_op jit(solution)/shard_map/all_to_all | solution.py:452
  9.3 15.7 %copy-start.2 = (bf16[64,512]{1,0:T(8,128)(2,1)S(1)}, bf16[64,512]{1,0:T(8,128)(2,1)}, u32[]{:S(2)}) copy-start(bf16[64,512]{1,0:T(8,128)(2,1)} %latent_ref.3) | copy-start | bytes 196612
  9.4 15.7 %copy-start.5 = (bf16[1024,512]{1,0:T(8,128)(2,1)S(1)}, bf16[1024,512]{1,0:T(8,128)(2,1)}, u32[]{:S(2)}) copy-start(bf16[1024,512]{1,0:T(8,128)(2,1)} %node_input_ref.1) | copy-start | bytes 3145732
  9.4 15.6 %copy-start.7 = (bf16[512,512]{1,0:T(8,128)(2,1)S(1)}, bf16[512,512]{1,0:T(8,128)(2,1)}, u32[]{:S(2)}) copy-start(bf16[512,512]{1,0:T(8,128)(2,1)} %edge_out_ref.1) | copy-start | bytes 1572868
  9.4 15.6 %copy-start.11 = (s32[1024]{0:T(1024)S(1)}, s32[1024]{0:T(1024)}, u32[]{:S(2)}) copy-start(s32[1024]{0:T(1024)} %param.53) | copy-start | bytes 12292
  9.4 15.6 %copy-start.12 = (f32[512]{0:T(512)S(1)}, f32[512]{0:T(512)}, u32[]{:S(2)}) copy-start(f32[512]{0:T(512)} %param.37) | copy-start | bytes 6148
  9.4 16.5 %copy-start.3 = (f32[512]{0:T(512)S(1)}, f32[512]{0:T(512)}, u32[]{:S(2)}) copy-start(f32[512]{0:T(512)} %param.39) | copy-start | bytes 6148
  20.8 5.1 %copy-start = (bf16[512,512]{1,0:T(8,128)(2,1)S(1)}, bf16[512,512]{1,0:T(8,128)(2,1)}, u32[]{:S(2)}) copy-start(bf16[512,512]{1,0:T(8,128)(2,1)} %node_out_ref.1) | copy-start | bytes 1572868
  20.9 5.1 %copy-start.1 = (bf16[512,512]{1,0:T(8,128)(2,1)S(1)}, bf16[512,512]{1,0:T(8,128)(2,1)}, u32[]{:S(2)}) copy-start(bf16[512,512]{1,0:T(8,128)(2,1)} %mesh_sender_ref.1) | copy-start | bytes 1572868
  20.9 4.9 %collective-permute-start = (bf16[64,512]{1,0:T(8,128)(2,1)S(1)}, bf16[64,512]{1,0:T(8,128)(2,1)S(1)}, u32[]{:S(2)}, u32[]{:S(2)}) collective-permute-start(bf16[64,512]{1,0:T(8,128)(2,1)S(1)} %get-tuple-element.21), channel_id=1, source_target_pairs={{1,2},{3,4},{5,6},{7,8},{9,10},{11,12},{13,14},{2,1},{4,3},{6,5},{... | collective-permute-start | bytes 196616 | tf_op jit(solution)/shard_map/ppermute | solution.py:491
  21.7 4.2 %collective-permute-start.1 = (bf16[64,512]{1,0:T(8,128)(2,1)S(1)}, bf16[64,512]{1,0:T(8,128)(2,1)S(1)}, u32[]{:S(2)}, u32[]{:S(2)}) collective-permute-start(bf16[64,512]{1,0:T(8,128)(2,1)S(1)} %get-tuple-element.22), channel_id=1, source_target_pairs={{0,1},{2,3},{4,5},{6,7},{8,9},{10,11},{12,13},{14,15},{1,0},{3,2},... | collective-permute-start | bytes 196616 | tf_op jit(solution)/shard_map/ppermute | solution.py:492
  25.0 9.4 %copy-start.4 = (s32[4,128]{1,0:T(4,128)S(1)}, s32[4,128]{1,0:T(4,128)}, u32[]{:S(2)}) copy-start(s32[4,128]{1,0:T(4,128)} %send_ref) | copy-start | bytes 6148
  27.5 16.8 %all-to-all-start.1 = ((bf16[16,16,512]{2,1,0:T(8,128)(2,1)}), bf16[16,16,512]{2,1,0:T(8,128)(2,1)S(1)}, u32[]{:S(2)}, u32[]{:S(2)}) async-start(bf16[16,16,512]{2,1,0:T(8,128)(2,1)} %bitcast.9), calls=%async_computation.1 | async-start | bytes 524288 | tf_op jit(solution)/shard_map/all_to_all | solution.py:518
  34.3 2.7 %copy-start.6 = (bf16[1024,512]{1,0:T(8,128)(2,1)S(1)}, bf16[1024,512]{1,0:T(8,128)(2,1)}, u32[]{:S(2)}) copy-start(bf16[1024,512]{1,0:T(8,128)(2,1)} %update_input_ref.1) | copy-start | bytes 3145732
  34.3 2.6 %copy-start.8 = (bf16[512,512]{1,0:T(8,128)(2,1)S(1)}, bf16[512,512]{1,0:T(8,128)(2,1)}, u32[]{:S(2)}) copy-start(bf16[512,512]{1,0:T(8,128)(2,1)} %mesh_receiver_ref.1) | copy-start | bytes 1572868
  34.3 2.6 %copy-start.9 = (bf16[512,512]{1,0:T(8,128)(2,1)S(1)}, bf16[512,512]{1,0:T(8,128)(2,1)}, u32[]{:S(2)}) copy-start(bf16[512,512]{1,0:T(8,128)(2,1)} %message_out_ref.1) | copy-start | bytes 1572868
  34.4 2.6 %copy-start.13 = (s32[4,128]{1,0:T(4,128)S(1)}, s32[4,128]{1,0:T(4,128)}, u32[]{:S(2)}) copy-start(s32[4,128]{1,0:T(4,128)} %recv_ref.1) | copy-start | bytes 6148
  34.4 2.6 %copy-start.14 = (f32[512]{0:T(512)S(1)}, f32[512]{0:T(512)}, u32[]{:S(2)}) copy-start(f32[512]{0:T(512)} %param.42) | copy-start | bytes 6148
  34.4 2.6 %copy-start.15 = (f32[512]{0:T(512)S(1)}, f32[512]{0:T(512)}, u32[]{:S(2)}) copy-start(f32[512]{0:T(512)} %param.45) | copy-start | bytes 6148
  36.9 7.4 %copy-start.10 = (bf16[512,512]{1,0:T(8,128)(2,1)S(1)}, bf16[512,512]{1,0:T(8,128)(2,1)}, u32[]{:S(2)}) copy-start(bf16[512,512]{1,0:T(8,128)(2,1)} %update_out_ref.1) | copy-start | bytes 1572868
  37.0 7.4 %copy-start.16 = (f32[512]{0:T(512)S(1)}, f32[512]{0:T(512)}, u32[]{:S(2)}) copy-start(f32[512]{0:T(512)} %param.47) | copy-start | bytes 6148

commit v16 on v15

--- a/solution.py
+++ b/solution.py
@@ -18,8 +18,7 @@
 HBM = pltpu.HBM
 GRID_STEPS = 2
 CHUNK_BLOCKS = 4
-ROW_PITCH = 5
-PIECE_PITCH = 2
+PART_ROWS = 64
 MEBI = 1024 * 1024
 
 
@@ -90,6 +89,7 @@
     feat_ref,
     count_ref,
     starts,
+    states,
     table,
     even_rows,
     odd_rows,
@@ -139,7 +139,7 @@
         grid_copy(step).start()
     send_copy.wait()
     senders = send_ref[...]
-    send_ref[...] = senders * ROW_PITCH
+    send_ref[...] = (senders // 8) * (8 * pieces) + senders % 8
     starts_copy.start()
     slot_copy.wait()
     place = place_ref[0]
@@ -156,21 +156,27 @@
     edge_bias_copy.wait()
     grid_bias = 0.5 * grid_bias_ref[...]
     edge_bias = 0.5 * edge_bias_ref[...]
+    parts = [(step, first) for step in range(GRID_STEPS) for first in range(0, step_rows, PART_ROWS)]
     values = []
     for step in range(GRID_STEPS):
         grid_copy(step).wait()
         value = grid_ref[:, step * step_rows : (step + 1) * step_rows].T
         values.append(mm(value, first_ref[...]))
-    values = [silu_half(value + grid_bias).astype(BF16) for value in values]
-    values = [mm(value, second_ref[...]) for value in values]
-    values = [layer_norm(value).astype(BF16) for value in values]
-    values = [mm(value, send_weight_ref[...]) for value in values]
-    for step, value in enumerate(values):
-        row = (value + edge_bias).astype(BF16).astype(F32)
-        for group in range(step_rows // 8):
+    for step, first in parts:
+        half = values[step][first : first + PART_ROWS] + grid_bias
+        states[step, first : first + PART_ROWS, :] = silu_half(half).astype(BF16)
+    values = [mm(states[step], second_ref[...]) for step in range(GRID_STEPS)]
+    for step, first in parts:
+        code = layer_norm(values[step][first : first + PART_ROWS])
+        states[step, first : first + PART_ROWS, :] = code.astype(BF16)
+    values = [mm(states[step], send_weight_ref[...]) for step in range(GRID_STEPS)]
+    for step, first in parts:
+        rows = (values[step][first : first + PART_ROWS] + edge_bias).astype(BF16).astype(F32)
+        base = (step * step_rows + first) * pieces + 8 * pieces
+        for group in range(PART_ROWS // 8):
             for piece in range(pieces):
-                at = (step * step_rows + group * 8) * ROW_PITCH + piece * PIECE_PITCH
-                table[pl.ds(at, 8, stride=ROW_PITCH), :] = row[
+                at = base + (group * pieces + piece) * 8
+                table[at : at + 8, :] = rows[
                     group * 8 : group * 8 + 8, piece * LANES : (piece + 1) * LANES
                 ]
     for copy in copies[7:]:
@@ -181,22 +187,23 @@
     feat_weight = feat_weight.astype(BF16)
     group = CHUNK_BLOCKS
     chunks = blocks // group
-    part_rows = 64
+
+    lower_half = iota((2 * pieces, LANES), 0) < pieces
 
     def gather(chunk, edges, target):
-        for edge in edges:
-            start = starts[chunk * group + edge // block_edges, edge % block_edges]
-            target[pl.ds(edge * ROW_PITCH, pieces, stride=PIECE_PITCH), :] = table[
-                pl.ds(start, pieces, stride=PIECE_PITCH), :
-            ]
+        for edge in edges[::2]:
+            place = [starts[chunk * group + e // block_edges, e % block_edges] for e in (edge, edge + 1)]
+            lower = table[pl.ds(place[0] + 8 * pieces, 2 * pieces, stride=8), :]
+            upper = table[pl.ds(place[1], 2 * pieces, stride=8), :]
+            target[edge * pieces : (edge + 2) * pieces, :] = jnp.where(lower_half, lower, upper)
 
     def rows_of(source, first, count):
         return jnp.concatenate(
             [
                 jnp.concatenate(
                     [
-                        source[pl.ds(at * 8 * ROW_PITCH + piece * PIECE_PITCH, 8, stride=ROW_PITCH), :]
-                        for at in range(first // 8, (first + count) // 8)
+                        source[pl.ds(at * pieces + piece, 8, stride=pieces), :]
+                        for at in range(first, first + count, 8)
                     ],
                     axis=0,
                 )
@@ -215,13 +222,14 @@
         here = [chunk * group + b for b in range(group)]
         feat = jnp.concatenate([feat_ref[b] for b in here], axis=1)
         feat = jnp.concatenate([feat, jnp.zeros((8 - feats, feat.shape[1]), F32)], axis=0)
-        extra = mm(feat.T.astype(BF16), feat_weight)
+        feat = feat.T.astype(BF16)
         add_sums(jnp.maximum(chunk - 1, 0), hidden_before)
         after = jnp.minimum(chunk + 1, chunks - 1)
-        for first in range(0, group * block_edges, part_rows):
-            gather(after, range(first, first + part_rows), target)
-            half = rows_of(source, first, part_rows) + extra[first : first + part_rows]
-            hidden[first : first + part_rows, :] = silu_half(half).astype(BF16)
+        for first in range(0, group * block_edges, PART_ROWS):
+            part = slice(first, first + PART_ROWS)
+            gather(after, range(first, first + PART_ROWS), target)
+            half = rows_of(source, first, PART_ROWS) + mm(feat[part], feat_weight)
+            hidden[part, :] = silu_half(half).astype(BF16)
 
     def edge_step(step, carry):
         work(2 * step, even_rows, odd_rows, even_hidden, odd_hidden)
@@ -471,9 +479,10 @@
         scratch=[VMEM(value.shape, value.dtype) for value in operands]
         + [
             SMEM(g2m_send.shape, I32),
-            VMEM((grid_rows * ROW_PITCH + 8, LANES), F32),
-            VMEM((CHUNK_BLOCKS * g2m_send.shape[1] * ROW_PITCH + 8, LANES), F32),
-            VMEM((CHUNK_BLOCKS * g2m_send.shape[1] * ROW_PITCH + 8, LANES), F32),
+            VMEM((GRID_STEPS, grid_rows // GRID_STEPS, width), BF16),
+            VMEM(((grid_rows + 16) * (width // LANES), LANES), F32),
+            VMEM((CHUNK_BLOCKS * g2m_send.shape[1] * (width // LANES), LANES), F32),
+            VMEM((CHUNK_BLOCKS * g2m_send.shape[1] * (width // LANES), LANES), F32),
             VMEM((CHUNK_BLOCKS * g2m_send.shape[1], width), BF16),
             VMEM((CHUNK_BLOCKS * g2m_send.shape[1], width), BF16),
             VMEM((3 * owned, LANES), I32),

time: 46.5 us -> 47.2 us (1.015)
  Pallas kernels: 18.7 us -> 19.3 us
    pallas_call x1, Pallas kernels: 11.4 us -> 12.1 us  [per_device(): call(edge_kernel, (shape(owned, width, kind=F32), shape(owned, width), sh...]
  transfers between devices with their start and end apart: 4 -> 4, of which waited for: 2 -> 2; matrix products, arithmetic and copies ran while one was open for 0% -> 0% of each run, Pallas kernels for 33% -> 34%
where the time goes in v16:
time: 47.2 us; the launch traced here: 46.8 us
  Pallas kernels  19.3 us (41%)
  starting transfers between devices  18.3 us (39%)
  waiting for transfers between devices  6.83 us (14%)
  local copies, waits for them, and re-layouts  1.41 us (3%)
  between operations  0.94 us (2%)
    pallas_call x1, Pallas kernels, per_device(): call(edge_kernel, (shape(owned, width, kind=F32), shape(owned, width), sh...  12.1 us
    all_to_all x1, starting transfers between devices, per_device(): lax.all_to_all(jnp.tile(mesh_send, (devices, 1)), 'bulk', 0, 0, tiled=True)  7.39 us
    all_to_all x1, starting transfers between devices, per_device(): piece = lax.all_to_all(rows, 'bulk', 0, 0, tiled=True)  6.79 us
    all_to_all x1, waiting for transfers between devices, per_device(): piece = lax.all_to_all(rows, 'bulk', 0, 0, tiled=True)  6.71 us
    ppermute x1, starting transfers between devices, per_device(): from_chip = lax.ppermute(chip, 'bulk', both(within))  3.36 us
    pallas_call x1, Pallas kernels, per_device(): call(functools.partial(wanted_kernel, owned), shape(edges, places), [VMEM...  2.53 us
    pallas_call x1, Pallas kernels, per_device(): call(message_kernel, shape(owned, width), [VMEM] * 10, flops=1000000000,...  1.77 us
    pallas_call x1, Pallas kernels, per_device(): call(node_kernel, (shape(owned, width), shape(places, width)), [VMEM] * 1...  1.63 us
  transfers between devices with their start and end apart: 4, of which 2 were waited for; matrix products, arithmetic and copies ran while one was open for 0% of the time, Pallas kernels for 34%

profile of v16, /device:TPU:0, one launch (start us, length us, event | category | flops | bytes accessed | tf_op | source)
XLA Modules:
  0.0 46.8 jit_solution(1792147117007450898)
XLA Ops:
  0.0 1.3 %tile.2 = s32[16,4,128]{2,1,0:T(4,128)} broadcast(s32[4,128]{1,0:T(4,128)} %send_ref), dimensions={1,2} | broadcast | bytes 34816 | tf_op jit(solution)/shard_map/tile | solution.py:460
  1.3 7.4 %all-to-all-start = ((s32[16,4,128]{2,1,0:T(4,128)}), s32[16,4,128]{2,1,0:T(4,128)S(1)}, u32[]{:S(2)}, u32[]{:S(2)}) async-start(s32[16,4,128]{2,1,0:T(4,128)} %tile.2), calls=%async_computation | async-start | bytes 65536 | tf_op jit(solution)/shard_map/all_to_all | solution.py:460
  9.3 0.0 copy-start.2
  9.4 0.0 copy-start.5
  9.4 0.0 copy-start.7
  9.4 0.0 copy-start.11
  9.4 0.0 copy-start.12
  9.4 0.0 copy-start.3
  9.4 12.1 %shard_map.262 = (f32[64,512]{1,0:T(8,128)S(1)}, bf16[64,512]{1,0:T(8,128)(2,1)S(1)}, bf16[64,512]{1,0:T(8,128)(2,1)S(1)}) custom-call(s32[1]{0:T(128)} %bitcast.1.place_ref, bf16[474,512]{1,0:T(8,128)(2,1)} %first_hbm.1, bf16[474,2048]{1,0:T(8,128)(2,1)} %bitcast.26, bf16[512,512]{1,0:T(8,128)(2,1)} %second_hbm.1, bf16[512,512]{1,0:T(8,128)(2,1)} %send_weight_hbm.1, ...), custom_call_target="tpu_custom_call" | custom-call | flops 10000000000 | bytes 4000000 | tf_op jit(solution)/shard_map/pallas_call | solution.py:475
  21.5 0.0 copy-start
  21.5 0.0 copy-start.1
  21.5 0.8 %collective-permute-start = (bf16[64,512]{1,0:T(8,128)(2,1)S(1)}, bf16[64,512]{1,0:T(8,128)(2,1)S(1)}, u32[]{:S(2)}, u32[]{:S(2)}) collective-permute-start(bf16[64,512]{1,0:T(8,128)(2,1)S(1)} %get-tuple-element.21), channel_id=1, source_target_pairs={{1,2},{3,4},{5,6},{7,8},{9,10},{11,12},{13,14},{2,1},{4,3},{6,5},{... | collective-permute-start | bytes 196616 | tf_op jit(solution)/shard_map/ppermute | solution.py:500
  22.3 3.4 %collective-permute-start.1 = (bf16[64,512]{1,0:T(8,128)(2,1)S(1)}, bf16[64,512]{1,0:T(8,128)(2,1)S(1)}, u32[]{:S(2)}, u32[]{:S(2)}) collective-permute-start(bf16[64,512]{1,0:T(8,128)(2,1)S(1)} %get-tuple-element.22), channel_id=1, source_target_pairs={{0,1},{2,3},{4,5},{6,7},{8,9},{10,11},{12,13},{14,15},{1,0},{3,2},... | collective-permute-start | bytes 196616 | tf_op jit(solution)/shard_map/ppermute | solution.py:501
  25.7 0.0 all-to-all-done
  25.7 0.0 copy-done.2
  25.7 0.0 copy-done.5
  25.7 0.0 copy-done.7
  25.7 0.0 copy-done.11
  25.7 0.0 copy-done.12
  25.7 0.0 copy-start.4
  25.7 0.7 %shard_map.263 = (bf16[256,64]{1,0:T(8,128)(2,1)S(1)}, f32[64,512]{1,0:T(8,128)S(1)}, bf16[512,512]{1,0:T(8,128)(2,1)S(1)}) custom-call(s32[1]{0:T(128)} %bitcast.1.place_ref, s32[1,1024]{1,0:T(1,128)S(1)} %bitcast.19, s32[64,128]{1,0:T(8,128)S(1)} %bitcast.16, bf16[64,512]{1,0:T(8,128)(2,1)S(1)} %copy-done.2, bf16[512,512]{1,0:T(8,128)(2,1)S(1)} %copy-done.7, ...), custom_call_target="tpu_custom_call" | custom-call | flops 500000000 | bytes 500000 | tf_op jit(solution)/shard_map/pallas_call | solution.py:502
  26.5 0.0 collective-permute-done.from_cross_ref
  26.5 0.1 collective-permute-done.1.from_chip_ref
  26.6 0.0 copy-done.3
  26.6 0.0 copy-done
  26.6 0.0 copy-done.1
  26.6 1.6 %shard_map.264 = (bf16[64,512]{1,0:T(8,128)(2,1)S(1)}, bf16[256,512]{1,0:T(8,128)(2,1)}) custom-call(f32[64,512]{1,0:T(8,128)S(1)} %get-tuple-element.20.own_ref, bf16[64,512]{1,0:T(8,128)(2,1)S(1)} %collective-permute-done.from_cross_ref, bf16[64,512]{1,0:T(8,128)(2,1)S(1)} %collective-permute-done.1.from_chip_ref, bf16[64,512]{1,0:T(8,128)(2,1)S(1)} %copy-done.2, ...), custom_call_target="tpu_custom_call" | custom-call | flops 500000000 | bytes 4000000 | tf_op jit(solution)/shard_map/pallas_call | solution.py:509
  28.2 6.8 %all-to-all-start.1 = ((bf16[16,16,512]{2,1,0:T(8,128)(2,1)}), bf16[16,16,512]{2,1,0:T(8,128)(2,1)S(1)}, u32[]{:S(2)}, u32[]{:S(2)}) async-start(bf16[16,16,512]{2,1,0:T(8,128)(2,1)} %bitcast.9), calls=%async_computation.1 | async-start | bytes 524288 | tf_op jit(solution)/shard_map/all_to_all | solution.py:527
  35.0 0.0 copy-start.6
  35.0 0.0 copy-start.8
  35.0 0.0 copy-start.9
  35.0 0.0 copy-start.13
  35.1 0.0 copy-start.14
  35.1 0.0 copy-start.15
  35.1 0.0 copy-done.4
  35.1 2.5 %shard_map.265.wanted_ref = bf16[512,256]{1,0:T(8,128)(2,1)S(1)} custom-call(s32[1,1024]{1,0:T(1,128)S(1)} %bitcast.20, s32[4,128]{1,0:T(4,128)S(1)} %copy-done.4), custom_call_target="tpu_custom_call" | custom-call | flops 1000000000 | bytes 500000 | tf_op jit(solution)/shard_map/pallas_call | solution.py:529
  37.6 0.0 copy-start.10
  37.6 0.0 copy-start.16
  37.7 0.0 copy-done.6
  37.7 0.0 copy-done.8
  37.7 0.0 copy-done.9
  37.7 0.0 copy-done.13
  37.7 0.0 copy-done.14
  37.7 0.0 copy-done.15
  37.7 0.6 %shard_map.266 = (bf16[64,512]{1,0:T(8,128)(2,1)S(1)}, bf16[512,128]{1,0:T(8,128)(2,1)S(1)}, bf16[128,512]{1,0:T(8,128)(2,1)S(1)}, f32[64,512]{1,0:T(8,128)S(1)}, bf16[512,512]{1,0:T(8,128)(2,1)S(1)}) custom-call(s32[1]{0:T(128)} %bitcast.1.place_ref, s32[1,1024]{1,0:T(1,128)S(1)} %bitcast.21, s32[4,128]{1,0:T(4,128)S(1)} %copy-done.13, ...), custom_call_target="tpu_custom_call" | custom-call | flops 1000000000 | bytes 4000000 | tf_op jit(solution)/shard_map/pallas_call | solution.py:536
  38.3 6.7 %all-to-all-done.1 = bf16[16,16,512]{2,1,0:T(8,128)(2,1)S(1)} async-done(((bf16[16,16,512]{2,1,0:T(8,128)(2,1)}), bf16[16,16,512]{2,1,0:T(8,128)(2,1)S(1)}, u32[]{:S(2)}, u32[]{:S(2)}) %all-to-all-start.1) | async-done | bytes 262176 | tf_op jit(solution)/shard_map/all_to_all | solution.py:527
  45.1 0.0 copy-done.10
  45.1 0.0 copy-done.16
  45.1 1.8 %shard_map.267 = bf16[64,512]{1,0:T(8,128)(2,1)} custom-call(bf16[512,256]{1,0:T(8,128)(2,1)S(1)} %shard_map.265.wanted_ref, bf16[256,512]{1,0:T(8,128)(2,1)S(1)} %bitcast.15, bf16[64,512]{1,0:T(8,128)(2,1)S(1)} %get-tuple-element.30.incoming_ref, bf16[512,128]{1,0:T(8,128)(2,1)S(1)} %get-tuple-element.31.pick_ref, ...), custom_call_target="tpu_custom_call" | custom-call | flops 1000000000 | bytes 4000000 | tf_op jit(solution)/shard_map/pallas_call | solution.py:559
Async XLA Ops:
  1.3 24.4 %all-to-all-start = ((s32[16,4,128]{2,1,0:T(4,128)}), s32[16,4,128]{2,1,0:T(4,128)S(1)}, u32[]{:S(2)}, u32[]{:S(2)}) async-start(s32[16,4,128]{2,1,0:T(4,128)} %tile.2), calls=%async_computation | async-start | bytes 65536 | tf_op jit(solution)/shard_map/all_to_all | solution.py:460
  9.3 16.3 %copy-start.2 = (bf16[64,512]{1,0:T(8,128)(2,1)S(1)}, bf16[64,512]{1,0:T(8,128)(2,1)}, u32[]{:S(2)}) copy-start(bf16[64,512]{1,0:T(8,128)(2,1)} %latent_ref.3) | copy-start | bytes 196612
  9.4 16.3 %copy-start.5 = (bf16[1024,512]{1,0:T(8,128)(2,1)S(1)}, bf16[1024,512]{1,0:T(8,128)(2,1)}, u32[]{:S(2)}) copy-start(bf16[1024,512]{1,0:T(8,128)(2,1)} %node_input_ref.1) | copy-start | bytes 3145732
  9.4 16.3 %copy-start.7 = (bf16[512,512]{1,0:T(8,128)(2,1)S(1)}, bf16[512,512]{1,0:T(8,128)(2,1)}, u32[]{:S(2)}) copy-start(bf16[512,512]{1,0:T(8,128)(2,1)} %edge_out_ref.1) | copy-start | bytes 1572868
  9.4 16.3 %copy-start.11 = (s32[1024]{0:T(1024)S(1)}, s32[1024]{0:T(1024)}, u32[]{:S(2)}) copy-start(s32[1024]{0:T(1024)} %param.53) | copy-start | bytes 12292
  9.4 16.3 %copy-start.12 = (f32[512]{0:T(512)S(1)}, f32[512]{0:T(512)}, u32[]{:S(2)}) copy-start(f32[512]{0:T(512)} %param.37) | copy-start | bytes 6148
  9.4 17.2 %copy-start.3 = (f32[512]{0:T(512)S(1)}, f32[512]{0:T(512)}, u32[]{:S(2)}) copy-start(f32[512]{0:T(512)} %param.39) | copy-start | bytes 6148
  21.5 5.1 %copy-start = (bf16[512,512]{1,0:T(8,128)(2,1)S(1)}, bf16[512,512]{1,0:T(8,128)(2,1)}, u32[]{:S(2)}) copy-start(bf16[512,512]{1,0:T(8,128)(2,1)} %node_out_ref.1) | copy-start | bytes 1572868
  21.5 5.1 %copy-start.1 = (bf16[512,512]{1,0:T(8,128)(2,1)S(1)}, bf16[512,512]{1,0:T(8,128)(2,1)}, u32[]{:S(2)}) copy-start(bf16[512,512]{1,0:T(8,128)(2,1)} %mesh_sender_ref.1) | copy-start | bytes 1572868
  21.5 4.9 %collective-permute-start = (bf16[64,512]{1,0:T(8,128)(2,1)S(1)}, bf16[64,512]{1,0:T(8,128)(2,1)S(1)}, u32[]{:S(2)}, u32[]{:S(2)}) collective-permute-start(bf16[64,512]{1,0:T(8,128)(2,1)S(1)} %get-tuple-element.21), channel_id=1, source_target_pairs={{1,2},{3,4},{5,6},{7,8},{9,10},{11,12},{13,14},{2,1},{4,3},{6,5},{... | collective-permute-start | bytes 196616 | tf_op jit(solution)/shard_map/ppermute | solution.py:500
  22.3 4.3 %collective-permute-start.1 = (bf16[64,512]{1,0:T(8,128)(2,1)S(1)}, bf16[64,512]{1,0:T(8,128)(2,1)S(1)}, u32[]{:S(2)}, u32[]{:S(2)}) collective-permute-start(bf16[64,512]{1,0:T(8,128)(2,1)S(1)} %get-tuple-element.22), channel_id=1, source_target_pairs={{0,1},{2,3},{4,5},{6,7},{8,9},{10,11},{12,13},{14,15},{1,0},{3,2},... | collective-permute-start | bytes 196616 | tf_op jit(solution)/shard_map/ppermute | solution.py:501
  25.7 9.4 %copy-start.4 = (s32[4,128]{1,0:T(4,128)S(1)}, s32[4,128]{1,0:T(4,128)}, u32[]{:S(2)}) copy-start(s32[4,128]{1,0:T(4,128)} %send_ref) | copy-start | bytes 6148
  28.2 16.8 %all-to-all-start.1 = ((bf16[16,16,512]{2,1,0:T(8,128)(2,1)}), bf16[16,16,512]{2,1,0:T(8,128)(2,1)S(1)}, u32[]{:S(2)}, u32[]{:S(2)}) async-start(bf16[16,16,512]{2,1,0:T(8,128)(2,1)} %bitcast.9), calls=%async_computation.1 | async-start | bytes 524288 | tf_op jit(solution)/shard_map/all_to_all | solution.py:527
  35.0 2.6 %copy-start.6 = (bf16[1024,512]{1,0:T(8,128)(2,1)S(1)}, bf16[1024,512]{1,0:T(8,128)(2,1)}, u32[]{:S(2)}) copy-start(bf16[1024,512]{1,0:T(8,128)(2,1)} %update_input_ref.1) | copy-start | bytes 3145732
  35.0 2.6 %copy-start.8 = (bf16[512,512]{1,0:T(8,128)(2,1)S(1)}, bf16[512,512]{1,0:T(8,128)(2,1)}, u32[]{:S(2)}) copy-start(bf16[512,512]{1,0:T(8,128)(2,1)} %mesh_receiver_ref.1) | copy-start | bytes 1572868
  35.0 2.6 %copy-start.9 = (bf16[512,512]{1,0:T(8,128)(2,1)S(1)}, bf16[512,512]{1,0:T(8,128)(2,1)}, u32[]{:S(2)}) copy-start(bf16[512,512]{1,0:T(8,128)(2,1)} %message_out_ref.1) | copy-start | bytes 1572868
  35.0 2.6 %copy-start.13 = (s32[4,128]{1,0:T(4,128)S(1)}, s32[4,128]{1,0:T(4,128)}, u32[]{:S(2)}) copy-start(s32[4,128]{1,0:T(4,128)} %recv_ref.1) | copy-start | bytes 6148
  35.1 2.6 %copy-start.14 = (f32[512]{0:T(512)S(1)}, f32[512]{0:T(512)}, u32[]{:S(2)}) copy-start(f32[512]{0:T(512)} %param.42) | copy-start | bytes 6148
  35.1 2.6 %copy-start.15 = (f32[512]{0:T(512)S(1)}, f32[512]{0:T(512)}, u32[]{:S(2)}) copy-start(f32[512]{0:T(512)} %param.45) | copy-start | bytes 6148
  37.6 7.4 %copy-start.10 = (bf16[512,512]{1,0:T(8,128)(2,1)S(1)}, bf16[512,512]{1,0:T(8,128)(2,1)}, u32[]{:S(2)}) copy-start(bf16[512,512]{1,0:T(8,128)(2,1)} %update_out_ref.1) | copy-start | bytes 1572868
  37.6 7.4 %copy-start.16 = (f32[512]{0:T(512)S(1)}, f32[512]{0:T(512)}, u32[]{:S(2)}) copy-start(f32[512]{0:T(512)} %param.47) | copy-start | bytes 6148

commit v17 on v16

--- a/solution.py
+++ b/solution.py
@@ -172,7 +172,7 @@
     values = [mm(states[step], send_weight_ref[...]) for step in range(GRID_STEPS)]
     for step, first in parts:
         rows = (values[step][first : first + PART_ROWS] + edge_bias).astype(BF16).astype(F32)
-        base = (step * step_rows + first) * pieces + 8 * pieces
+        base = (step * step_rows + first) * pieces
         for group in range(PART_ROWS // 8):
             for piece in range(pieces):
                 at = base + (group * pieces + piece) * 8
@@ -188,22 +188,20 @@
     group = CHUNK_BLOCKS
     chunks = blocks // group
 
-    lower_half = iota((2 * pieces, LANES), 0) < pieces
-
     def gather(chunk, edges, target):
-        for edge in edges[::2]:
-            place = [starts[chunk * group + e // block_edges, e % block_edges] for e in (edge, edge + 1)]
-            lower = table[pl.ds(place[0] + 8 * pieces, 2 * pieces, stride=8), :]
-            upper = table[pl.ds(place[1], 2 * pieces, stride=8), :]
-            target[edge * pieces : (edge + 2) * pieces, :] = jnp.where(lower_half, lower, upper)
+        for edge in edges:
+            start = starts[chunk * group + edge // block_edges, edge % block_edges]
+            target[pl.ds(edge // 8 * (8 * pieces) + edge % 8, pieces, stride=8), :] = table[
+                pl.ds(start, pieces, stride=8), :
+            ]
 
     def rows_of(source, first, count):
         return jnp.concatenate(
             [
                 jnp.concatenate(
                     [
-                        source[pl.ds(at * pieces + piece, 8, stride=pieces), :]
-                        for at in range(first, first + count, 8)
+                        source[pl.ds((at * pieces + piece) * 8, 8), :]
+                        for at in range(first // 8, (first + count) // 8)
                     ],
                     axis=0,
                 )
@@ -222,14 +220,13 @@
         here = [chunk * group + b for b in range(group)]
         feat = jnp.concatenate([feat_ref[b] for b in here], axis=1)
         feat = jnp.concatenate([feat, jnp.zeros((8 - feats, feat.shape[1]), F32)], axis=0)
-        feat = feat.T.astype(BF16)
+        extra = mm(feat.T.astype(BF16), feat_weight)
         add_sums(jnp.maximum(chunk - 1, 0), hidden_before)
         after = jnp.minimum(chunk + 1, chunks - 1)
         for first in range(0, group * block_edges, PART_ROWS):
-            part = slice(first, first + PART_ROWS)
             gather(after, range(first, first + PART_ROWS), target)
-            half = rows_of(source, first, PART_ROWS) + mm(feat[part], feat_weight)
-            hidden[part, :] = silu_half(half).astype(BF16)
+            half = rows_of(source, first, PART_ROWS) + extra[first : first + PART_ROWS]
+            hidden[first : first + PART_ROWS, :] = silu_half(half).astype(BF16)
 
     def edge_step(step, carry):
         work(2 * step, even_rows, odd_rows, even_hidden, odd_hidden)
@@ -480,7 +477,7 @@
         + [
             SMEM(g2m_send.shape, I32),
             VMEM((GRID_STEPS, grid_rows // GRID_STEPS, width), BF16),
-            VMEM(((grid_rows + 16) * (width // LANES), LANES), F32),
+            VMEM((grid_rows * (width // LANES), LANES), F32),
             VMEM((CHUNK_BLOCKS * g2m_send.shape[1] * (width // LANES), LANES), F32),
             VMEM((CHUNK_BLOCKS * g2m_send.shape[1] * (width // LANES), LANES), F32),
             VMEM((CHUNK_BLOCKS * g2m_send.shape[1], width), BF16),

time: 47.2 us -> 46.1 us (0.977)
  Pallas kernels: 19.3 us -> 18.3 us
    pallas_call x1, Pallas kernels: 12.1 us -> 11 us  [per_device(): call(edge_kernel, (shape(owned, width, kind=F32), shape(owned, width), sh...]
  transfers between devices with their start and end apart: 4 -> 4, of which waited for: 2 -> 2; matrix products, arithmetic and copies ran while one was open for 0% -> 0% of each run, Pallas kernels for 34% -> 33%
where the time goes in v17:
time: 46.1 us; the launch traced here: 45.8 us
  starting transfers between devices  18.3 us (40%)
  Pallas kernels  18.3 us (40%)
  waiting for transfers between devices  6.83 us (15%)
  local copies, waits for them, and re-layouts  1.41 us (3%)
  between operations  0.94 us (2%)
    pallas_call x1, Pallas kernels, per_device(): call(edge_kernel, (shape(owned, width, kind=F32), shape(owned, width), sh...  11 us
    all_to_all x1, starting transfers between devices, per_device(): lax.all_to_all(jnp.tile(mesh_send, (devices, 1)), 'bulk', 0, 0, tiled=True)  7.39 us
    all_to_all x1, starting transfers between devices, per_device(): piece = lax.all_to_all(rows, 'bulk', 0, 0, tiled=True)  6.8 us
    all_to_all x1, waiting for transfers between devices, per_device(): piece = lax.all_to_all(rows, 'bulk', 0, 0, tiled=True)  6.71 us
    ppermute x1, starting transfers between devices, per_device(): from_chip = lax.ppermute(chip, 'bulk', both(within))  3.34 us
    pallas_call x1, Pallas kernels, per_device(): call(functools.partial(wanted_kernel, owned), shape(edges, places), [VMEM...  2.53 us
    pallas_call x1, Pallas kernels, per_device(): call(message_kernel, shape(owned, width), [VMEM] * 10, flops=1000000000,...  1.77 us
    pallas_call x1, Pallas kernels, per_device(): call(node_kernel, (shape(owned, width), shape(places, width)), [VMEM] * 1...  1.63 us
  transfers between devices with their start and end apart: 4, of which 2 were waited for; matrix products, arithmetic and copies ran while one was open for 0% of the time, Pallas kernels for 33%

profile of v17, /device:TPU:0, one launch (start us, length us, event | category | flops | bytes accessed | tf_op | source)
XLA Modules:
  0.0 45.8 jit_solution(3241660402438581011)
XLA Ops:
  0.0 1.3 %tile.2 = s32[16,4,128]{2,1,0:T(4,128)} broadcast(s32[4,128]{1,0:T(4,128)} %send_ref), dimensions={1,2} | broadcast | bytes 34816 | tf_op jit(solution)/shard_map/tile | solution.py:457
  1.3 7.4 %all-to-all-start = ((s32[16,4,128]{2,1,0:T(4,128)}), s32[16,4,128]{2,1,0:T(4,128)S(1)}, u32[]{:S(2)}, u32[]{:S(2)}) async-start(s32[16,4,128]{2,1,0:T(4,128)} %tile.2), calls=%async_computation | async-start | bytes 65536 | tf_op jit(solution)/shard_map/all_to_all | solution.py:457
  9.3 0.0 copy-start.2
  9.4 0.0 copy-start.5
  9.4 0.0 copy-start.7
  9.4 0.0 copy-start.11
  9.4 0.0 copy-start.12
  9.4 0.0 copy-start.3
  9.4 11.0 %shard_map.262 = (f32[64,512]{1,0:T(8,128)S(1)}, bf16[64,512]{1,0:T(8,128)(2,1)S(1)}, bf16[64,512]{1,0:T(8,128)(2,1)S(1)}) custom-call(s32[1]{0:T(128)} %bitcast.1.place_ref, bf16[474,512]{1,0:T(8,128)(2,1)} %first_hbm.1, bf16[474,2048]{1,0:T(8,128)(2,1)} %bitcast.26, bf16[512,512]{1,0:T(8,128)(2,1)} %second_hbm.1, bf16[512,512]{1,0:T(8,128)(2,1)} %send_weight_hbm.1, ...), custom_call_target="tpu_custom_call" | custom-call | flops 10000000000 | bytes 4000000 | tf_op jit(solution)/shard_map/pallas_call | solution.py:472
  20.5 0.0 copy-start
  20.5 0.0 copy-start.1
  20.5 0.8 %collective-permute-start = (bf16[64,512]{1,0:T(8,128)(2,1)S(1)}, bf16[64,512]{1,0:T(8,128)(2,1)S(1)}, u32[]{:S(2)}, u32[]{:S(2)}) collective-permute-start(bf16[64,512]{1,0:T(8,128)(2,1)S(1)} %get-tuple-element.21), channel_id=1, source_target_pairs={{1,2},{3,4},{5,6},{7,8},{9,10},{11,12},{13,14},{2,1},{4,3},{6,5},{... | collective-permute-start | bytes 196616 | tf_op jit(solution)/shard_map/ppermute | solution.py:497
  21.3 3.3 %collective-permute-start.1 = (bf16[64,512]{1,0:T(8,128)(2,1)S(1)}, bf16[64,512]{1,0:T(8,128)(2,1)S(1)}, u32[]{:S(2)}, u32[]{:S(2)}) collective-permute-start(bf16[64,512]{1,0:T(8,128)(2,1)S(1)} %get-tuple-element.22), channel_id=1, source_target_pairs={{0,1},{2,3},{4,5},{6,7},{8,9},{10,11},{12,13},{14,15},{1,0},{3,2},... | collective-permute-start | bytes 196616 | tf_op jit(solution)/shard_map/ppermute | solution.py:498
  24.6 0.0 all-to-all-done
  24.6 0.0 copy-done.2
  24.6 0.0 copy-done.5
  24.6 0.0 copy-done.7
  24.6 0.0 copy-done.11
  24.7 0.0 copy-done.12
  24.7 0.0 copy-start.4
  24.7 0.7 %shard_map.263 = (bf16[256,64]{1,0:T(8,128)(2,1)S(1)}, f32[64,512]{1,0:T(8,128)S(1)}, bf16[512,512]{1,0:T(8,128)(2,1)S(1)}) custom-call(s32[1]{0:T(128)} %bitcast.1.place_ref, s32[1,1024]{1,0:T(1,128)S(1)} %bitcast.19, s32[64,128]{1,0:T(8,128)S(1)} %bitcast.16, bf16[64,512]{1,0:T(8,128)(2,1)S(1)} %copy-done.2, bf16[512,512]{1,0:T(8,128)(2,1)S(1)} %copy-done.7, ...), custom_call_target="tpu_custom_call" | custom-call | flops 500000000 | bytes 500000 | tf_op jit(solution)/shard_map/pallas_call | solution.py:499
  25.4 0.0 collective-permute-done.from_cross_ref
  25.4 0.1 collective-permute-done.1.from_chip_ref
  25.5 0.0 copy-done.3
  25.5 0.0 copy-done
  25.5 0.0 copy-done.1
  25.5 1.6 %shard_map.264 = (bf16[64,512]{1,0:T(8,128)(2,1)S(1)}, bf16[256,512]{1,0:T(8,128)(2,1)}) custom-call(f32[64,512]{1,0:T(8,128)S(1)} %get-tuple-element.20.own_ref, bf16[64,512]{1,0:T(8,128)(2,1)S(1)} %collective-permute-done.from_cross_ref, bf16[64,512]{1,0:T(8,128)(2,1)S(1)} %collective-permute-done.1.from_chip_ref, bf16[64,512]{1,0:T(8,128)(2,1)S(1)} %copy-done.2, ...), custom_call_target="tpu_custom_call" | custom-call | flops 500000000 | bytes 4000000 | tf_op jit(solution)/shard_map/pallas_call | solution.py:506
  27.2 6.8 %all-to-all-start.1 = ((bf16[16,16,512]{2,1,0:T(8,128)(2,1)}), bf16[16,16,512]{2,1,0:T(8,128)(2,1)S(1)}, u32[]{:S(2)}, u32[]{:S(2)}) async-start(bf16[16,16,512]{2,1,0:T(8,128)(2,1)} %bitcast.9), calls=%async_computation.1 | async-start | bytes 524288 | tf_op jit(solution)/shard_map/all_to_all | solution.py:524
  34.0 0.0 copy-start.6
  34.0 0.0 copy-start.8
  34.0 0.0 copy-start.9
  34.0 0.0 copy-start.13
  34.0 0.0 copy-start.14
  34.0 0.0 copy-start.15
  34.0 0.0 copy-done.4
  34.0 2.5 %shard_map.265.wanted_ref = bf16[512,256]{1,0:T(8,128)(2,1)S(1)} custom-call(s32[1,1024]{1,0:T(1,128)S(1)} %bitcast.20, s32[4,128]{1,0:T(4,128)S(1)} %copy-done.4), custom_call_target="tpu_custom_call" | custom-call | flops 1000000000 | bytes 500000 | tf_op jit(solution)/shard_map/pallas_call | solution.py:526
  36.6 0.0 copy-start.10
  36.6 0.0 copy-start.16
  36.6 0.0 copy-done.6
  36.6 0.0 copy-done.8
  36.6 0.0 copy-done.9
  36.6 0.0 copy-done.13
  36.7 0.0 copy-done.14
  36.7 0.0 copy-done.15
  36.7 0.6 %shard_map.266 = (bf16[64,512]{1,0:T(8,128)(2,1)S(1)}, bf16[512,128]{1,0:T(8,128)(2,1)S(1)}, bf16[128,512]{1,0:T(8,128)(2,1)S(1)}, f32[64,512]{1,0:T(8,128)S(1)}, bf16[512,512]{1,0:T(8,128)(2,1)S(1)}) custom-call(s32[1]{0:T(128)} %bitcast.1.place_ref, s32[1,1024]{1,0:T(1,128)S(1)} %bitcast.21, s32[4,128]{1,0:T(4,128)S(1)} %copy-done.13, ...), custom_call_target="tpu_custom_call" | custom-call | flops 1000000000 | bytes 4000000 | tf_op jit(solution)/shard_map/pallas_call | solution.py:533
  37.3 6.7 %all-to-all-done.1 = bf16[16,16,512]{2,1,0:T(8,128)(2,1)S(1)} async-done(((bf16[16,16,512]{2,1,0:T(8,128)(2,1)}), bf16[16,16,512]{2,1,0:T(8,128)(2,1)S(1)}, u32[]{:S(2)}, u32[]{:S(2)}) %all-to-all-start.1) | async-done | bytes 262176 | tf_op jit(solution)/shard_map/all_to_all | solution.py:524
  44.0 0.0 copy-done.10
  44.0 0.0 copy-done.16
  44.0 1.8 %shard_map.267 = bf16[64,512]{1,0:T(8,128)(2,1)} custom-call(bf16[512,256]{1,0:T(8,128)(2,1)S(1)} %shard_map.265.wanted_ref, bf16[256,512]{1,0:T(8,128)(2,1)S(1)} %bitcast.15, bf16[64,512]{1,0:T(8,128)(2,1)S(1)} %get-tuple-element.30.incoming_ref, bf16[512,128]{1,0:T(8,128)(2,1)S(1)} %get-tuple-element.31.pick_ref, ...), custom_call_target="tpu_custom_call" | custom-call | flops 1000000000 | bytes 4000000 | tf_op jit(solution)/shard_map/pallas_call | solution.py:556
Async XLA Ops:
  1.3 23.3 %all-to-all-start = ((s32[16,4,128]{2,1,0:T(4,128)}), s32[16,4,128]{2,1,0:T(4,128)S(1)}, u32[]{:S(2)}, u32[]{:S(2)}) async-start(s32[16,4,128]{2,1,0:T(4,128)} %tile.2), calls=%async_computation | async-start | bytes 65536 | tf_op jit(solution)/shard_map/all_to_all | solution.py:457
  9.3 15.3 %copy-start.2 = (bf16[64,512]{1,0:T(8,128)(2,1)S(1)}, bf16[64,512]{1,0:T(8,128)(2,1)}, u32[]{:S(2)}) copy-start(bf16[64,512]{1,0:T(8,128)(2,1)} %latent_ref.3) | copy-start | bytes 196612
  9.4 15.3 %copy-start.5 = (bf16[1024,512]{1,0:T(8,128)(2,1)S(1)}, bf16[1024,512]{1,0:T(8,128)(2,1)}, u32[]{:S(2)}) copy-start(bf16[1024,512]{1,0:T(8,128)(2,1)} %node_input_ref.1) | copy-start | bytes 3145732
  9.4 15.3 %copy-start.7 = (bf16[512,512]{1,0:T(8,128)(2,1)S(1)}, bf16[512,512]{1,0:T(8,128)(2,1)}, u32[]{:S(2)}) copy-start(bf16[512,512]{1,0:T(8,128)(2,1)} %edge_out_ref.1) | copy-start | bytes 1572868
  9.4 15.3 %copy-start.11 = (s32[1024]{0:T(1024)S(1)}, s32[1024]{0:T(1024)}, u32[]{:S(2)}) copy-start(s32[1024]{0:T(1024)} %param.53) | copy-start | bytes 12292
  9.4 15.3 %copy-start.12 = (f32[512]{0:T(512)S(1)}, f32[512]{0:T(512)}, u32[]{:S(2)}) copy-start(f32[512]{0:T(512)} %param.37) | copy-start | bytes 6148
  9.4 16.1 %copy-start.3 = (f32[512]{0:T(512)S(1)}, f32[512]{0:T(512)}, u32[]{:S(2)}) copy-start(f32[512]{0:T(512)} %param.39) | copy-start | bytes 6148
  20.5 5.1 %copy-start = (bf16[512,512]{1,0:T(8,128)(2,1)S(1)}, bf16[512,512]{1,0:T(8,128)(2,1)}, u32[]{:S(2)}) copy-start(bf16[512,512]{1,0:T(8,128)(2,1)} %node_out_ref.1) | copy-start | bytes 1572868
  20.5 5.1 %copy-start.1 = (bf16[512,512]{1,0:T(8,128)(2,1)S(1)}, bf16[512,512]{1,0:T(8,128)(2,1)}, u32[]{:S(2)}) copy-start(bf16[512,512]{1,0:T(8,128)(2,1)} %mesh_sender_ref.1) | copy-start | bytes 1572868
  20.5 4.9 %collective-permute-start = (bf16[64,512]{1,0:T(8,128)(2,1)S(1)}, bf16[64,512]{1,0:T(8,128)(2,1)S(1)}, u32[]{:S(2)}, u32[]{:S(2)}) collective-permute-start(bf16[64,512]{1,0:T(8,128)(2,1)S(1)} %get-tuple-element.21), channel_id=1, source_target_pairs={{1,2},{3,4},{5,6},{7,8},{9,10},{11,12},{13,14},{2,1},{4,3},{6,5},{... | collective-permute-start | bytes 196616 | tf_op jit(solution)/shard_map/ppermute | solution.py:497
  21.3 4.2 %collective-permute-start.1 = (bf16[64,512]{1,0:T(8,128)(2,1)S(1)}, bf16[64,512]{1,0:T(8,128)(2,1)S(1)}, u32[]{:S(2)}, u32[]{:S(2)}) collective-permute-start(bf16[64,512]{1,0:T(8,128)(2,1)S(1)} %get-tuple-element.22), channel_id=1, source_target_pairs={{0,1},{2,3},{4,5},{6,7},{8,9},{10,11},{12,13},{14,15},{1,0},{3,2},... | collective-permute-start | bytes 196616 | tf_op jit(solution)/shard_map/ppermute | solution.py:498
  24.7 9.4 %copy-start.4 = (s32[4,128]{1,0:T(4,128)S(1)}, s32[4,128]{1,0:T(4,128)}, u32[]{:S(2)}) copy-start(s32[4,128]{1,0:T(4,128)} %send_ref) | copy-start | bytes 6148
  27.2 16.9 %all-to-all-start.1 = ((bf16[16,16,512]{2,1,0:T(8,128)(2,1)}), bf16[16,16,512]{2,1,0:T(8,128)(2,1)S(1)}, u32[]{:S(2)}, u32[]{:S(2)}) async-start(bf16[16,16,512]{2,1,0:T(8,128)(2,1)} %bitcast.9), calls=%async_computation.1 | async-start | bytes 524288 | tf_op jit(solution)/shard_map/all_to_all | solution.py:524
  34.0 2.6 %copy-start.6 = (bf16[1024,512]{1,0:T(8,128)(2,1)S(1)}, bf16[1024,512]{1,0:T(8,128)(2,1)}, u32[]{:S(2)}) copy-start(bf16[1024,512]{1,0:T(8,128)(2,1)} %update_input_ref.1) | copy-start | bytes 3145732
  34.0 2.6 %copy-start.8 = (bf16[512,512]{1,0:T(8,128)(2,1)S(1)}, bf16[512,512]{1,0:T(8,128)(2,1)}, u32[]{:S(2)}) copy-start(bf16[512,512]{1,0:T(8,128)(2,1)} %mesh_receiver_ref.1) | copy-start | bytes 1572868
  34.0 2.6 %copy-start.9 = (bf16[512,512]{1,0:T(8,128)(2,1)S(1)}, bf16[512,512]{1,0:T(8,128)(2,1)}, u32[]{:S(2)}) copy-start(bf16[512,512]{1,0:T(8,128)(2,1)} %message_out_ref.1) | copy-start | bytes 1572868
  34.0 2.6 %copy-start.13 = (s32[4,128]{1,0:T(4,128)S(1)}, s32[4,128]{1,0:T(4,128)}, u32[]{:S(2)}) copy-start(s32[4,128]{1,0:T(4,128)} %recv_ref.1) | copy-start | bytes 6148
  34.0 2.6 %copy-start.14 = (f32[512]{0:T(512)S(1)}, f32[512]{0:T(512)}, u32[]{:S(2)}) copy-start(f32[512]{0:T(512)} %param.42) | copy-start | bytes 6148
  34.0 2.6 %copy-start.15 = (f32[512]{0:T(512)S(1)}, f32[512]{0:T(512)}, u32[]{:S(2)}) copy-start(f32[512]{0:T(512)} %param.45) | copy-start | bytes 6148
  36.6 7.4 %copy-start.10 = (bf16[512,512]{1,0:T(8,128)(2,1)S(1)}, bf16[512,512]{1,0:T(8,128)(2,1)}, u32[]{:S(2)}) copy-start(bf16[512,512]{1,0:T(8,128)(2,1)} %update_out_ref.1) | copy-start | bytes 1572868
  36.6 7.4 %copy-start.16 = (f32[512]{0:T(512)S(1)}, f32[512]{0:T(512)}, u32[]{:S(2)}) copy-start(f32[512]{0:T(512)} %param.47) | copy-start | bytes 6148

commit v18 on v15

--- a/solution.py
+++ b/solution.py
@@ -16,10 +16,8 @@
 VMEM = pltpu.VMEM
 SMEM = pltpu.SMEM
 HBM = pltpu.HBM
-GRID_STEPS = 2
+GRID_STEPS = 4
 CHUNK_BLOCKS = 4
-ROW_PITCH = 5
-PIECE_PITCH = 2
 MEBI = 1024 * 1024
 
 
@@ -139,7 +137,7 @@
         grid_copy(step).start()
     send_copy.wait()
     senders = send_ref[...]
-    send_ref[...] = senders * ROW_PITCH
+    send_ref[...] = (senders // 8) * (8 * pieces) + senders % 8
     starts_copy.start()
     slot_copy.wait()
     place = place_ref[0]
@@ -156,23 +154,41 @@
     edge_bias_copy.wait()
     grid_bias = 0.5 * grid_bias_ref[...]
     edge_bias = 0.5 * edge_bias_ref[...]
-    values = []
-    for step in range(GRID_STEPS):
-        grid_copy(step).wait()
-        value = grid_ref[:, step * step_rows : (step + 1) * step_rows].T
-        values.append(mm(value, first_ref[...]))
-    values = [silu_half(value + grid_bias).astype(BF16) for value in values]
-    values = [mm(value, second_ref[...]) for value in values]
-    values = [layer_norm(value).astype(BF16) for value in values]
-    values = [mm(value, send_weight_ref[...]) for value in values]
-    for step, value in enumerate(values):
-        row = (value + edge_bias).astype(BF16).astype(F32)
+    def turn(step):
+        return grid_ref[:, step * step_rows : (step + 1) * step_rows].T
+
+    def store(step, value):
+        rows = (value + edge_bias).astype(BF16).astype(F32)
         for group in range(step_rows // 8):
             for piece in range(pieces):
-                at = (step * step_rows + group * 8) * ROW_PITCH + piece * PIECE_PITCH
-                table[pl.ds(at, 8, stride=ROW_PITCH), :] = row[
+                at = ((step * step_rows // 8 + group) * pieces + piece) * 8
+                table[at : at + 8, :] = rows[
                     group * 8 : group * 8 + 8, piece * LANES : (piece + 1) * LANES
                 ]
+
+    grid_copy(0).wait()
+    first, second, third = {}, {}, {}
+    first[0] = mm(turn(0), first_ref[...])
+    for step in range(1, GRID_STEPS):
+        grid_copy(step).wait()
+    for step in range(1, GRID_STEPS + 3):
+        turned = turn(step) if step < GRID_STEPS else None
+        if step - 3 in third:
+            store(step - 3, third.pop(step - 3))
+        if step - 2 in second:
+            code = layer_norm(second.pop(step - 2)).astype(BF16)
+        else:
+            code = None
+        if step - 1 in first:
+            hidden = silu_half(first.pop(step - 1) + grid_bias).astype(BF16)
+        else:
+            hidden = None
+        if code is not None:
+            third[step - 2] = mm(code, send_weight_ref[...])
+        if hidden is not None:
+            second[step - 1] = mm(hidden, second_ref[...])
+        if turned is not None:
+            first[step] = mm(turned, first_ref[...])
     for copy in copies[7:]:
         copy.wait()
     used = count_ref[...]
@@ -186,8 +202,8 @@
     def gather(chunk, edges, target):
         for edge in edges:
             start = starts[chunk * group + edge // block_edges, edge % block_edges]
-            target[pl.ds(edge * ROW_PITCH, pieces, stride=PIECE_PITCH), :] = table[
-                pl.ds(start, pieces, stride=PIECE_PITCH), :
+            target[pl.ds(edge // 8 * (8 * pieces) + edge % 8, pieces, stride=8), :] = table[
+                pl.ds(start, pieces, stride=8), :
             ]
 
     def rows_of(source, first, count):
@@ -195,7 +211,7 @@
             [
                 jnp.concatenate(
                     [
-                        source[pl.ds(at * 8 * ROW_PITCH + piece * PIECE_PITCH, 8, stride=ROW_PITCH), :]
+                        source[pl.ds((at * pieces + piece) * 8, 8), :]
                         for at in range(first // 8, (first + count) // 8)
                     ],
                     axis=0,
@@ -471,9 +487,9 @@
         scratch=[VMEM(value.shape, value.dtype) for value in operands]
         + [
             SMEM(g2m_send.shape, I32),
-            VMEM((grid_rows * ROW_PITCH + 8, LANES), F32),
-            VMEM((CHUNK_BLOCKS * g2m_send.shape[1] * ROW_PITCH + 8, LANES), F32),
-            VMEM((CHUNK_BLOCKS * g2m_send.shape[1] * ROW_PITCH + 8, LANES), F32),
+            VMEM((grid_rows * (width // LANES), LANES), F32),
+            VMEM((CHUNK_BLOCKS * g2m_send.shape[1] * (width // LANES), LANES), F32),
+            VMEM((CHUNK_BLOCKS * g2m_send.shape[1] * (width // LANES), LANES), F32),
             VMEM((CHUNK_BLOCKS * g2m_send.shape[1], width), BF16),
             VMEM((CHUNK_BLOCKS * g2m_send.shape[1], width), BF16),
             VMEM((3 * owned, LANES), I32),

time: 46.5 us -> 46 us (0.989)
  Pallas kernels: 18.7 us -> 18.2 us
    pallas_call x1, Pallas kernels: 11.4 us -> 10.9 us  [per_device(): call(edge_kernel, (shape(owned, width, kind=F32), shape(owned, width), sh...]
  transfers between devices with their start and end apart: 4 -> 4, of which waited for: 2 -> 2; matrix products, arithmetic and copies ran while one was open for 0% -> 0% of each run, Pallas kernels for 33% -> 32%
where the time goes in v18:
time: 46 us; the launch traced here: 45.7 us
  starting transfers between devices  18.3 us (40%)
  Pallas kernels  18.2 us (40%)
  waiting for transfers between devices  6.83 us (15%)
  local copies, waits for them, and re-layouts  1.41 us (3%)
  between operations  0.94 us (2%)
    pallas_call x1, Pallas kernels, per_device(): call(edge_kernel, (shape(owned, width, kind=F32), shape(owned, width), sh...  10.9 us
    all_to_all x1, starting transfers between devices, per_device(): lax.all_to_all(jnp.tile(mesh_send, (devices, 1)), 'bulk', 0, 0, tiled=True)  7.39 us
    all_to_all x1, starting transfers between devices, per_device(): piece = lax.all_to_all(rows, 'bulk', 0, 0, tiled=True)  6.8 us
    all_to_all x1, waiting for transfers between devices, per_device(): piece = lax.all_to_all(rows, 'bulk', 0, 0, tiled=True)  6.71 us
    ppermute x1, starting transfers between devices, per_device(): from_chip = lax.ppermute(chip, 'bulk', both(within))  3.34 us
    pallas_call x1, Pallas kernels, per_device(): call(functools.partial(wanted_kernel, owned), shape(edges, places), [VMEM...  2.53 us
    pallas_call x1, Pallas kernels, per_device(): call(message_kernel, shape(owned, width), [VMEM] * 10, flops=1000000000,...  1.77 us
    pallas_call x1, Pallas kernels, per_device(): call(node_kernel, (shape(owned, width), shape(places, width)), [VMEM] * 1...  1.63 us
  transfers between devices with their start and end apart: 4, of which 2 were waited for; matrix products, arithmetic and copies ran while one was open for 0% of the time, Pallas kernels for 32%

profile of v18, /device:TPU:0, one launch (start us, length us, event | category | flops | bytes accessed | tf_op | source)
XLA Modules:
  0.0 45.7 jit_solution(10195695876705755010)
XLA Ops:
  0.0 1.3 %tile.2 = s32[16,4,128]{2,1,0:T(4,128)} broadcast(s32[4,128]{1,0:T(4,128)} %send_ref), dimensions={1,2} | broadcast | bytes 34816 | tf_op jit(solution)/shard_map/tile | solution.py:468
  1.3 7.4 %all-to-all-start = ((s32[16,4,128]{2,1,0:T(4,128)}), s32[16,4,128]{2,1,0:T(4,128)S(1)}, u32[]{:S(2)}, u32[]{:S(2)}) async-start(s32[16,4,128]{2,1,0:T(4,128)} %tile.2), calls=%async_computation | async-start | bytes 65536 | tf_op jit(solution)/shard_map/all_to_all | solution.py:468
  9.3 0.0 copy-start.2
  9.4 0.0 copy-start.5
  9.4 0.0 copy-start.7
  9.4 0.0 copy-start.11
  9.4 0.0 copy-start.12
  9.4 0.0 copy-start.3
  9.4 10.9 %shard_map.262 = (f32[64,512]{1,0:T(8,128)S(1)}, bf16[64,512]{1,0:T(8,128)(2,1)S(1)}, bf16[64,512]{1,0:T(8,128)(2,1)S(1)}) custom-call(s32[1]{0:T(128)} %bitcast.1.place_ref, bf16[474,512]{1,0:T(8,128)(2,1)} %first_hbm.1, bf16[474,2048]{1,0:T(8,128)(2,1)} %bitcast.26, bf16[512,512]{1,0:T(8,128)(2,1)} %second_hbm.1, bf16[512,512]{1,0:T(8,128)(2,1)} %send_weight_hbm.1, ...), custom_call_target="tpu_custom_call" | custom-call | flops 10000000000 | bytes 4000000 | tf_op jit(solution)/shard_map/pallas_call | solution.py:483
  20.4 0.0 copy-start
  20.4 0.0 copy-start.1
  20.4 0.8 %collective-permute-start = (bf16[64,512]{1,0:T(8,128)(2,1)S(1)}, bf16[64,512]{1,0:T(8,128)(2,1)S(1)}, u32[]{:S(2)}, u32[]{:S(2)}) collective-permute-start(bf16[64,512]{1,0:T(8,128)(2,1)S(1)} %get-tuple-element.21), channel_id=1, source_target_pairs={{1,2},{3,4},{5,6},{7,8},{9,10},{11,12},{13,14},{2,1},{4,3},{6,5},{... | collective-permute-start | bytes 196616 | tf_op jit(solution)/shard_map/ppermute | solution.py:507
  21.2 3.3 %collective-permute-start.1 = (bf16[64,512]{1,0:T(8,128)(2,1)S(1)}, bf16[64,512]{1,0:T(8,128)(2,1)S(1)}, u32[]{:S(2)}, u32[]{:S(2)}) collective-permute-start(bf16[64,512]{1,0:T(8,128)(2,1)S(1)} %get-tuple-element.22), channel_id=1, source_target_pairs={{0,1},{2,3},{4,5},{6,7},{8,9},{10,11},{12,13},{14,15},{1,0},{3,2},... | collective-permute-start | bytes 196616 | tf_op jit(solution)/shard_map/ppermute | solution.py:508
  24.5 0.0 all-to-all-done
  24.5 0.0 copy-done.2
  24.5 0.0 copy-done.5
  24.5 0.0 copy-done.7
  24.5 0.0 copy-done.11
  24.6 0.0 copy-done.12
  24.6 0.0 copy-start.4
  24.6 0.7 %shard_map.263 = (bf16[256,64]{1,0:T(8,128)(2,1)S(1)}, f32[64,512]{1,0:T(8,128)S(1)}, bf16[512,512]{1,0:T(8,128)(2,1)S(1)}) custom-call(s32[1]{0:T(128)} %bitcast.1.place_ref, s32[1,1024]{1,0:T(1,128)S(1)} %bitcast.19, s32[64,128]{1,0:T(8,128)S(1)} %bitcast.16, bf16[64,512]{1,0:T(8,128)(2,1)S(1)} %copy-done.2, bf16[512,512]{1,0:T(8,128)(2,1)S(1)} %copy-done.7, ...), custom_call_target="tpu_custom_call" | custom-call | flops 500000000 | bytes 500000 | tf_op jit(solution)/shard_map/pallas_call | solution.py:509
  25.3 0.0 collective-permute-done.from_cross_ref
  25.3 0.1 collective-permute-done.1.from_chip_ref
  25.4 0.0 copy-done.3
  25.4 0.0 copy-done
  25.4 0.0 copy-done.1
  25.4 1.6 %shard_map.264 = (bf16[64,512]{1,0:T(8,128)(2,1)S(1)}, bf16[256,512]{1,0:T(8,128)(2,1)}) custom-call(f32[64,512]{1,0:T(8,128)S(1)} %get-tuple-element.20.own_ref, bf16[64,512]{1,0:T(8,128)(2,1)S(1)} %collective-permute-done.from_cross_ref, bf16[64,512]{1,0:T(8,128)(2,1)S(1)} %collective-permute-done.1.from_chip_ref, bf16[64,512]{1,0:T(8,128)(2,1)S(1)} %copy-done.2, ...), custom_call_target="tpu_custom_call" | custom-call | flops 500000000 | bytes 4000000 | tf_op jit(solution)/shard_map/pallas_call | solution.py:516
  27.1 6.8 %all-to-all-start.1 = ((bf16[16,16,512]{2,1,0:T(8,128)(2,1)}), bf16[16,16,512]{2,1,0:T(8,128)(2,1)S(1)}, u32[]{:S(2)}, u32[]{:S(2)}) async-start(bf16[16,16,512]{2,1,0:T(8,128)(2,1)} %bitcast.9), calls=%async_computation.1 | async-start | bytes 524288 | tf_op jit(solution)/shard_map/all_to_all | solution.py:534
  33.9 0.0 copy-start.6
  33.9 0.0 copy-start.8
  33.9 0.0 copy-start.9
  33.9 0.0 copy-start.13
  33.9 0.0 copy-start.14
  33.9 0.0 copy-start.15
  33.9 0.0 copy-done.4
  34.0 2.5 %shard_map.265.wanted_ref = bf16[512,256]{1,0:T(8,128)(2,1)S(1)} custom-call(s32[1,1024]{1,0:T(1,128)S(1)} %bitcast.20, s32[4,128]{1,0:T(4,128)S(1)} %copy-done.4), custom_call_target="tpu_custom_call" | custom-call | flops 1000000000 | bytes 500000 | tf_op jit(solution)/shard_map/pallas_call | solution.py:536
  36.5 0.0 copy-start.10
  36.5 0.0 copy-start.16
  36.5 0.0 copy-done.6
  36.5 0.0 copy-done.8
  36.5 0.0 copy-done.9
  36.6 0.0 copy-done.13
  36.6 0.0 copy-done.14
  36.6 0.0 copy-done.15
  36.6 0.6 %shard_map.266 = (bf16[64,512]{1,0:T(8,128)(2,1)S(1)}, bf16[512,128]{1,0:T(8,128)(2,1)S(1)}, bf16[128,512]{1,0:T(8,128)(2,1)S(1)}, f32[64,512]{1,0:T(8,128)S(1)}, bf16[512,512]{1,0:T(8,128)(2,1)S(1)}) custom-call(s32[1]{0:T(128)} %bitcast.1.place_ref, s32[1,1024]{1,0:T(1,128)S(1)} %bitcast.21, s32[4,128]{1,0:T(4,128)S(1)} %copy-done.13, ...), custom_call_target="tpu_custom_call" | custom-call | flops 1000000000 | bytes 4000000 | tf_op jit(solution)/shard_map/pallas_call | solution.py:543
  37.2 6.7 %all-to-all-done.1 = bf16[16,16,512]{2,1,0:T(8,128)(2,1)S(1)} async-done(((bf16[16,16,512]{2,1,0:T(8,128)(2,1)}), bf16[16,16,512]{2,1,0:T(8,128)(2,1)S(1)}, u32[]{:S(2)}, u32[]{:S(2)}) %all-to-all-start.1) | async-done | bytes 262176 | tf_op jit(solution)/shard_map/all_to_all | solution.py:534
  43.9 0.0 copy-done.10
  43.9 0.0 copy-done.16
  43.9 1.8 %shard_map.267 = bf16[64,512]{1,0:T(8,128)(2,1)} custom-call(bf16[512,256]{1,0:T(8,128)(2,1)S(1)} %shard_map.265.wanted_ref, bf16[256,512]{1,0:T(8,128)(2,1)S(1)} %bitcast.15, bf16[64,512]{1,0:T(8,128)(2,1)S(1)} %get-tuple-element.30.incoming_ref, bf16[512,128]{1,0:T(8,128)(2,1)S(1)} %get-tuple-element.31.pick_ref, ...), custom_call_target="tpu_custom_call" | custom-call | flops 1000000000 | bytes 4000000 | tf_op jit(solution)/shard_map/pallas_call | solution.py:566
Async XLA Ops:
  1.3 23.2 %all-to-all-start = ((s32[16,4,128]{2,1,0:T(4,128)}), s32[16,4,128]{2,1,0:T(4,128)S(1)}, u32[]{:S(2)}, u32[]{:S(2)}) async-start(s32[16,4,128]{2,1,0:T(4,128)} %tile.2), calls=%async_computation | async-start | bytes 65536 | tf_op jit(solution)/shard_map/all_to_all | solution.py:468
  9.3 15.2 %copy-start.2 = (bf16[64,512]{1,0:T(8,128)(2,1)S(1)}, bf16[64,512]{1,0:T(8,128)(2,1)}, u32[]{:S(2)}) copy-start(bf16[64,512]{1,0:T(8,128)(2,1)} %latent_ref.3) | copy-start | bytes 196612
  9.4 15.2 %copy-start.5 = (bf16[1024,512]{1,0:T(8,128)(2,1)S(1)}, bf16[1024,512]{1,0:T(8,128)(2,1)}, u32[]{:S(2)}) copy-start(bf16[1024,512]{1,0:T(8,128)(2,1)} %node_input_ref.1) | copy-start | bytes 3145732
  9.4 15.2 %copy-start.7 = (bf16[512,512]{1,0:T(8,128)(2,1)S(1)}, bf16[512,512]{1,0:T(8,128)(2,1)}, u32[]{:S(2)}) copy-start(bf16[512,512]{1,0:T(8,128)(2,1)} %edge_out_ref.1) | copy-start | bytes 1572868
  9.4 15.2 %copy-start.11 = (s32[1024]{0:T(1024)S(1)}, s32[1024]{0:T(1024)}, u32[]{:S(2)}) copy-start(s32[1024]{0:T(1024)} %param.53) | copy-start | bytes 12292
  9.4 15.2 %copy-start.12 = (f32[512]{0:T(512)S(1)}, f32[512]{0:T(512)}, u32[]{:S(2)}) copy-start(f32[512]{0:T(512)} %param.37) | copy-start | bytes 6148
  9.4 16.0 %copy-start.3 = (f32[512]{0:T(512)S(1)}, f32[512]{0:T(512)}, u32[]{:S(2)}) copy-start(f32[512]{0:T(512)} %param.39) | copy-start | bytes 6148
  20.4 5.1 %copy-start = (bf16[512,512]{1,0:T(8,128)(2,1)S(1)}, bf16[512,512]{1,0:T(8,128)(2,1)}, u32[]{:S(2)}) copy-start(bf16[512,512]{1,0:T(8,128)(2,1)} %node_out_ref.1) | copy-start | bytes 1572868
  20.4 5.1 %copy-start.1 = (bf16[512,512]{1,0:T(8,128)(2,1)S(1)}, bf16[512,512]{1,0:T(8,128)(2,1)}, u32[]{:S(2)}) copy-start(bf16[512,512]{1,0:T(8,128)(2,1)} %mesh_sender_ref.1) | copy-start | bytes 1572868
  20.4 4.9 %collective-permute-start = (bf16[64,512]{1,0:T(8,128)(2,1)S(1)}, bf16[64,512]{1,0:T(8,128)(2,1)S(1)}, u32[]{:S(2)}, u32[]{:S(2)}) collective-permute-start(bf16[64,512]{1,0:T(8,128)(2,1)S(1)} %get-tuple-element.21), channel_id=1, source_target_pairs={{1,2},{3,4},{5,6},{7,8},{9,10},{11,12},{13,14},{2,1},{4,3},{6,5},{... | collective-permute-start | bytes 196616 | tf_op jit(solution)/shard_map/ppermute | solution.py:507
  21.2 4.2 %collective-permute-start.1 = (bf16[64,512]{1,0:T(8,128)(2,1)S(1)}, bf16[64,512]{1,0:T(8,128)(2,1)S(1)}, u32[]{:S(2)}, u32[]{:S(2)}) collective-permute-start(bf16[64,512]{1,0:T(8,128)(2,1)S(1)} %get-tuple-element.22), channel_id=1, source_target_pairs={{0,1},{2,3},{4,5},{6,7},{8,9},{10,11},{12,13},{14,15},{1,0},{3,2},... | collective-permute-start | bytes 196616 | tf_op jit(solution)/shard_map/ppermute | solution.py:508
  24.6 9.4 %copy-start.4 = (s32[4,128]{1,0:T(4,128)S(1)}, s32[4,128]{1,0:T(4,128)}, u32[]{:S(2)}) copy-start(s32[4,128]{1,0:T(4,128)} %send_ref) | copy-start | bytes 6148
  27.1 16.9 %all-to-all-start.1 = ((bf16[16,16,512]{2,1,0:T(8,128)(2,1)}), bf16[16,16,512]{2,1,0:T(8,128)(2,1)S(1)}, u32[]{:S(2)}, u32[]{:S(2)}) async-start(bf16[16,16,512]{2,1,0:T(8,128)(2,1)} %bitcast.9), calls=%async_computation.1 | async-start | bytes 524288 | tf_op jit(solution)/shard_map/all_to_all | solution.py:534
  33.9 2.6 %copy-start.6 = (bf16[1024,512]{1,0:T(8,128)(2,1)S(1)}, bf16[1024,512]{1,0:T(8,128)(2,1)}, u32[]{:S(2)}) copy-start(bf16[1024,512]{1,0:T(8,128)(2,1)} %update_input_ref.1) | copy-start | bytes 3145732
  33.9 2.6 %copy-start.8 = (bf16[512,512]{1,0:T(8,128)(2,1)S(1)}, bf16[512,512]{1,0:T(8,128)(2,1)}, u32[]{:S(2)}) copy-start(bf16[512,512]{1,0:T(8,128)(2,1)} %mesh_receiver_ref.1) | copy-start | bytes 1572868
  33.9 2.6 %copy-start.9 = (bf16[512,512]{1,0:T(8,128)(2,1)S(1)}, bf16[512,512]{1,0:T(8,128)(2,1)}, u32[]{:S(2)}) copy-start(bf16[512,512]{1,0:T(8,128)(2,1)} %message_out_ref.1) | copy-start | bytes 1572868
  33.9 2.6 %copy-start.13 = (s32[4,128]{1,0:T(4,128)S(1)}, s32[4,128]{1,0:T(4,128)}, u32[]{:S(2)}) copy-start(s32[4,128]{1,0:T(4,128)} %recv_ref.1) | copy-start | bytes 6148
  33.9 2.6 %copy-start.14 = (f32[512]{0:T(512)S(1)}, f32[512]{0:T(512)}, u32[]{:S(2)}) copy-start(f32[512]{0:T(512)} %param.42) | copy-start | bytes 6148
  33.9 2.6 %copy-start.15 = (f32[512]{0:T(512)S(1)}, f32[512]{0:T(512)}, u32[]{:S(2)}) copy-start(f32[512]{0:T(512)} %param.45) | copy-start | bytes 6148
  36.5 7.4 %copy-start.10 = (bf16[512,512]{1,0:T(8,128)(2,1)S(1)}, bf16[512,512]{1,0:T(8,128)(2,1)}, u32[]{:S(2)}) copy-start(bf16[512,512]{1,0:T(8,128)(2,1)} %update_out_ref.1) | copy-start | bytes 1572868
  36.5 7.4 %copy-start.16 = (f32[512]{0:T(512)S(1)}, f32[512]{0:T(512)}, u32[]{:S(2)}) copy-start(f32[512]{0:T(512)} %param.47) | copy-start | bytes 6148

commit v19 on v18

--- a/solution.py
+++ b/solution.py
@@ -17,7 +17,7 @@
 SMEM = pltpu.SMEM
 HBM = pltpu.HBM
 GRID_STEPS = 4
-CHUNK_BLOCKS = 4
+CHUNK_BLOCKS = 6
 MEBI = 1024 * 1024
 
 

time: 46 us -> 46.2 us (level)
  transfers between devices with their start and end apart: 4 -> 4, of which waited for: 2 -> 2; matrix products, arithmetic and copies ran while one was open for 0% -> 0% of each run, Pallas kernels for 32% -> 33%
where the time goes in v19:
time: 46.2 us; the launch traced here: 45.9 us
  Pallas kernels  18.4 us (40%)
  starting transfers between devices  18.3 us (40%)
  waiting for transfers between devices  6.83 us (15%)
  local copies, waits for them, and re-layouts  1.41 us (3%)
  between operations  0.94 us (2%)
    pallas_call x1, Pallas kernels, per_device(): call(edge_kernel, (shape(owned, width, kind=F32), shape(owned, width), sh...  11.1 us
    all_to_all x1, starting transfers between devices, per_device(): lax.all_to_all(jnp.tile(mesh_send, (devices, 1)), 'bulk', 0, 0, tiled=True)  7.39 us
    all_to_all x1, starting transfers between devices, per_device(): piece = lax.all_to_all(rows, 'bulk', 0, 0, tiled=True)  6.81 us
    all_to_all x1, waiting for transfers between devices, per_device(): piece = lax.all_to_all(rows, 'bulk', 0, 0, tiled=True)  6.71 us
    ppermute x1, starting transfers between devices, per_device(): from_chip = lax.ppermute(chip, 'bulk', both(within))  3.35 us
    pallas_call x1, Pallas kernels, per_device(): call(functools.partial(wanted_kernel, owned), shape(edges, places), [VMEM...  2.53 us
    pallas_call x1, Pallas kernels, per_device(): call(message_kernel, shape(owned, width), [VMEM] * 10, flops=1000000000,...  1.77 us
    pallas_call x1, Pallas kernels, per_device(): call(node_kernel, (shape(owned, width), shape(places, width)), [VMEM] * 1...  1.62 us
  transfers between devices with their start and end apart: 4, of which 2 were waited for; matrix products, arithmetic and copies ran while one was open for 0% of the time, Pallas kernels for 33%

profile of v19, /device:TPU:0, one launch (start us, length us, event | category | flops | bytes accessed | tf_op | source)
XLA Modules:
  0.0 45.9 jit_solution(5699290248737688070)
XLA Ops:
  0.0 1.3 %tile.2 = s32[16,4,128]{2,1,0:T(4,128)} broadcast(s32[4,128]{1,0:T(4,128)} %send_ref), dimensions={1,2} | broadcast | bytes 34816 | tf_op jit(solution)/shard_map/tile | solution.py:468
  1.3 7.4 %all-to-all-start = ((s32[16,4,128]{2,1,0:T(4,128)}), s32[16,4,128]{2,1,0:T(4,128)S(1)}, u32[]{:S(2)}, u32[]{:S(2)}) async-start(s32[16,4,128]{2,1,0:T(4,128)} %tile.2), calls=%async_computation | async-start | bytes 65536 | tf_op jit(solution)/shard_map/all_to_all | solution.py:468
  9.3 0.0 copy-start.2
  9.4 0.0 copy-start.5
  9.4 0.0 copy-start.7
  9.4 0.0 copy-start.11
  9.4 0.0 copy-start.12
  9.4 0.0 copy-start.3
  9.4 11.1 %shard_map.262 = (f32[64,512]{1,0:T(8,128)S(1)}, bf16[64,512]{1,0:T(8,128)(2,1)S(1)}, bf16[64,512]{1,0:T(8,128)(2,1)S(1)}) custom-call(s32[1]{0:T(128)} %bitcast.1.place_ref, bf16[474,512]{1,0:T(8,128)(2,1)} %first_hbm.1, bf16[474,2048]{1,0:T(8,128)(2,1)} %bitcast.26, bf16[512,512]{1,0:T(8,128)(2,1)} %second_hbm.1, bf16[512,512]{1,0:T(8,128)(2,1)} %send_weight_hbm.1, ...), custom_call_target="tpu_custom_call" | custom-call | flops 10000000000 | bytes 4000000 | tf_op jit(solution)/shard_map/pallas_call | solution.py:483
  20.5 0.0 copy-start
  20.6 0.0 copy-start.1
  20.6 0.8 %collective-permute-start = (bf16[64,512]{1,0:T(8,128)(2,1)S(1)}, bf16[64,512]{1,0:T(8,128)(2,1)S(1)}, u32[]{:S(2)}, u32[]{:S(2)}) collective-permute-start(bf16[64,512]{1,0:T(8,128)(2,1)S(1)} %get-tuple-element.21), channel_id=1, source_target_pairs={{1,2},{3,4},{5,6},{7,8},{9,10},{11,12},{13,14},{2,1},{4,3},{6,5},{... | collective-permute-start | bytes 196616 | tf_op jit(solution)/shard_map/ppermute | solution.py:507
  21.4 3.4 %collective-permute-start.1 = (bf16[64,512]{1,0:T(8,128)(2,1)S(1)}, bf16[64,512]{1,0:T(8,128)(2,1)S(1)}, u32[]{:S(2)}, u32[]{:S(2)}) collective-permute-start(bf16[64,512]{1,0:T(8,128)(2,1)S(1)} %get-tuple-element.22), channel_id=1, source_target_pairs={{0,1},{2,3},{4,5},{6,7},{8,9},{10,11},{12,13},{14,15},{1,0},{3,2},... | collective-permute-start | bytes 196616 | tf_op jit(solution)/shard_map/ppermute | solution.py:508
  24.7 0.0 all-to-all-done
  24.7 0.0 copy-done.2
  24.7 0.0 copy-done.5
  24.7 0.0 copy-done.7
  24.7 0.0 copy-done.11
  24.8 0.0 copy-done.12
  24.8 0.0 copy-start.4
  24.8 0.7 %shard_map.263 = (bf16[256,64]{1,0:T(8,128)(2,1)S(1)}, f32[64,512]{1,0:T(8,128)S(1)}, bf16[512,512]{1,0:T(8,128)(2,1)S(1)}) custom-call(s32[1]{0:T(128)} %bitcast.1.place_ref, s32[1,1024]{1,0:T(1,128)S(1)} %bitcast.19, s32[64,128]{1,0:T(8,128)S(1)} %bitcast.16, bf16[64,512]{1,0:T(8,128)(2,1)S(1)} %copy-done.2, bf16[512,512]{1,0:T(8,128)(2,1)S(1)} %copy-done.7, ...), custom_call_target="tpu_custom_call" | custom-call | flops 500000000 | bytes 500000 | tf_op jit(solution)/shard_map/pallas_call | solution.py:509
  25.5 0.0 collective-permute-done.from_cross_ref
  25.5 0.1 collective-permute-done.1.from_chip_ref
  25.6 0.0 copy-done.3
  25.6 0.0 copy-done
  25.6 0.0 copy-done.1
  25.6 1.6 %shard_map.264 = (bf16[64,512]{1,0:T(8,128)(2,1)S(1)}, bf16[256,512]{1,0:T(8,128)(2,1)}) custom-call(f32[64,512]{1,0:T(8,128)S(1)} %get-tuple-element.20.own_ref, bf16[64,512]{1,0:T(8,128)(2,1)S(1)} %collective-permute-done.from_cross_ref, bf16[64,512]{1,0:T(8,128)(2,1)S(1)} %collective-permute-done.1.from_chip_ref, bf16[64,512]{1,0:T(8,128)(2,1)S(1)} %copy-done.2, ...), custom_call_target="tpu_custom_call" | custom-call | flops 500000000 | bytes 4000000 | tf_op jit(solution)/shard_map/pallas_call | solution.py:516
  27.3 6.8 %all-to-all-start.1 = ((bf16[16,16,512]{2,1,0:T(8,128)(2,1)}), bf16[16,16,512]{2,1,0:T(8,128)(2,1)S(1)}, u32[]{:S(2)}, u32[]{:S(2)}) async-start(bf16[16,16,512]{2,1,0:T(8,128)(2,1)} %bitcast.9), calls=%async_computation.1 | async-start | bytes 524288 | tf_op jit(solution)/shard_map/all_to_all | solution.py:534
  34.1 0.0 copy-start.6
  34.1 0.0 copy-start.8
  34.1 0.0 copy-start.9
  34.1 0.0 copy-start.13
  34.1 0.0 copy-start.14
  34.1 0.0 copy-start.15
  34.2 0.0 copy-done.4
  34.2 2.5 %shard_map.265.wanted_ref = bf16[512,256]{1,0:T(8,128)(2,1)S(1)} custom-call(s32[1,1024]{1,0:T(1,128)S(1)} %bitcast.20, s32[4,128]{1,0:T(4,128)S(1)} %copy-done.4), custom_call_target="tpu_custom_call" | custom-call | flops 1000000000 | bytes 500000 | tf_op jit(solution)/shard_map/pallas_call | solution.py:536
  36.7 0.0 copy-start.10
  36.7 0.0 copy-start.16
  36.7 0.0 copy-done.6
  36.7 0.0 copy-done.8
  36.7 0.0 copy-done.9
  36.8 0.0 copy-done.13
  36.8 0.0 copy-done.14
  36.8 0.0 copy-done.15
  36.8 0.6 %shard_map.266 = (bf16[64,512]{1,0:T(8,128)(2,1)S(1)}, bf16[512,128]{1,0:T(8,128)(2,1)S(1)}, bf16[128,512]{1,0:T(8,128)(2,1)S(1)}, f32[64,512]{1,0:T(8,128)S(1)}, bf16[512,512]{1,0:T(8,128)(2,1)S(1)}) custom-call(s32[1]{0:T(128)} %bitcast.1.place_ref, s32[1,1024]{1,0:T(1,128)S(1)} %bitcast.21, s32[4,128]{1,0:T(4,128)S(1)} %copy-done.13, ...), custom_call_target="tpu_custom_call" | custom-call | flops 1000000000 | bytes 4000000 | tf_op jit(solution)/shard_map/pallas_call | solution.py:543
  37.4 6.7 %all-to-all-done.1 = bf16[16,16,512]{2,1,0:T(8,128)(2,1)S(1)} async-done(((bf16[16,16,512]{2,1,0:T(8,128)(2,1)}), bf16[16,16,512]{2,1,0:T(8,128)(2,1)S(1)}, u32[]{:S(2)}, u32[]{:S(2)}) %all-to-all-start.1) | async-done | bytes 262176 | tf_op jit(solution)/shard_map/all_to_all | solution.py:534
  44.1 0.0 copy-done.10
  44.1 0.0 copy-done.16
  44.1 1.8 %shard_map.267 = bf16[64,512]{1,0:T(8,128)(2,1)} custom-call(bf16[512,256]{1,0:T(8,128)(2,1)S(1)} %shard_map.265.wanted_ref, bf16[256,512]{1,0:T(8,128)(2,1)S(1)} %bitcast.15, bf16[64,512]{1,0:T(8,128)(2,1)S(1)} %get-tuple-element.30.incoming_ref, bf16[512,128]{1,0:T(8,128)(2,1)S(1)} %get-tuple-element.31.pick_ref, ...), custom_call_target="tpu_custom_call" | custom-call | flops 1000000000 | bytes 4000000 | tf_op jit(solution)/shard_map/pallas_call | solution.py:566
Async XLA Ops:
  1.3 23.4 %all-to-all-start = ((s32[16,4,128]{2,1,0:T(4,128)}), s32[16,4,128]{2,1,0:T(4,128)S(1)}, u32[]{:S(2)}, u32[]{:S(2)}) async-start(s32[16,4,128]{2,1,0:T(4,128)} %tile.2), calls=%async_computation | async-start | bytes 65536 | tf_op jit(solution)/shard_map/all_to_all | solution.py:468
  9.3 15.4 %copy-start.2 = (bf16[64,512]{1,0:T(8,128)(2,1)S(1)}, bf16[64,512]{1,0:T(8,128)(2,1)}, u32[]{:S(2)}) copy-start(bf16[64,512]{1,0:T(8,128)(2,1)} %latent_ref.3) | copy-start | bytes 196612
  9.4 15.4 %copy-start.5 = (bf16[1024,512]{1,0:T(8,128)(2,1)S(1)}, bf16[1024,512]{1,0:T(8,128)(2,1)}, u32[]{:S(2)}) copy-start(bf16[1024,512]{1,0:T(8,128)(2,1)} %node_input_ref.1) | copy-start | bytes 3145732
  9.4 15.4 %copy-start.7 = (bf16[512,512]{1,0:T(8,128)(2,1)S(1)}, bf16[512,512]{1,0:T(8,128)(2,1)}, u32[]{:S(2)}) copy-start(bf16[512,512]{1,0:T(8,128)(2,1)} %edge_out_ref.1) | copy-start | bytes 1572868
  9.4 15.4 %copy-start.11 = (s32[1024]{0:T(1024)S(1)}, s32[1024]{0:T(1024)}, u32[]{:S(2)}) copy-start(s32[1024]{0:T(1024)} %param.53) | copy-start | bytes 12292
  9.4 15.4 %copy-start.12 = (f32[512]{0:T(512)S(1)}, f32[512]{0:T(512)}, u32[]{:S(2)}) copy-start(f32[512]{0:T(512)} %param.37) | copy-start | bytes 6148
  9.4 16.2 %copy-start.3 = (f32[512]{0:T(512)S(1)}, f32[512]{0:T(512)}, u32[]{:S(2)}) copy-start(f32[512]{0:T(512)} %param.39) | copy-start | bytes 6148
  20.5 5.1 %copy-start = (bf16[512,512]{1,0:T(8,128)(2,1)S(1)}, bf16[512,512]{1,0:T(8,128)(2,1)}, u32[]{:S(2)}) copy-start(bf16[512,512]{1,0:T(8,128)(2,1)} %node_out_ref.1) | copy-start | bytes 1572868
  20.6 5.1 %copy-start.1 = (bf16[512,512]{1,0:T(8,128)(2,1)S(1)}, bf16[512,512]{1,0:T(8,128)(2,1)}, u32[]{:S(2)}) copy-start(bf16[512,512]{1,0:T(8,128)(2,1)} %mesh_sender_ref.1) | copy-start | bytes 1572868
  20.6 4.9 %collective-permute-start = (bf16[64,512]{1,0:T(8,128)(2,1)S(1)}, bf16[64,512]{1,0:T(8,128)(2,1)S(1)}, u32[]{:S(2)}, u32[]{:S(2)}) collective-permute-start(bf16[64,512]{1,0:T(8,128)(2,1)S(1)} %get-tuple-element.21), channel_id=1, source_target_pairs={{1,2},{3,4},{5,6},{7,8},{9,10},{11,12},{13,14},{2,1},{4,3},{6,5},{... | collective-permute-start | bytes 196616 | tf_op jit(solution)/shard_map/ppermute | solution.py:507
  21.4 4.3 %collective-permute-start.1 = (bf16[64,512]{1,0:T(8,128)(2,1)S(1)}, bf16[64,512]{1,0:T(8,128)(2,1)S(1)}, u32[]{:S(2)}, u32[]{:S(2)}) collective-permute-start(bf16[64,512]{1,0:T(8,128)(2,1)S(1)} %get-tuple-element.22), channel_id=1, source_target_pairs={{0,1},{2,3},{4,5},{6,7},{8,9},{10,11},{12,13},{14,15},{1,0},{3,2},... | collective-permute-start | bytes 196616 | tf_op jit(solution)/shard_map/ppermute | solution.py:508
  24.8 9.4 %copy-start.4 = (s32[4,128]{1,0:T(4,128)S(1)}, s32[4,128]{1,0:T(4,128)}, u32[]{:S(2)}) copy-start(s32[4,128]{1,0:T(4,128)} %send_ref) | copy-start | bytes 6148
  27.3 16.9 %all-to-all-start.1 = ((bf16[16,16,512]{2,1,0:T(8,128)(2,1)}), bf16[16,16,512]{2,1,0:T(8,128)(2,1)S(1)}, u32[]{:S(2)}, u32[]{:S(2)}) async-start(bf16[16,16,512]{2,1,0:T(8,128)(2,1)} %bitcast.9), calls=%async_computation.1 | async-start | bytes 524288 | tf_op jit(solution)/shard_map/all_to_all | solution.py:534
  34.1 2.7 %copy-start.6 = (bf16[1024,512]{1,0:T(8,128)(2,1)S(1)}, bf16[1024,512]{1,0:T(8,128)(2,1)}, u32[]{:S(2)}) copy-start(bf16[1024,512]{1,0:T(8,128)(2,1)} %update_input_ref.1) | copy-start | bytes 3145732
  34.1 2.6 %copy-start.8 = (bf16[512,512]{1,0:T(8,128)(2,1)S(1)}, bf16[512,512]{1,0:T(8,128)(2,1)}, u32[]{:S(2)}) copy-start(bf16[512,512]{1,0:T(8,128)(2,1)} %mesh_receiver_ref.1) | copy-start | bytes 1572868
  34.1 2.6 %copy-start.9 = (bf16[512,512]{1,0:T(8,128)(2,1)S(1)}, bf16[512,512]{1,0:T(8,128)(2,1)}, u32[]{:S(2)}) copy-start(bf16[512,512]{1,0:T(8,128)(2,1)} %message_out_ref.1) | copy-start | bytes 1572868
  34.1 2.6 %copy-start.13 = (s32[4,128]{1,0:T(4,128)S(1)}, s32[4,128]{1,0:T(4,128)}, u32[]{:S(2)}) copy-start(s32[4,128]{1,0:T(4,128)} %recv_ref.1) | copy-start | bytes 6148
  34.1 2.6 %copy-start.14 = (f32[512]{0:T(512)S(1)}, f32[512]{0:T(512)}, u32[]{:S(2)}) copy-start(f32[512]{0:T(512)} %param.42) | copy-start | bytes 6148
  34.1 2.6 %copy-start.15 = (f32[512]{0:T(512)S(1)}, f32[512]{0:T(512)}, u32[]{:S(2)}) copy-start(f32[512]{0:T(512)} %param.45) | copy-start | bytes 6148
  36.7 7.4 %copy-start.10 = (bf16[512,512]{1,0:T(8,128)(2,1)S(1)}, bf16[512,512]{1,0:T(8,128)(2,1)}, u32[]{:S(2)}) copy-start(bf16[512,512]{1,0:T(8,128)(2,1)} %update_out_ref.1) | copy-start | bytes 1572868
  36.7 7.4 %copy-start.16 = (f32[512]{0:T(512)S(1)}, f32[512]{0:T(512)}, u32[]{:S(2)}) copy-start(f32[512]{0:T(512)} %param.47) | copy-start | bytes 6148

commit v20 on v18

--- a/solution.py
+++ b/solution.py
@@ -129,12 +129,14 @@
     ]
     first_copy, second_copy, send_weight_copy, grid_bias_copy, edge_bias_copy, send_copy = copies[:6]
     slot_copy, starts_copy = copies[6], copies[-1]
-    first_copy.start()
-    grid_copy(0).start()
-    for copy in copies[1:-1]:
+    for copy in (send_copy, slot_copy, grid_copy(0), first_copy, grid_bias_copy, second_copy):
+        copy.start()
+    for copy in (edge_bias_copy, send_weight_copy):
         copy.start()
     for step in range(1, GRID_STEPS):
         grid_copy(step).start()
+    for copy in copies[7:-1]:
+        copy.start()
     send_copy.wait()
     senders = send_ref[...]
     send_ref[...] = (senders // 8) * (8 * pieces) + senders % 8
@@ -145,15 +147,7 @@
         ids_of_rows(slot_ref[...], (place - 1) * owned, 3 * owned), ids_ref.shape
     )
     total[...] = jnp.zeros_like(total)
-    first_copy.wait()
-    first_ref[...] = first_ref[...] * 0.5
-    second_copy.wait()
-    send_weight_copy.wait()
-    send_weight_ref[...] = send_weight_ref[...] * 0.5
-    grid_bias_copy.wait()
-    edge_bias_copy.wait()
-    grid_bias = 0.5 * grid_bias_ref[...]
-    edge_bias = 0.5 * edge_bias_ref[...]
+
     def turn(step):
         return grid_ref[:, step * step_rows : (step + 1) * step_rows].T
 
@@ -167,8 +161,15 @@
                 ]
 
     grid_copy(0).wait()
-    first, second, third = {}, {}, {}
-    first[0] = mm(turn(0), first_ref[...])
+    turned = turn(0)
+    first_copy.wait()
+    first_ref[...] = first_ref[...] * 0.5
+    first, second, third = {0: mm(turned, first_ref[...])}, {}, {}
+    for copy in (grid_bias_copy, second_copy, edge_bias_copy, send_weight_copy):
+        copy.wait()
+    grid_bias = 0.5 * grid_bias_ref[...]
+    edge_bias = 0.5 * edge_bias_ref[...]
+    send_weight_ref[...] = send_weight_ref[...] * 0.5
     for step in range(1, GRID_STEPS):
         grid_copy(step).wait()
     for step in range(1, GRID_STEPS + 3):

time: 46 us -> 46 us (level)
  no operation moved by 1% of the time
where the time goes in v20:
time: 46 us; the launch traced here: 45.7 us
  starting transfers between devices  18.3 us (40%)
  Pallas kernels  18.2 us (40%)
  waiting for transfers between devices  6.83 us (15%)
  local copies, waits for them, and re-layouts  1.41 us (3%)
  between operations  0.94 us (2%)
    pallas_call x1, Pallas kernels, per_device(): call(edge_kernel, (shape(owned, width, kind=F32), shape(owned, width), sh...  10.9 us
    all_to_all x1, starting transfers between devices, per_device(): lax.all_to_all(jnp.tile(mesh_send, (devices, 1)), 'bulk', 0, 0, tiled=True)  7.39 us
    all_to_all x1, starting transfers between devices, per_device(): piece = lax.all_to_all(rows, 'bulk', 0, 0, tiled=True)  6.78 us
    all_to_all x1, waiting for transfers between devices, per_device(): piece = lax.all_to_all(rows, 'bulk', 0, 0, tiled=True)  6.71 us
    ppermute x1, starting transfers between devices, per_device(): from_chip = lax.ppermute(chip, 'bulk', both(within))  3.36 us
    pallas_call x1, Pallas kernels, per_device(): call(functools.partial(wanted_kernel, owned), shape(edges, places), [VMEM...  2.53 us
    pallas_call x1, Pallas kernels, per_device(): call(message_kernel, shape(owned, width), [VMEM] * 10, flops=1000000000,...  1.77 us
    pallas_call x1, Pallas kernels, per_device(): call(node_kernel, (shape(owned, width), shape(places, width)), [VMEM] * 1...  1.63 us
  transfers between devices with their start and end apart: 4, of which 2 were waited for; matrix products, arithmetic and copies ran while one was open for 0% of the time, Pallas kernels for 32%

profile of v20, /device:TPU:0, one launch (start us, length us, event | category | flops | bytes accessed | tf_op | source)
XLA Modules:
  0.0 45.7 jit_solution(845071108303952761)
XLA Ops:
  0.0 1.3 %tile.2 = s32[16,4,128]{2,1,0:T(4,128)} broadcast(s32[4,128]{1,0:T(4,128)} %send_ref), dimensions={1,2} | broadcast | bytes 34816 | tf_op jit(solution)/shard_map/tile | solution.py:469
  1.3 7.4 %all-to-all-start = ((s32[16,4,128]{2,1,0:T(4,128)}), s32[16,4,128]{2,1,0:T(4,128)S(1)}, u32[]{:S(2)}, u32[]{:S(2)}) async-start(s32[16,4,128]{2,1,0:T(4,128)} %tile.2), calls=%async_computation | async-start | bytes 65536 | tf_op jit(solution)/shard_map/all_to_all | solution.py:469
  9.3 0.0 copy-start.2
  9.4 0.0 copy-start.5
  9.4 0.0 copy-start.7
  9.4 0.0 copy-start.11
  9.4 0.0 copy-start.12
  9.4 0.0 copy-start.3
  9.4 10.9 %shard_map.262 = (f32[64,512]{1,0:T(8,128)S(1)}, bf16[64,512]{1,0:T(8,128)(2,1)S(1)}, bf16[64,512]{1,0:T(8,128)(2,1)S(1)}) custom-call(s32[1]{0:T(128)} %bitcast.1.place_ref, bf16[474,512]{1,0:T(8,128)(2,1)} %first_hbm.1, bf16[474,2048]{1,0:T(8,128)(2,1)} %bitcast.26, bf16[512,512]{1,0:T(8,128)(2,1)} %second_hbm.1, bf16[512,512]{1,0:T(8,128)(2,1)} %send_weight_hbm.1, ...), custom_call_target="tpu_custom_call" | custom-call | flops 10000000000 | bytes 4000000 | tf_op jit(solution)/shard_map/pallas_call | solution.py:484
  20.4 0.0 copy-start
  20.4 0.0 copy-start.1
  20.4 0.8 %collective-permute-start = (bf16[64,512]{1,0:T(8,128)(2,1)S(1)}, bf16[64,512]{1,0:T(8,128)(2,1)S(1)}, u32[]{:S(2)}, u32[]{:S(2)}) collective-permute-start(bf16[64,512]{1,0:T(8,128)(2,1)S(1)} %get-tuple-element.21), channel_id=1, source_target_pairs={{1,2},{3,4},{5,6},{7,8},{9,10},{11,12},{13,14},{2,1},{4,3},{6,5},{... | collective-permute-start | bytes 196616 | tf_op jit(solution)/shard_map/ppermute | solution.py:508
  21.2 3.4 %collective-permute-start.1 = (bf16[64,512]{1,0:T(8,128)(2,1)S(1)}, bf16[64,512]{1,0:T(8,128)(2,1)S(1)}, u32[]{:S(2)}, u32[]{:S(2)}) collective-permute-start(bf16[64,512]{1,0:T(8,128)(2,1)S(1)} %get-tuple-element.22), channel_id=1, source_target_pairs={{0,1},{2,3},{4,5},{6,7},{8,9},{10,11},{12,13},{14,15},{1,0},{3,2},... | collective-permute-start | bytes 196616 | tf_op jit(solution)/shard_map/ppermute | solution.py:509
  24.5 0.0 all-to-all-done
  24.5 0.0 copy-done.2
  24.5 0.0 copy-done.5
  24.6 0.0 copy-done.7
  24.6 0.0 copy-done.11
  24.6 0.0 copy-done.12
  24.6 0.0 copy-start.4
  24.6 0.7 %shard_map.263 = (bf16[256,64]{1,0:T(8,128)(2,1)S(1)}, f32[64,512]{1,0:T(8,128)S(1)}, bf16[512,512]{1,0:T(8,128)(2,1)S(1)}) custom-call(s32[1]{0:T(128)} %bitcast.1.place_ref, s32[1,1024]{1,0:T(1,128)S(1)} %bitcast.19, s32[64,128]{1,0:T(8,128)S(1)} %bitcast.16, bf16[64,512]{1,0:T(8,128)(2,1)S(1)} %copy-done.2, bf16[512,512]{1,0:T(8,128)(2,1)S(1)} %copy-done.7, ...), custom_call_target="tpu_custom_call" | custom-call | flops 500000000 | bytes 500000 | tf_op jit(solution)/shard_map/pallas_call | solution.py:510
  25.3 0.0 collective-permute-done.from_cross_ref
  25.3 0.1 collective-permute-done.1.from_chip_ref
  25.4 0.0 copy-done.3
  25.4 0.0 copy-done
  25.4 0.0 copy-done.1
  25.5 1.6 %shard_map.264 = (bf16[64,512]{1,0:T(8,128)(2,1)S(1)}, bf16[256,512]{1,0:T(8,128)(2,1)}) custom-call(f32[64,512]{1,0:T(8,128)S(1)} %get-tuple-element.20.own_ref, bf16[64,512]{1,0:T(8,128)(2,1)S(1)} %collective-permute-done.from_cross_ref, bf16[64,512]{1,0:T(8,128)(2,1)S(1)} %collective-permute-done.1.from_chip_ref, bf16[64,512]{1,0:T(8,128)(2,1)S(1)} %copy-done.2, ...), custom_call_target="tpu_custom_call" | custom-call | flops 500000000 | bytes 4000000 | tf_op jit(solution)/shard_map/pallas_call | solution.py:517
  27.1 6.8 %all-to-all-start.1 = ((bf16[16,16,512]{2,1,0:T(8,128)(2,1)}), bf16[16,16,512]{2,1,0:T(8,128)(2,1)S(1)}, u32[]{:S(2)}, u32[]{:S(2)}) async-start(bf16[16,16,512]{2,1,0:T(8,128)(2,1)} %bitcast.9), calls=%async_computation.1 | async-start | bytes 524288 | tf_op jit(solution)/shard_map/all_to_all | solution.py:535
  33.9 0.0 copy-start.6
  33.9 0.0 copy-start.8
  33.9 0.0 copy-start.9
  33.9 0.0 copy-start.13
  33.9 0.0 copy-start.14
  33.9 0.0 copy-start.15
  33.9 0.0 copy-done.4
  34.0 2.5 %shard_map.265.wanted_ref = bf16[512,256]{1,0:T(8,128)(2,1)S(1)} custom-call(s32[1,1024]{1,0:T(1,128)S(1)} %bitcast.20, s32[4,128]{1,0:T(4,128)S(1)} %copy-done.4), custom_call_target="tpu_custom_call" | custom-call | flops 1000000000 | bytes 500000 | tf_op jit(solution)/shard_map/pallas_call | solution.py:537
  36.5 0.0 copy-start.10
  36.5 0.0 copy-start.16
  36.5 0.0 copy-done.6
  36.5 0.0 copy-done.8
  36.5 0.0 copy-done.9
  36.5 0.0 copy-done.13
  36.6 0.0 copy-done.14
  36.6 0.0 copy-done.15
  36.6 0.6 %shard_map.266 = (bf16[64,512]{1,0:T(8,128)(2,1)S(1)}, bf16[512,128]{1,0:T(8,128)(2,1)S(1)}, bf16[128,512]{1,0:T(8,128)(2,1)S(1)}, f32[64,512]{1,0:T(8,128)S(1)}, bf16[512,512]{1,0:T(8,128)(2,1)S(1)}) custom-call(s32[1]{0:T(128)} %bitcast.1.place_ref, s32[1,1024]{1,0:T(1,128)S(1)} %bitcast.21, s32[4,128]{1,0:T(4,128)S(1)} %copy-done.13, ...), custom_call_target="tpu_custom_call" | custom-call | flops 1000000000 | bytes 4000000 | tf_op jit(solution)/shard_map/pallas_call | solution.py:544
  37.2 6.7 %all-to-all-done.1 = bf16[16,16,512]{2,1,0:T(8,128)(2,1)S(1)} async-done(((bf16[16,16,512]{2,1,0:T(8,128)(2,1)}), bf16[16,16,512]{2,1,0:T(8,128)(2,1)S(1)}, u32[]{:S(2)}, u32[]{:S(2)}) %all-to-all-start.1) | async-done | bytes 262176 | tf_op jit(solution)/shard_map/all_to_all | solution.py:535
  43.9 0.0 copy-done.10
  43.9 0.0 copy-done.16
  43.9 1.8 %shard_map.267 = bf16[64,512]{1,0:T(8,128)(2,1)} custom-call(bf16[512,256]{1,0:T(8,128)(2,1)S(1)} %shard_map.265.wanted_ref, bf16[256,512]{1,0:T(8,128)(2,1)S(1)} %bitcast.15, bf16[64,512]{1,0:T(8,128)(2,1)S(1)} %get-tuple-element.30.incoming_ref, bf16[512,128]{1,0:T(8,128)(2,1)S(1)} %get-tuple-element.31.pick_ref, ...), custom_call_target="tpu_custom_call" | custom-call | flops 1000000000 | bytes 4000000 | tf_op jit(solution)/shard_map/pallas_call | solution.py:567
Async XLA Ops:
  1.3 23.2 %all-to-all-start = ((s32[16,4,128]{2,1,0:T(4,128)}), s32[16,4,128]{2,1,0:T(4,128)S(1)}, u32[]{:S(2)}, u32[]{:S(2)}) async-start(s32[16,4,128]{2,1,0:T(4,128)} %tile.2), calls=%async_computation | async-start | bytes 65536 | tf_op jit(solution)/shard_map/all_to_all | solution.py:469
  9.3 15.2 %copy-start.2 = (bf16[64,512]{1,0:T(8,128)(2,1)S(1)}, bf16[64,512]{1,0:T(8,128)(2,1)}, u32[]{:S(2)}) copy-start(bf16[64,512]{1,0:T(8,128)(2,1)} %latent_ref.3) | copy-start | bytes 196612
  9.4 15.2 %copy-start.5 = (bf16[1024,512]{1,0:T(8,128)(2,1)S(1)}, bf16[1024,512]{1,0:T(8,128)(2,1)}, u32[]{:S(2)}) copy-start(bf16[1024,512]{1,0:T(8,128)(2,1)} %node_input_ref.1) | copy-start | bytes 3145732
  9.4 15.2 %copy-start.7 = (bf16[512,512]{1,0:T(8,128)(2,1)S(1)}, bf16[512,512]{1,0:T(8,128)(2,1)}, u32[]{:S(2)}) copy-start(bf16[512,512]{1,0:T(8,128)(2,1)} %edge_out_ref.1) | copy-start | bytes 1572868
  9.4 15.2 %copy-start.11 = (s32[1024]{0:T(1024)S(1)}, s32[1024]{0:T(1024)}, u32[]{:S(2)}) copy-start(s32[1024]{0:T(1024)} %param.53) | copy-start | bytes 12292
  9.4 15.2 %copy-start.12 = (f32[512]{0:T(512)S(1)}, f32[512]{0:T(512)}, u32[]{:S(2)}) copy-start(f32[512]{0:T(512)} %param.37) | copy-start | bytes 6148
  9.4 16.0 %copy-start.3 = (f32[512]{0:T(512)S(1)}, f32[512]{0:T(512)}, u32[]{:S(2)}) copy-start(f32[512]{0:T(512)} %param.39) | copy-start | bytes 6148
  20.4 5.1 %copy-start = (bf16[512,512]{1,0:T(8,128)(2,1)S(1)}, bf16[512,512]{1,0:T(8,128)(2,1)}, u32[]{:S(2)}) copy-start(bf16[512,512]{1,0:T(8,128)(2,1)} %node_out_ref.1) | copy-start | bytes 1572868
  20.4 5.1 %copy-start.1 = (bf16[512,512]{1,0:T(8,128)(2,1)S(1)}, bf16[512,512]{1,0:T(8,128)(2,1)}, u32[]{:S(2)}) copy-start(bf16[512,512]{1,0:T(8,128)(2,1)} %mesh_sender_ref.1) | copy-start | bytes 1572868
  20.4 4.9 %collective-permute-start = (bf16[64,512]{1,0:T(8,128)(2,1)S(1)}, bf16[64,512]{1,0:T(8,128)(2,1)S(1)}, u32[]{:S(2)}, u32[]{:S(2)}) collective-permute-start(bf16[64,512]{1,0:T(8,128)(2,1)S(1)} %get-tuple-element.21), channel_id=1, source_target_pairs={{1,2},{3,4},{5,6},{7,8},{9,10},{11,12},{13,14},{2,1},{4,3},{6,5},{... | collective-permute-start | bytes 196616 | tf_op jit(solution)/shard_map/ppermute | solution.py:508
  21.2 4.3 %collective-permute-start.1 = (bf16[64,512]{1,0:T(8,128)(2,1)S(1)}, bf16[64,512]{1,0:T(8,128)(2,1)S(1)}, u32[]{:S(2)}, u32[]{:S(2)}) collective-permute-start(bf16[64,512]{1,0:T(8,128)(2,1)S(1)} %get-tuple-element.22), channel_id=1, source_target_pairs={{0,1},{2,3},{4,5},{6,7},{8,9},{10,11},{12,13},{14,15},{1,0},{3,2},... | collective-permute-start | bytes 196616 | tf_op jit(solution)/shard_map/ppermute | solution.py:509
  24.6 9.4 %copy-start.4 = (s32[4,128]{1,0:T(4,128)S(1)}, s32[4,128]{1,0:T(4,128)}, u32[]{:S(2)}) copy-start(s32[4,128]{1,0:T(4,128)} %send_ref) | copy-start | bytes 6148
  27.1 16.8 %all-to-all-start.1 = ((bf16[16,16,512]{2,1,0:T(8,128)(2,1)}), bf16[16,16,512]{2,1,0:T(8,128)(2,1)S(1)}, u32[]{:S(2)}, u32[]{:S(2)}) async-start(bf16[16,16,512]{2,1,0:T(8,128)(2,1)} %bitcast.9), calls=%async_computation.1 | async-start | bytes 524288 | tf_op jit(solution)/shard_map/all_to_all | solution.py:535
  33.9 2.7 %copy-start.6 = (bf16[1024,512]{1,0:T(8,128)(2,1)S(1)}, bf16[1024,512]{1,0:T(8,128)(2,1)}, u32[]{:S(2)}) copy-start(bf16[1024,512]{1,0:T(8,128)(2,1)} %update_input_ref.1) | copy-start | bytes 3145732
  33.9 2.6 %copy-start.8 = (bf16[512,512]{1,0:T(8,128)(2,1)S(1)}, bf16[512,512]{1,0:T(8,128)(2,1)}, u32[]{:S(2)}) copy-start(bf16[512,512]{1,0:T(8,128)(2,1)} %mesh_receiver_ref.1) | copy-start | bytes 1572868
  33.9 2.6 %copy-start.9 = (bf16[512,512]{1,0:T(8,128)(2,1)S(1)}, bf16[512,512]{1,0:T(8,128)(2,1)}, u32[]{:S(2)}) copy-start(bf16[512,512]{1,0:T(8,128)(2,1)} %message_out_ref.1) | copy-start | bytes 1572868
  33.9 2.6 %copy-start.13 = (s32[4,128]{1,0:T(4,128)S(1)}, s32[4,128]{1,0:T(4,128)}, u32[]{:S(2)}) copy-start(s32[4,128]{1,0:T(4,128)} %recv_ref.1) | copy-start | bytes 6148
  33.9 2.6 %copy-start.14 = (f32[512]{0:T(512)S(1)}, f32[512]{0:T(512)}, u32[]{:S(2)}) copy-start(f32[512]{0:T(512)} %param.42) | copy-start | bytes 6148
  33.9 2.6 %copy-start.15 = (f32[512]{0:T(512)S(1)}, f32[512]{0:T(512)}, u32[]{:S(2)}) copy-start(f32[512]{0:T(512)} %param.45) | copy-start | bytes 6148
  36.5 7.4 %copy-start.10 = (bf16[512,512]{1,0:T(8,128)(2,1)S(1)}, bf16[512,512]{1,0:T(8,128)(2,1)}, u32[]{:S(2)}) copy-start(bf16[512,512]{1,0:T(8,128)(2,1)} %update_out_ref.1) | copy-start | bytes 1572868
  36.5 7.4 %copy-start.16 = (f32[512]{0:T(512)S(1)}, f32[512]{0:T(512)}, u32[]{:S(2)}) copy-start(f32[512]{0:T(512)} %param.47) | copy-start | bytes 6148

commit v21 on v18

--- a/solution.py
+++ b/solution.py
@@ -41,6 +41,21 @@
     center = value - jnp.mean(value, axis=-1, keepdims=True)
     spread = jnp.mean(center * center, axis=-1, keepdims=True)
     return center * lax.rsqrt(spread + 1e-05)
+
+
+def lane_mean(value):
+    width = value.shape[1]
+    sums = sum(value[:, at : at + LANES] for at in range(0, width, LANES))
+    high = sums.astype(BF16)
+    low = (sums - high.astype(F32)).astype(BF16)
+    weight = jnp.full((2 * LANES, LANES), 1.0 / width, BF16)
+    return mm(jnp.concatenate([high, low], axis=1), weight)
+
+
+def wide_layer_norm(value):
+    wide = lambda mean: jnp.concatenate([mean] * (value.shape[1] // LANES), axis=1)
+    center = value - wide(lane_mean(value))
+    return center * wide(lax.rsqrt(lane_mean(center * center) + 1e-05))
 
 
 def iota(shape, dim):
@@ -176,7 +191,7 @@
         if step - 3 in third:
             store(step - 3, third.pop(step - 3))
         if step - 2 in second:
-            code = layer_norm(second.pop(step - 2)).astype(BF16)
+            code = wide_layer_norm(second.pop(step - 2)).astype(BF16)
         else:
             code = None
         if step - 1 in first:

time: 46 us -> 46.7 us (1.015)
  Pallas kernels: 18.2 us -> 18.9 us
    pallas_call x1, Pallas kernels: 10.9 us -> 11.6 us  [per_device(): call(edge_kernel, (shape(owned, width, kind=F32), shape(owned, width), sh...]
  transfers between devices with their start and end apart: 4 -> 4, of which waited for: 2 -> 2; matrix products, arithmetic and copies ran while one was open for 0% -> 0% of each run, Pallas kernels for 32% -> 33%
where the time goes in v21:
time: 46.7 us; the launch traced here: 46.4 us
  Pallas kernels  18.9 us (40%)
  starting transfers between devices  18.3 us (39%)
  waiting for transfers between devices  6.83 us (15%)
  local copies, waits for them, and re-layouts  1.41 us (3%)
  between operations  0.94 us (2%)
    pallas_call x1, Pallas kernels, per_device(): call(edge_kernel, (shape(owned, width, kind=F32), shape(owned, width), sh...  11.6 us
    all_to_all x1, starting transfers between devices, per_device(): lax.all_to_all(jnp.tile(mesh_send, (devices, 1)), 'bulk', 0, 0, tiled=True)  7.39 us
    all_to_all x1, starting transfers between devices, per_device(): piece = lax.all_to_all(rows, 'bulk', 0, 0, tiled=True)  6.81 us
    all_to_all x1, waiting for transfers between devices, per_device(): piece = lax.all_to_all(rows, 'bulk', 0, 0, tiled=True)  6.71 us
    ppermute x1, starting transfers between devices, per_device(): from_chip = lax.ppermute(chip, 'bulk', both(within))  3.35 us
    pallas_call x1, Pallas kernels, per_device(): call(functools.partial(wanted_kernel, owned), shape(edges, places), [VMEM...  2.53 us
    pallas_call x1, Pallas kernels, per_device(): call(message_kernel, shape(owned, width), [VMEM] * 10, flops=1000000000,...  1.77 us
    pallas_call x1, Pallas kernels, per_device(): call(node_kernel, (shape(owned, width), shape(places, width)), [VMEM] * 1...  1.63 us
  transfers between devices with their start and end apart: 4, of which 2 were waited for; matrix products, arithmetic and copies ran while one was open for 0% of the time, Pallas kernels for 33%

profile of v21, /device:TPU:0, one launch (start us, length us, event | category | flops | bytes accessed | tf_op | source)
XLA Modules:
  0.0 46.4 jit_solution(11268205327284084602)
XLA Ops:
  0.0 1.3 %tile.2 = s32[16,4,128]{2,1,0:T(4,128)} broadcast(s32[4,128]{1,0:T(4,128)} %send_ref), dimensions={1,2} | broadcast | bytes 34816 | tf_op jit(solution)/shard_map/tile | solution.py:483
  1.3 7.4 %all-to-all-start = ((s32[16,4,128]{2,1,0:T(4,128)}), s32[16,4,128]{2,1,0:T(4,128)S(1)}, u32[]{:S(2)}, u32[]{:S(2)}) async-start(s32[16,4,128]{2,1,0:T(4,128)} %tile.2), calls=%async_computation | async-start | bytes 65536 | tf_op jit(solution)/shard_map/all_to_all | solution.py:483
  9.3 0.0 copy-start.2
  9.4 0.0 copy-start.5
  9.4 0.0 copy-start.7
  9.4 0.0 copy-start.11
  9.4 0.0 copy-start.12
  9.4 0.0 copy-start.3
  9.4 11.6 %shard_map.262 = (f32[64,512]{1,0:T(8,128)S(1)}, bf16[64,512]{1,0:T(8,128)(2,1)S(1)}, bf16[64,512]{1,0:T(8,128)(2,1)S(1)}) custom-call(s32[1]{0:T(128)} %bitcast.1.place_ref, bf16[474,512]{1,0:T(8,128)(2,1)} %first_hbm.1, bf16[474,2048]{1,0:T(8,128)(2,1)} %bitcast.26, bf16[512,512]{1,0:T(8,128)(2,1)} %second_hbm.1, bf16[512,512]{1,0:T(8,128)(2,1)} %send_weight_hbm.1, ...), custom_call_target="tpu_custom_call" | custom-call | flops 10000000000 | bytes 4000000 | tf_op jit(solution)/shard_map/pallas_call | solution.py:498
  21.1 0.0 copy-start
  21.1 0.0 copy-start.1
  21.1 0.8 %collective-permute-start = (bf16[64,512]{1,0:T(8,128)(2,1)S(1)}, bf16[64,512]{1,0:T(8,128)(2,1)S(1)}, u32[]{:S(2)}, u32[]{:S(2)}) collective-permute-start(bf16[64,512]{1,0:T(8,128)(2,1)S(1)} %get-tuple-element.21), channel_id=1, source_target_pairs={{1,2},{3,4},{5,6},{7,8},{9,10},{11,12},{13,14},{2,1},{4,3},{6,5},{... | collective-permute-start | bytes 196616 | tf_op jit(solution)/shard_map/ppermute | solution.py:522
  21.9 3.3 %collective-permute-start.1 = (bf16[64,512]{1,0:T(8,128)(2,1)S(1)}, bf16[64,512]{1,0:T(8,128)(2,1)S(1)}, u32[]{:S(2)}, u32[]{:S(2)}) collective-permute-start(bf16[64,512]{1,0:T(8,128)(2,1)S(1)} %get-tuple-element.22), channel_id=1, source_target_pairs={{0,1},{2,3},{4,5},{6,7},{8,9},{10,11},{12,13},{14,15},{1,0},{3,2},... | collective-permute-start | bytes 196616 | tf_op jit(solution)/shard_map/ppermute | solution.py:523
  25.2 0.0 all-to-all-done
  25.2 0.0 copy-done.2
  25.2 0.0 copy-done.5
  25.2 0.0 copy-done.7
  25.3 0.0 copy-done.11
  25.3 0.0 copy-done.12
  25.3 0.0 copy-start.4
  25.3 0.7 %shard_map.263 = (bf16[256,64]{1,0:T(8,128)(2,1)S(1)}, f32[64,512]{1,0:T(8,128)S(1)}, bf16[512,512]{1,0:T(8,128)(2,1)S(1)}) custom-call(s32[1]{0:T(128)} %bitcast.1.place_ref, s32[1,1024]{1,0:T(1,128)S(1)} %bitcast.19, s32[64,128]{1,0:T(8,128)S(1)} %bitcast.16, bf16[64,512]{1,0:T(8,128)(2,1)S(1)} %copy-done.2, bf16[512,512]{1,0:T(8,128)(2,1)S(1)} %copy-done.7, ...), custom_call_target="tpu_custom_call" | custom-call | flops 500000000 | bytes 500000 | tf_op jit(solution)/shard_map/pallas_call | solution.py:524
  26.0 0.0 collective-permute-done.from_cross_ref
  26.0 0.1 collective-permute-done.1.from_chip_ref
  26.1 0.0 copy-done.3
  26.1 0.0 copy-done
  26.1 0.0 copy-done.1
  26.1 1.6 %shard_map.264 = (bf16[64,512]{1,0:T(8,128)(2,1)S(1)}, bf16[256,512]{1,0:T(8,128)(2,1)}) custom-call(f32[64,512]{1,0:T(8,128)S(1)} %get-tuple-element.20.own_ref, bf16[64,512]{1,0:T(8,128)(2,1)S(1)} %collective-permute-done.from_cross_ref, bf16[64,512]{1,0:T(8,128)(2,1)S(1)} %collective-permute-done.1.from_chip_ref, bf16[64,512]{1,0:T(8,128)(2,1)S(1)} %copy-done.2, ...), custom_call_target="tpu_custom_call" | custom-call | flops 500000000 | bytes 4000000 | tf_op jit(solution)/shard_map/pallas_call | solution.py:531
  27.8 6.8 %all-to-all-start.1 = ((bf16[16,16,512]{2,1,0:T(8,128)(2,1)}), bf16[16,16,512]{2,1,0:T(8,128)(2,1)S(1)}, u32[]{:S(2)}, u32[]{:S(2)}) async-start(bf16[16,16,512]{2,1,0:T(8,128)(2,1)} %bitcast.9), calls=%async_computation.1 | async-start | bytes 524288 | tf_op jit(solution)/shard_map/all_to_all | solution.py:549
  34.6 0.0 copy-start.6
  34.6 0.0 copy-start.8
  34.6 0.0 copy-start.9
  34.6 0.0 copy-start.13
  34.6 0.0 copy-start.14
  34.6 0.0 copy-start.15
  34.7 0.0 copy-done.4
  34.7 2.5 %shard_map.265.wanted_ref = bf16[512,256]{1,0:T(8,128)(2,1)S(1)} custom-call(s32[1,1024]{1,0:T(1,128)S(1)} %bitcast.20, s32[4,128]{1,0:T(4,128)S(1)} %copy-done.4), custom_call_target="tpu_custom_call" | custom-call | flops 1000000000 | bytes 500000 | tf_op jit(solution)/shard_map/pallas_call | solution.py:551
  37.2 0.0 copy-start.10
  37.2 0.0 copy-start.16
  37.2 0.0 copy-done.6
  37.2 0.0 copy-done.8
  37.3 0.0 copy-done.9
  37.3 0.0 copy-done.13
  37.3 0.0 copy-done.14
  37.3 0.0 copy-done.15
  37.3 0.6 %shard_map.266 = (bf16[64,512]{1,0:T(8,128)(2,1)S(1)}, bf16[512,128]{1,0:T(8,128)(2,1)S(1)}, bf16[128,512]{1,0:T(8,128)(2,1)S(1)}, f32[64,512]{1,0:T(8,128)S(1)}, bf16[512,512]{1,0:T(8,128)(2,1)S(1)}) custom-call(s32[1]{0:T(128)} %bitcast.1.place_ref, s32[1,1024]{1,0:T(1,128)S(1)} %bitcast.21, s32[4,128]{1,0:T(4,128)S(1)} %copy-done.13, ...), custom_call_target="tpu_custom_call" | custom-call | flops 1000000000 | bytes 4000000 | tf_op jit(solution)/shard_map/pallas_call | solution.py:558
  37.9 6.7 %all-to-all-done.1 = bf16[16,16,512]{2,1,0:T(8,128)(2,1)S(1)} async-done(((bf16[16,16,512]{2,1,0:T(8,128)(2,1)}), bf16[16,16,512]{2,1,0:T(8,128)(2,1)S(1)}, u32[]{:S(2)}, u32[]{:S(2)}) %all-to-all-start.1) | async-done | bytes 262176 | tf_op jit(solution)/shard_map/all_to_all | solution.py:549
  44.6 0.0 copy-done.10
  44.6 0.0 copy-done.16
  44.6 1.8 %shard_map.267 = bf16[64,512]{1,0:T(8,128)(2,1)} custom-call(bf16[512,256]{1,0:T(8,128)(2,1)S(1)} %shard_map.265.wanted_ref, bf16[256,512]{1,0:T(8,128)(2,1)S(1)} %bitcast.15, bf16[64,512]{1,0:T(8,128)(2,1)S(1)} %get-tuple-element.30.incoming_ref, bf16[512,128]{1,0:T(8,128)(2,1)S(1)} %get-tuple-element.31.pick_ref, ...), custom_call_target="tpu_custom_call" | custom-call | flops 1000000000 | bytes 4000000 | tf_op jit(solution)/shard_map/pallas_call | solution.py:581
Async XLA Ops:
  1.3 23.9 %all-to-all-start = ((s32[16,4,128]{2,1,0:T(4,128)}), s32[16,4,128]{2,1,0:T(4,128)S(1)}, u32[]{:S(2)}, u32[]{:S(2)}) async-start(s32[16,4,128]{2,1,0:T(4,128)} %tile.2), calls=%async_computation | async-start | bytes 65536 | tf_op jit(solution)/shard_map/all_to_all | solution.py:483
  9.3 15.9 %copy-start.2 = (bf16[64,512]{1,0:T(8,128)(2,1)S(1)}, bf16[64,512]{1,0:T(8,128)(2,1)}, u32[]{:S(2)}) copy-start(bf16[64,512]{1,0:T(8,128)(2,1)} %latent_ref.3) | copy-start | bytes 196612
  9.4 15.9 %copy-start.5 = (bf16[1024,512]{1,0:T(8,128)(2,1)S(1)}, bf16[1024,512]{1,0:T(8,128)(2,1)}, u32[]{:S(2)}) copy-start(bf16[1024,512]{1,0:T(8,128)(2,1)} %node_input_ref.1) | copy-start | bytes 3145732
  9.4 15.9 %copy-start.7 = (bf16[512,512]{1,0:T(8,128)(2,1)S(1)}, bf16[512,512]{1,0:T(8,128)(2,1)}, u32[]{:S(2)}) copy-start(bf16[512,512]{1,0:T(8,128)(2,1)} %edge_out_ref.1) | copy-start | bytes 1572868
  9.4 15.9 %copy-start.11 = (s32[1024]{0:T(1024)S(1)}, s32[1024]{0:T(1024)}, u32[]{:S(2)}) copy-start(s32[1024]{0:T(1024)} %param.53) | copy-start | bytes 12292
  9.4 15.9 %copy-start.12 = (f32[512]{0:T(512)S(1)}, f32[512]{0:T(512)}, u32[]{:S(2)}) copy-start(f32[512]{0:T(512)} %param.37) | copy-start | bytes 6148
  9.4 16.7 %copy-start.3 = (f32[512]{0:T(512)S(1)}, f32[512]{0:T(512)}, u32[]{:S(2)}) copy-start(f32[512]{0:T(512)} %param.39) | copy-start | bytes 6148
  21.1 5.1 %copy-start = (bf16[512,512]{1,0:T(8,128)(2,1)S(1)}, bf16[512,512]{1,0:T(8,128)(2,1)}, u32[]{:S(2)}) copy-start(bf16[512,512]{1,0:T(8,128)(2,1)} %node_out_ref.1) | copy-start | bytes 1572868
  21.1 5.1 %copy-start.1 = (bf16[512,512]{1,0:T(8,128)(2,1)S(1)}, bf16[512,512]{1,0:T(8,128)(2,1)}, u32[]{:S(2)}) copy-start(bf16[512,512]{1,0:T(8,128)(2,1)} %mesh_sender_ref.1) | copy-start | bytes 1572868
  21.1 4.9 %collective-permute-start = (bf16[64,512]{1,0:T(8,128)(2,1)S(1)}, bf16[64,512]{1,0:T(8,128)(2,1)S(1)}, u32[]{:S(2)}, u32[]{:S(2)}) collective-permute-start(bf16[64,512]{1,0:T(8,128)(2,1)S(1)} %get-tuple-element.21), channel_id=1, source_target_pairs={{1,2},{3,4},{5,6},{7,8},{9,10},{11,12},{13,14},{2,1},{4,3},{6,5},{... | collective-permute-start | bytes 196616 | tf_op jit(solution)/shard_map/ppermute | solution.py:522
  21.9 4.2 %collective-permute-start.1 = (bf16[64,512]{1,0:T(8,128)(2,1)S(1)}, bf16[64,512]{1,0:T(8,128)(2,1)S(1)}, u32[]{:S(2)}, u32[]{:S(2)}) collective-permute-start(bf16[64,512]{1,0:T(8,128)(2,1)S(1)} %get-tuple-element.22), channel_id=1, source_target_pairs={{0,1},{2,3},{4,5},{6,7},{8,9},{10,11},{12,13},{14,15},{1,0},{3,2},... | collective-permute-start | bytes 196616 | tf_op jit(solution)/shard_map/ppermute | solution.py:523
  25.3 9.4 %copy-start.4 = (s32[4,128]{1,0:T(4,128)S(1)}, s32[4,128]{1,0:T(4,128)}, u32[]{:S(2)}) copy-start(s32[4,128]{1,0:T(4,128)} %send_ref) | copy-start | bytes 6148
  27.8 16.9 %all-to-all-start.1 = ((bf16[16,16,512]{2,1,0:T(8,128)(2,1)}), bf16[16,16,512]{2,1,0:T(8,128)(2,1)S(1)}, u32[]{:S(2)}, u32[]{:S(2)}) async-start(bf16[16,16,512]{2,1,0:T(8,128)(2,1)} %bitcast.9), calls=%async_computation.1 | async-start | bytes 524288 | tf_op jit(solution)/shard_map/all_to_all | solution.py:549
  34.6 2.7 %copy-start.6 = (bf16[1024,512]{1,0:T(8,128)(2,1)S(1)}, bf16[1024,512]{1,0:T(8,128)(2,1)}, u32[]{:S(2)}) copy-start(bf16[1024,512]{1,0:T(8,128)(2,1)} %update_input_ref.1) | copy-start | bytes 3145732
  34.6 2.6 %copy-start.8 = (bf16[512,512]{1,0:T(8,128)(2,1)S(1)}, bf16[512,512]{1,0:T(8,128)(2,1)}, u32[]{:S(2)}) copy-start(bf16[512,512]{1,0:T(8,128)(2,1)} %mesh_receiver_ref.1) | copy-start | bytes 1572868
  34.6 2.6 %copy-start.9 = (bf16[512,512]{1,0:T(8,128)(2,1)S(1)}, bf16[512,512]{1,0:T(8,128)(2,1)}, u32[]{:S(2)}) copy-start(bf16[512,512]{1,0:T(8,128)(2,1)} %message_out_ref.1) | copy-start | bytes 1572868
  34.6 2.6 %copy-start.13 = (s32[4,128]{1,0:T(4,128)S(1)}, s32[4,128]{1,0:T(4,128)}, u32[]{:S(2)}) copy-start(s32[4,128]{1,0:T(4,128)} %recv_ref.1) | copy-start | bytes 6148
  34.6 2.6 %copy-start.14 = (f32[512]{0:T(512)S(1)}, f32[512]{0:T(512)}, u32[]{:S(2)}) copy-start(f32[512]{0:T(512)} %param.42) | copy-start | bytes 6148
  34.6 2.6 %copy-start.15 = (f32[512]{0:T(512)S(1)}, f32[512]{0:T(512)}, u32[]{:S(2)}) copy-start(f32[512]{0:T(512)} %param.45) | copy-start | bytes 6148
  37.2 7.4 %copy-start.10 = (bf16[512,512]{1,0:T(8,128)(2,1)S(1)}, bf16[512,512]{1,0:T(8,128)(2,1)}, u32[]{:S(2)}) copy-start(bf16[512,512]{1,0:T(8,128)(2,1)} %update_out_ref.1) | copy-start | bytes 1572868
  37.2 7.4 %copy-start.16 = (f32[512]{0:T(512)S(1)}, f32[512]{0:T(512)}, u32[]{:S(2)}) copy-start(f32[512]{0:T(512)} %param.47) | copy-start | bytes 6148

commit v22 on v19

--- a/solution.py
+++ b/solution.py
@@ -17,7 +17,7 @@
 SMEM = pltpu.SMEM
 HBM = pltpu.HBM
 GRID_STEPS = 4
-CHUNK_BLOCKS = 6
+CHUNK_BLOCKS = 2
 MEBI = 1024 * 1024
 
 

time: 46.2 us -> 46.1 us (level)
  no operation moved by 1% of the time
where the time goes in v22:
time: 46.1 us; the launch traced here: 45.7 us
  starting transfers between devices  18.3 us (40%)
  Pallas kernels  18.2 us (39%)
  waiting for transfers between devices  6.83 us (15%)
  local copies, waits for them, and re-layouts  1.41 us (3%)
  between operations  0.94 us (2%)
    pallas_call x1, Pallas kernels, per_device(): call(edge_kernel, (shape(owned, width, kind=F32), shape(owned, width), sh...  11 us
    all_to_all x1, starting transfers between devices, per_device(): lax.all_to_all(jnp.tile(mesh_send, (devices, 1)), 'bulk', 0, 0, tiled=True)  7.39 us
    all_to_all x1, starting transfers between devices, per_device(): piece = lax.all_to_all(rows, 'bulk', 0, 0, tiled=True)  6.79 us
    all_to_all x1, waiting for transfers between devices, per_device(): piece = lax.all_to_all(rows, 'bulk', 0, 0, tiled=True)  6.71 us
    ppermute x1, starting transfers between devices, per_device(): from_chip = lax.ppermute(chip, 'bulk', both(within))  3.36 us
    pallas_call x1, Pallas kernels, per_device(): call(functools.partial(wanted_kernel, owned), shape(edges, places), [VMEM...  2.53 us
    pallas_call x1, Pallas kernels, per_device(): call(message_kernel, shape(owned, width), [VMEM] * 10, flops=1000000000,...  1.77 us
    pallas_call x1, Pallas kernels, per_device(): call(node_kernel, (shape(owned, width), shape(places, width)), [VMEM] * 1...  1.62 us
  transfers between devices with their start and end apart: 4, of which 2 were waited for; matrix products, arithmetic and copies ran while one was open for 0% of the time, Pallas kernels for 33%

profile of v22, /device:TPU:0, one launch (start us, length us, event | category | flops | bytes accessed | tf_op | source)
XLA Modules:
  0.0 45.7 jit_solution(12237514373700007793)
XLA Ops:
  0.0 1.3 %tile.2 = s32[16,4,128]{2,1,0:T(4,128)} broadcast(s32[4,128]{1,0:T(4,128)} %send_ref), dimensions={1,2} | broadcast | bytes 34816 | tf_op jit(solution)/shard_map/tile | solution.py:468
  1.3 7.4 %all-to-all-start = ((s32[16,4,128]{2,1,0:T(4,128)}), s32[16,4,128]{2,1,0:T(4,128)S(1)}, u32[]{:S(2)}, u32[]{:S(2)}) async-start(s32[16,4,128]{2,1,0:T(4,128)} %tile.2), calls=%async_computation | async-start | bytes 65536 | tf_op jit(solution)/shard_map/all_to_all | solution.py:468
  9.3 0.0 copy-start.2
  9.4 0.0 copy-start.5
  9.4 0.0 copy-start.7
  9.4 0.0 copy-start.11
  9.4 0.0 copy-start.12
  9.4 0.0 copy-start.3
  9.4 11.0 %shard_map.262 = (f32[64,512]{1,0:T(8,128)S(1)}, bf16[64,512]{1,0:T(8,128)(2,1)S(1)}, bf16[64,512]{1,0:T(8,128)(2,1)S(1)}) custom-call(s32[1]{0:T(128)} %bitcast.1.place_ref, bf16[474,512]{1,0:T(8,128)(2,1)} %first_hbm.1, bf16[474,2048]{1,0:T(8,128)(2,1)} %bitcast.26, bf16[512,512]{1,0:T(8,128)(2,1)} %second_hbm.1, bf16[512,512]{1,0:T(8,128)(2,1)} %send_weight_hbm.1, ...), custom_call_target="tpu_custom_call" | custom-call | flops 10000000000 | bytes 4000000 | tf_op jit(solution)/shard_map/pallas_call | solution.py:483
  20.4 0.0 copy-start
  20.4 0.0 copy-start.1
  20.4 0.8 %collective-permute-start = (bf16[64,512]{1,0:T(8,128)(2,1)S(1)}, bf16[64,512]{1,0:T(8,128)(2,1)S(1)}, u32[]{:S(2)}, u32[]{:S(2)}) collective-permute-start(bf16[64,512]{1,0:T(8,128)(2,1)S(1)} %get-tuple-element.21), channel_id=1, source_target_pairs={{1,2},{3,4},{5,6},{7,8},{9,10},{11,12},{13,14},{2,1},{4,3},{6,5},{... | collective-permute-start | bytes 196616 | tf_op jit(solution)/shard_map/ppermute | solution.py:507
  21.2 3.4 %collective-permute-start.1 = (bf16[64,512]{1,0:T(8,128)(2,1)S(1)}, bf16[64,512]{1,0:T(8,128)(2,1)S(1)}, u32[]{:S(2)}, u32[]{:S(2)}) collective-permute-start(bf16[64,512]{1,0:T(8,128)(2,1)S(1)} %get-tuple-element.22), channel_id=1, source_target_pairs={{0,1},{2,3},{4,5},{6,7},{8,9},{10,11},{12,13},{14,15},{1,0},{3,2},... | collective-permute-start | bytes 196616 | tf_op jit(solution)/shard_map/ppermute | solution.py:508
  24.6 0.0 all-to-all-done
  24.6 0.0 copy-done.2
  24.6 0.0 copy-done.5
  24.6 0.0 copy-done.7
  24.6 0.0 copy-done.11
  24.6 0.0 copy-done.12
  24.6 0.0 copy-start.4
  24.6 0.7 %shard_map.263 = (bf16[256,64]{1,0:T(8,128)(2,1)S(1)}, f32[64,512]{1,0:T(8,128)S(1)}, bf16[512,512]{1,0:T(8,128)(2,1)S(1)}) custom-call(s32[1]{0:T(128)} %bitcast.1.place_ref, s32[1,1024]{1,0:T(1,128)S(1)} %bitcast.19, s32[64,128]{1,0:T(8,128)S(1)} %bitcast.16, bf16[64,512]{1,0:T(8,128)(2,1)S(1)} %copy-done.2, bf16[512,512]{1,0:T(8,128)(2,1)S(1)} %copy-done.7, ...), custom_call_target="tpu_custom_call" | custom-call | flops 500000000 | bytes 500000 | tf_op jit(solution)/shard_map/pallas_call | solution.py:509
  25.4 0.0 collective-permute-done.from_cross_ref
  25.4 0.1 collective-permute-done.1.from_chip_ref
  25.5 0.0 copy-done.3
  25.5 0.0 copy-done
  25.5 0.0 copy-done.1
  25.5 1.6 %shard_map.264 = (bf16[64,512]{1,0:T(8,128)(2,1)S(1)}, bf16[256,512]{1,0:T(8,128)(2,1)}) custom-call(f32[64,512]{1,0:T(8,128)S(1)} %get-tuple-element.20.own_ref, bf16[64,512]{1,0:T(8,128)(2,1)S(1)} %collective-permute-done.from_cross_ref, bf16[64,512]{1,0:T(8,128)(2,1)S(1)} %collective-permute-done.1.from_chip_ref, bf16[64,512]{1,0:T(8,128)(2,1)S(1)} %copy-done.2, ...), custom_call_target="tpu_custom_call" | custom-call | flops 500000000 | bytes 4000000 | tf_op jit(solution)/shard_map/pallas_call | solution.py:516
  27.1 6.8 %all-to-all-start.1 = ((bf16[16,16,512]{2,1,0:T(8,128)(2,1)}), bf16[16,16,512]{2,1,0:T(8,128)(2,1)S(1)}, u32[]{:S(2)}, u32[]{:S(2)}) async-start(bf16[16,16,512]{2,1,0:T(8,128)(2,1)} %bitcast.9), calls=%async_computation.1 | async-start | bytes 524288 | tf_op jit(solution)/shard_map/all_to_all | solution.py:534
  33.9 0.0 copy-start.6
  33.9 0.0 copy-start.8
  33.9 0.0 copy-start.9
  34.0 0.0 copy-start.13
  34.0 0.0 copy-start.14
  34.0 0.0 copy-start.15
  34.0 0.0 copy-done.4
  34.0 2.5 %shard_map.265.wanted_ref = bf16[512,256]{1,0:T(8,128)(2,1)S(1)} custom-call(s32[1,1024]{1,0:T(1,128)S(1)} %bitcast.20, s32[4,128]{1,0:T(4,128)S(1)} %copy-done.4), custom_call_target="tpu_custom_call" | custom-call | flops 1000000000 | bytes 500000 | tf_op jit(solution)/shard_map/pallas_call | solution.py:536
  36.5 0.0 copy-start.10
  36.6 0.0 copy-start.16
  36.6 0.0 copy-done.6
  36.6 0.0 copy-done.8
  36.6 0.0 copy-done.9
  36.6 0.0 copy-done.13
  36.6 0.0 copy-done.14
  36.6 0.0 copy-done.15
  36.6 0.6 %shard_map.266 = (bf16[64,512]{1,0:T(8,128)(2,1)S(1)}, bf16[512,128]{1,0:T(8,128)(2,1)S(1)}, bf16[128,512]{1,0:T(8,128)(2,1)S(1)}, f32[64,512]{1,0:T(8,128)S(1)}, bf16[512,512]{1,0:T(8,128)(2,1)S(1)}) custom-call(s32[1]{0:T(128)} %bitcast.1.place_ref, s32[1,1024]{1,0:T(1,128)S(1)} %bitcast.21, s32[4,128]{1,0:T(4,128)S(1)} %copy-done.13, ...), custom_call_target="tpu_custom_call" | custom-call | flops 1000000000 | bytes 4000000 | tf_op jit(solution)/shard_map/pallas_call | solution.py:543
  37.3 6.7 %all-to-all-done.1 = bf16[16,16,512]{2,1,0:T(8,128)(2,1)S(1)} async-done(((bf16[16,16,512]{2,1,0:T(8,128)(2,1)}), bf16[16,16,512]{2,1,0:T(8,128)(2,1)S(1)}, u32[]{:S(2)}, u32[]{:S(2)}) %all-to-all-start.1) | async-done | bytes 262176 | tf_op jit(solution)/shard_map/all_to_all | solution.py:534
  44.0 0.0 copy-done.10
  44.0 0.0 copy-done.16
  44.0 1.8 %shard_map.267 = bf16[64,512]{1,0:T(8,128)(2,1)} custom-call(bf16[512,256]{1,0:T(8,128)(2,1)S(1)} %shard_map.265.wanted_ref, bf16[256,512]{1,0:T(8,128)(2,1)S(1)} %bitcast.15, bf16[64,512]{1,0:T(8,128)(2,1)S(1)} %get-tuple-element.30.incoming_ref, bf16[512,128]{1,0:T(8,128)(2,1)S(1)} %get-tuple-element.31.pick_ref, ...), custom_call_target="tpu_custom_call" | custom-call | flops 1000000000 | bytes 4000000 | tf_op jit(solution)/shard_map/pallas_call | solution.py:566
Async XLA Ops:
  1.3 23.3 %all-to-all-start = ((s32[16,4,128]{2,1,0:T(4,128)}), s32[16,4,128]{2,1,0:T(4,128)S(1)}, u32[]{:S(2)}, u32[]{:S(2)}) async-start(s32[16,4,128]{2,1,0:T(4,128)} %tile.2), calls=%async_computation | async-start | bytes 65536 | tf_op jit(solution)/shard_map/all_to_all | solution.py:468
  9.3 15.3 %copy-start.2 = (bf16[64,512]{1,0:T(8,128)(2,1)S(1)}, bf16[64,512]{1,0:T(8,128)(2,1)}, u32[]{:S(2)}) copy-start(bf16[64,512]{1,0:T(8,128)(2,1)} %latent_ref.3) | copy-start | bytes 196612
  9.4 15.2 %copy-start.5 = (bf16[1024,512]{1,0:T(8,128)(2,1)S(1)}, bf16[1024,512]{1,0:T(8,128)(2,1)}, u32[]{:S(2)}) copy-start(bf16[1024,512]{1,0:T(8,128)(2,1)} %node_input_ref.1) | copy-start | bytes 3145732
  9.4 15.2 %copy-start.7 = (bf16[512,512]{1,0:T(8,128)(2,1)S(1)}, bf16[512,512]{1,0:T(8,128)(2,1)}, u32[]{:S(2)}) copy-start(bf16[512,512]{1,0:T(8,128)(2,1)} %edge_out_ref.1) | copy-start | bytes 1572868
  9.4 15.2 %copy-start.11 = (s32[1024]{0:T(1024)S(1)}, s32[1024]{0:T(1024)}, u32[]{:S(2)}) copy-start(s32[1024]{0:T(1024)} %param.53) | copy-start | bytes 12292
  9.4 15.2 %copy-start.12 = (f32[512]{0:T(512)S(1)}, f32[512]{0:T(512)}, u32[]{:S(2)}) copy-start(f32[512]{0:T(512)} %param.37) | copy-start | bytes 6148
  9.4 16.1 %copy-start.3 = (f32[512]{0:T(512)S(1)}, f32[512]{0:T(512)}, u32[]{:S(2)}) copy-start(f32[512]{0:T(512)} %param.39) | copy-start | bytes 6148
  20.4 5.1 %copy-start = (bf16[512,512]{1,0:T(8,128)(2,1)S(1)}, bf16[512,512]{1,0:T(8,128)(2,1)}, u32[]{:S(2)}) copy-start(bf16[512,512]{1,0:T(8,128)(2,1)} %node_out_ref.1) | copy-start | bytes 1572868
  20.4 5.1 %copy-start.1 = (bf16[512,512]{1,0:T(8,128)(2,1)S(1)}, bf16[512,512]{1,0:T(8,128)(2,1)}, u32[]{:S(2)}) copy-start(bf16[512,512]{1,0:T(8,128)(2,1)} %mesh_sender_ref.1) | copy-start | bytes 1572868
  20.4 4.9 %collective-permute-start = (bf16[64,512]{1,0:T(8,128)(2,1)S(1)}, bf16[64,512]{1,0:T(8,128)(2,1)S(1)}, u32[]{:S(2)}, u32[]{:S(2)}) collective-permute-start(bf16[64,512]{1,0:T(8,128)(2,1)S(1)} %get-tuple-element.21), channel_id=1, source_target_pairs={{1,2},{3,4},{5,6},{7,8},{9,10},{11,12},{13,14},{2,1},{4,3},{6,5},{... | collective-permute-start | bytes 196616 | tf_op jit(solution)/shard_map/ppermute | solution.py:507
  21.2 4.3 %collective-permute-start.1 = (bf16[64,512]{1,0:T(8,128)(2,1)S(1)}, bf16[64,512]{1,0:T(8,128)(2,1)S(1)}, u32[]{:S(2)}, u32[]{:S(2)}) collective-permute-start(bf16[64,512]{1,0:T(8,128)(2,1)S(1)} %get-tuple-element.22), channel_id=1, source_target_pairs={{0,1},{2,3},{4,5},{6,7},{8,9},{10,11},{12,13},{14,15},{1,0},{3,2},... | collective-permute-start | bytes 196616 | tf_op jit(solution)/shard_map/ppermute | solution.py:508
  24.6 9.4 %copy-start.4 = (s32[4,128]{1,0:T(4,128)S(1)}, s32[4,128]{1,0:T(4,128)}, u32[]{:S(2)}) copy-start(s32[4,128]{1,0:T(4,128)} %send_ref) | copy-start | bytes 6148
  27.1 16.8 %all-to-all-start.1 = ((bf16[16,16,512]{2,1,0:T(8,128)(2,1)}), bf16[16,16,512]{2,1,0:T(8,128)(2,1)S(1)}, u32[]{:S(2)}, u32[]{:S(2)}) async-start(bf16[16,16,512]{2,1,0:T(8,128)(2,1)} %bitcast.9), calls=%async_computation.1 | async-start | bytes 524288 | tf_op jit(solution)/shard_map/all_to_all | solution.py:534
  33.9 2.7 %copy-start.6 = (bf16[1024,512]{1,0:T(8,128)(2,1)S(1)}, bf16[1024,512]{1,0:T(8,128)(2,1)}, u32[]{:S(2)}) copy-start(bf16[1024,512]{1,0:T(8,128)(2,1)} %update_input_ref.1) | copy-start | bytes 3145732
  33.9 2.6 %copy-start.8 = (bf16[512,512]{1,0:T(8,128)(2,1)S(1)}, bf16[512,512]{1,0:T(8,128)(2,1)}, u32[]{:S(2)}) copy-start(bf16[512,512]{1,0:T(8,128)(2,1)} %mesh_receiver_ref.1) | copy-start | bytes 1572868
  33.9 2.6 %copy-start.9 = (bf16[512,512]{1,0:T(8,128)(2,1)S(1)}, bf16[512,512]{1,0:T(8,128)(2,1)}, u32[]{:S(2)}) copy-start(bf16[512,512]{1,0:T(8,128)(2,1)} %message_out_ref.1) | copy-start | bytes 1572868
  34.0 2.6 %copy-start.13 = (s32[4,128]{1,0:T(4,128)S(1)}, s32[4,128]{1,0:T(4,128)}, u32[]{:S(2)}) copy-start(s32[4,128]{1,0:T(4,128)} %recv_ref.1) | copy-start | bytes 6148
  34.0 2.6 %copy-start.14 = (f32[512]{0:T(512)S(1)}, f32[512]{0:T(512)}, u32[]{:S(2)}) copy-start(f32[512]{0:T(512)} %param.42) | copy-start | bytes 6148
  34.0 2.6 %copy-start.15 = (f32[512]{0:T(512)S(1)}, f32[512]{0:T(512)}, u32[]{:S(2)}) copy-start(f32[512]{0:T(512)} %param.45) | copy-start | bytes 6148
  36.5 7.4 %copy-start.10 = (bf16[512,512]{1,0:T(8,128)(2,1)S(1)}, bf16[512,512]{1,0:T(8,128)(2,1)}, u32[]{:S(2)}) copy-start(bf16[512,512]{1,0:T(8,128)(2,1)} %update_out_ref.1) | copy-start | bytes 1572868
  36.6 7.4 %copy-start.16 = (f32[512]{0:T(512)S(1)}, f32[512]{0:T(512)}, u32[]{:S(2)}) copy-start(f32[512]{0:T(512)} %param.47) | copy-start | bytes 6148

commit v23 on v18

--- a/solution.py
+++ b/solution.py
@@ -47,8 +47,11 @@
     return lax.broadcasted_iota(I32, shape, dim)
 
 
-def one_hot(columns, rows):
-    hit = columns.astype(jnp.int16) == lax.broadcasted_iota(jnp.int16, (rows, columns.shape[1]), 0)
+def one_hot(places, columns):
+    count = places.shape[1]
+    places = jnp.broadcast_to(places.astype(F32), (LANES, count)).T.astype(I32).astype(jnp.int16)
+    places = jnp.concatenate([places] * (columns // LANES), axis=1)
+    hit = places == lax.broadcasted_iota(jnp.int16, (count, columns), 1)
     return jnp.where(hit, jnp.ones((), BF16), jnp.zeros((), BF16))
 
 
@@ -88,6 +91,8 @@
     feat_ref,
     count_ref,
     starts,
+    senders_ref,
+    flat,
     table,
     even_rows,
     odd_rows,
@@ -137,6 +142,7 @@
         grid_copy(step).start()
     send_copy.wait()
     senders = send_ref[...]
+    senders_ref[...] = senders
     send_ref[...] = (senders // 8) * (8 * pieces) + senders % 8
     starts_copy.start()
     slot_copy.wait()
@@ -158,7 +164,9 @@
         return grid_ref[:, step * step_rows : (step + 1) * step_rows].T
 
     def store(step, value):
-        rows = (value + edge_bias).astype(BF16).astype(F32)
+        rows = (value + edge_bias).astype(BF16)
+        flat[step * step_rows : (step + 1) * step_rows, :] = rows
+        rows = rows.astype(F32)
         for group in range(step_rows // 8):
             for piece in range(pieces):
                 at = ((step * step_rows // 8 + group) * pieces + piece) * 8
@@ -232,11 +240,19 @@
         feat = jnp.concatenate([feat_ref[b] for b in here], axis=1)
         feat = jnp.concatenate([feat, jnp.zeros((8 - feats, feat.shape[1]), F32)], axis=0)
         extra = mm(feat.T.astype(BF16), feat_weight)
+        picker = one_hot(senders_ref[pl.ds(here[-1], 1), :], grid_rows)
+        chosen = mm(picker, flat[...])
         add_sums(jnp.maximum(chunk - 1, 0), hidden_before)
         after = jnp.minimum(chunk + 1, chunks - 1)
-        for first in range(0, group * block_edges, part_rows):
-            gather(after, range(first, first + part_rows), target)
-            half = rows_of(source, first, part_rows) + extra[first : first + part_rows]
+        loaded = (group - 1) * block_edges
+        each = loaded // (group * block_edges // part_rows)
+        for at, first in enumerate(range(0, group * block_edges, part_rows)):
+            gather(after, range(at * each, (at + 1) * each), target)
+            if first < loaded:
+                half = rows_of(source, first, part_rows)
+            else:
+                half = chosen[first - loaded : first - loaded + part_rows]
+            half = half + extra[first : first + part_rows]
             hidden[first : first + part_rows, :] = silu_half(half).astype(BF16)
 
     def edge_step(step, carry):
@@ -245,7 +261,7 @@
         return carry
 
     odd_hidden[...] = jnp.zeros_like(odd_hidden)
-    gather(0, range(group * block_edges), even_rows)
+    gather(0, range((group - 1) * block_edges), even_rows)
     lax.fori_loop(0, chunks // 2, edge_step, 0)
     add_sums(chunks - 1, odd_hidden)
     odd = place % 2 == 1
@@ -487,6 +503,8 @@
         scratch=[VMEM(value.shape, value.dtype) for value in operands]
         + [
             SMEM(g2m_send.shape, I32),
+            VMEM(g2m_send.shape, I32),
+            VMEM((grid_rows, width), BF16),
             VMEM((grid_rows * (width // LANES), LANES), F32),
             VMEM((CHUNK_BLOCKS * g2m_send.shape[1] * (width // LANES), LANES), F32),
             VMEM((CHUNK_BLOCKS * g2m_send.shape[1] * (width // LANES), LANES), F32),

time: 46 us -> 47.2 us (1.026)
  Pallas kernels: 18.2 us -> 19.4 us
    pallas_call x1, Pallas kernels: 10.9 us -> 12.1 us  [per_device(): call(edge_kernel, (shape(owned, width, kind=F32), shape(owned, width), sh...]
  transfers between devices with their start and end apart: 4 -> 4, of which waited for: 2 -> 2; matrix products, arithmetic and copies ran while one was open for 0% -> 0% of each run, Pallas kernels for 32% -> 34%
where the time goes in v23:
time: 47.2 us; the launch traced here: 46.9 us
  Pallas kernels  19.4 us (41%)
  starting transfers between devices  18.3 us (39%)
  waiting for transfers between devices  6.83 us (14%)
  local copies, waits for them, and re-layouts  1.41 us (3%)
  between operations  0.94 us (2%)
    pallas_call x1, Pallas kernels, per_device(): call(edge_kernel, (shape(owned, width, kind=F32), shape(owned, width), sh...  12.1 us
    all_to_all x1, starting transfers between devices, per_device(): lax.all_to_all(jnp.tile(mesh_send, (devices, 1)), 'bulk', 0, 0, tiled=True)  7.39 us
    all_to_all x1, starting transfers between devices, per_device(): piece = lax.all_to_all(rows, 'bulk', 0, 0, tiled=True)  6.8 us
    all_to_all x1, waiting for transfers between devices, per_device(): piece = lax.all_to_all(rows, 'bulk', 0, 0, tiled=True)  6.71 us
    ppermute x1, starting transfers between devices, per_device(): from_chip = lax.ppermute(chip, 'bulk', both(within))  3.35 us
    pallas_call x1, Pallas kernels, per_device(): call(functools.partial(wanted_kernel, owned), shape(edges, places), [VMEM...  2.53 us
    pallas_call x1, Pallas kernels, per_device(): call(message_kernel, shape(owned, width), [VMEM] * 10, flops=1000000000,...  1.77 us
    pallas_call x1, Pallas kernels, per_device(): call(node_kernel, (shape(owned, width), shape(places, width)), [VMEM] * 1...  1.63 us
  transfers between devices with their start and end apart: 4, of which 2 were waited for; matrix products, arithmetic and copies ran while one was open for 0% of the time, Pallas kernels for 34%

profile of v23, /device:TPU:0, one launch (start us, length us, event | category | flops | bytes accessed | tf_op | source)
XLA Modules:
  0.0 46.9 jit_solution(9627297412181973971)
XLA Ops:
  0.0 1.3 %tile.2 = s32[16,4,128]{2,1,0:T(4,128)} broadcast(s32[4,128]{1,0:T(4,128)} %send_ref), dimensions={1,2} | broadcast | bytes 34816 | tf_op jit(solution)/shard_map/tile | solution.py:484
  1.3 7.4 %all-to-all-start = ((s32[16,4,128]{2,1,0:T(4,128)}), s32[16,4,128]{2,1,0:T(4,128)S(1)}, u32[]{:S(2)}, u32[]{:S(2)}) async-start(s32[16,4,128]{2,1,0:T(4,128)} %tile.2), calls=%async_computation | async-start | bytes 65536 | tf_op jit(solution)/shard_map/all_to_all | solution.py:484
  9.3 0.0 copy-start.2
  9.4 0.0 copy-start.5
  9.4 0.0 copy-start.7
  9.4 0.0 copy-start.11
  9.4 0.0 copy-start.12
  9.4 0.0 copy-start.3
  9.4 12.1 %shard_map.262 = (f32[64,512]{1,0:T(8,128)S(1)}, bf16[64,512]{1,0:T(8,128)(2,1)S(1)}, bf16[64,512]{1,0:T(8,128)(2,1)S(1)}) custom-call(s32[1]{0:T(128)} %bitcast.1.place_ref, bf16[474,512]{1,0:T(8,128)(2,1)} %first_hbm.1, bf16[474,2048]{1,0:T(8,128)(2,1)} %bitcast.26, bf16[512,512]{1,0:T(8,128)(2,1)} %second_hbm.1, bf16[512,512]{1,0:T(8,128)(2,1)} %send_weight_hbm.1, ...), custom_call_target="tpu_custom_call" | custom-call | flops 10000000000 | bytes 4000000 | tf_op jit(solution)/shard_map/pallas_call | solution.py:499
  21.5 0.0 copy-start
  21.5 0.0 copy-start.1
  21.6 0.8 %collective-permute-start = (bf16[64,512]{1,0:T(8,128)(2,1)S(1)}, bf16[64,512]{1,0:T(8,128)(2,1)S(1)}, u32[]{:S(2)}, u32[]{:S(2)}) collective-permute-start(bf16[64,512]{1,0:T(8,128)(2,1)S(1)} %get-tuple-element.21), channel_id=1, source_target_pairs={{1,2},{3,4},{5,6},{7,8},{9,10},{11,12},{13,14},{2,1},{4,3},{6,5},{... | collective-permute-start | bytes 196616 | tf_op jit(solution)/shard_map/ppermute | solution.py:525
  22.4 3.3 %collective-permute-start.1 = (bf16[64,512]{1,0:T(8,128)(2,1)S(1)}, bf16[64,512]{1,0:T(8,128)(2,1)S(1)}, u32[]{:S(2)}, u32[]{:S(2)}) collective-permute-start(bf16[64,512]{1,0:T(8,128)(2,1)S(1)} %get-tuple-element.22), channel_id=1, source_target_pairs={{0,1},{2,3},{4,5},{6,7},{8,9},{10,11},{12,13},{14,15},{1,0},{3,2},... | collective-permute-start | bytes 196616 | tf_op jit(solution)/shard_map/ppermute | solution.py:526
  25.7 0.0 all-to-all-done
  25.7 0.0 copy-done.2
  25.7 0.0 copy-done.5
  25.7 0.0 copy-done.7
  25.7 0.0 copy-done.11
  25.7 0.0 copy-done.12
  25.7 0.0 copy-start.4
  25.8 0.7 %shard_map.263 = (bf16[256,64]{1,0:T(8,128)(2,1)S(1)}, f32[64,512]{1,0:T(8,128)S(1)}, bf16[512,512]{1,0:T(8,128)(2,1)S(1)}) custom-call(s32[1]{0:T(128)} %bitcast.1.place_ref, s32[1,1024]{1,0:T(1,128)S(1)} %bitcast.19, s32[64,128]{1,0:T(8,128)S(1)} %bitcast.16, bf16[64,512]{1,0:T(8,128)(2,1)S(1)} %copy-done.2, bf16[512,512]{1,0:T(8,128)(2,1)S(1)} %copy-done.7, ...), custom_call_target="tpu_custom_call" | custom-call | flops 500000000 | bytes 500000 | tf_op jit(solution)/shard_map/pallas_call | solution.py:527
  26.5 0.0 collective-permute-done.from_cross_ref
  26.5 0.1 collective-permute-done.1.from_chip_ref
  26.6 0.0 copy-done.3
  26.6 0.0 copy-done
  26.6 0.0 copy-done.1
  26.6 1.6 %shard_map.264 = (bf16[64,512]{1,0:T(8,128)(2,1)S(1)}, bf16[256,512]{1,0:T(8,128)(2,1)}) custom-call(f32[64,512]{1,0:T(8,128)S(1)} %get-tuple-element.20.own_ref, bf16[64,512]{1,0:T(8,128)(2,1)S(1)} %collective-permute-done.from_cross_ref, bf16[64,512]{1,0:T(8,128)(2,1)S(1)} %collective-permute-done.1.from_chip_ref, bf16[64,512]{1,0:T(8,128)(2,1)S(1)} %copy-done.2, ...), custom_call_target="tpu_custom_call" | custom-call | flops 500000000 | bytes 4000000 | tf_op jit(solution)/shard_map/pallas_call | solution.py:534
  28.2 6.8 %all-to-all-start.1 = ((bf16[16,16,512]{2,1,0:T(8,128)(2,1)}), bf16[16,16,512]{2,1,0:T(8,128)(2,1)S(1)}, u32[]{:S(2)}, u32[]{:S(2)}) async-start(bf16[16,16,512]{2,1,0:T(8,128)(2,1)} %bitcast.9), calls=%async_computation.1 | async-start | bytes 524288 | tf_op jit(solution)/shard_map/all_to_all | solution.py:552
  35.0 0.0 copy-start.6
  35.1 0.0 copy-start.8
  35.1 0.0 copy-start.9
  35.1 0.0 copy-start.13
  35.1 0.0 copy-start.14
  35.1 0.0 copy-start.15
  35.1 0.0 copy-done.4
  35.1 2.5 %shard_map.265.wanted_ref = bf16[512,256]{1,0:T(8,128)(2,1)S(1)} custom-call(s32[1,1024]{1,0:T(1,128)S(1)} %bitcast.20, s32[4,128]{1,0:T(4,128)S(1)} %copy-done.4), custom_call_target="tpu_custom_call" | custom-call | flops 1000000000 | bytes 500000 | tf_op jit(solution)/shard_map/pallas_call | solution.py:554
  37.7 0.0 copy-start.10
  37.7 0.0 copy-start.16
  37.7 0.0 copy-done.6
  37.7 0.0 copy-done.8
  37.7 0.0 copy-done.9
  37.7 0.0 copy-done.13
  37.7 0.0 copy-done.14
  37.7 0.0 copy-done.15
  37.8 0.6 %shard_map.266 = (bf16[64,512]{1,0:T(8,128)(2,1)S(1)}, bf16[512,128]{1,0:T(8,128)(2,1)S(1)}, bf16[128,512]{1,0:T(8,128)(2,1)S(1)}, f32[64,512]{1,0:T(8,128)S(1)}, bf16[512,512]{1,0:T(8,128)(2,1)S(1)}) custom-call(s32[1]{0:T(128)} %bitcast.1.place_ref, s32[1,1024]{1,0:T(1,128)S(1)} %bitcast.21, s32[4,128]{1,0:T(4,128)S(1)} %copy-done.13, ...), custom_call_target="tpu_custom_call" | custom-call | flops 1000000000 | bytes 4000000 | tf_op jit(solution)/shard_map/pallas_call | solution.py:561
  38.4 6.7 %all-to-all-done.1 = bf16[16,16,512]{2,1,0:T(8,128)(2,1)S(1)} async-done(((bf16[16,16,512]{2,1,0:T(8,128)(2,1)}), bf16[16,16,512]{2,1,0:T(8,128)(2,1)S(1)}, u32[]{:S(2)}, u32[]{:S(2)}) %all-to-all-start.1) | async-done | bytes 262176 | tf_op jit(solution)/shard_map/all_to_all | solution.py:552
  45.1 0.0 copy-done.10
  45.1 0.0 copy-done.16
  45.1 1.8 %shard_map.267 = bf16[64,512]{1,0:T(8,128)(2,1)} custom-call(bf16[512,256]{1,0:T(8,128)(2,1)S(1)} %shard_map.265.wanted_ref, bf16[256,512]{1,0:T(8,128)(2,1)S(1)} %bitcast.15, bf16[64,512]{1,0:T(8,128)(2,1)S(1)} %get-tuple-element.30.incoming_ref, bf16[512,128]{1,0:T(8,128)(2,1)S(1)} %get-tuple-element.31.pick_ref, ...), custom_call_target="tpu_custom_call" | custom-call | flops 1000000000 | bytes 4000000 | tf_op jit(solution)/shard_map/pallas_call | solution.py:584
Async XLA Ops:
  1.3 24.4 %all-to-all-start = ((s32[16,4,128]{2,1,0:T(4,128)}), s32[16,4,128]{2,1,0:T(4,128)S(1)}, u32[]{:S(2)}, u32[]{:S(2)}) async-start(s32[16,4,128]{2,1,0:T(4,128)} %tile.2), calls=%async_computation | async-start | bytes 65536 | tf_op jit(solution)/shard_map/all_to_all | solution.py:484
  9.3 16.4 %copy-start.2 = (bf16[64,512]{1,0:T(8,128)(2,1)S(1)}, bf16[64,512]{1,0:T(8,128)(2,1)}, u32[]{:S(2)}) copy-start(bf16[64,512]{1,0:T(8,128)(2,1)} %latent_ref.3) | copy-start | bytes 196612
  9.4 16.4 %copy-start.5 = (bf16[1024,512]{1,0:T(8,128)(2,1)S(1)}, bf16[1024,512]{1,0:T(8,128)(2,1)}, u32[]{:S(2)}) copy-start(bf16[1024,512]{1,0:T(8,128)(2,1)} %node_input_ref.1) | copy-start | bytes 3145732
  9.4 16.3 %copy-start.7 = (bf16[512,512]{1,0:T(8,128)(2,1)S(1)}, bf16[512,512]{1,0:T(8,128)(2,1)}, u32[]{:S(2)}) copy-start(bf16[512,512]{1,0:T(8,128)(2,1)} %edge_out_ref.1) | copy-start | bytes 1572868
  9.4 16.3 %copy-start.11 = (s32[1024]{0:T(1024)S(1)}, s32[1024]{0:T(1024)}, u32[]{:S(2)}) copy-start(s32[1024]{0:T(1024)} %param.53) | copy-start | bytes 12292
  9.4 16.3 %copy-start.12 = (f32[512]{0:T(512)S(1)}, f32[512]{0:T(512)}, u32[]{:S(2)}) copy-start(f32[512]{0:T(512)} %param.37) | copy-start | bytes 6148
  9.4 17.2 %copy-start.3 = (f32[512]{0:T(512)S(1)}, f32[512]{0:T(512)}, u32[]{:S(2)}) copy-start(f32[512]{0:T(512)} %param.39) | copy-start | bytes 6148
  21.5 5.1 %copy-start = (bf16[512,512]{1,0:T(8,128)(2,1)S(1)}, bf16[512,512]{1,0:T(8,128)(2,1)}, u32[]{:S(2)}) copy-start(bf16[512,512]{1,0:T(8,128)(2,1)} %node_out_ref.1) | copy-start | bytes 1572868
  21.5 5.1 %copy-start.1 = (bf16[512,512]{1,0:T(8,128)(2,1)S(1)}, bf16[512,512]{1,0:T(8,128)(2,1)}, u32[]{:S(2)}) copy-start(bf16[512,512]{1,0:T(8,128)(2,1)} %mesh_sender_ref.1) | copy-start | bytes 1572868
  21.6 4.9 %collective-permute-start = (bf16[64,512]{1,0:T(8,128)(2,1)S(1)}, bf16[64,512]{1,0:T(8,128)(2,1)S(1)}, u32[]{:S(2)}, u32[]{:S(2)}) collective-permute-start(bf16[64,512]{1,0:T(8,128)(2,1)S(1)} %get-tuple-element.21), channel_id=1, source_target_pairs={{1,2},{3,4},{5,6},{7,8},{9,10},{11,12},{13,14},{2,1},{4,3},{6,5},{... | collective-permute-start | bytes 196616 | tf_op jit(solution)/shard_map/ppermute | solution.py:525
  22.4 4.2 %collective-permute-start.1 = (bf16[64,512]{1,0:T(8,128)(2,1)S(1)}, bf16[64,512]{1,0:T(8,128)(2,1)S(1)}, u32[]{:S(2)}, u32[]{:S(2)}) collective-permute-start(bf16[64,512]{1,0:T(8,128)(2,1)S(1)} %get-tuple-element.22), channel_id=1, source_target_pairs={{0,1},{2,3},{4,5},{6,7},{8,9},{10,11},{12,13},{14,15},{1,0},{3,2},... | collective-permute-start | bytes 196616 | tf_op jit(solution)/shard_map/ppermute | solution.py:526
  25.7 9.4 %copy-start.4 = (s32[4,128]{1,0:T(4,128)S(1)}, s32[4,128]{1,0:T(4,128)}, u32[]{:S(2)}) copy-start(s32[4,128]{1,0:T(4,128)} %send_ref) | copy-start | bytes 6148
  28.2 16.9 %all-to-all-start.1 = ((bf16[16,16,512]{2,1,0:T(8,128)(2,1)}), bf16[16,16,512]{2,1,0:T(8,128)(2,1)S(1)}, u32[]{:S(2)}, u32[]{:S(2)}) async-start(bf16[16,16,512]{2,1,0:T(8,128)(2,1)} %bitcast.9), calls=%async_computation.1 | async-start | bytes 524288 | tf_op jit(solution)/shard_map/all_to_all | solution.py:552
  35.0 2.6 %copy-start.6 = (bf16[1024,512]{1,0:T(8,128)(2,1)S(1)}, bf16[1024,512]{1,0:T(8,128)(2,1)}, u32[]{:S(2)}) copy-start(bf16[1024,512]{1,0:T(8,128)(2,1)} %update_input_ref.1) | copy-start | bytes 3145732
  35.1 2.6 %copy-start.8 = (bf16[512,512]{1,0:T(8,128)(2,1)S(1)}, bf16[512,512]{1,0:T(8,128)(2,1)}, u32[]{:S(2)}) copy-start(bf16[512,512]{1,0:T(8,128)(2,1)} %mesh_receiver_ref.1) | copy-start | bytes 1572868
  35.1 2.6 %copy-start.9 = (bf16[512,512]{1,0:T(8,128)(2,1)S(1)}, bf16[512,512]{1,0:T(8,128)(2,1)}, u32[]{:S(2)}) copy-start(bf16[512,512]{1,0:T(8,128)(2,1)} %message_out_ref.1) | copy-start | bytes 1572868
  35.1 2.6 %copy-start.13 = (s32[4,128]{1,0:T(4,128)S(1)}, s32[4,128]{1,0:T(4,128)}, u32[]{:S(2)}) copy-start(s32[4,128]{1,0:T(4,128)} %recv_ref.1) | copy-start | bytes 6148
  35.1 2.6 %copy-start.14 = (f32[512]{0:T(512)S(1)}, f32[512]{0:T(512)}, u32[]{:S(2)}) copy-start(f32[512]{0:T(512)} %param.42) | copy-start | bytes 6148
  35.1 2.6 %copy-start.15 = (f32[512]{0:T(512)S(1)}, f32[512]{0:T(512)}, u32[]{:S(2)}) copy-start(f32[512]{0:T(512)} %param.45) | copy-start | bytes 6148
  37.7 7.4 %copy-start.10 = (bf16[512,512]{1,0:T(8,128)(2,1)S(1)}, bf16[512,512]{1,0:T(8,128)(2,1)}, u32[]{:S(2)}) copy-start(bf16[512,512]{1,0:T(8,128)(2,1)} %update_out_ref.1) | copy-start | bytes 1572868
  37.7 7.4 %copy-start.16 = (f32[512]{0:T(512)S(1)}, f32[512]{0:T(512)}, u32[]{:S(2)}) copy-start(f32[512]{0:T(512)} %param.47) | copy-start | bytes 6148

commit v24 on v18

--- a/solution.py
+++ b/solution.py
@@ -197,7 +197,7 @@
     feat_weight = feat_weight.astype(BF16)
     group = CHUNK_BLOCKS
     chunks = blocks // group
-    part_rows = 64
+    part_rows = 128
 
     def gather(chunk, edges, target):
         for edge in edges:

time: 46 us -> 46 us (level)
  no operation moved by 1% of the time
where the time goes in v24:
time: 46 us; the launch traced here: 45.7 us
  starting transfers between devices  18.3 us (40%)
  Pallas kernels  18.2 us (40%)
  waiting for transfers between devices  6.83 us (15%)
  local copies, waits for them, and re-layouts  1.41 us (3%)
  between operations  0.94 us (2%)
    pallas_call x1, Pallas kernels, per_device(): call(edge_kernel, (shape(owned, width, kind=F32), shape(owned, width), sh...  10.9 us
    all_to_all x1, starting transfers between devices, per_device(): lax.all_to_all(jnp.tile(mesh_send, (devices, 1)), 'bulk', 0, 0, tiled=True)  7.39 us
    all_to_all x1, starting transfers between devices, per_device(): piece = lax.all_to_all(rows, 'bulk', 0, 0, tiled=True)  6.79 us
    all_to_all x1, waiting for transfers between devices, per_device(): piece = lax.all_to_all(rows, 'bulk', 0, 0, tiled=True)  6.71 us
    ppermute x1, starting transfers between devices, per_device(): from_chip = lax.ppermute(chip, 'bulk', both(within))  3.35 us
    pallas_call x1, Pallas kernels, per_device(): call(functools.partial(wanted_kernel, owned), shape(edges, places), [VMEM...  2.53 us
    pallas_call x1, Pallas kernels, per_device(): call(message_kernel, shape(owned, width), [VMEM] * 10, flops=1000000000,...  1.77 us
    pallas_call x1, Pallas kernels, per_device(): call(node_kernel, (shape(owned, width), shape(places, width)), [VMEM] * 1...  1.63 us
  transfers between devices with their start and end apart: 4, of which 2 were waited for; matrix products, arithmetic and copies ran while one was open for 0% of the time, Pallas kernels for 32%

profile of v24, /device:TPU:0, one launch (start us, length us, event | category | flops | bytes accessed | tf_op | source)
XLA Modules:
  0.0 45.7 jit_solution(10195695876705755010)
XLA Ops:
  0.0 1.3 %tile.2 = s32[16,4,128]{2,1,0:T(4,128)} broadcast(s32[4,128]{1,0:T(4,128)} %send_ref), dimensions={1,2} | broadcast | bytes 34816 | tf_op jit(solution)/shard_map/tile | solution.py:468
  1.3 7.4 %all-to-all-start = ((s32[16,4,128]{2,1,0:T(4,128)}), s32[16,4,128]{2,1,0:T(4,128)S(1)}, u32[]{:S(2)}, u32[]{:S(2)}) async-start(s32[16,4,128]{2,1,0:T(4,128)} %tile.2), calls=%async_computation | async-start | bytes 65536 | tf_op jit(solution)/shard_map/all_to_all | solution.py:468
  9.3 0.0 copy-start.2
  9.4 0.0 copy-start.5
  9.4 0.0 copy-start.7
  9.4 0.0 copy-start.11
  9.4 0.0 copy-start.12
  9.4 0.0 copy-start.3
  9.4 10.9 %shard_map.262 = (f32[64,512]{1,0:T(8,128)S(1)}, bf16[64,512]{1,0:T(8,128)(2,1)S(1)}, bf16[64,512]{1,0:T(8,128)(2,1)S(1)}) custom-call(s32[1]{0:T(128)} %bitcast.1.place_ref, bf16[474,512]{1,0:T(8,128)(2,1)} %first_hbm.1, bf16[474,2048]{1,0:T(8,128)(2,1)} %bitcast.26, bf16[512,512]{1,0:T(8,128)(2,1)} %second_hbm.1, bf16[512,512]{1,0:T(8,128)(2,1)} %send_weight_hbm.1, ...), custom_call_target="tpu_custom_call" | custom-call | flops 10000000000 | bytes 4000000 | tf_op jit(solution)/shard_map/pallas_call | solution.py:483
  20.3 0.0 copy-start
  20.4 0.0 copy-start.1
  20.4 0.8 %collective-permute-start = (bf16[64,512]{1,0:T(8,128)(2,1)S(1)}, bf16[64,512]{1,0:T(8,128)(2,1)S(1)}, u32[]{:S(2)}, u32[]{:S(2)}) collective-permute-start(bf16[64,512]{1,0:T(8,128)(2,1)S(1)} %get-tuple-element.21), channel_id=1, source_target_pairs={{1,2},{3,4},{5,6},{7,8},{9,10},{11,12},{13,14},{2,1},{4,3},{6,5},{... | collective-permute-start | bytes 196616 | tf_op jit(solution)/shard_map/ppermute | solution.py:507
  21.2 3.3 %collective-permute-start.1 = (bf16[64,512]{1,0:T(8,128)(2,1)S(1)}, bf16[64,512]{1,0:T(8,128)(2,1)S(1)}, u32[]{:S(2)}, u32[]{:S(2)}) collective-permute-start(bf16[64,512]{1,0:T(8,128)(2,1)S(1)} %get-tuple-element.22), channel_id=1, source_target_pairs={{0,1},{2,3},{4,5},{6,7},{8,9},{10,11},{12,13},{14,15},{1,0},{3,2},... | collective-permute-start | bytes 196616 | tf_op jit(solution)/shard_map/ppermute | solution.py:508
  24.5 0.0 all-to-all-done
  24.5 0.0 copy-done.2
  24.5 0.0 copy-done.5
  24.5 0.0 copy-done.7
  24.5 0.0 copy-done.11
  24.6 0.0 copy-done.12
  24.6 0.0 copy-start.4
  24.6 0.7 %shard_map.263 = (bf16[256,64]{1,0:T(8,128)(2,1)S(1)}, f32[64,512]{1,0:T(8,128)S(1)}, bf16[512,512]{1,0:T(8,128)(2,1)S(1)}) custom-call(s32[1]{0:T(128)} %bitcast.1.place_ref, s32[1,1024]{1,0:T(1,128)S(1)} %bitcast.19, s32[64,128]{1,0:T(8,128)S(1)} %bitcast.16, bf16[64,512]{1,0:T(8,128)(2,1)S(1)} %copy-done.2, bf16[512,512]{1,0:T(8,128)(2,1)S(1)} %copy-done.7, ...), custom_call_target="tpu_custom_call" | custom-call | flops 500000000 | bytes 500000 | tf_op jit(solution)/shard_map/pallas_call | solution.py:509
  25.3 0.0 collective-permute-done.from_cross_ref
  25.3 0.1 collective-permute-done.1.from_chip_ref
  25.4 0.0 copy-done.3
  25.4 0.0 copy-done
  25.4 0.0 copy-done.1
  25.4 1.6 %shard_map.264 = (bf16[64,512]{1,0:T(8,128)(2,1)S(1)}, bf16[256,512]{1,0:T(8,128)(2,1)}) custom-call(f32[64,512]{1,0:T(8,128)S(1)} %get-tuple-element.20.own_ref, bf16[64,512]{1,0:T(8,128)(2,1)S(1)} %collective-permute-done.from_cross_ref, bf16[64,512]{1,0:T(8,128)(2,1)S(1)} %collective-permute-done.1.from_chip_ref, bf16[64,512]{1,0:T(8,128)(2,1)S(1)} %copy-done.2, ...), custom_call_target="tpu_custom_call" | custom-call | flops 500000000 | bytes 4000000 | tf_op jit(solution)/shard_map/pallas_call | solution.py:516
  27.1 6.8 %all-to-all-start.1 = ((bf16[16,16,512]{2,1,0:T(8,128)(2,1)}), bf16[16,16,512]{2,1,0:T(8,128)(2,1)S(1)}, u32[]{:S(2)}, u32[]{:S(2)}) async-start(bf16[16,16,512]{2,1,0:T(8,128)(2,1)} %bitcast.9), calls=%async_computation.1 | async-start | bytes 524288 | tf_op jit(solution)/shard_map/all_to_all | solution.py:534
  33.9 0.0 copy-start.6
  33.9 0.0 copy-start.8
  33.9 0.0 copy-start.9
  33.9 0.0 copy-start.13
  33.9 0.0 copy-start.14
  33.9 0.0 copy-start.15
  33.9 0.0 copy-done.4
  33.9 2.5 %shard_map.265.wanted_ref = bf16[512,256]{1,0:T(8,128)(2,1)S(1)} custom-call(s32[1,1024]{1,0:T(1,128)S(1)} %bitcast.20, s32[4,128]{1,0:T(4,128)S(1)} %copy-done.4), custom_call_target="tpu_custom_call" | custom-call | flops 1000000000 | bytes 500000 | tf_op jit(solution)/shard_map/pallas_call | solution.py:536
  36.5 0.0 copy-start.10
  36.5 0.0 copy-start.16
  36.5 0.0 copy-done.6
  36.5 0.0 copy-done.8
  36.5 0.0 copy-done.9
  36.5 0.0 copy-done.13
  36.5 0.0 copy-done.14
  36.6 0.0 copy-done.15
  36.6 0.6 %shard_map.266 = (bf16[64,512]{1,0:T(8,128)(2,1)S(1)}, bf16[512,128]{1,0:T(8,128)(2,1)S(1)}, bf16[128,512]{1,0:T(8,128)(2,1)S(1)}, f32[64,512]{1,0:T(8,128)S(1)}, bf16[512,512]{1,0:T(8,128)(2,1)S(1)}) custom-call(s32[1]{0:T(128)} %bitcast.1.place_ref, s32[1,1024]{1,0:T(1,128)S(1)} %bitcast.21, s32[4,128]{1,0:T(4,128)S(1)} %copy-done.13, ...), custom_call_target="tpu_custom_call" | custom-call | flops 1000000000 | bytes 4000000 | tf_op jit(solution)/shard_map/pallas_call | solution.py:543
  37.2 6.7 %all-to-all-done.1 = bf16[16,16,512]{2,1,0:T(8,128)(2,1)S(1)} async-done(((bf16[16,16,512]{2,1,0:T(8,128)(2,1)}), bf16[16,16,512]{2,1,0:T(8,128)(2,1)S(1)}, u32[]{:S(2)}, u32[]{:S(2)}) %all-to-all-start.1) | async-done | bytes 262176 | tf_op jit(solution)/shard_map/all_to_all | solution.py:534
  43.9 0.0 copy-done.10
  43.9 0.0 copy-done.16
  43.9 1.8 %shard_map.267 = bf16[64,512]{1,0:T(8,128)(2,1)} custom-call(bf16[512,256]{1,0:T(8,128)(2,1)S(1)} %shard_map.265.wanted_ref, bf16[256,512]{1,0:T(8,128)(2,1)S(1)} %bitcast.15, bf16[64,512]{1,0:T(8,128)(2,1)S(1)} %get-tuple-element.30.incoming_ref, bf16[512,128]{1,0:T(8,128)(2,1)S(1)} %get-tuple-element.31.pick_ref, ...), custom_call_target="tpu_custom_call" | custom-call | flops 1000000000 | bytes 4000000 | tf_op jit(solution)/shard_map/pallas_call | solution.py:566
Async XLA Ops:
  1.3 23.2 %all-to-all-start = ((s32[16,4,128]{2,1,0:T(4,128)}), s32[16,4,128]{2,1,0:T(4,128)S(1)}, u32[]{:S(2)}, u32[]{:S(2)}) async-start(s32[16,4,128]{2,1,0:T(4,128)} %tile.2), calls=%async_computation | async-start | bytes 65536 | tf_op jit(solution)/shard_map/all_to_all | solution.py:468
  9.3 15.2 %copy-start.2 = (bf16[64,512]{1,0:T(8,128)(2,1)S(1)}, bf16[64,512]{1,0:T(8,128)(2,1)}, u32[]{:S(2)}) copy-start(bf16[64,512]{1,0:T(8,128)(2,1)} %latent_ref.3) | copy-start | bytes 196612
  9.4 15.2 %copy-start.5 = (bf16[1024,512]{1,0:T(8,128)(2,1)S(1)}, bf16[1024,512]{1,0:T(8,128)(2,1)}, u32[]{:S(2)}) copy-start(bf16[1024,512]{1,0:T(8,128)(2,1)} %node_input_ref.1) | copy-start | bytes 3145732
  9.4 15.2 %copy-start.7 = (bf16[512,512]{1,0:T(8,128)(2,1)S(1)}, bf16[512,512]{1,0:T(8,128)(2,1)}, u32[]{:S(2)}) copy-start(bf16[512,512]{1,0:T(8,128)(2,1)} %edge_out_ref.1) | copy-start | bytes 1572868
  9.4 15.2 %copy-start.11 = (s32[1024]{0:T(1024)S(1)}, s32[1024]{0:T(1024)}, u32[]{:S(2)}) copy-start(s32[1024]{0:T(1024)} %param.53) | copy-start | bytes 12292
  9.4 15.2 %copy-start.12 = (f32[512]{0:T(512)S(1)}, f32[512]{0:T(512)}, u32[]{:S(2)}) copy-start(f32[512]{0:T(512)} %param.37) | copy-start | bytes 6148
  9.4 16.0 %copy-start.3 = (f32[512]{0:T(512)S(1)}, f32[512]{0:T(512)}, u32[]{:S(2)}) copy-start(f32[512]{0:T(512)} %param.39) | copy-start | bytes 6148
  20.3 5.1 %copy-start = (bf16[512,512]{1,0:T(8,128)(2,1)S(1)}, bf16[512,512]{1,0:T(8,128)(2,1)}, u32[]{:S(2)}) copy-start(bf16[512,512]{1,0:T(8,128)(2,1)} %node_out_ref.1) | copy-start | bytes 1572868
  20.4 5.1 %copy-start.1 = (bf16[512,512]{1,0:T(8,128)(2,1)S(1)}, bf16[512,512]{1,0:T(8,128)(2,1)}, u32[]{:S(2)}) copy-start(bf16[512,512]{1,0:T(8,128)(2,1)} %mesh_sender_ref.1) | copy-start | bytes 1572868
  20.4 4.9 %collective-permute-start = (bf16[64,512]{1,0:T(8,128)(2,1)S(1)}, bf16[64,512]{1,0:T(8,128)(2,1)S(1)}, u32[]{:S(2)}, u32[]{:S(2)}) collective-permute-start(bf16[64,512]{1,0:T(8,128)(2,1)S(1)} %get-tuple-element.21), channel_id=1, source_target_pairs={{1,2},{3,4},{5,6},{7,8},{9,10},{11,12},{13,14},{2,1},{4,3},{6,5},{... | collective-permute-start | bytes 196616 | tf_op jit(solution)/shard_map/ppermute | solution.py:507
  21.2 4.2 %collective-permute-start.1 = (bf16[64,512]{1,0:T(8,128)(2,1)S(1)}, bf16[64,512]{1,0:T(8,128)(2,1)S(1)}, u32[]{:S(2)}, u32[]{:S(2)}) collective-permute-start(bf16[64,512]{1,0:T(8,128)(2,1)S(1)} %get-tuple-element.22), channel_id=1, source_target_pairs={{0,1},{2,3},{4,5},{6,7},{8,9},{10,11},{12,13},{14,15},{1,0},{3,2},... | collective-permute-start | bytes 196616 | tf_op jit(solution)/shard_map/ppermute | solution.py:508
  24.6 9.4 %copy-start.4 = (s32[4,128]{1,0:T(4,128)S(1)}, s32[4,128]{1,0:T(4,128)}, u32[]{:S(2)}) copy-start(s32[4,128]{1,0:T(4,128)} %send_ref) | copy-start | bytes 6148
  27.1 16.8 %all-to-all-start.1 = ((bf16[16,16,512]{2,1,0:T(8,128)(2,1)}), bf16[16,16,512]{2,1,0:T(8,128)(2,1)S(1)}, u32[]{:S(2)}, u32[]{:S(2)}) async-start(bf16[16,16,512]{2,1,0:T(8,128)(2,1)} %bitcast.9), calls=%async_computation.1 | async-start | bytes 524288 | tf_op jit(solution)/shard_map/all_to_all | solution.py:534
  33.9 2.7 %copy-start.6 = (bf16[1024,512]{1,0:T(8,128)(2,1)S(1)}, bf16[1024,512]{1,0:T(8,128)(2,1)}, u32[]{:S(2)}) copy-start(bf16[1024,512]{1,0:T(8,128)(2,1)} %update_input_ref.1) | copy-start | bytes 3145732
  33.9 2.6 %copy-start.8 = (bf16[512,512]{1,0:T(8,128)(2,1)S(1)}, bf16[512,512]{1,0:T(8,128)(2,1)}, u32[]{:S(2)}) copy-start(bf16[512,512]{1,0:T(8,128)(2,1)} %mesh_receiver_ref.1) | copy-start | bytes 1572868
  33.9 2.6 %copy-start.9 = (bf16[512,512]{1,0:T(8,128)(2,1)S(1)}, bf16[512,512]{1,0:T(8,128)(2,1)}, u32[]{:S(2)}) copy-start(bf16[512,512]{1,0:T(8,128)(2,1)} %message_out_ref.1) | copy-start | bytes 1572868
  33.9 2.6 %copy-start.13 = (s32[4,128]{1,0:T(4,128)S(1)}, s32[4,128]{1,0:T(4,128)}, u32[]{:S(2)}) copy-start(s32[4,128]{1,0:T(4,128)} %recv_ref.1) | copy-start | bytes 6148
  33.9 2.6 %copy-start.14 = (f32[512]{0:T(512)S(1)}, f32[512]{0:T(512)}, u32[]{:S(2)}) copy-start(f32[512]{0:T(512)} %param.42) | copy-start | bytes 6148
  33.9 2.6 %copy-start.15 = (f32[512]{0:T(512)S(1)}, f32[512]{0:T(512)}, u32[]{:S(2)}) copy-start(f32[512]{0:T(512)} %param.45) | copy-start | bytes 6148
  36.5 7.4 %copy-start.10 = (bf16[512,512]{1,0:T(8,128)(2,1)S(1)}, bf16[512,512]{1,0:T(8,128)(2,1)}, u32[]{:S(2)}) copy-start(bf16[512,512]{1,0:T(8,128)(2,1)} %update_out_ref.1) | copy-start | bytes 1572868
  36.5 7.4 %copy-start.16 = (f32[512]{0:T(512)S(1)}, f32[512]{0:T(512)}, u32[]{:S(2)}) copy-start(f32[512]{0:T(512)} %param.47) | copy-start | bytes 6148
